TPU v7x, 32 devices: a whole 2x2x4 slice. The times are simulated.
32 devices in a mesh: section: 2 (over core), inner: 4 (over y, x), outer: 4 (over z).
Axes of the slice: x: 2, y: 2, z: 4, core: 2. Of those that a mesh axis runs over, the one named last changes fastest.
Arguments:
- hidden_in: bfloat16 [128, 128, 768], P(('inner', 'outer')), may hold values from -6 to 6
- caption_len: int32 [128], P(('inner', 'outer')), may hold values from 1 to 28, as said below
- region_len: int32 [128], P(('inner', 'outer')), may hold values from 10 to 100, as said below
- cotangent: bfloat16 [128, 128, 768], P(('inner', 'outer')), may hold values from -6 to 6
- w_qkv: bfloat16 [2, 768, 2304], P('section'), may hold values from -0.21875 to 0.21875
- b_qv: float32 [2, 2, 768], P('section'), may hold values from -3 to 3
- w_out: bfloat16 [2, 768, 768], P('section'), may hold values from -1.75 to 1.75
- b_out: float32 [2, 768], P('section'), may hold values from -3 to 3
- ln_gain: float32 [2, 2, 768], P('section'), may hold values from 0.5 to 1.5
- ln_bias: float32 [2, 2, 768], P('section'), may hold values from -2 to 2
- w_up: bfloat16 [2, 768, 3072], P('section'), may hold values from -0.21875 to 0.21875
- b_up: float32 [2, 3072], P('section'), may hold values from -3 to 3
- w_down: bfloat16 [2, 3072, 768], P('section'), may hold values from -0.109375 to 0.109375
- b_down: float32 [2, 768], P('section'), may hold values from -3 to 3
Outputs:
- activations: bfloat16 [2, 128, 128, 768], P('section', ('inner', 'outer'))
- input_grads: float32 [2, 128, 128, 768], P('section', ('inner', 'outer'))
- grad_w_qkv: float32 [2, 768, 2304], P('section', 'inner')
- grad_b_qv: float32 [2, 2, 768], P('section', None, 'inner')
- grad_w_out: float32 [2, 768, 768], P('section', 'inner')
- grad_b_out: float32 [2, 768], P('section', 'inner')
- grad_ln_gain: float32 [2, 2, 768], P('section', None, 'inner')
- grad_ln_bias: float32 [2, 2, 768], P('section', None, 'inner')
- grad_w_up: float32 [2, 768, 3072], P('section', 'inner')
- grad_b_up: float32 [2, 3072], P('section', 'inner')
- grad_w_down: float32 [2, 3072, 768], P('section', 'inner')
- grad_b_down: float32 [2, 768], P('section', 'inner')
Inputs may be any that keep to these rules, and one draw needn't show every extreme that they name: `caption_len`: some sequence has 28 caption tokens. `region_len`: some sequence has 100 regions.
All inputs are finite; a program needn't handle non-finite values.
Results may differ from a plain program's by a relative error of at most 0.018.
Values may be sent and summed in bfloat16 or wider, within the bound.
No kernel may reach another device: no remote copies, remote signals or barrier semaphores. Data moves between devices by JAX's collectives and lax.ppermute only.
A program may use at most 192 MiB of HBM per device.

v0:
```python
import jax
import jax.numpy as jnp
from jax import lax
from jax.sharding import PartitionSpec as P

HEADS = 12
CAP = 28
MICRO = 2


layer_eps = 1e-12


def shifted_2(shard, axis, by):
    length = lax.axis_size(axis)
    pairs = [(i, i + by) for i in range(length) if 0 <= i + by < length]
    return lax.ppermute(shard, axis, pairs)


def normalize(summed, gain, offset):
    centre = jnp.mean(summed, axis=-1, keepdims=True)
    shifted = summed - centre
    spread = jnp.mean(shifted * shifted, axis=-1, keepdims=True)
    return shifted * lax.rsqrt(spread + layer_eps) * gain + offset


def gelu_exact(values):
    return jax.nn.gelu(values, approximate=False)


def contract_rows(left_rows, right_rows):
    return lax.dot_general(
        left_rows, right_rows, (((0,), (0,)), ((), ())), preferred_element_type=jnp.float32
    )


def back_project(grad_rows, matrix):
    return lax.dot_general(
        grad_rows, matrix, (((1,), (1,)), ((), ())), preferred_element_type=jnp.float32
    )


def score_block(projected, key_valid):
    head_size = projected.shape[-1]
    products = jnp.einsum(
        "sqhe,skhe->shqk",
        projected[:, :, 0],
        projected[:, :, 1],
        preferred_element_type=jnp.float32,
    )
    return jnp.where(key_valid[:, None, None, :], products * head_size ** (-0.5), -1e30)


def layer_forward(layer_in, weights, key_valid):
    w_qkv, b_qv, w_out, b_out, gains, offsets, w_up, b_up, w_down, b_down = weights
    seq_count, length, width = layer_in.shape
    head_size = width // HEADS
    in_rows = layer_in.reshape(seq_count * length, width)
    bias_row = jnp.concatenate([b_qv[0], jnp.zeros_like(b_qv[0]), b_qv[1]])
    projected = (jnp.dot(in_rows, w_qkv, preferred_element_type=jnp.float32) + bias_row).astype(
        jnp.bfloat16
    )
    projected = projected.reshape(seq_count, length, 3, HEADS, head_size)
    scores = score_block(projected, key_valid)
    top_score = jnp.max(scores, axis=-1, keepdims=True)
    exp_scores = jnp.exp(scores - top_score)
    totals = jnp.sum(exp_scores, axis=-1, keepdims=True)
    probs = (exp_scores / totals).astype(jnp.bfloat16)
    log_total = top_score + jnp.log(totals)
    context = jnp.einsum(
        "shqk,skhe->sqhe", probs, projected[:, :, 2], preferred_element_type=jnp.float32
    )
    context = context.astype(jnp.bfloat16).reshape(seq_count * length, width)
    attended = jnp.dot(context, w_out, preferred_element_type=jnp.float32) + b_out
    first_sum = in_rows.astype(jnp.float32) + attended
    normed = normalize(first_sum, gains[0], offsets[0])
    normed_low = normed.astype(jnp.bfloat16)
    pre_act = jnp.dot(normed_low, w_up, preferred_element_type=jnp.float32) + b_up
    act_low = gelu_exact(pre_act).astype(jnp.bfloat16)
    branch = jnp.dot(act_low, w_down, preferred_element_type=jnp.float32) + b_down
    second_sum = normed + branch
    result = normalize(second_sum, gains[1], offsets[1])
    cache = (
        in_rows,
        projected,
        log_total,
        context,
        first_sum,
        normed_low,
        pre_act,
        act_low,
        second_sum,
    )
    return (result, cache)


def layer_backward(grad_out_rows, weights, cache, key_valid):
    w_qkv, b_qv, w_out, b_out, gains, offsets, w_up, b_up, w_down, b_down = weights
    in_rows, projected, log_total, context, first_sum, normed_low, pre_act, act_low, second_sum = (
        cache
    )
    seq_count, length = key_valid.shape
    width = in_rows.shape[1]
    head_size = width // HEADS
    unused, norm_two_back = jax.vjp(normalize, second_sum, gains[1], offsets[1])
    grad_second, grad_gain_two, grad_offset_two = norm_two_back(grad_out_rows)
    branch_low = grad_second.astype(jnp.bfloat16)
    grad_w_down = contract_rows(act_low, branch_low)
    grad_b_down = jnp.sum(branch_low.astype(jnp.float32), axis=0)
    unused, gelu_back = jax.vjp(gelu_exact, pre_act)
    grad_pre = gelu_back(back_project(branch_low, w_down))[0].astype(jnp.bfloat16)
    grad_w_up = contract_rows(normed_low, grad_pre)
    grad_b_up = jnp.sum(grad_pre.astype(jnp.float32), axis=0)
    grad_normed = grad_second + back_project(grad_pre, w_up)
    unused, norm_one_back = jax.vjp(normalize, first_sum, gains[0], offsets[0])
    grad_first, grad_gain_one, grad_offset_one = norm_one_back(grad_normed)
    attend_low = grad_first.astype(jnp.bfloat16)
    grad_w_out = contract_rows(context, attend_low)
    grad_b_out = jnp.sum(attend_low.astype(jnp.float32), axis=0)
    grad_context = (
        back_project(attend_low, w_out)
        .astype(jnp.bfloat16)
        .reshape(seq_count, length, HEADS, head_size)
    )
    scores = score_block(projected, key_valid)
    probs = jnp.exp(scores - log_total)
    grad_values = jnp.einsum(
        "shqk,sqhe->skhe",
        probs.astype(jnp.bfloat16),
        grad_context,
        preferred_element_type=jnp.float32,
    )
    grad_probs = jnp.einsum(
        "sqhe,skhe->shqk", grad_context, projected[:, :, 2], preferred_element_type=jnp.float32
    )
    grad_scores = (
        probs * (grad_probs - jnp.sum(grad_probs * probs, axis=-1, keepdims=True))
    ).astype(jnp.bfloat16)
    scale = head_size ** (-0.5)
    grad_queries = (
        jnp.einsum(
            "shqk,skhe->sqhe", grad_scores, projected[:, :, 1], preferred_element_type=jnp.float32
        )
        * scale
    )
    grad_keys = (
        jnp.einsum(
            "shqk,sqhe->skhe", grad_scores, projected[:, :, 0], preferred_element_type=jnp.float32
        )
        * scale
    )
    grad_projected = jnp.stack([grad_queries, grad_keys, grad_values], axis=2).astype(jnp.bfloat16)
    grad_projected = grad_projected.reshape(seq_count * length, 3 * width)
    grad_w_qkv = contract_rows(in_rows, grad_projected)
    column_sums = jnp.sum(grad_projected.astype(jnp.float32), axis=0)
    grad_b_qv = jnp.stack([column_sums[:width], column_sums[2 * width :]])
    grad_in = grad_first + back_project(grad_projected, w_qkv)
    grads = (
        grad_w_qkv,
        grad_b_qv,
        grad_w_out,
        grad_b_out,
        jnp.stack([grad_gain_one, grad_gain_two]),
        jnp.stack([grad_offset_one, grad_offset_two]),
        grad_w_up,
        grad_b_up,
        grad_w_down,
        grad_b_down,
    )
    return (grad_in, grads)


def pick_tree(chooser, former, latter):
    return jax.tree.map(
        lambda left_item, right_item: jnp.where(chooser, left_item, right_item), former, latter
    )


def local(
    hidden_in,
    caption_len,
    region_len,
    cotangent,
    w_qkv,
    b_qv,
    w_out,
    b_out,
    ln_gain,
    ln_bias,
    w_up,
    b_up,
    w_down,
    b_down,
):
    weights = tuple(
        (
            item[0]
            for item in (w_qkv, b_qv, w_out, b_out, ln_gain, ln_bias, w_up, b_up, w_down, b_down)
        )
    )
    seqs_local, length, width = hidden_in.shape
    micro = MICRO
    per_batch = seqs_local // micro
    positions = jnp.arange(length, dtype=jnp.int32)
    key_valid = (positions[None, :] < caption_len[:, None]) | (positions[None, :] >= CAP) & (
        positions[None, :] < CAP + region_len[:, None]
    )
    masks = [key_valid[index * per_batch : (index + 1) * per_batch] for index in range(micro)]
    first_section = lax.axis_index("section") == 0
    received = jnp.zeros((per_batch, length, width), jnp.bfloat16)
    kept = []
    outputs = []
    for period in range(micro + 1):
        lead = min(period, micro - 1)
        trail = max(period - 1, 0)
        batch_mask = jnp.where(first_section, masks[lead], masks[trail])
        layer_in = jnp.where(
            first_section, hidden_in[lead * per_batch : (lead + 1) * per_batch], received
        )
        result, cache = layer_forward(layer_in, weights, batch_mask)
        result_low = result.astype(jnp.bfloat16).reshape(per_batch, length, width)
        if period < micro:
            received = shifted_2(result_low, "section", 1)
        kept.append(cache)
        outputs.append(result_low)
    activations = jnp.concatenate(
        [jnp.where(first_section, outputs[index], outputs[index + 1]) for index in range(micro)],
        axis=0,
    )
    received = jnp.zeros((per_batch, length, width), jnp.bfloat16)
    summed_grads = None
    grad_full = []
    grad_sent = []
    for period in range(micro + 1):
        second_index = min(period, micro - 1)
        first_index = max(period - 1, 0)
        batch_mask = jnp.where(first_section, masks[first_index], masks[second_index])
        grad_last = cotangent[second_index * per_batch : (second_index + 1) * per_batch].astype(
            jnp.float32
        ) * masks[second_index][:, :, None].astype(jnp.float32)
        grad_out = jnp.where(first_section, received.astype(jnp.float32), grad_last).reshape(
            per_batch * length, width
        )
        cache = pick_tree(first_section, kept[first_index], kept[second_index + 1])
        grad_in, grads = layer_backward(grad_out, weights, cache, batch_mask)
        weight_valid = jnp.where(first_section, float(period >= 1), float(period < micro))
        scaled = jax.tree.map(lambda latest: latest * weight_valid, grads)
        if summed_grads is None:
            summed_grads = scaled
        else:
            summed_grads = jax.tree.map(
                lambda summed, latest: summed + latest, summed_grads, scaled
            )
        grad_in = grad_in.reshape(per_batch, length, width)
        grad_low = grad_in.astype(jnp.bfloat16)
        if period < micro:
            received = shifted_2(grad_low, "section", -1)
        grad_full.append(grad_in)
        grad_sent.append(grad_low)
    input_grads = jnp.concatenate(
        [
            jnp.where(first_section, grad_full[index + 1], grad_sent[index].astype(jnp.float32))
            for index in range(micro)
        ],
        axis=0,
    )
    g_w_qkv, g_b_qv, g_w_out, g_b_out, g_gain, g_offset, g_w_up, g_b_up, g_w_down, g_b_down = tuple(
        (item[None] for item in summed_grads)
    )
    shards = (
        lax.psum_scatter(
            g_w_qkv.astype(jnp.bfloat16), "inner", scatter_dimension=1, tiled=True
        ).astype(jnp.float32),
        lax.psum_scatter(
            g_b_qv.astype(jnp.bfloat16), "inner", scatter_dimension=2, tiled=True
        ).astype(jnp.float32),
        lax.psum_scatter(
            g_w_out.astype(jnp.bfloat16), "inner", scatter_dimension=1, tiled=True
        ).astype(jnp.float32),
        lax.psum_scatter(
            g_b_out.astype(jnp.bfloat16), "inner", scatter_dimension=1, tiled=True
        ).astype(jnp.float32),
        lax.psum_scatter(
            g_gain.astype(jnp.bfloat16), "inner", scatter_dimension=2, tiled=True
        ).astype(jnp.float32),
        lax.psum_scatter(
            g_offset.astype(jnp.bfloat16), "inner", scatter_dimension=2, tiled=True
        ).astype(jnp.float32),
        lax.psum_scatter(
            g_w_up.astype(jnp.bfloat16), "inner", scatter_dimension=1, tiled=True
        ).astype(jnp.float32),
        lax.psum_scatter(
            g_b_up.astype(jnp.bfloat16), "inner", scatter_dimension=1, tiled=True
        ).astype(jnp.float32),
        lax.psum_scatter(
            g_w_down.astype(jnp.bfloat16), "inner", scatter_dimension=1, tiled=True
        ).astype(jnp.float32),
        lax.psum_scatter(
            g_b_down.astype(jnp.bfloat16), "inner", scatter_dimension=1, tiled=True
        ).astype(jnp.float32),
    )
    reduced = (
        lax.psum(shards[0].astype(jnp.bfloat16), "outer").astype(jnp.float32),
        lax.psum(shards[1].astype(jnp.bfloat16), "outer").astype(jnp.float32),
        lax.psum(shards[2].astype(jnp.bfloat16), "outer").astype(jnp.float32),
        lax.psum(shards[3].astype(jnp.bfloat16), "outer").astype(jnp.float32),
        lax.psum(shards[4].astype(jnp.bfloat16), "outer").astype(jnp.float32),
        lax.psum(shards[5].astype(jnp.bfloat16), "outer").astype(jnp.float32),
        lax.psum(shards[6].astype(jnp.bfloat16), "outer").astype(jnp.float32),
        lax.psum(shards[7].astype(jnp.bfloat16), "outer").astype(jnp.float32),
        lax.psum(shards[8].astype(jnp.bfloat16), "outer").astype(jnp.float32),
        lax.psum(shards[9].astype(jnp.bfloat16), "outer").astype(jnp.float32),
    )
    return (
        activations[None],
        input_grads[None],
        reduced[0],
        reduced[1],
        reduced[2],
        reduced[3],
        reduced[4],
        reduced[5],
        reduced[6],
        reduced[7],
        reduced[8],
        reduced[9],
    )


def solution(mesh):
    return jax.shard_map(
        local,
        mesh=mesh,
        in_specs=(
            P(("inner", "outer"), None, None),
            P(("inner", "outer")),
            P(("inner", "outer")),
            P(("inner", "outer"), None, None),
            P("section", None, None),
            P("section", None, None),
            P("section", None, None),
            P("section", None),
            P("section", None, None),
            P("section", None, None),
            P("section", None, None),
            P("section", None),
            P("section", None, None),
            P("section", None),
        ),
        out_specs=(
            P("section", ("inner", "outer"), None, None),
            P("section", ("inner", "outer"), None, None),
            P("section", "inner", None),
            P("section", None, "inner"),
            P("section", "inner", None),
            P("section", "inner"),
            P("section", None, "inner"),
            P("section", None, "inner"),
            P("section", "inner", None),
            P("section", "inner"),
            P("section", "inner", None),
            P("section", "inner"),
        ),
        check_vma=False,
    )
```

profile of v0, /device:TPU:0, one launch (start us, length us, event | category | flops | bytes accessed | tf_op | source)
XLA Modules:
  0.0 893.8 jit_solution(14514020134388678172)
XLA Ops:
  14.0 3.4 fusion.90
  17.5 4.3 copy.112
  21.7 5.3 reshape.885
  34.6 18.3 %fusion.2 = (bf16[512,3072]{1,0:T(8,128)(2,1)S(1)}, f32[512,3072]{1,0:T(8,128)}) fusion(f32[3072]{0:T(1024)S(1)} %bitcast.475, bf16[1,768,3072]{2,1,0:T(8,128)(2,1)S(1)} %bitcast.466, f32[512,768]{1,0:T(8,128)S(1)} %get-tuple-element.135, f32[768]{0:T(1024)S(1)} %get-tuple-element.30, f32[768]{0:T(1024)S(1)} %get-tuple-element.165, ...), kind=kOutput, calls=%fused_computation.11 | convolution fusion | flops 2521694208 | bytes 15751168 | tf_op jit(solution)/shard_map/dot_general | solution.py:78
  53.0 2.8 fusion.287
  56.4 2.5 collective-permute-start
  62.8 3.4 fusion.91
  66.2 4.3 copy.118
  70.5 5.3 reshape.889
  83.2 28.6 %fusion.5 = (bf16[512,3072]{1,0:T(8,128)(2,1)S(1)}, f32[512,3072]{1,0:T(8,128)}) fusion(f32[3072]{0:T(1024)S(1)} %bitcast.476, bf16[1,768,3072]{2,1,0:T(8,128)(2,1)S(1)} %bitcast.468, f32[512,768]{1,0:T(8,128)S(1)} %get-tuple-element.143, f32[512]{0:T(512)S(1)} %add_rsqrt_fusion.3, f32[512]{0:T(512)S(1)} %broadcast_multiply_fusion.9, ...), kind=kOutput, calls=%fused_computation.14 | convolution fusion | flops 2521694208 | bytes 15751168 | tf_op jit(solution)/shard_map/dot_general | solution.py:78
  111.9 2.8 fusion.289
  117.0 3.1 collective-permute-start.1
  122.3 2.3 copy.157
  124.6 3.1 fusion.241
  129.9 2.3 copy.158
  132.2 2.4 broadcast_select_fusion.10
  135.5 3.4 fusion.92
  138.9 4.3 copy.124
  143.2 5.3 reshape.893
  148.5 6.1 broadcast_select_fusion
  161.2 3.1 fusion.272
  164.4 18.5 %fusion.8 = (bf16[512,3072]{1,0:T(8,128)(2,1)S(1)}, f32[512,3072]{1,0:T(8,128)}) fusion(f32[3072]{0:T(1024)S(1)} %bitcast.477, bf16[512,768]{1,0:T(8,128)(2,1)S(1)} %get-tuple-element.105, bf16[1,768,3072]{2,1,0:T(8,128)(2,1)S(1)} %bitcast.470), kind=kOutput, calls=%fused_computation.17 | convolution fusion | flops 2519728128 | bytes 14954496 | tf_op jit(solution)/shard_map/dot_general | solution.py:78
  183.0 2.8 fusion.291
  186.1 3.3 fusion.274
  193.5 20.4 %convert_reduce_fusion.2 = (f32[3072]{0:T(1024)}, bf16[512,3072]{1,0:T(8,128)(2,1)S(1)}) fusion(f32[512,3072]{1,0:T(8,128)S(1)} %bitcast.482, f32[512,3072]{1,0:T(8,128)} %get-tuple-element.137, f32[3072]{0:T(1024)S(1)} %bitcast.478, pred[]{:T(512)S(6)} %eq.3, bf16[512,768]{1,0:T(8,128)(2,1)S(1)} %get-tuple-element.44, bf16[1,3072,768]{2,1,0:T(8,128)(2,1)S(1)} %bitcast.460), kind=kOutput, calls=%fused_computation.35 | convolution fusion | flops 2537026560 | bytes 21258240 | tf_op jit(solution)/shard_map/dot_general | solution.py:38
  213.9 3.7 multiply_reduce_fusion.5
  222.8 2.3 copy.132
  225.1 2.6 reshape.897
  227.7 2.5 subtract_exponential_fusion.2
  241.5 3.1 add_convert_fusion.4
  247.6 2.8 subtract_exponential_fusion
  252.6 2.8 subtract_exponential_fusion.1
  257.0 2.3 copy.160
  261.5 7.0 fusion.124
  273.4 21.0 %convert_reduce_fusion.1 = (f32[3072]{0:T(1024)}, bf16[512,3072]{1,0:T(8,128)(2,1)S(1)}) fusion(f32[512,3072]{1,0:T(8,128)} %get-tuple-element.153, f32[512,3072]{1,0:T(8,128)} %get-tuple-element.137, f32[3072]{0:T(1024)S(1)} %bitcast.479, pred[]{:T(512)S(6)} %eq.3, bf16[512,768]{1,0:T(8,128)(2,1)S(1)} %get-tuple-element.46, ...), kind=kOutput, calls=%fused_computation.34 | convolution fusion | flops 2537026560 | bytes 21258240 | tf_op jit(solution)/shard_map/dot_general | solution.py:38
  294.5 3.7 multiply_reduce_fusion.4
  303.4 2.3 copy.141
  305.7 2.9 reshape.899
  308.7 3.5 fusion.189
  327.2 5.0 fusion.121
  336.3 20.4 %convert_reduce_fusion = (f32[3072]{0:T(1024)}, bf16[512,3072]{1,0:T(8,128)(2,1)S(1)}) fusion(f32[512,3072]{1,0:T(8,128)} %get-tuple-element.153, f32[512,3072]{1,0:T(8,128)S(1)} %bitcast.484, f32[3072]{0:T(1024)S(1)} %bitcast.480, pred[]{:T(512)S(6)} %eq.3, bf16[512,768]{1,0:T(8,128)(2,1)S(1)} %get-tuple-element.48, bf16[1,3072,768]{2,1,0:T(8,128)(2,1)S(1)} %bitcast.464), kind=kOutput, calls=%fused_computation.33 | convolution fusion | flops 2537026560 | bytes 21258240 | tf_op jit(solution)/shard_map/dot_general | solution.py:38
  356.7 3.7 multiply_reduce_fusion.3
  365.7 2.4 copy.150
  368.1 2.4 reshape.902
  370.5 4.7 fusion.185
  375.5 3.3 multiply_reduce_fusion
  388.5 4.2 fusion.93
  393.4 9.7 %fusion.222 = f32[768,3072]{1,0:T(8,128)} fusion(bf16[512,3072]{1,0:T(8,128)(2,1)} %copy-done.155, pred[]{:T(512)S(6)} %eq.3, f32[512,768]{1,0:T(8,128)} %copy-done.26, f32[512]{0:T(512)} %copy-done.121, f32[512]{0:T(512)} %copy-done.98, f32[768]{0:T(1024)S(1)} %copy-done.83, f32[768]{0:T(1024)S(1)} %get-tuple-element.165, f32[512,768]{1,0:T(8,128)} %copy-done.23, ...), kind=kOutput, calls=%fused_computation.378 | convolution fusion | flops 2420244480 | bytes 15742977 | tf_op jit(solution)/shard_map/dot_general | solution.py:32
  403.1 2.9 fusion.220
  406.1 9.2 %fusion.94 = bf16[1,768,3072]{2,1,0:T(8,128)(2,1)} fusion(f32[]{:T(128)S(6)} %select_n.291, bf16[512,3072]{1,0:T(8,128)(2,1)} %copy-done.73, f32[768,3072]{1,0:T(8,128)S(1)} %fusion.220, f32[768,3072]{1,0:T(8,128)} %fusion.222, f32[]{:T(128)S(6)} %select_n.286, bf16[512,768]{1,0:T(8,128)(2,1)S(1)} %copy-done.38, pred[]{:T(512)S(6)} %eq.3, ...), kind=kOutput, calls=%fused_computation.160 | convolution fusion | flops 2430074880 | bytes 29108232 | tf_op jit(solution)/shard_map/dot_general | solution.py:32
  415.6 4.7 fusion.108
  420.3 5.2 fusion.106
  425.5 10.5 %fusion.95 = bf16[1,3072,768]{2,1,0:T(8,128)(2,1)} fusion(f32[]{:T(128)S(6)} %select_n.291, bf16[512,768]{1,0:T(8,128)(2,1)} %copy-done.75, f32[3072,768]{1,0:T(8,128)} %fusion.106, f32[3072,768]{1,0:T(8,128)S(1)} %fusion.108, f32[]{:T(128)S(6)} %select_n.286, bf16[512,3072]{1,0:T(8,128)(2,1)} %copy-done.9, bf16[512,3072]{1,0:T(8,128)(2,1)} %copy-done.10, ...), kind=kOutput, calls=%fused_computation.161 | convolution fusion | flops 2429288448 | bytes 30670856 | tf_op jit(solution)/shard_map/dot_general | solution.py:32
  473.7 44.5 %reduce-scatter.27.cloned.1.call-done = bf16[1,192,3072]{2,1,0:T(8,128)(2,1)} async-done(((bf16[1,768,3072]{2,1,0:T(8,128)(2,1)}), bf16[1,192,3072]{2,1,0:T(8,128)(2,1)}) %reduce-scatter.27.cloned.1.call-update) | async-done | bytes 1179664 | tf_op jit(solution)/shard_map/reduce_scatter | solution.py:289
  518.2 60.0 %reduce-scatter.29.cloned.1.call-done = bf16[1,768,768]{2,1,0:T(8,128)(2,1)} async-done(((bf16[1,3072,768]{2,1,0:T(8,128)(2,1)}), bf16[1,768,768]{2,1,0:T(8,128)(2,1)}) %reduce-scatter.29.cloned.1.call-update) | async-done | bytes 1179664 | tf_op jit(solution)/shard_map/reduce_scatter | solution.py:295
  587.1 17.7 %reduce-scatter.33.cloned.1.call-done = bf16[192,1]{1,0:T(8,128)(2,1)} async-done(((bf16[768,1]{1,0:T(8,128)(2,1)}), bf16[192,1]{1,0:T(8,128)(2,1)}) %reduce-scatter.33.cloned.1.call-update) | async-done | bytes 400
  606.3 25.2 %reduce-scatter.41.cloned.1.call-done = bf16[192,1]{1,0:T(8,128)(2,1)} async-done(((bf16[768,1]{1,0:T(8,128)(2,1)}), bf16[192,1]{1,0:T(8,128)(2,1)}) %reduce-scatter.41.cloned.1.call-update) | async-done | bytes 400
  632.9 25.9 %reduce-scatter.31.cloned.1.call-done = bf16[192,2]{1,0:T(8,128)(2,1)} async-done(((bf16[768,2]{1,0:T(8,128)(2,1)}), bf16[192,2]{1,0:T(8,128)(2,1)}) %reduce-scatter.31.cloned.1.call-update) | async-done | bytes 784
  661.3 24.3 %reduce-scatter.35.cloned.1.call-done = bf16[192,2]{1,0:T(8,128)(2,1)} async-done(((bf16[768,2]{1,0:T(8,128)(2,1)}), bf16[192,2]{1,0:T(8,128)(2,1)}) %reduce-scatter.35.cloned.1.call-update) | async-done | bytes 784
  688.0 24.3 %reduce-scatter.37.cloned.1.call-done = bf16[192,2]{1,0:T(8,128)(2,1)} async-done(((bf16[768,2]{1,0:T(8,128)(2,1)}), bf16[192,2]{1,0:T(8,128)(2,1)}) %reduce-scatter.37.cloned.1.call-update) | async-done | bytes 784
  714.8 27.0 %reduce-scatter.39.cloned.1.call-done = bf16[768,1]{1,0:T(8,128)(2,1)} async-done(((bf16[3072,1]{1,0:T(8,128)(2,1)}), bf16[768,1]{1,0:T(8,128)(2,1)}) %reduce-scatter.39.cloned.1.call-update) | async-done | bytes 1552
  742.8 12.8 %all-reduce = (bf16[1,2,192]{2,1,0:T(2,128)(2,1)}, bf16[1,192]{1,0:T(2,128)(2,1)}, bf16[1,2,192]{2,1,0:T(2,128)(2,1)}, bf16[1,2,192]{2,1,0:T(2,128)(2,1)}, bf16[...) all-reduce(bf16[1,2,192]{2,1,0:T(2,128)(2,1)S(1)} %copy.176, ...), channel_id=1, replica_groups=mesh['section'=2,'inner'=4,'outer'=4] {'outer'}, use_global_device_ids=true, to_apply=%region_51.52 | all-reduce | flops 2304 | bytes 9216 | tf_op jit(solution)/shard_map/psum | solution.py:304
  763.1 116.3 %all-reduce.4.cloned.1.call-done = (bf16[1,192,2304]{2,1,0:T(8,128)(2,1)}, bf16[1,192,768]{2,1,0:T(8,128)(2,1)}, bf16[1,192,3072]{2,1,0:T(8,128)(2,1)}, bf16[1,768,768]{2,1,0:T(8,128)(2,1)}) async-done(((bf16[1,192,2304]{2,1,0:T(8,128)(2,1)}, bf16[1,192,768]{2,1,0:T(8,128)(2,1)}, bf16[1,192,3072]{2,1,0:T(8,128)(2,1)}, bf16[1,768,768]{2,1,0:T(8,128)(2,1)}), (bf16[1,192,2304]{2,1,0:T(8,128)(2,1)}, ...) | async-done | bytes 3538960 | tf_op jit(solution)/shard_map/psum | solution.py:303
  879.4 2.6 convert_element_type.459
  (599 shorter events, 184.6 us)
Async XLA Ops:
  7.2 6.8 copy-start
  7.2 466.4 %reduce-scatter.25.cloned.1.call-start = ((), (), s32[]{:S(2)}) async-start(), calls=%async_computation.11 | async-start | bytes 1474560 | tf_op jit(solution)/shard_map/reduce_scatter | solution.py:277
  9.4 23.7 %copy-start.136 = (f32[768]{0:T(1024)}, f32[768]{0:T(1024)S(1)}, u32[]{:S(2)}) copy-start(f32[768]{0:T(1024)S(1)} %reduce.8) | copy-start | bytes 9220
  11.4 19.8 %copy-start.141 = (pred[4,128]{1,0:T(4,128)(4,1)}, pred[4,128]{1,0:T(4,128)(4,1)S(1)}, u32[]{:S(2)}) copy-start(pred[4,128]{1,0:T(4,128)(4,1)S(1)} %get-tuple-element.130) | copy-start | bytes 1540
  33.1 19.8 %slice-start.4 = ((s8[4718592]{0:T(1024)(128)(4,1)}), s8[4194304]{0:T(1024)(128)(4,1)S(1)}, s32[]{:S(2)}) async-start(s8[4718592]{0:T(1024)(128)(4,1)} %bitcast.455), calls=%async_computation.25 | async-start | bytes 8388608
  34.1 18.8 %copy-start.23 = (f32[512,768]{1,0:T(8,128)}, f32[512,768]{1,0:T(8,128)S(1)}, u32[]{:S(2)}) copy-start(f32[512,768]{1,0:T(8,128)S(1)} %get-tuple-element.135) | copy-start | bytes 4718596
  34.1 18.8 %copy-start.92 = (f32[512]{0:T(512)}, f32[512]{0:T(512)S(1)}, u32[]{:S(2)}) copy-start(f32[512]{0:T(512)S(1)} %broadcast_multiply_fusion.11) | copy-start | bytes 6148
  34.5 18.5 %copy-start.94 = (f32[512]{0:T(512)}, f32[512]{0:T(512)S(1)}, u32[]{:S(2)}) copy-start(f32[512]{0:T(512)S(1)} %add_rsqrt_fusion.5) | copy-start | bytes 6148
  34.5 148.4 %copy-start.82 = (f32[768]{0:T(1024)}, f32[768]{0:T(1024)S(1)}, u32[]{:S(2)}) copy-start(f32[768]{0:T(1024)S(1)} %get-tuple-element.30) | copy-start | bytes 9220
  34.6 18.4 %copy-start.133 = (f32[768]{0:T(1024)S(1)}, f32[768]{0:T(1024)}, u32[]{:S(2)}) copy-start(f32[768]{0:T(1024)} %reduce.11) | copy-start | bytes 9220
  34.6 18.4 %slice-start.5 = ((s8[4718592]{0:T(1024)(128)(4,1)}), s8[524288]{0:T(1024)(128)(4,1)S(1)}, s32[]{:S(2)}) async-start(s8[4718592]{0:T(1024)(128)(4,1)} %bitcast.455), calls=%async_computation.26 | async-start | bytes 1048576
  56.1 6.7 copy-start.118
  56.4 4.4 collective-permute-start
  81.9 30.0 %slice-start.6 = ((s8[4718592]{0:T(1024)(128)(4,1)}), s8[4194304]{0:T(1024)(128)(4,1)S(1)}, s32[]{:S(2)}) async-start(s8[4718592]{0:T(1024)(128)(4,1)} %bitcast.457), calls=%async_computation.27 | async-start | bytes 8388608
  82.8 29.0 %copy-start.26 = (f32[512,768]{1,0:T(8,128)}, f32[512,768]{1,0:T(8,128)S(1)}, u32[]{:S(2)}) copy-start(f32[512,768]{1,0:T(8,128)S(1)} %get-tuple-element.143) | copy-start | bytes 4718596
  82.8 29.0 %copy-start.98 = (f32[512]{0:T(512)}, f32[512]{0:T(512)S(1)}, u32[]{:S(2)}) copy-start(f32[512]{0:T(512)S(1)} %broadcast_multiply_fusion.9) | copy-start | bytes 6148
  83.2 28.6 %copy-start.121 = (f32[512]{0:T(512)}, f32[512]{0:T(512)S(1)}, u32[]{:S(2)}) copy-start(f32[512]{0:T(512)S(1)} %add_rsqrt_fusion.3) | copy-start | bytes 6148
  83.2 28.6 %copy-start.134 = (f32[768]{0:T(1024)S(1)}, f32[768]{0:T(1024)}, u32[]{:S(2)}) copy-start(f32[768]{0:T(1024)} %reduce.11) | copy-start | bytes 9220
  83.2 28.6 %slice-start.7 = ((s8[4718592]{0:T(1024)(128)(4,1)}), s8[524288]{0:T(1024)(128)(4,1)S(1)}, s32[]{:S(2)}) async-start(s8[4718592]{0:T(1024)(128)(4,1)} %bitcast.457), calls=%async_computation.28 | async-start | bytes 1048576
  117.0 15.2 %collective-permute-start.1 = (bf16[4,128,768]{2,1,0:T(8,128)(2,1)}, bf16[4,128,768]{2,1,0:T(8,128)(2,1)}, u32[]{:S(2)}, u32[]{:S(2)}) collective-permute-start(bf16[4,128,768]{2,1,0:T(8,128)(2,1)} %bitcast.16), channel_id=1, source_target_pairs={{0,16},{1,17},{2,18},{3,19},{4,20},{5,21},{6,22},{7,23},{8,24},{9,... | collective-permute-start | bytes 2359304 | tf_op jit(solution)/shard_map/ppermute | solution.py:17
  156.6 7.7 slice-start.18
  161.2 21.6 %slice-start.8 = ((s8[4718592]{0:T(1024)(128)(4,1)}), s8[4194304]{0:T(1024)(128)(4,1)S(1)}, s32[]{:S(2)}) async-start(s8[4718592]{0:T(1024)(128)(4,1)} %bitcast.459), calls=%async_computation.29 | async-start | bytes 8388608
  164.3 18.5 %copy-start.37 = (bf16[512,768]{1,0:T(8,128)(2,1)}, bf16[512,768]{1,0:T(8,128)(2,1)S(1)}, u32[]{:S(2)}) copy-start(bf16[512,768]{1,0:T(8,128)(2,1)S(1)} %get-tuple-element.105) | copy-start | bytes 2359300
  164.3 18.6 %copy-start.135 = (f32[768]{0:T(1024)S(1)}, f32[768]{0:T(1024)}, u32[]{:S(2)}) copy-start(f32[768]{0:T(1024)} %reduce.11) | copy-start | bytes 9220
  164.3 18.6 %slice-start.9 = ((s8[4718592]{0:T(1024)(128)(4,1)}), s8[524288]{0:T(1024)(128)(4,1)S(1)}, s32[]{:S(2)}) async-start(s8[4718592]{0:T(1024)(128)(4,1)} %bitcast.459), calls=%async_computation.30 | async-start | bytes 1048576
  186.1 7.4 slice-start.24
  193.5 20.4 %copy-start.54 = (bf16[512,768]{1,0:T(8,128)(2,1)}, bf16[512,768]{1,0:T(8,128)(2,1)S(1)}, u32[]{:S(2)}) copy-start(bf16[512,768]{1,0:T(8,128)(2,1)S(1)} %get-tuple-element.44) | copy-start | bytes 2359300
  244.6 23.8 %collective-permute-start.2 = (bf16[4,128,768]{2,1,0:T(8,128)(2,1)}, bf16[4,128,768]{2,1,0:T(8,128)(2,1)}, u32[]{:S(2)}, u32[]{:S(2)}) collective-permute-start(bf16[4,128,768]{2,1,0:T(8,128)(2,1)} %bitcast.34), channel_id=1, source_target_pairs={{16,0},{17,1},{18,2},{19,3},{20,4},{21,5},{22,6},{23,7},{24,8},{25... | collective-permute-start | bytes 2359304 | tf_op jit(solution)/shard_map/ppermute | solution.py:17
  247.5 7.9 copy-start.108
  261.5 7.0 copy-start.52
  261.5 7.0 copy-start.104
  261.5 11.9 %slice-start.10 = ((s8[4718592]{0:T(1024)(128)(4,1)}), s8[4194304]{0:T(1024)(128)(4,1)S(1)}, s32[]{:S(2)}) async-start(s8[4718592]{0:T(1024)(128)(4,1)} %bitcast.461), calls=%async_computation.31 | async-start | bytes 8388608
  271.9 22.5 %slice-start.20 = ((s8[4718592]{0:T(1024)(128)(4,1)}), s8[4194304]{0:T(1024)(128)(4,1)S(1)}, s32[]{:S(2)}) async-start(s8[4718592]{0:T(1024)(128)(4,1)} %bitcast.471), calls=%async_computation.41 | async-start | bytes 8388608
  273.4 21.0 %copy-start.55 = (bf16[512,768]{1,0:T(8,128)(2,1)}, bf16[512,768]{1,0:T(8,128)(2,1)S(1)}, u32[]{:S(2)}) copy-start(bf16[512,768]{1,0:T(8,128)(2,1)S(1)} %get-tuple-element.46) | copy-start | bytes 2359300
  273.4 21.0 %copy-start.22 = (f32[512,768]{1,0:T(8,128)S(1)}, f32[512,768]{1,0:T(8,128)}, u32[]{:S(2)}) copy-start(f32[512,768]{1,0:T(8,128)} %get-tuple-element.107) | copy-start | bytes 4718596
  273.4 21.0 %copy-start.103 = (f32[512]{0:T(512)S(1)}, f32[512]{0:T(512)}, u32[]{:S(2)}) copy-start(f32[512]{0:T(512)} %copy-done.102) | copy-start | bytes 6148
  273.4 21.0 %copy-start.124 = (f32[512]{0:T(512)S(1)}, f32[512]{0:T(512)}, u32[]{:S(2)}) copy-start(f32[512]{0:T(512)} %fusion.256) | copy-start | bytes 6148
  273.4 21.0 %slice-start.21 = ((s8[4718592]{0:T(1024)(128)(4,1)}), s8[524288]{0:T(1024)(128)(4,1)S(1)}, s32[]{:S(2)}) async-start(s8[4718592]{0:T(1024)(128)(4,1)} %bitcast.471), calls=%async_computation.42 | async-start | bytes 1048576
  323.3 8.9 collective-permute-start.3
  324.9 11.3 %slice-start.26 = ((s8[6291456]{0:T(1024)(128)(4,1)}), s8[4194304]{0:T(1024)(128)(4,1)S(1)}, s32[]{:S(2)}) async-start(s8[6291456]{0:T(1024)(128)(4,1)} %bitcast.483), calls=%async_computation.47 | async-start | bytes 8388608
  327.2 9.1 %slice-start.12 = ((s8[4718592]{0:T(1024)(128)(4,1)}), s8[4194304]{0:T(1024)(128)(4,1)S(1)}, s32[]{:S(2)}) async-start(s8[4718592]{0:T(1024)(128)(4,1)} %bitcast.463), calls=%async_computation.33 | async-start | bytes 8388608
  327.2 9.0 %slice-start.27 = ((s8[6291456]{0:T(1024)(128)(4,1)}), s8[2097152]{0:T(1024)(128)(4,1)S(1)}, s32[]{:S(2)}) async-start(s8[6291456]{0:T(1024)(128)(4,1)} %bitcast.483), calls=%async_computation.48 | async-start | bytes 4194304
  334.8 21.9 %slice-start.22 = ((s8[4718592]{0:T(1024)(128)(4,1)}), s8[4194304]{0:T(1024)(128)(4,1)S(1)}, s32[]{:S(2)}) async-start(s8[4718592]{0:T(1024)(128)(4,1)} %bitcast.473), calls=%async_computation.43 | async-start | bytes 8388608
  336.2 20.5 %copy-start.75 = (bf16[512,768]{1,0:T(8,128)(2,1)}, bf16[512,768]{1,0:T(8,128)(2,1)S(1)}, u32[]{:S(2)}) copy-start(bf16[512,768]{1,0:T(8,128)(2,1)S(1)} %get-tuple-element.48) | copy-start | bytes 2359300
  336.3 20.4 %copy-start.20 = (f32[512,768]{1,0:T(8,128)S(1)}, f32[512,768]{1,0:T(8,128)}, u32[]{:S(2)}) copy-start(f32[512,768]{1,0:T(8,128)} %get-tuple-element.78) | copy-start | bytes 4718596
  336.3 20.4 %copy-start.101 = (f32[512]{0:T(512)S(1)}, f32[512]{0:T(512)}, u32[]{:S(2)}) copy-start(f32[512]{0:T(512)} %copy-done.100) | copy-start | bytes 6148
  336.3 20.4 %copy-start.123 = (f32[512]{0:T(512)S(1)}, f32[512]{0:T(512)}, u32[]{:S(2)}) copy-start(f32[512]{0:T(512)} %fusion.258) | copy-start | bytes 6148
  336.3 20.4 %slice-start.23 = ((s8[4718592]{0:T(1024)(128)(4,1)}), s8[524288]{0:T(1024)(128)(4,1)S(1)}, s32[]{:S(2)}) async-start(s8[4718592]{0:T(1024)(128)(4,1)} %bitcast.473), calls=%async_computation.44 | async-start | bytes 1048576
  375.3 98.4 %reduce-scatter.23.cloned.1.call-start = ((), (), s32[]{:S(2)}) async-start(), calls=%async_computation.10 | async-start | bytes 4423680 | tf_op jit(solution)/shard_map/reduce_scatter | solution.py:271
  378.8 9.6 %slice-start.2 = ((s8[7077888]{0:T(1024)(128)(4,1)}), s8[4194304]{0:T(1024)(128)(4,1)S(1)}, s32[]{:S(2)}) async-start(s8[7077888]{0:T(1024)(128)(4,1)} %bitcast.418), calls=%async_computation.23 | async-start | bytes 8388608
  381.7 6.8 slice-start.3
  392.7 125.5 %reduce-scatter.27.cloned.1.call-start = ((), (), s32[]{:S(2)}) async-start(), calls=%async_computation.12 | async-start | bytes 5898240 | tf_op jit(solution)/shard_map/reduce_scatter | solution.py:289
  393.4 9.7 %copy-start.25 = (f32[512,768]{1,0:T(8,128)S(1)}, f32[512,768]{1,0:T(8,128)}, u32[]{:S(2)}) copy-start(f32[512,768]{1,0:T(8,128)} %copy-done.23) | copy-start | bytes 4718596
  393.4 9.7 %copy-start.38 = (bf16[512,768]{1,0:T(8,128)(2,1)S(1)}, bf16[512,768]{1,0:T(8,128)(2,1)}, u32[]{:S(2)}) copy-start(bf16[512,768]{1,0:T(8,128)(2,1)} %copy-done.37) | copy-start | bytes 2359300
  393.4 9.7 %copy-start.72 = (bf16[512,3072]{1,0:T(8,128)(2,1)S(1)}, bf16[512,3072]{1,0:T(8,128)(2,1)}, u32[]{:S(2)}) copy-start(bf16[512,3072]{1,0:T(8,128)(2,1)} %copy-done.71) | copy-start | bytes 9437188
  415.3 162.9 %reduce-scatter.29.cloned.1.call-start = ((), (), s32[]{:S(2)}) async-start(), calls=%async_computation.13 | async-start | bytes 5898240 | tf_op jit(solution)/shard_map/reduce_scatter | solution.py:295
  436.0 168.8 %reduce-scatter.33.cloned.1.call-start = ((), (), s32[]{:S(2)}) async-start(), calls=%async_computation.15 | async-start | bytes 245760
  452.4 179.0 %reduce-scatter.41.cloned.1.call-start = ((), (), s32[]{:S(2)}) async-start(), calls=%async_computation.19 | async-start | bytes 245760
  455.4 16.1 %copy-start.120 = (f32[3072]{0:T(1024)S(1)}, f32[3072]{0:T(1024)}, u32[]{:S(2)}) copy-start(f32[3072]{0:T(1024)} %get-tuple-element.49) | copy-start | bytes 36868
  455.4 203.4 %reduce-scatter.31.cloned.1.call-start = ((), (), s32[]{:S(2)}) async-start(), calls=%async_computation.14 | async-start | bytes 245760
  461.6 223.9 %reduce-scatter.35.cloned.1.call-start = ((), (), s32[]{:S(2)}) async-start(), calls=%async_computation.16 | async-start | bytes 245760
  467.8 244.5 %reduce-scatter.37.cloned.1.call-start = ((), (), s32[]{:S(2)}) async-start(), calls=%async_computation.17 | async-start | bytes 245760
  471.4 270.4 %reduce-scatter.39.cloned.1.call-start = ((), (), s32[]{:S(2)}) async-start(), calls=%async_computation.18 | async-start | bytes 983040
  473.6 405.8 %all-reduce.4.cloned.1.call-start = ((), (), s32[]{:S(2)}) async-start(), calls=%async_computation.20 | async-start | bytes 7077888 | tf_op jit(solution)/shard_map/psum | solution.py:303
  (135 other events, 360.0 us)
Sparse Core Ops, SparseCore 0:
  375.4 32.3 reduce-scatter.24
  410.8 47.2 reduce-scatter.22
  461.1 57.0 reduce-scatter.26
  521.0 57.0 reduce-scatter.28
  580.8 23.9 reduce-scatter.32
  607.4 23.9 reduce-scatter.40
  634.8 23.9 reduce-scatter.30
  661.5 23.9 reduce-scatter.34
  688.3 23.9 reduce-scatter.36
  715.6 26.0 reduce-scatter.38
  744.4 134.9 all-reduce.3
where the time goes:
time: 905 us; the launch traced here: 894 us
  waiting for transfers between devices  367 us (41%)
  matrix products  271 us (30%)
  local copies, waits for them, and re-layouts  131 us (14%)
  other arithmetic  85.6 us (9%)
  between operations  16.6 us (2%)
  blocking collectives  12.8 us (1%)
  starting transfers between devices  10.2 us (1%)
    unnamed x17, waiting for transfers between devices  145 us
    psum x1, waiting for transfers between devices, local(): lax.psum(shards[0].astype(jnp.bfloat16), 'outer').astype(jnp.float32)  116 us
    dot_general x12, matrix products, back_project(): lax.dot_general(grad_rows, matrix, (((1,), (1,)), ((), ())), preferred_el...  85.1 us
    dot_general x12, matrix products, contract_rows(): lax.dot_general(left_rows, right_rows, (((0,), (0,)), ((), ())), preferre...  67.5 us
    dot_general x3, matrix products, layer_forward(): jnp.dot(normed_low, w_up, preferred_element_type=jnp.float32) + b_up  65.3 us
    reduce_scatter x1, waiting for transfers between devices, local(): lax.psum_scatter(g_w_down.astype(jnp.bfloat16), 'inner', scatter_dimensio...  60 us
    unnamed x389, local copies, waits for them, and re-layouts  45.7 us
    reduce_scatter x1, waiting for transfers between devices, local(): lax.psum_scatter(g_w_up.astype(jnp.bfloat16), 'inner', scatter_dimension=...  44.5 us
  transfers between devices with their start and end apart: 15, of which 10 were waited for; matrix products, arithmetic and copies ran while one was open for 18% of the time, Pallas kernels for 0%

commit v1 on v0

v1 whole, which is shorter than its diff:
```python
import functools

import jax
import jax.numpy as jnp
from jax import lax
from jax.experimental import pallas as pl
from jax.experimental.pallas import tpu as pltpu
from jax.sharding import PartitionSpec as P

HEADS = 12
CAP = 28
EPS = 1e-12
VMEM = 56 * 1024 * 1024
F32 = jnp.float32
BF16 = jnp.bfloat16


def dot(left, right):
    return jnp.dot(left, right, preferred_element_type=F32)


def dot_t(left, right):
    return lax.dot_general(left, right, (((1,), (1,)), ((), ())), preferred_element_type=F32)


def t_dot(left, right):
    return lax.dot_general(left, right, (((0,), (0,)), ((), ())), preferred_element_type=F32)


def column_sum(values):
    return jnp.sum(values, axis=0, keepdims=True)


def either(flag, body):
    pl.when(flag)(lambda: body(0))
    pl.when(jnp.logical_not(flag))(lambda: body(1))


def standardize(summed):
    centre = jnp.mean(summed, axis=-1, keepdims=True)
    shifted = summed - centre
    spread = jnp.mean(shifted * shifted, axis=-1, keepdims=True)
    scale = lax.rsqrt(spread + EPS)
    return shifted * scale, scale


def norm_back(grad, hat, scale, gain):
    scaled = grad * gain
    return scale * (
        scaled
        - jnp.mean(scaled, axis=-1, keepdims=True)
        - hat * jnp.mean(scaled * hat, axis=-1, keepdims=True)
    )


def lane_halves():
    lane = lax.broadcasted_iota(jnp.int32, (1, 128), 1)
    lower = jnp.where(lane < 64, 1.0, 0.0)
    return lower.astype(BF16), (1.0 - lower).astype(BF16)


def two_heads(block, halves):
    return jnp.concatenate([block * halves[0], block * halves[1]], axis=0)


def call(kernel, grid, in_specs, out_specs, out_shape, scratch, name, flops, nbytes):
    return pl.pallas_call(
        kernel,
        grid_spec=pltpu.PrefetchScalarGridSpec(
            num_scalar_prefetch=1,
            grid=grid,
            in_specs=in_specs,
            out_specs=out_specs,
            scratch_shapes=scratch,
        ),
        out_shape=out_shape,
        compiler_params=pltpu.CompilerParams(vmem_limit_bytes=VMEM),
        cost_estimate=pl.CostEstimate(flops=flops, bytes_accessed=nbytes, transcendentals=0),
        name=name,
    )


def whole(shape):
    return pl.BlockSpec(shape, lambda *_: (0,) * len(shape))


def sds(shape, dtype):
    return jax.ShapeDtypeStruct(shape, dtype)


def attend_kernel(layer, seqs, sec, x, q_a, k_a, v_a, q_b, k_b, v_b, bq, bv, mask, q_o, k_o, v_o, p_o, c_o):
    halves = lane_halves()

    def body(pick):
        wq, wk, wv = ((q_a, k_a, v_a), (q_b, k_b, v_b))[pick]
        rows = x[...]
        q_o[...] = (dot(rows, wq[...]) + bq[...]).astype(BF16)
        k_o[...] = dot(rows, wk[...]).astype(BF16)
        v_o[...] = (dot(rows, wv[...]) + bv[...]).astype(BF16)

    either(sec[0] == layer, body)
    for pair in range(q_o.shape[1] // 128):
        lanes = slice(pair * 128, pair * 128 + 128)
        for seq in range(seqs):
            rows = slice(seq * 128, seq * 128 + 128)
            scores = dot_t(q_o[rows, lanes], two_heads(k_o[rows, lanes], halves)) * 0.125
            scores = jnp.where(mask[seq : seq + 1, :] > 0.5, scores, -1e30)
            probs = []
            for part in (scores[:, :128], scores[:, 128:]):
                e = jnp.exp(part - jnp.max(part, axis=-1, keepdims=True))
                probs.append(e / jnp.sum(e, axis=-1, keepdims=True))
            probs = jnp.concatenate(probs, axis=1)
            p_o[seq, pair] = probs
            c_o[rows, lanes] = dot(
                probs.astype(BF16), two_heads(v_o[rows, lanes], halves)
            ).astype(BF16)


def attend_forward(layer, sec, x, w_own, w_other, bias_q, bias_v, mask):
    rows, width = x.shape
    seqs = mask.shape[0]
    wide = 256
    steps = width // wide
    own = lambda part: pl.BlockSpec(
        (width, wide), lambda j, s: (0, part * steps + jnp.where(s[0] == layer, j, 0))
    )
    other = lambda part: pl.BlockSpec(
        (width, wide), lambda j, s: (0, part * steps + jnp.where(s[0] == layer, 0, j))
    )
    column = pl.BlockSpec((rows, wide), lambda j, s: (0, j))
    bias = pl.BlockSpec((1, wide), lambda j, s: (0, j))
    return call(
        functools.partial(attend_kernel, layer, seqs),
        (steps,),
        [whole((rows, width)), own(0), own(1), own(2), other(0), other(1), other(2), bias, bias, whole(mask.shape)],
        [column, column, column, pl.BlockSpec((seqs, wide // 128, 128, 256), lambda j, s: (0, j, 0, 0)), column],
        [sds((rows, width), BF16)] * 3 + [sds((seqs, HEADS // 2, 128, 256), F32), sds((rows, width), BF16)],
        [],
        "attend_forward",
        2 * rows * width * width * 4,
        20 << 20,
    )(sec, x, w_own, w_own, w_own, w_other, w_other, w_other, bias_q, bias_v, mask)


def erf(value):
    value = jnp.clip(value, -4.0, 4.0)
    square = value * value
    top = -2.72614225801306e-10
    for item in (
        2.77068142495902e-08,
        -2.10102402082508e-06,
        -5.69250639462346e-05,
        -7.34990630326855e-04,
        -2.95459980854025e-03,
        -1.60960333262415e-02,
    ):
        top = top * square + item
    low = -1.45660718464996e-05
    for item in (
        -2.13374055278905e-04,
        -1.68282697438203e-03,
        -7.37332916720468e-03,
        -1.42647390514189e-02,
    ):
        low = low * square + item
    return value * top / low


def up_kernel(layer, sec, x, ctx, wo_a, wo_b, b_out, gain, offset, wu_a, wu_b, b_up, hat_o, scale_o, low_o, act_o, slope_o):
    step = pl.program_id(0)

    def first(pick):
        summed = x[...].astype(F32) + dot(ctx[...], (wo_a, wo_b)[pick][...]) + b_out[...]
        hat, scale = standardize(summed)
        hat_o[...] = hat
        scale_o[...] = scale
        low_o[...] = (hat * gain[...] + offset[...]).astype(BF16)

    def body(pick):
        pl.when(step == 0)(lambda: first(pick))
        pre = dot(low_o[...], (wu_a, wu_b)[pick][...]) + b_up[...]
        share = 0.5 + 0.5 * erf(pre * 0.7071067811865476)
        act_o[...] = (pre * share).astype(BF16)
        slope_o[...] = share + pre * (0.3989422804014327 * jnp.exp(-0.5 * pre * pre))

    either(sec[0] == layer, body)


def up_forward(layer, sec, x, ctx, wo, wo_other, b_out, gain, offset, wu, wu_other, b_up):
    rows, width = x.shape
    hidden = wu.shape[1]
    wide = 768
    steps = hidden // wide
    row = whole((1, width))
    flat = whole((rows, width))
    column = pl.BlockSpec((rows, wide), lambda j, s: (0, j))
    return call(
        functools.partial(up_kernel, layer),
        (steps,),
        [
            flat,
            flat,
            whole((width, width)),
            whole((width, width)),
            row,
            row,
            row,
            pl.BlockSpec((width, wide), lambda j, s: (0, jnp.where(s[0] == layer, j, 0))),
            pl.BlockSpec((width, wide), lambda j, s: (0, jnp.where(s[0] == layer, 0, j))),
            pl.BlockSpec((1, wide), lambda j, s: (0, j)),
        ],
        [flat, whole((rows, 1)), flat, column, column],
        [sds((rows, width), F32), sds((rows, 1), F32), sds((rows, width), BF16), sds((rows, hidden), BF16), sds((rows, hidden), F32)],
        [],
        "up_forward",
        2 * rows * width * (width + hidden),
        20 << 20,
    )(sec, x, ctx, wo, wo_other, b_out, gain, offset, wu, wu_other, b_up)


def down_kernel(layer, sec, act, wd_a, wd_b, hat_one, gain_one, offset_one, b_down, gain, offset, y_o, hat_o, scale_o, total):
    step = pl.program_id(0)

    @pl.when(step == 0)
    def _():
        total[...] = hat_one[...] * gain_one[...] + offset_one[...] + b_down[...]

    def body(pick):
        total[...] += dot(act[...], (wd_a, wd_b)[pick][...])

    either(sec[0] == layer, body)

    @pl.when(step == pl.num_programs(0) - 1)
    def _():
        hat, scale = standardize(total[...])
        hat_o[...] = hat
        scale_o[...] = scale
        y_o[...] = (hat * gain[...] + offset[...]).astype(BF16)


def down_forward(layer, sec, act, wd, wd_other, hat_one, gain_one, offset_one, b_down, gain, offset):
    rows, hidden = act.shape
    width = wd.shape[1]
    wide = 768
    row = whole((1, width))
    flat = whole((rows, width))
    return call(
        functools.partial(down_kernel, layer),
        (hidden // wide,),
        [
            pl.BlockSpec((rows, wide), lambda j, s: (0, j)),
            pl.BlockSpec((wide, width), lambda j, s: (jnp.where(s[0] == layer, j, 0), 0)),
            pl.BlockSpec((wide, width), lambda j, s: (jnp.where(s[0] == layer, 0, j), 0)),
            flat,
            row,
            row,
            row,
            row,
            row,
        ],
        [flat, flat, whole((rows, 1))],
        [sds((rows, width), BF16), sds((rows, width), F32), sds((rows, 1), F32)],
        [pltpu.VMEM((rows, width), F32)],
        "down_forward",
        2 * rows * width * hidden,
        14 << 20,
    )(sec, act, wd, wd_other, hat_one, gain_one, offset_one, b_down, gain, offset)


def down_grad_kernel(sec, gy, hat, scale, gain, act, second_o, branch_o, gain_o, offset_o, bias_o, send_o, keep_o):
    step = pl.program_id(0)
    half = pl.num_programs(0) // 2

    @pl.when(step == 0)
    def _():
        grad = gy[...].astype(F32)
        offset_o[...] = column_sum(grad)
        gain_o[...] = column_sum(grad * hat[...])
        second = norm_back(grad, hat[...], scale[...], gain[...])
        second_o[...] = second
        low = second.astype(BF16)
        branch_o[...] = low
        bias_o[...] = column_sum(low.astype(F32))

    block = t_dot(act[...], branch_o[...]).astype(BF16)

    @pl.when(step < half)
    def _():
        send_o[0] = block

    @pl.when(step >= half)
    def _():
        keep_o[0] = block


def down_grad(sec, gy, hat, scale, gain, act, shards):
    rows, width = gy.shape
    hidden = act.shape[1]
    tall = hidden // shards // 2
    row = whole((1, width))
    flat = whole((rows, width))
    return call(
        down_grad_kernel,
        (2 * shards,),
        [
            flat,
            flat,
            whole((rows, 1)),
            row,
            pl.BlockSpec(
                (rows, tall),
                lambda j, s: (0, 2 * (j % shards) + jnp.where(j < shards, 1 - s[0], s[0])),
            ),
        ],
        [
            flat,
            flat,
            row,
            row,
            row,
            pl.BlockSpec((1, tall, width), lambda j, s: (jnp.minimum(j, shards - 1), 0, 0)),
            pl.BlockSpec((1, tall, width), lambda j, s: (jnp.maximum(j - shards, 0), 0, 0)),
        ],
        [sds((rows, width), F32), sds((rows, width), BF16)]
        + [sds((1, width), F32)] * 3
        + [sds((shards, tall, width), BF16)] * 2,
        [],
        "down_grad",
        2 * rows * width * hidden,
        14 << 20,
    )(sec, gy, hat, scale, gain, act)


def up_grad_kernel(
    layer, sec, branch, second, wd_a, wd_b, slope, low, wu_a, wu_b, hat, scale, gain,
    first_o, attend_o, gain_o, offset_o, b_out_o, b_up_o, send_o, keep_o, total, pre,
):
    step = pl.program_id(0)
    half = pl.num_programs(0) // 2

    @pl.when(step == 0)
    def _():
        total[...] = second[...]

    def body(pick):
        grad = (dot_t(branch[...], (wd_a, wd_b)[pick][...]) * slope[...]).astype(BF16)
        pre[...] = grad
        total[...] += dot_t(grad, (wu_a, wu_b)[pick][...])

    either(sec[0] == layer, body)
    b_up_o[...] = column_sum(pre[...].astype(F32))
    block = t_dot(low[...], pre[...]).astype(BF16)

    @pl.when(step < half)
    def _():
        send_o[...] = block

    @pl.when(step >= half)
    def _():
        keep_o[...] = block

    @pl.when(step == pl.num_programs(0) - 1)
    def _():
        grad = total[...]
        offset_o[...] = column_sum(grad)
        gain_o[...] = column_sum(grad * hat[...])
        first = norm_back(grad, hat[...], scale[...], gain[...])
        first_o[...] = first
        attend = first.astype(BF16)
        attend_o[...] = attend
        b_out_o[...] = column_sum(attend.astype(F32))


def up_grad(layer, sec, branch, second, wd, wd_other, slope, low, wu, wu_other, hat, scale, gain):
    rows, width = branch.shape
    hidden = slope.shape[1]
    wide = 768
    steps = hidden // wide
    half = steps // 2
    row = whole((1, width))
    flat = whole((rows, width))
    at = lambda j, s: (j + half * (1 - s[0])) % steps
    mine = lambda j, s: jnp.where(s[0] == layer, at(j, s), 0)
    theirs = lambda j, s: jnp.where(s[0] == layer, 0, at(j, s))
    return call(
        functools.partial(up_grad_kernel, layer),
        (steps,),
        [
            flat,
            flat,
            pl.BlockSpec((wide, width), lambda j, s: (mine(j, s), 0)),
            pl.BlockSpec((wide, width), lambda j, s: (theirs(j, s), 0)),
            pl.BlockSpec((rows, wide), lambda j, s: (0, at(j, s))),
            flat,
            pl.BlockSpec((width, wide), lambda j, s: (0, mine(j, s))),
            pl.BlockSpec((width, wide), lambda j, s: (0, theirs(j, s))),
            flat,
            whole((rows, 1)),
            row,
        ],
        [
            flat,
            flat,
            row,
            row,
            row,
            pl.BlockSpec((1, wide), lambda j, s: (0, at(j, s))),
            pl.BlockSpec((width, wide), lambda j, s: (0, jnp.minimum(j, half - 1))),
            pl.BlockSpec((width, wide), lambda j, s: (0, jnp.maximum(j - half, 0))),
        ],
        [sds((rows, width), F32), sds((rows, width), BF16)]
        + [sds((1, width), F32)] * 3
        + [sds((1, hidden), F32)]
        + [sds((width, hidden // 2), BF16)] * 2,
        [pltpu.VMEM((rows, width), F32), pltpu.VMEM((rows, wide), BF16)],
        "up_grad",
        6 * rows * width * hidden,
        30 << 20,
    )(sec, branch, second, wd, wd_other, slope, low, wu, wu_other, hat, scale, gain)


def attend_grad_kernel(
    layer, seqs, sec, attend, attend_part, ctx, first, x, q, k, v, probs, wo_a, wo_b,
    q_a, k_a, v_a, q_b, k_b, v_b, bq_o, bv_o, gx_o, low_o, send_o, keep_o, total, gc, gq, gk, gv,
):
    step = pl.program_id(0)
    halves = lane_halves()
    wide = q.shape[1]

    @pl.when(step == 0)
    def _():
        total[...] = first[...]

    def before(pick):
        gc[...] = dot_t(attend[...], (wo_a, wo_b)[pick][...]).astype(BF16)

    either(sec[0] == layer, before)
    lower = lax.broadcasted_iota(jnp.int32, (128, 128), 1) < 64
    for pair in range(wide // 128):
        lanes = slice(pair * 128, pair * 128 + 128)
        for seq in range(seqs):
            rows = slice(seq * 128, seq * 128 + 128)
            grad = gc[rows, lanes]
            p = probs[seq, pair]
            gv_full = t_dot(p.astype(BF16), grad)
            gv[rows, lanes] = jnp.where(lower, gv_full[:128], gv_full[128:]).astype(BF16)
            gp = dot_t(grad, two_heads(v[rows, lanes], halves))
            parts = []
            for side in (slice(0, 128), slice(128, 256)):
                g, pp = gp[:, side], p[:, side]
                parts.append(pp * (g - jnp.sum(g * pp, axis=-1, keepdims=True)))
            gs = jnp.concatenate(parts, axis=1).astype(BF16)
            gq[rows, lanes] = (dot(gs, two_heads(k[rows, lanes], halves)) * 0.125).astype(BF16)
            gk_full = t_dot(gs, q[rows, lanes]) * 0.125
            gk[rows, lanes] = jnp.where(lower, gk_full[:128], gk_full[128:]).astype(BF16)

    bq_o[...] = column_sum(gq[...].astype(F32))
    bv_o[...] = column_sum(gv[...].astype(F32))

    def after(pick):
        wq, wk, wv = ((q_a, k_a, v_a), (q_b, k_b, v_b))[pick]
        total[...] += dot_t(gq[...], wq[...]) + dot_t(gk[...], wk[...]) + dot_t(gv[...], wv[...])

    either(sec[0] == layer, after)

    def store(out):
        rows = x[...]
        out[:, 0:wide] = t_dot(rows, gq[...]).astype(BF16)
        out[:, wide : 2 * wide] = t_dot(rows, gk[...]).astype(BF16)
        out[:, 2 * wide : 3 * wide] = t_dot(rows, gv[...]).astype(BF16)
        out[:, 3 * wide :] = t_dot(ctx[...], attend_part[...]).astype(BF16)

    pl.when(step == 0)(lambda: store(send_o))

    @pl.when(step == 1)
    def _():
        store(keep_o)
        gx_o[...] = total[...]
        low_o[...] = total[...].astype(BF16)


def attend_grad(layer, sec, attend, ctx, first, x, q, k, v, probs, wo, wo_other, w, w_other):
    rows, width = x.shape
    seqs = probs.shape[0]
    wide = width // 2
    row = pl.BlockSpec((1, wide), lambda j, s: (0, at(j, s)))
    flat = whole((rows, width))
    at = lambda j, s: jnp.where(j == 0, 1 - s[0], s[0])
    mine = lambda j, s: jnp.where(s[0] == layer, at(j, s), 0)
    theirs = lambda j, s: jnp.where(s[0] == layer, 0, at(j, s))
    column = pl.BlockSpec((rows, wide), lambda j, s: (0, at(j, s)))
    own = lambda part: pl.BlockSpec((width, wide), lambda j, s: (0, 2 * part + mine(j, s)))
    other = lambda part: pl.BlockSpec((width, wide), lambda j, s: (0, 2 * part + theirs(j, s)))
    return call(
        functools.partial(attend_grad_kernel, layer, seqs),
        (2,),
        [
            flat,
            column,
            flat,
            flat,
            flat,
            column,
            column,
            column,
            pl.BlockSpec((seqs, wide // 128, 128, 256), lambda j, s: (0, at(j, s), 0, 0)),
            pl.BlockSpec((wide, width), lambda j, s: (mine(j, s), 0)),
            pl.BlockSpec((wide, width), lambda j, s: (theirs(j, s), 0)),
            own(0),
            own(1),
            own(2),
            other(0),
            other(1),
            other(2),
        ],
        [row, row, flat, flat, whole((width, 4 * wide)), whole((width, 4 * wide))],
        [sds((1, width), F32)] * 2
        + [sds((rows, width), F32), sds((rows, width), BF16)]
        + [sds((width, 4 * wide), BF16)] * 2,
        [pltpu.VMEM((rows, width), F32)] + [pltpu.VMEM((rows, wide), BF16)] * 4,
        "attend_grad",
        2 * rows * width * width * 10,
        30 << 20,
    )(sec, attend, attend, ctx, first, x, q, k, v, probs, wo, wo_other, w, w, w, w_other, w_other, w_other)


def layer_forward(layer, sec, x, mask, big, other, small):
    w_qkv, w_out, w_up, w_down = big
    o_qkv, o_out, o_up, o_down = other
    b_q, b_v, b_out, gain_one, gain_two, offset_one, offset_two, b_up, b_down = small
    q, k, v, probs, ctx = attend_forward(layer, sec, x, w_qkv, o_qkv, b_q, b_v, mask)
    hat_one, scale_one, low, act, slope = up_forward(
        layer, sec, x, ctx, w_out, o_out, b_out, gain_one, offset_one, w_up, o_up, b_up
    )
    y, hat_two, scale_two = down_forward(
        layer, sec, act, w_down, o_down, hat_one, gain_one, offset_one, b_down, gain_two, offset_two
    )
    return y, (x, q, k, v, probs, ctx, hat_one, scale_one, low, act, slope, hat_two, scale_two)


def layer_backward(layer, sec, gy, cache, big, other, small, shards):
    w_qkv, w_out, w_up, w_down = big
    o_qkv, o_out, o_up, o_down = other
    b_q, b_v, b_out, gain_one, gain_two, offset_one, offset_two, b_up, b_down = small
    x, q, k, v, probs, ctx, hat_one, scale_one, low, act, slope, hat_two, scale_two = cache
    second, branch, g_gain_two, g_offset_two, g_b_down, d_send, d_keep = down_grad(
        sec, gy, hat_two, scale_two, gain_two, act, shards
    )
    first, attend, g_gain_one, g_offset_one, g_b_out, g_b_up, u_send, u_keep = up_grad(
        layer, sec, branch, second, w_down, o_down, slope, low, w_up, o_up, hat_one, scale_one, gain_one
    )
    g_bq, g_bv, gx, gx_low, a_send, a_keep = attend_grad(
        layer, sec, attend, ctx, first, x, q, k, v, probs, w_out, o_out, w_qkv, o_qkv
    )
    little = (g_bq, g_bv, g_b_out, g_gain_one, g_gain_two, g_offset_one, g_offset_two, g_b_up, g_b_down)
    return gx, gx_low, little, ((d_send, d_keep), (u_send, u_keep), (a_send, a_keep))


def exchange(array, axis, bit):
    length = lax.axis_size(axis)
    return lax.ppermute(array, axis, [(i, i ^ bit) for i in range(length)])


def plus(left, right):
    return (left.astype(F32) + right.astype(F32)).astype(BF16)


def pick(array, index, axis):
    return lax.dynamic_index_in_dim(array, index, axis, keepdims=False)


def inner_sum(part):
    shards, rows, columns = part.shape
    if shards != 4:
        return lax.psum_scatter(part, "inner", scatter_dimension=0, tiled=False)
    place = lax.axis_index("inner")
    low_bit, high_bit = place % 2, place // 2
    top = part[:, : rows // 2].reshape(2, 2, rows // 2, columns)
    bottom = part[:, rows // 2 :].reshape(2, 2, rows // 2, columns)
    top_got = exchange(pick(top, 1 - low_bit, 1), "inner", 1)
    bottom_got = exchange(pick(bottom, 1 - high_bit, 0), "inner", 2)
    top = plus(pick(top, low_bit, 1), top_got)
    bottom = plus(pick(bottom, high_bit, 0), bottom_got)
    top_got = exchange(pick(top, 1 - high_bit, 0), "inner", 2)
    bottom_got = exchange(pick(bottom, 1 - low_bit, 0), "inner", 1)
    top = plus(pick(top, high_bit, 0), top_got)
    bottom = plus(pick(bottom, low_bit, 0), bottom_got)
    return jnp.concatenate([top, bottom], axis=0)


def outer_sum(part):
    length = lax.axis_size("outer")
    if length != 4:
        return lax.psum(part, "outer")
    place = lax.axis_index("outer")
    part = plus(part, lax.ppermute(part, "outer", [(0, 1), (3, 2)]))
    part = plus(part, lax.ppermute(part, "outer", [(1, 2), (2, 1)]))
    last = lax.ppermute(part, "outer", [(1, 0), (2, 3)])
    return jnp.where((place == 0) | (place == 3), last, part)


def total_sum(send, keep, shards):
    got = exchange(send, "section", 1)
    part = plus(keep, got)
    part = part.reshape(shards, part.size // shards // part.shape[-1], part.shape[-1])
    return outer_sum(inner_sum(part))


def local(
    hidden_in, caption_len, region_len, cotangent, w_qkv, b_qv, w_out, b_out, ln_gain, ln_bias, w_up, b_up, w_down, b_down
):
    section = lax.axis_index("section")
    shards = lax.axis_size("inner")
    sec = section.astype(jnp.int32)[None]
    seqs_local, length, width = hidden_in.shape
    seqs = seqs_local // 2
    rows = seqs * length
    positions = jnp.arange(length, dtype=jnp.int32)[None, :]
    mine = lambda array: lax.dynamic_slice_in_dim(array, section * seqs, seqs, 0)
    caption, region = mine(caption_len)[:, None], mine(region_len)[:, None]
    valid = (positions < caption) | (positions >= CAP) & (positions < CAP + region)
    mask = jnp.concatenate([valid, valid], axis=1).astype(F32)
    x = mine(hidden_in).reshape(rows, width)
    gy = jnp.where(valid[:, :, None], mine(cotangent), jnp.zeros((), BF16)).reshape(rows, width)

    little = jnp.concatenate(
        [b_qv[0, 0], b_qv[0, 1], b_out[0], ln_gain[0, 0], ln_gain[0, 1], ln_bias[0, 0], ln_bias[0, 1], b_up[0], b_down[0]]
    )
    little_other = exchange(little, "section", 1)
    big = (w_qkv[0], w_out[0], w_up[0], w_down[0])
    other = tuple(exchange(item, "section", 1) for item in big)

    def split(flat):
        flat = flat[None]
        cuts = [0, 1, 2, 3, 4, 5, 6, 7, 11, 12]
        return tuple(flat[:, a * width : b * width] for a, b in zip(cuts[:-1], cuts[1:]))

    smalls = [split(jnp.where(section == layer, little, little_other)) for layer in (0, 1)]
    y_one, cache_one = layer_forward(0, sec, x, mask, big, other, smalls[0])
    y_two, cache_two = layer_forward(1, sec, y_one, mask, big, other, smalls[1])
    gx_two, gx_two_low, little_two, chunks_two = layer_backward(
        1, sec, gy, cache_two, big, other, smalls[1], shards
    )
    gx_one, gx_one_low, little_one, chunks_one = layer_backward(
        0, sec, gx_two_low, cache_one, big, other, smalls[0], shards
    )

    def gather(for_zero, for_one):
        kept = jnp.where(section == 0, for_zero, for_one)
        got = exchange(jnp.where(section == 0, for_one, for_zero), "section", 1)
        return jnp.where(section == 0, kept, got), jnp.where(section == 0, got, kept)

    activations = jnp.concatenate(gather(y_one, y_two), axis=0).reshape(seqs_local, length, width)
    input_grads = jnp.concatenate(
        gather(gx_one, gx_two_low.astype(F32)), axis=0
    ).reshape(seqs_local, length, width)
    sums_two = [total_sum(send, keep, shards) for send, keep in chunks_two]
    sums_one = [total_sum(send, keep, shards) for send, keep in chunks_one]
    down, up, attend = [gather(one, two) for one, two in zip(sums_one, sums_two)]
    g_w_down = jnp.concatenate(down, axis=0).astype(F32)
    g_w_up = jnp.concatenate(up, axis=1).astype(F32)
    part = width // 2
    g_w_qkv = jnp.concatenate(
        [side[:, i * part : (i + 1) * part] for i in range(3) for side in attend], axis=1
    ).astype(F32)
    g_w_out = jnp.concatenate([side[:, 3 * part :] for side in attend], axis=1).astype(F32)

    stacked = jnp.stack([jnp.concatenate([item[0] for item in little_one]), jnp.concatenate([item[0] for item in little_two])])
    stacked = lax.psum(stacked, ("section", "inner", "outer"))
    summed = pick(stacked, section, 0)
    place = lax.axis_index("inner")

    def shard(first, count):
        span = count * width // shards
        return lax.dynamic_slice_in_dim(summed[first * width : (first + count) * width], place * span, span, 0)

    return (
        activations[None],
        input_grads[None],
        g_w_qkv[None],
        jnp.stack([shard(0, 1), shard(1, 1)])[None],
        g_w_out[None],
        shard(2, 1)[None],
        jnp.stack([shard(3, 1), shard(4, 1)])[None],
        jnp.stack([shard(5, 1), shard(6, 1)])[None],
        g_w_up[None],
        shard(7, 4)[None],
        g_w_down[None],
        shard(11, 1)[None],
    )


def solution(mesh):
    rows = ("inner", "outer")
    return jax.shard_map(
        local,
        mesh=mesh,
        in_specs=(
            P(rows, None, None),
            P(rows),
            P(rows),
            P(rows, None, None),
            P("section", None, None),
            P("section", None, None),
            P("section", None, None),
            P("section", None),
            P("section", None, None),
            P("section", None, None),
            P("section", None, None),
            P("section", None),
            P("section", None, None),
            P("section", None),
        ),
        out_specs=(
            P("section", rows, None, None),
            P("section", rows, None, None),
            P("section", "inner", None),
            P("section", None, "inner"),
            P("section", "inner", None),
            P("section", "inner"),
            P("section", None, "inner"),
            P("section", None, "inner"),
            P("section", "inner", None),
            P("section", "inner"),
            P("section", "inner", None),
            P("section", "inner"),
        ),
        check_vma=False,
    )
```

time: 905 us -> 669 us (0.74)
  matrix products: 271 us -> 0 us
  Pallas kernels: 0 us -> 177 us
  local copies, waits for them, and re-layouts: 131 us -> 16.4 us
  starting transfers between devices: 10.2 us -> 61.6 us
  other arithmetic: 85.6 us -> 34.3 us
  waiting for transfers between devices: 367 us -> 352 us
  blocking collectives: 12.8 us -> 0 us
    dot_general x57 -> x0, matrix products: 271 us -> none  [the longest x12 85.1 us: back_project(): lax.dot_general(grad_rows, matrix, (((1,), (1,)), ((), ())), preferred_el...]
    ppermute x4 -> x58, waiting for transfers between devices: 1.84 us -> 232 us  [the longest x40 111 us: exchange(): return lax.ppermute(array, axis, [(i, i ^ bit) for i in range(length)])]
    pallas_call x0 -> x12, Pallas kernels: none -> 177 us  [the longest x2 47.4 us: attend_grad(): call(functools.partial(attend_grad_kernel, layer, seqs), (2,), [flat, col...]
    unnamed x17 -> x1, waiting for transfers between devices: 145 us -> 0.02 us
    reduce_scatter x4 -> x0, waiting for transfers between devices: 105 us -> none  [the longest x1 60 us: local(): lax.psum_scatter(g_w_down.astype(jnp.bfloat16), 'inner', scatter_dimensio...]
    ppermute x4 -> x58, starting transfers between devices: 8.91 us -> 61.5 us  [the longest x40 33.1 us: exchange(): return lax.ppermute(array, axis, [(i, i ^ bit) for i in range(length)])]
    unnamed x389 -> x93, local copies, waits for them, and re-layouts: 45.7 us -> 5.05 us
    reshape x11 -> x0, local copies, waits for them, and re-layouts: 35.3 us -> none  [the longest x5 20.4 us: layer_forward(): projected = projected.reshape(seq_count, length, 3, HEADS, head_size)]
  transfers between devices with their start and end apart: 15 -> 59, of which waited for: 10 -> 23; matrix products, arithmetic and copies ran while one was open for 18% -> 7% of each run, Pallas kernels for 0% -> 19%
where the time goes in v1:
time: 669 us; the launch traced here: 658 us
  waiting for transfers between devices  352 us (53%)
  Pallas kernels  177 us (26%)
  starting transfers between devices  61.6 us (9%)
  other arithmetic  34.3 us (5%)
  local copies, waits for them, and re-layouts  16.4 us (2%)
  between operations  16.3 us (2%)
    psum x1, waiting for transfers between devices, local(): stacked = lax.psum(stacked, ('section', 'inner', 'outer'))  121 us
    ppermute x40, waiting for transfers between devices, exchange(): return lax.ppermute(array, axis, [(i, i ^ bit) for i in range(length)])  111 us
    ppermute x6, waiting for transfers between devices, outer_sum(): last = lax.ppermute(part, 'outer', [(1, 0), (2, 3)])  67.6 us
    ppermute x6, waiting for transfers between devices, outer_sum(): part = plus(part, lax.ppermute(part, 'outer', [(0, 1), (3, 2)]))  52.7 us
    pallas_call x2, Pallas kernels, attend_grad(): call(functools.partial(attend_grad_kernel, layer, seqs), (2,), [flat, col...  47.4 us
    pallas_call x2, Pallas kernels, up_grad(): call(functools.partial(up_grad_kernel, layer), (steps,), [flat, flat, pl....  37.3 us
    ppermute x40, starting transfers between devices, exchange(): return lax.ppermute(array, axis, [(i, i ^ bit) for i in range(length)])  33.1 us
    pallas_call x2, Pallas kernels, up_forward(): call(functools.partial(up_kernel, layer), (steps,), [flat, flat, whole((w...  33.1 us
  transfers between devices with their start and end apart: 59, of which 23 were waited for; matrix products, arithmetic and copies ran while one was open for 7% of the time, Pallas kernels for 19%

profile of v1, /device:TPU:0, one launch (start us, length us, event | category | flops | bytes accessed | tf_op | source)
XLA Modules:
  0.0 658.2 jit_solution(11894380427947360655)
XLA Ops:
  20.1 9.0 %collective-permute-done.q_b.k_b.v_b = bf16[768,2304]{1,0:T(8,128)(2,1)} collective-permute-done((bf16[768,2304]{1,0:T(8,128)(2,1)}, bf16[768,2304]{1,0:T(8,128)(2,1)}, u32[]{:S(2)}, u32[]{:S(2)}) %collective-permute-start) | collective-permute-done | bytes 3538976 | tf_op jit(solution)/shard_map/ppermute | solution.py:561
  29.2 9.3 %attend_forward.2 = (bf16[512,768]{1,0:T(8,128)(2,1)}, bf16[512,768]{1,0:T(8,128)(2,1)}, bf16[512,768]{1,0:T(8,128)(2,1)}, f32[4,6,128,256]{3,2,1,0:T(8,128)}, bf16[512,768]{1,0:T(8,128)(2,1)}) custom-call(s32[1]{0:T(128)} %bitcast.sec, bf16[512,768]{1,0:T(8,128)(2,1)} %bitcast.232, bf16[768,2304]{1,0:T(8,128)(2,1)} %bitcast.205, ...), custom_call_target="tpu_custom_call" | custom-call | flops 2415919104 | bytes 20971520 | tf_op jit(solution)/shard_map/attend_forward/pallas_call | solution.py:132
  39.5 16.4 %up_forward.2 = (f32[512,768]{1,0:T(8,128)}, f32[512,1]{1,0:T(8,128)}, bf16[512,768]{1,0:T(8,128)(2,1)}, bf16[512,3072]{1,0:T(8,128)(2,1)}, f32[512,3072]{1,0:T(8,128)}) custom-call(s32[1]{0:T(128)} %bitcast.sec, bf16[512,768]{1,0:T(8,128)(2,1)} %bitcast.233, bf16[512,768]{1,0:T(8,128)(2,1)} %get-tuple-element.78.ctx, bf16[768,768]{1,0:T(8,128)(2,1)} %bitcast.228, ...), custom_call_target="tpu_custom_call" | custom-call | flops 3019898880 | bytes 20971520 | tf_op jit(solution)/shard_map/up_forward/pallas_call | solution.py:197
  55.9 9.0 %down_forward.2 = (bf16[512,768]{1,0:T(8,128)(2,1)}, f32[512,768]{1,0:T(8,128)}, f32[512,1]{1,0:T(8,128)}) custom-call(s32[1]{0:T(128)} %bitcast.sec, bf16[512,3072]{1,0:T(8,128)(2,1)} %get-tuple-element.79.act, bf16[3072,768]{1,0:T(8,128)(2,1)} %bitcast.218, bf16[3072,768]{1,0:T(8,128)(2,1)} %collective-permute-done.4.wd_b, ...), custom_call_target="tpu_custom_call" | custom-call | flops 2415919104 | bytes 14680064 | tf_op jit(solution)/shard_map/down_forward/pallas_call | solution.py:247
  64.9 9.6 %attend_forward.3 = (bf16[512,768]{1,0:T(8,128)(2,1)}, bf16[512,768]{1,0:T(8,128)(2,1)}, bf16[512,768]{1,0:T(8,128)(2,1)}, f32[4,6,128,256]{3,2,1,0:T(8,128)}, bf16[512,768]{1,0:T(8,128)(2,1)}) custom-call(s32[1]{0:T(128)} %bitcast.sec, bf16[512,768]{1,0:T(8,128)(2,1)} %get-tuple-element.81.x, bf16[768,2304]{1,0:T(8,128)(2,1)} %bitcast.208, ...), custom_call_target="tpu_custom_call" | custom-call | flops 2415919104 | bytes 20971520 | tf_op jit(solution)/shard_map/attend_forward/pallas_call | solution.py:132
  74.5 16.7 %up_forward.3 = (f32[512,768]{1,0:T(8,128)}, f32[512,1]{1,0:T(8,128)}, bf16[512,768]{1,0:T(8,128)(2,1)}, bf16[512,3072]{1,0:T(8,128)(2,1)}, f32[512,3072]{1,0:T(8,128)}) custom-call(s32[1]{0:T(128)} %bitcast.sec, bf16[512,768]{1,0:T(8,128)(2,1)} %get-tuple-element.81.x, bf16[512,768]{1,0:T(8,128)(2,1)} %get-tuple-element.82.ctx, bf16[768,768]{1,0:T(8,128)(2,1)} %bitcast.229, ...), custom_call_target="tpu_custom_call" | custom-call | flops 3019898880 | bytes 20971520 | tf_op jit(solution)/shard_map/up_forward/pallas_call | solution.py:197
  91.2 8.7 %down_forward.3 = (bf16[512,768]{1,0:T(8,128)(2,1)}, f32[512,768]{1,0:T(8,128)}, f32[512,1]{1,0:T(8,128)}) custom-call(s32[1]{0:T(128)} %bitcast.sec, bf16[512,3072]{1,0:T(8,128)(2,1)} %get-tuple-element.83.act, bf16[3072,768]{1,0:T(8,128)(2,1)} %bitcast.219, bf16[3072,768]{1,0:T(8,128)(2,1)} %collective-permute-done.4.wd_b, ...), custom_call_target="tpu_custom_call" | custom-call | flops 2415919104 | bytes 14680064 | tf_op jit(solution)/shard_map/down_forward/pallas_call | solution.py:247
  99.9 11.5 %down_grad.2 = (f32[512,768]{1,0:T(8,128)}, bf16[512,768]{1,0:T(8,128)(2,1)}, f32[1,768]{1,0:T(1,128)}, f32[1,768]{1,0:T(1,128)}, f32[1,768]{1,0:T(1,128)}, /*in...) custom-call(s32[1]{0:T(128)} %bitcast.sec, bf16[512,768]{1,0:T(8,128)(2,1)} %bitcast.265, ...), custom_call_target="tpu_custom_call" | custom-call | flops 2415919104 | bytes 14680064 | tf_op jit(solution)/shard_map/down_grad/pallas_call | solution.py:302
  111.7 18.6 %up_grad.2 = (f32[512,768]{1,0:T(8,128)}, bf16[512,768]{1,0:T(8,128)(2,1)}, f32[1,768]{1,0:T(1,128)}, f32[1,768]{1,0:T(1,128)}, f32[1,768]{1,0:T(1,128)}, /*inde...) custom-call(s32[1]{0:T(128)} %bitcast.sec, bf16[512,768]{1,0:T(8,128)(2,1)} %get-tuple-element.88.branch, ...), custom_call_target="tpu_custom_call" | custom-call | flops 7247757312 | bytes 31457280 | tf_op jit(solution)/shard_map/up_grad/pallas_call | solution.py:385
  130.4 23.8 %attend_grad.2 = (f32[1,768]{1,0:T(1,128)}, f32[1,768]{1,0:T(1,128)}, f32[512,768]{1,0:T(8,128)}, bf16[512,768]{1,0:T(8,128)(2,1)}, bf16[768,1536]{1,0:T(8,128)(2,1)}, /*index=5*/bf16[768,1536]{1,0:T(8,128)(2,1)}) custom-call(s32[1]{0:T(128)} %bitcast.sec, bf16[512,768]{1,0:T(8,128)(2,1)} %get-tuple-element.93.attend.attend_part, ...), custom_call_target="tpu_custom_call" | custom-call | flops 6039797760 | bytes 31457280 | tf_op jit(solution)/shard_map/attend_grad/pallas_call | solution.py:494
  154.2 11.4 %down_grad.3 = (f32[512,768]{1,0:T(8,128)}, bf16[512,768]{1,0:T(8,128)(2,1)}, f32[1,768]{1,0:T(1,128)}, f32[1,768]{1,0:T(1,128)}, f32[1,768]{1,0:T(1,128)}, /*in...) custom-call(s32[1]{0:T(128)} %bitcast.sec, bf16[512,768]{1,0:T(8,128)(2,1)} %get-tuple-element.99.gy, ...), custom_call_target="tpu_custom_call" | custom-call | flops 2415919104 | bytes 14680064 | tf_op jit(solution)/shard_map/down_grad/pallas_call | solution.py:302
  165.6 18.7 %up_grad.3 = (f32[512,768]{1,0:T(8,128)}, bf16[512,768]{1,0:T(8,128)(2,1)}, f32[1,768]{1,0:T(1,128)}, f32[1,768]{1,0:T(1,128)}, f32[1,768]{1,0:T(1,128)}, /*inde...) custom-call(s32[1]{0:T(128)} %bitcast.sec, bf16[512,768]{1,0:T(8,128)(2,1)} %get-tuple-element.102.branch, ...), custom_call_target="tpu_custom_call" | custom-call | flops 7247757312 | bytes 31457280 | tf_op jit(solution)/shard_map/up_grad/pallas_call | solution.py:385
  184.4 23.6 %attend_grad.3 = (f32[1,768]{1,0:T(1,128)}, f32[1,768]{1,0:T(1,128)}, f32[512,768]{1,0:T(8,128)}, bf16[512,768]{1,0:T(8,128)(2,1)}, bf16[768,1536]{1,0:T(8,128)(2,1)}, /*index=5*/bf16[768,1536]{1,0:T(8,128)(2,1)}) custom-call(s32[1]{0:T(128)} %bitcast.sec, bf16[512,768]{1,0:T(8,128)(2,1)} %get-tuple-element.107.attend.attend_part, ...), custom_call_target="tpu_custom_call" | custom-call | flops 6039797760 | bytes 31457280 | tf_op jit(solution)/shard_map/attend_grad/pallas_call | solution.py:494
  211.2 1.4 collective-permute-start.6
  214.8 120.7 %all-reduce.2.cloned.1.call-done = f32[2,9216]{1,0:T(2,128)} async-done(((f32[2,9216]{1,0:T(2,128)}), f32[2,9216]{1,0:T(2,128)}) %all-reduce.2.cloned.1.call-update) | async-done | bytes 73744 | tf_op jit(solution)/shard_map/psum | solution.py:669
  335.5 1.3 dynamic-slice.24
  336.8 1.4 fusion.40
  340.6 1.4 broadcast_select_fusion.1
  344.1 1.7 fusion.13
  345.8 1.9 pad_maximum_fusion
  349.2 2.2 add_convert_fusion
  351.8 1.5 collective-permute-start.50
  353.3 2.2 add_convert_fusion.1
  355.7 1.5 collective-permute-start.52
  357.2 2.3 add_convert_fusion.2
  359.7 1.5 collective-permute-start.42
  362.3 1.4 collective-permute-start.44
  364.7 1.4 collective-permute-start.33
  367.2 25.2 %collective-permute-done.33 = bf16[2,96,1536]{2,1,0:T(8,128)(2,1)S(1)} collective-permute-done((bf16[2,96,1536]{2,1,0:T(8,128)(2,1)S(1)}, bf16[2,96,1536]{2,1,0:T(8,128)(2,1)S(1)}, u32[]{:S(2)}, u32[]{:S(2)}) %collective-permute-start.33) | collective-permute-done | bytes 589856 | tf_op jit(solution)/shard_map/ppermute | solution.py:561
  392.3 1.4 collective-permute-start.25
  394.7 12.0 %collective-permute-done.25 = bf16[2,96,1536]{2,1,0:T(8,128)(2,1)S(1)} collective-permute-done((bf16[2,96,1536]{2,1,0:T(8,128)(2,1)S(1)}, bf16[2,96,1536]{2,1,0:T(8,128)(2,1)S(1)}, u32[]{:S(2)}, u32[]{:S(2)}) %collective-permute-start.25) | collective-permute-done | bytes 589856 | tf_op jit(solution)/shard_map/ppermute | solution.py:561
  406.7 1.5 collective-permute-start.27
  409.3 1.8 collective-permute-start.18
  411.8 11.2 %collective-permute-done.27 = bf16[2,96,1536]{2,1,0:T(8,128)(2,1)S(1)} collective-permute-done((bf16[2,96,1536]{2,1,0:T(8,128)(2,1)S(1)}, bf16[2,96,1536]{2,1,0:T(8,128)(2,1)S(1)}, u32[]{:S(2)}, u32[]{:S(2)}) %collective-permute-start.27) | collective-permute-done | bytes 589856 | tf_op jit(solution)/shard_map/ppermute | solution.py:561
  423.0 1.5 collective-permute-start.10
  425.4 10.2 %collective-permute-done.18 = bf16[2,96,1536]{2,1,0:T(8,128)(2,1)S(1)} collective-permute-done((bf16[2,96,1536]{2,1,0:T(8,128)(2,1)S(1)}, bf16[2,96,1536]{2,1,0:T(8,128)(2,1)S(1)}, u32[]{:S(2)}, u32[]{:S(2)}) %collective-permute-start.18) | collective-permute-done | bytes 589856 | tf_op jit(solution)/shard_map/ppermute | solution.py:561
  435.6 1.4 collective-permute-start.53
  438.2 1.6 collective-permute-start.45
  439.9 8.4 %collective-permute-done.10 = bf16[2,96,1536]{2,1,0:T(8,128)(2,1)S(1)} collective-permute-done((bf16[2,96,1536]{2,1,0:T(8,128)(2,1)S(1)}, bf16[2,96,1536]{2,1,0:T(8,128)(2,1)S(1)}, u32[]{:S(2)}, u32[]{:S(2)}) %collective-permute-start.10) | collective-permute-done | bytes 589856 | tf_op jit(solution)/shard_map/ppermute | solution.py:561
  448.3 1.5 collective-permute-start.34
  450.0 15.0 %collective-permute-done.34 = bf16[96,1536]{1,0:T(8,128)(2,1)S(1)} collective-permute-done((bf16[96,1536]{1,0:T(8,128)(2,1)S(1)}, bf16[96,1536]{1,0:T(8,128)(2,1)S(1)}, u32[]{:S(2)}, u32[]{:S(2)}) %collective-permute-start.34) | collective-permute-done | bytes 294944 | tf_op jit(solution)/shard_map/ppermute | solution.py:561
  466.0 5.8 collective-permute-done.36
  472.7 5.8 collective-permute-done.26
  479.4 8.1 %collective-permute-done.28 = bf16[96,1536]{1,0:T(8,128)(2,1)S(1)} collective-permute-done((bf16[96,1536]{1,0:T(8,128)(2,1)S(1)}, bf16[96,1536]{1,0:T(8,128)(2,1)S(1)}, u32[]{:S(2)}, u32[]{:S(2)}) %collective-permute-start.28) | collective-permute-done | bytes 294944 | tf_op jit(solution)/shard_map/ppermute | solution.py:561
  487.9 2.2 collective-permute-start.19
  490.4 2.0 collective-permute-start.11
  492.4 5.5 collective-permute-start.54
  498.1 1.7 collective-permute-start.46
  499.9 2.0 collective-permute-start.37
  502.1 1.3 collective-permute-start.29
  503.6 1.5 collective-permute-start.20
  505.3 6.4 collective-permute-done.54
  511.7 4.4 collective-permute-start.12
  516.2 8.1 %collective-permute-done.46 = bf16[384,768]{1,0:T(8,128)(2,1)S(1)} collective-permute-done((bf16[384,768]{1,0:T(8,128)(2,1)S(1)}, bf16[384,768]{1,0:T(8,128)(2,1)S(1)}, u32[]{:S(2)}, u32[]{:S(2)}) %collective-permute-start.46) | collective-permute-done | bytes 589856 | tf_op jit(solution)/shard_map/ppermute | solution.py:596
  525.2 11.8 %collective-permute-done.37 = bf16[192,1536]{1,0:T(8,128)(2,1)S(1)} collective-permute-done((bf16[192,1536]{1,0:T(8,128)(2,1)S(1)}, bf16[192,1536]{1,0:T(8,128)(2,1)S(1)}, u32[]{:S(2)}, u32[]{:S(2)}) %collective-permute-start.37) | collective-permute-done | bytes 589856 | tf_op jit(solution)/shard_map/ppermute | solution.py:596
  537.8 11.8 %collective-permute-done.29 = bf16[192,1536]{1,0:T(8,128)(2,1)S(1)} collective-permute-done((bf16[192,1536]{1,0:T(8,128)(2,1)S(1)}, bf16[192,1536]{1,0:T(8,128)(2,1)S(1)}, u32[]{:S(2)}, u32[]{:S(2)}) %collective-permute-start.29) | collective-permute-done | bytes 589856 | tf_op jit(solution)/shard_map/ppermute | solution.py:596
  550.4 9.1 %collective-permute-done.20 = bf16[192,1536]{1,0:T(8,128)(2,1)S(1)} collective-permute-done((bf16[192,1536]{1,0:T(8,128)(2,1)S(1)}, bf16[192,1536]{1,0:T(8,128)(2,1)S(1)}, u32[]{:S(2)}, u32[]{:S(2)}) %collective-permute-start.20) | collective-permute-done | bytes 589856 | tf_op jit(solution)/shard_map/ppermute | solution.py:596
  560.4 5.5 collective-permute-done.12
  574.9 42.5 %collective-permute-done.22 = bf16[192,1536]{1,0:T(8,128)(2,1)S(1)} collective-permute-done((bf16[192,1536]{1,0:T(8,128)(2,1)S(1)}, bf16[192,1536]{1,0:T(8,128)(2,1)S(1)}, u32[]{:S(2)}, u32[]{:S(2)}) %collective-permute-start.22) | collective-permute-done | bytes 589856 | tf_op jit(solution)/shard_map/ppermute | solution.py:598
  618.7 11.4 %collective-permute-done.14 = bf16[192,1536]{1,0:T(8,128)(2,1)S(1)} collective-permute-done((bf16[192,1536]{1,0:T(8,128)(2,1)S(1)}, bf16[192,1536]{1,0:T(8,128)(2,1)S(1)}, u32[]{:S(2)}, u32[]{:S(2)}) %collective-permute-start.14) | collective-permute-done | bytes 589856 | tf_op jit(solution)/shard_map/ppermute | solution.py:598
  631.0 7.4 %collective-permute-done.39 = bf16[192,1536]{1,0:T(8,128)(2,1)S(1)} collective-permute-done((bf16[192,1536]{1,0:T(8,128)(2,1)S(1)}, bf16[192,1536]{1,0:T(8,128)(2,1)S(1)}, u32[]{:S(2)}, u32[]{:S(2)}) %collective-permute-start.39) | collective-permute-done | bytes 589856 | tf_op jit(solution)/shard_map/ppermute | solution.py:598
  638.4 6.3 collective-permute-done.31
  646.7 1.6 maximum_convert_fusion.1
  648.4 1.7 maximum_convert_fusion
  (300 shorter events, 55.2 us)
Async XLA Ops:
  7.2 328.3 %all-reduce.2.cloned.1.call-start = ((), (), s32[]{:S(2)}) async-start(), calls=%async_computation | async-start | bytes 147456 | tf_op jit(solution)/shard_map/psum | solution.py:669
  7.2 31.3 %collective-permute-start.3 = (bf16[768,3072]{1,0:T(8,128)(2,1)}, bf16[768,3072]{1,0:T(8,128)(2,1)}, u32[]{:S(2)}, u32[]{:S(2)}) collective-permute-start(bf16[768,3072]{1,0:T(8,128)(2,1)} %bitcast.222), channel_id=1, source_target_pairs={{0,16},{16,0},{1,17},{17,1},{2,18},{18,2},{3,19},{19,3},{4,20},{20... | collective-permute-start | bytes 14155784 | tf_op jit(solution)/shard_map/ppermute | solution.py:561
  7.8 48.1 %collective-permute-start.4 = (bf16[3072,768]{1,0:T(8,128)(2,1)}, bf16[3072,768]{1,0:T(8,128)(2,1)}, u32[]{:S(2)}, u32[]{:S(2)}) collective-permute-start(bf16[3072,768]{1,0:T(8,128)(2,1)} %bitcast.217), channel_id=1, source_target_pairs={{0,16},{16,0},{1,17},{17,1},{2,18},{18,2},{3,19},{19,3},{4,20},{20... | collective-permute-start | bytes 14155784 | tf_op jit(solution)/shard_map/ppermute | solution.py:561
  7.8 21.3 %collective-permute-start = (bf16[768,2304]{1,0:T(8,128)(2,1)}, bf16[768,2304]{1,0:T(8,128)(2,1)}, u32[]{:S(2)}, u32[]{:S(2)}) collective-permute-start(bf16[768,2304]{1,0:T(8,128)(2,1)} %bitcast.204), channel_id=1, source_target_pairs={{0,16},{16,0},{1,17},{17,1},{2,18},{18,2},{3,19},{19,3},{4,20},{20... | collective-permute-start | bytes 10616840 | tf_op jit(solution)/shard_map/ppermute | solution.py:561
  12.9 4.8 collective-permute-start.1
  13.0 25.5 %collective-permute-start.2 = (bf16[768,768]{1,0:T(8,128)(2,1)}, bf16[768,768]{1,0:T(8,128)(2,1)S(1)}, u32[]{:S(2)}, u32[]{:S(2)}) collective-permute-start(bf16[768,768]{1,0:T(8,128)(2,1)} %bitcast.227), channel_id=1, source_target_pairs={{0,16},{16,0},{1,17},{17,1},{2,18},{18,2},{3,19},{19,3},{4,20},{20... | collective-permute-start | bytes 3538952 | tf_op jit(solution)/shard_map/ppermute | solution.py:561
  111.4 236.2 %collective-permute-start.49 = (bf16[4,384,768]{2,1,0:T(8,128)(2,1)}, bf16[4,384,768]{2,1,0:T(8,128)(2,1)}, u32[]{:S(2)}, u32[]{:S(2)}) collective-permute-start(bf16[4,384,768]{2,1,0:T(8,128)(2,1)} %get-tuple-element.143), channel_id=1, source_target_pairs={{0,16},{16,0},{1,17},{17,1},{2,18},{18,2},{3,19},{19,3},{4,20},{20... | collective-permute-start | bytes 7077896 | tf_op jit(solution)/shard_map/ppermute | solution.py:561
  184.4 25.4 %copy-start.18 = (f32[1,768]{1,0:T(1,128)S(1)}, f32[1,768]{1,0:T(1,128)}, u32[]{:S(2)}) copy-start(f32[1,768]{1,0:T(1,128)} %get-tuple-element.131) | copy-start | bytes 9220
  184.4 25.4 %copy-start.19 = (f32[1,768]{1,0:T(1,128)S(1)}, f32[1,768]{1,0:T(1,128)}, u32[]{:S(2)}) copy-start(f32[1,768]{1,0:T(1,128)} %get-tuple-element.132) | copy-start | bytes 9220
  184.4 25.4 %copy-start.17 = (f32[1,768]{1,0:T(1,128)S(1)}, f32[1,768]{1,0:T(1,128)}, u32[]{:S(2)}) copy-start(f32[1,768]{1,0:T(1,128)} %get-tuple-element.133) | copy-start | bytes 9220
  184.4 25.5 %copy-start.16 = (f32[1,768]{1,0:T(1,128)S(1)}, f32[1,768]{1,0:T(1,128)}, u32[]{:S(2)}) copy-start(f32[1,768]{1,0:T(1,128)} %get-tuple-element.135) | copy-start | bytes 9220
  184.4 25.5 %copy-start.6 = (bf16[512,768]{1,0:T(8,128)(2,1)S(1)}, bf16[512,768]{1,0:T(8,128)(2,1)}, u32[]{:S(2)}) copy-start(bf16[512,768]{1,0:T(8,128)(2,1)} %get-tuple-element.99.gy) | copy-start | bytes 2359300
  211.2 132.0 %collective-permute-start.6 = (f32[512,768]{1,0:T(8,128)}, f32[512,768]{1,0:T(8,128)}, u32[]{:S(2)}, u32[]{:S(2)}) collective-permute-start(f32[512,768]{1,0:T(8,128)} %convert_select_fusion), channel_id=1, source_target_pairs={{0,16},{16,0},{1,17},{17,1},{2,18},{18,2},{3,19},{19,3},{4,20},{20... | collective-permute-start | bytes 4718600 | tf_op jit(solution)/shard_map/ppermute | solution.py:561
  212.7 126.7 %collective-permute-start.5 = (bf16[512,768]{1,0:T(8,128)(2,1)S(1)}, bf16[512,768]{1,0:T(8,128)(2,1)}, u32[]{:S(2)}, u32[]{:S(2)}) collective-permute-start(bf16[512,768]{1,0:T(8,128)(2,1)S(1)} %broadcast_select_fusion.2), channel_id=1, source_target_pairs={{0,16},{16,0},{1,17},{17,1},{2,18},{18,2},{3,19},{19,3},{4,20},{20... | collective-permute-start | bytes 2359304 | tf_op jit(solution)/shard_map/ppermute | solution.py:561
  214.3 137.5 %collective-permute-start.41 = (bf16[4,384,768]{2,1,0:T(8,128)(2,1)}, bf16[4,384,768]{2,1,0:T(8,128)(2,1)}, u32[]{:S(2)}, u32[]{:S(2)}) collective-permute-start(bf16[4,384,768]{2,1,0:T(8,128)(2,1)} %get-tuple-element.141), channel_id=1, source_target_pairs={{0,16},{16,0},{1,17},{17,1},{2,18},{18,2},{3,19},{19,3},{4,20},{20... | collective-permute-start | bytes 7077896 | tf_op jit(solution)/shard_map/ppermute | solution.py:561
  214.4 141.3 %collective-permute-start.32 = (bf16[768,1536]{1,0:T(8,128)(2,1)}, bf16[768,1536]{1,0:T(8,128)(2,1)}, u32[]{:S(2)}, u32[]{:S(2)}) collective-permute-start(bf16[768,1536]{1,0:T(8,128)(2,1)} %get-tuple-element.139), channel_id=1, source_target_pairs={{0,16},{16,0},{1,17},{17,1},{2,18},{18,2},{3,19},{19,3},{4,20},{20... | collective-permute-start | bytes 7077896 | tf_op jit(solution)/shard_map/ppermute | solution.py:561
  339.4 20.4 %collective-permute-start.24 = (bf16[768,1536]{1,0:T(8,128)(2,1)}, bf16[768,1536]{1,0:T(8,128)(2,1)S(1)}, u32[]{:S(2)}, u32[]{:S(2)}) collective-permute-start(bf16[768,1536]{1,0:T(8,128)(2,1)} %get-tuple-element.137), channel_id=1, source_target_pairs={{0,16},{16,0},{1,17},{17,1},{2,18},{18,2},{3,19},{19,3},{4,20},{20... | collective-permute-start | bytes 7077896 | tf_op jit(solution)/shard_map/ppermute | solution.py:561
  343.2 19.1 %collective-permute-start.15 = (bf16[768,1536]{1,0:T(8,128)(2,1)S(1)}, bf16[768,1536]{1,0:T(8,128)(2,1)S(1)}, u32[]{:S(2)}, u32[]{:S(2)}) collective-permute-start(bf16[768,1536]{1,0:T(8,128)(2,1)S(1)} %copy-done.30), channel_id=1, source_target_pairs={{0,16},{16,0},{1,17},{17,1},{2,18},{18,2},{3,19},{19,3},{4,20},{20... | collective-permute-start | bytes 7077896 | tf_op jit(solution)/shard_map/ppermute | solution.py:561
  348.5 16.2 %collective-permute-start.7 = (bf16[768,1536]{1,0:T(8,128)(2,1)S(1)}, bf16[768,1536]{1,0:T(8,128)(2,1)S(1)}, u32[]{:S(2)}, u32[]{:S(2)}) collective-permute-start(bf16[768,1536]{1,0:T(8,128)(2,1)S(1)} %copy-done.31), channel_id=1, source_target_pairs={{0,16},{16,0},{1,17},{17,1},{2,18},{18,2},{3,19},{19,3},{4,20},{20... | collective-permute-start | bytes 7077896 | tf_op jit(solution)/shard_map/ppermute | solution.py:561
  351.8 42.2 %collective-permute-start.50 = (bf16[2,192,768]{2,1,0:T(8,128)(2,1)S(1)}, bf16[2,192,768]{2,1,0:T(8,128)(2,1)S(1)}, u32[]{:S(2)}, u32[]{:S(2)}) collective-permute-start(bf16[2,192,768]{2,1,0:T(8,128)(2,1)S(1)} %dynamic-slice_bitcast_fusion.1), channel_id=1, source_target_pairs={{0,4},{4,0},{8,12},{12,8},{1,5},{5,1},{9,13},{13,9},{2,6},{6,2},{1... | collective-permute-start | bytes 1769480 | tf_op jit(solution)/shard_map/ppermute | solution.py:561
  355.7 53.6 %collective-permute-start.52 = (bf16[2,192,768]{2,1,0:T(8,128)(2,1)S(1)}, bf16[2,192,768]{2,1,0:T(8,128)(2,1)S(1)}, u32[]{:S(2)}, u32[]{:S(2)}) collective-permute-start(bf16[2,192,768]{2,1,0:T(8,128)(2,1)S(1)} %dynamic-slice_bitcast_fusion), channel_id=1, source_target_pairs={{0,8},{4,12},{8,0},{12,4},{1,9},{5,13},{9,1},{13,5},{2,10},{6,14},... | collective-permute-start | bytes 1769480 | tf_op jit(solution)/shard_map/ppermute | solution.py:561
  359.7 51.5 %collective-permute-start.42 = (bf16[2,192,768]{2,1,0:T(8,128)(2,1)S(1)}, bf16[2,192,768]{2,1,0:T(8,128)(2,1)S(1)}, u32[]{:S(2)}, u32[]{:S(2)}) collective-permute-start(bf16[2,192,768]{2,1,0:T(8,128)(2,1)S(1)} %dynamic-slice_bitcast_fusion.3), channel_id=1, source_target_pairs={{0,4},{4,0},{8,12},{12,8},{1,5},{5,1},{9,13},{13,9},{2,6},{6,2},{1... | collective-permute-start | bytes 1769480 | tf_op jit(solution)/shard_map/ppermute | solution.py:561
  362.3 75.1 %collective-permute-start.44 = (bf16[2,192,768]{2,1,0:T(8,128)(2,1)S(1)}, bf16[2,192,768]{2,1,0:T(8,128)(2,1)S(1)}, u32[]{:S(2)}, u32[]{:S(2)}) collective-permute-start(bf16[2,192,768]{2,1,0:T(8,128)(2,1)S(1)} %dynamic-slice_bitcast_fusion.2), channel_id=1, source_target_pairs={{0,8},{4,12},{8,0},{12,4},{1,9},{5,13},{9,1},{13,5},{2,10},{6,14},... | collective-permute-start | bytes 1769480 | tf_op jit(solution)/shard_map/ppermute | solution.py:561
  364.7 27.6 %collective-permute-start.33 = (bf16[2,96,1536]{2,1,0:T(8,128)(2,1)S(1)}, bf16[2,96,1536]{2,1,0:T(8,128)(2,1)S(1)}, u32[]{:S(2)}, u32[]{:S(2)}) collective-permute-start(bf16[2,96,1536]{2,1,0:T(8,128)(2,1)S(1)} %dynamic-slice_bitcast_fusion.5), channel_id=1, source_target_pairs={{0,4},{4,0},{8,12},{12,8},{1,5},{5,1},{9,13},{13,9},{2,6},{6,2},{1... | collective-permute-start | bytes 1769480 | tf_op jit(solution)/shard_map/ppermute | solution.py:561
  392.3 14.4 %collective-permute-start.25 = (bf16[2,96,1536]{2,1,0:T(8,128)(2,1)S(1)}, bf16[2,96,1536]{2,1,0:T(8,128)(2,1)S(1)}, u32[]{:S(2)}, u32[]{:S(2)}) collective-permute-start(bf16[2,96,1536]{2,1,0:T(8,128)(2,1)S(1)} %dynamic-slice_bitcast_fusion.7), channel_id=1, source_target_pairs={{0,4},{4,0},{8,12},{12,8},{1,5},{5,1},{9,13},{13,9},{2,6},{6,2},{1... | collective-permute-start | bytes 1769480 | tf_op jit(solution)/shard_map/ppermute | solution.py:561
  394.0 14.7 %collective-permute-start.35 = (bf16[2,96,1536]{2,1,0:T(8,128)(2,1)S(1)}, bf16[2,96,1536]{2,1,0:T(8,128)(2,1)S(1)}, u32[]{:S(2)}, u32[]{:S(2)}) collective-permute-start(bf16[2,96,1536]{2,1,0:T(8,128)(2,1)S(1)} %dynamic-slice_bitcast_fusion.4), channel_id=1, source_target_pairs={{0,8},{4,12},{8,0},{12,4},{1,9},{5,13},{9,1},{13,5},{2,10},{6,14},... | collective-permute-start | bytes 1769480 | tf_op jit(solution)/shard_map/ppermute | solution.py:561
  406.7 16.3 %collective-permute-start.27 = (bf16[2,96,1536]{2,1,0:T(8,128)(2,1)S(1)}, bf16[2,96,1536]{2,1,0:T(8,128)(2,1)S(1)}, u32[]{:S(2)}, u32[]{:S(2)}) collective-permute-start(bf16[2,96,1536]{2,1,0:T(8,128)(2,1)S(1)} %dynamic-slice_bitcast_fusion.6), channel_id=1, source_target_pairs={{0,8},{4,12},{8,0},{12,4},{1,9},{5,13},{9,1},{13,5},{2,10},{6,14},... | collective-permute-start | bytes 1769480 | tf_op jit(solution)/shard_map/ppermute | solution.py:561
  408.6 16.3 %collective-permute-start.16 = (bf16[2,96,1536]{2,1,0:T(8,128)(2,1)S(1)}, bf16[2,96,1536]{2,1,0:T(8,128)(2,1)S(1)}, u32[]{:S(2)}, u32[]{:S(2)}) collective-permute-start(bf16[2,96,1536]{2,1,0:T(8,128)(2,1)S(1)} %dynamic-slice_bitcast_fusion.9), channel_id=1, source_target_pairs={{0,4},{4,0},{8,12},{12,8},{1,5},{5,1},{9,13},{13,9},{2,6},{6,2},{1... | collective-permute-start | bytes 1769480 | tf_op jit(solution)/shard_map/ppermute | solution.py:561
  409.3 26.4 %collective-permute-start.18 = (bf16[2,96,1536]{2,1,0:T(8,128)(2,1)S(1)}, bf16[2,96,1536]{2,1,0:T(8,128)(2,1)S(1)}, u32[]{:S(2)}, u32[]{:S(2)}) collective-permute-start(bf16[2,96,1536]{2,1,0:T(8,128)(2,1)S(1)} %dynamic-slice_bitcast_fusion.8), channel_id=1, source_target_pairs={{0,8},{4,12},{8,0},{12,4},{1,9},{5,13},{9,1},{13,5},{2,10},{6,14},... | collective-permute-start | bytes 1769480 | tf_op jit(solution)/shard_map/ppermute | solution.py:561
  411.2 26.9 %collective-permute-start.8 = (bf16[2,96,1536]{2,1,0:T(8,128)(2,1)S(1)}, bf16[2,96,1536]{2,1,0:T(8,128)(2,1)S(1)}, u32[]{:S(2)}, u32[]{:S(2)}) collective-permute-start(bf16[2,96,1536]{2,1,0:T(8,128)(2,1)S(1)} %dynamic-slice_bitcast_fusion.11), channel_id=1, source_target_pairs={{0,4},{4,0},{8,12},{12,8},{1,5},{5,1},{9,13},{13,9},{2,6},{6,2},{1... | collective-permute-start | bytes 1769480 | tf_op jit(solution)/shard_map/ppermute | solution.py:561
  423.0 25.3 %collective-permute-start.10 = (bf16[2,96,1536]{2,1,0:T(8,128)(2,1)S(1)}, bf16[2,96,1536]{2,1,0:T(8,128)(2,1)S(1)}, u32[]{:S(2)}, u32[]{:S(2)}) collective-permute-start(bf16[2,96,1536]{2,1,0:T(8,128)(2,1)S(1)} %dynamic-slice_bitcast_fusion.10), channel_id=1, source_target_pairs={{0,8},{4,12},{8,0},{12,4},{1,9},{5,13},{9,1},{13,5},{2,10},{6,14},... | collective-permute-start | bytes 1769480 | tf_op jit(solution)/shard_map/ppermute | solution.py:561
  424.9 62.9 %collective-permute-start.51 = (bf16[192,768]{1,0:T(8,128)(2,1)S(1)}, bf16[192,768]{1,0:T(8,128)(2,1)S(1)}, u32[]{:S(2)}, u32[]{:S(2)}) collective-permute-start(bf16[192,768]{1,0:T(8,128)(2,1)S(1)} %dynamic-slice_bitcast_fusion.13), channel_id=1, source_target_pairs={{0,8},{4,12},{8,0},{12,4},{1,9},{5,13},{9,1},{13,5},{2,10},{6,14},... | collective-permute-start | bytes 884744 | tf_op jit(solution)/shard_map/ppermute | solution.py:561
  435.6 54.5 %collective-permute-start.53 = (bf16[192,768]{1,0:T(8,128)(2,1)S(1)}, bf16[192,768]{1,0:T(8,128)(2,1)S(1)}, u32[]{:S(2)}, u32[]{:S(2)}) collective-permute-start(bf16[192,768]{1,0:T(8,128)(2,1)S(1)} %dynamic-slice_bitcast_fusion.12), channel_id=1, source_target_pairs={{0,4},{4,0},{8,12},{12,8},{1,5},{5,1},{9,13},{13,9},{2,6},{6,2},{1... | collective-permute-start | bytes 884744 | tf_op jit(solution)/shard_map/ppermute | solution.py:561
  437.4 53.0 %collective-permute-start.43 = (bf16[192,768]{1,0:T(8,128)(2,1)S(1)}, bf16[192,768]{1,0:T(8,128)(2,1)S(1)}, u32[]{:S(2)}, u32[]{:S(2)}) collective-permute-start(bf16[192,768]{1,0:T(8,128)(2,1)S(1)} %dynamic-slice_bitcast_fusion.15), channel_id=1, source_target_pairs={{0,8},{4,12},{8,0},{12,4},{1,9},{5,13},{9,1},{13,5},{2,10},{6,14},... | collective-permute-start | bytes 884744 | tf_op jit(solution)/shard_map/ppermute | solution.py:561
  438.2 54.2 %collective-permute-start.45 = (bf16[192,768]{1,0:T(8,128)(2,1)S(1)}, bf16[192,768]{1,0:T(8,128)(2,1)S(1)}, u32[]{:S(2)}, u32[]{:S(2)}) collective-permute-start(bf16[192,768]{1,0:T(8,128)(2,1)S(1)} %dynamic-slice_bitcast_fusion.14), channel_id=1, source_target_pairs={{0,4},{4,0},{8,12},{12,8},{1,5},{5,1},{9,13},{13,9},{2,6},{6,2},{1... | collective-permute-start | bytes 884744 | tf_op jit(solution)/shard_map/ppermute | solution.py:561
  448.3 16.7 %collective-permute-start.34 = (bf16[96,1536]{1,0:T(8,128)(2,1)S(1)}, bf16[96,1536]{1,0:T(8,128)(2,1)S(1)}, u32[]{:S(2)}, u32[]{:S(2)}) collective-permute-start(bf16[96,1536]{1,0:T(8,128)(2,1)S(1)} %dynamic-slice_bitcast_fusion.17), channel_id=1, source_target_pairs={{0,8},{4,12},{8,0},{12,4},{1,9},{5,13},{9,1},{13,5},{2,10},{6,14},... | collective-permute-start | bytes 884744 | tf_op jit(solution)/shard_map/ppermute | solution.py:561
  465.0 6.8 %collective-permute-start.36 = (bf16[96,1536]{1,0:T(8,128)(2,1)S(1)}, bf16[96,1536]{1,0:T(8,128)(2,1)S(1)}, u32[]{:S(2)}, u32[]{:S(2)}) collective-permute-start(bf16[96,1536]{1,0:T(8,128)(2,1)S(1)} %dynamic-slice_bitcast_fusion.16), channel_id=1, source_target_pairs={{0,4},{4,0},{8,12},{12,8},{1,5},{5,1},{9,13},{13,9},{2,6},{6,2},{1... | collective-permute-start | bytes 884744 | tf_op jit(solution)/shard_map/ppermute | solution.py:561
  471.8 6.7 %collective-permute-start.26 = (bf16[96,1536]{1,0:T(8,128)(2,1)S(1)}, bf16[96,1536]{1,0:T(8,128)(2,1)S(1)}, u32[]{:S(2)}, u32[]{:S(2)}) collective-permute-start(bf16[96,1536]{1,0:T(8,128)(2,1)S(1)} %dynamic-slice_bitcast_fusion.19), channel_id=1, source_target_pairs={{0,8},{4,12},{8,0},{12,4},{1,9},{5,13},{9,1},{13,5},{2,10},{6,14},... | collective-permute-start | bytes 884744 | tf_op jit(solution)/shard_map/ppermute | solution.py:561
  478.5 9.0 %collective-permute-start.28 = (bf16[96,1536]{1,0:T(8,128)(2,1)S(1)}, bf16[96,1536]{1,0:T(8,128)(2,1)S(1)}, u32[]{:S(2)}, u32[]{:S(2)}) collective-permute-start(bf16[96,1536]{1,0:T(8,128)(2,1)S(1)} %dynamic-slice_bitcast_fusion.18), channel_id=1, source_target_pairs={{0,4},{4,0},{8,12},{12,8},{1,5},{5,1},{9,13},{13,9},{2,6},{6,2},{1... | collective-permute-start | bytes 884744 | tf_op jit(solution)/shard_map/ppermute | solution.py:561
  487.5 10.6 %collective-permute-start.17 = (bf16[96,1536]{1,0:T(8,128)(2,1)S(1)}, bf16[96,1536]{1,0:T(8,128)(2,1)S(1)}, u32[]{:S(2)}, u32[]{:S(2)}) collective-permute-start(bf16[96,1536]{1,0:T(8,128)(2,1)S(1)} %dynamic-slice_bitcast_fusion.21), channel_id=1, source_target_pairs={{0,8},{4,12},{8,0},{12,4},{1,9},{5,13},{9,1},{13,5},{2,10},{6,14},... | collective-permute-start | bytes 884744 | tf_op jit(solution)/shard_map/ppermute | solution.py:561
  487.9 12.1 %collective-permute-start.19 = (bf16[96,1536]{1,0:T(8,128)(2,1)S(1)}, bf16[96,1536]{1,0:T(8,128)(2,1)S(1)}, u32[]{:S(2)}, u32[]{:S(2)}) collective-permute-start(bf16[96,1536]{1,0:T(8,128)(2,1)S(1)} %dynamic-slice_bitcast_fusion.20), channel_id=1, source_target_pairs={{0,4},{4,0},{8,12},{12,8},{1,5},{5,1},{9,13},{13,9},{2,6},{6,2},{1... | collective-permute-start | bytes 884744 | tf_op jit(solution)/shard_map/ppermute | solution.py:561
  490.1 12.0 %collective-permute-start.9 = (bf16[96,1536]{1,0:T(8,128)(2,1)S(1)}, bf16[96,1536]{1,0:T(8,128)(2,1)S(1)}, u32[]{:S(2)}, u32[]{:S(2)}) collective-permute-start(bf16[96,1536]{1,0:T(8,128)(2,1)S(1)} %dynamic-slice_bitcast_fusion.23), channel_id=1, source_target_pairs={{0,8},{4,12},{8,0},{12,4},{1,9},{5,13},{9,1},{13,5},{2,10},{6,14},... | collective-permute-start | bytes 884744 | tf_op jit(solution)/shard_map/ppermute | solution.py:561
  490.4 13.2 %collective-permute-start.11 = (bf16[96,1536]{1,0:T(8,128)(2,1)S(1)}, bf16[96,1536]{1,0:T(8,128)(2,1)S(1)}, u32[]{:S(2)}, u32[]{:S(2)}) collective-permute-start(bf16[96,1536]{1,0:T(8,128)(2,1)S(1)} %dynamic-slice_bitcast_fusion.22), channel_id=1, source_target_pairs={{0,4},{4,0},{8,12},{12,8},{1,5},{5,1},{9,13},{13,9},{2,6},{6,2},{1... | collective-permute-start | bytes 884744 | tf_op jit(solution)/shard_map/ppermute | solution.py:561
  492.4 19.3 %collective-permute-start.54 = (bf16[384,768]{1,0:T(8,128)(2,1)S(1)}, bf16[384,768]{1,0:T(8,128)(2,1)S(1)}, u32[]{:S(2)}, u32[]{:S(2)}) collective-permute-start(bf16[384,768]{1,0:T(8,128)(2,1)S(1)} %pad_maximum_fusion.7), channel_id=1, source_target_pairs={{0,1},{3,2},{4,5},{7,6},{8,9},{11,10},{12,13},{15,14},{16,17},{19,... | collective-permute-start | bytes 1769480 | tf_op jit(solution)/shard_map/ppermute | solution.py:596
  498.1 26.2 %collective-permute-start.46 = (bf16[384,768]{1,0:T(8,128)(2,1)S(1)}, bf16[384,768]{1,0:T(8,128)(2,1)S(1)}, u32[]{:S(2)}, u32[]{:S(2)}) collective-permute-start(bf16[384,768]{1,0:T(8,128)(2,1)S(1)} %pad_maximum_fusion.6), channel_id=1, source_target_pairs={{0,1},{3,2},{4,5},{7,6},{8,9},{11,10},{12,13},{15,14},{16,17},{19,... | collective-permute-start | bytes 1769480 | tf_op jit(solution)/shard_map/ppermute | solution.py:596
  499.9 37.0 %collective-permute-start.37 = (bf16[192,1536]{1,0:T(8,128)(2,1)S(1)}, bf16[192,1536]{1,0:T(8,128)(2,1)S(1)}, u32[]{:S(2)}, u32[]{:S(2)}) collective-permute-start(bf16[192,1536]{1,0:T(8,128)(2,1)S(1)} %pad_maximum_fusion.5), channel_id=1, source_target_pairs={{0,1},{3,2},{4,5},{7,6},{8,9},{11,10},{12,13},{15,14},{16,17},{19,... | collective-permute-start | bytes 1769480 | tf_op jit(solution)/shard_map/ppermute | solution.py:596
  502.1 47.5 %collective-permute-start.29 = (bf16[192,1536]{1,0:T(8,128)(2,1)S(1)}, bf16[192,1536]{1,0:T(8,128)(2,1)S(1)}, u32[]{:S(2)}, u32[]{:S(2)}) collective-permute-start(bf16[192,1536]{1,0:T(8,128)(2,1)S(1)} %pad_maximum_fusion.4), channel_id=1, source_target_pairs={{0,1},{3,2},{4,5},{7,6},{8,9},{11,10},{12,13},{15,14},{16,17},{19,... | collective-permute-start | bytes 1769480 | tf_op jit(solution)/shard_map/ppermute | solution.py:596
  503.6 55.9 %collective-permute-start.20 = (bf16[192,1536]{1,0:T(8,128)(2,1)S(1)}, bf16[192,1536]{1,0:T(8,128)(2,1)S(1)}, u32[]{:S(2)}, u32[]{:S(2)}) collective-permute-start(bf16[192,1536]{1,0:T(8,128)(2,1)S(1)} %pad_maximum_fusion.3), channel_id=1, source_target_pairs={{0,1},{3,2},{4,5},{7,6},{8,9},{11,10},{12,13},{15,14},{16,17},{19,... | collective-permute-start | bytes 1769480 | tf_op jit(solution)/shard_map/ppermute | solution.py:596
  511.7 54.2 %collective-permute-start.12 = (bf16[192,1536]{1,0:T(8,128)(2,1)S(1)}, bf16[192,1536]{1,0:T(8,128)(2,1)S(1)}, u32[]{:S(2)}, u32[]{:S(2)}) collective-permute-start(bf16[192,1536]{1,0:T(8,128)(2,1)S(1)} %pad_maximum_fusion.2), channel_id=1, source_target_pairs={{0,1},{3,2},{4,5},{7,6},{8,9},{11,10},{12,13},{15,14},{16,17},{19,... | collective-permute-start | bytes 1769480 | tf_op jit(solution)/shard_map/ppermute | solution.py:596
  524.3 42.4 %collective-permute-start.55 = (bf16[384,768]{1,0:T(8,128)(2,1)S(1)}, bf16[384,768]{1,0:T(8,128)(2,1)S(1)}, u32[]{:S(2)}, u32[]{:S(2)}) collective-permute-start(bf16[384,768]{1,0:T(8,128)(2,1)S(1)} %add_convert_fusion.7), channel_id=1, source_target_pairs={{1,2},{2,1},{5,6},{6,5},{9,10},{10,9},{13,14},{14,13},{17,18},{18,... | collective-permute-start | bytes 1769480 | tf_op jit(solution)/shard_map/ppermute | solution.py:597
  537.0 30.6 %collective-permute-start.47 = (bf16[384,768]{1,0:T(8,128)(2,1)S(1)}, bf16[384,768]{1,0:T(8,128)(2,1)S(1)}, u32[]{:S(2)}, u32[]{:S(2)}) collective-permute-start(bf16[384,768]{1,0:T(8,128)(2,1)S(1)} %add_convert_fusion.9), channel_id=1, source_target_pairs={{1,2},{2,1},{5,6},{6,5},{9,10},{10,9},{13,14},{14,13},{17,18},{18,... | collective-permute-start | bytes 1769480 | tf_op jit(solution)/shard_map/ppermute | solution.py:597
  549.6 22.3 %collective-permute-start.38 = (bf16[192,1536]{1,0:T(8,128)(2,1)S(1)}, bf16[192,1536]{1,0:T(8,128)(2,1)S(1)}, u32[]{:S(2)}, u32[]{:S(2)}) collective-permute-start(bf16[192,1536]{1,0:T(8,128)(2,1)S(1)} %add_convert_fusion.11), channel_id=1, source_target_pairs={{1,2},{2,1},{5,6},{6,5},{9,10},{10,9},{13,14},{14,13},{17,18},{18,... | collective-permute-start | bytes 1769480 | tf_op jit(solution)/shard_map/ppermute | solution.py:597
  559.6 13.8 %collective-permute-start.30 = (bf16[192,1536]{1,0:T(8,128)(2,1)S(1)}, bf16[192,1536]{1,0:T(8,128)(2,1)S(1)}, u32[]{:S(2)}, u32[]{:S(2)}) collective-permute-start(bf16[192,1536]{1,0:T(8,128)(2,1)S(1)} %add_convert_fusion.13), channel_id=1, source_target_pairs={{1,2},{2,1},{5,6},{6,5},{9,10},{10,9},{13,14},{14,13},{17,18},{18,... | collective-permute-start | bytes 1769480 | tf_op jit(solution)/shard_map/ppermute | solution.py:597
  565.9 3.2 collective-permute-start.21
  566.7 3.8 collective-permute-start.13
  567.6 62.6 %collective-permute-start.56 = (bf16[384,768]{1,0:T(8,128)(2,1)S(1)}, bf16[384,768]{1,0:T(8,128)(2,1)S(1)}, u32[]{:S(2)}, u32[]{:S(2)}) collective-permute-start(bf16[384,768]{1,0:T(8,128)(2,1)S(1)} %add_convert_fusion.6), channel_id=1, source_target_pairs={{1,0},{2,3},{5,4},{6,7},{9,8},{10,11},{13,12},{14,15},{17,16},{18,... | collective-permute-start | bytes 1769480 | tf_op jit(solution)/shard_map/ppermute | solution.py:598
  569.0 61.2 %collective-permute-start.48 = (bf16[384,768]{1,0:T(8,128)(2,1)S(1)}, bf16[384,768]{1,0:T(8,128)(2,1)S(1)}, u32[]{:S(2)}, u32[]{:S(2)}) collective-permute-start(bf16[384,768]{1,0:T(8,128)(2,1)S(1)} %add_convert_fusion.8), channel_id=1, source_target_pairs={{1,0},{2,3},{5,4},{6,7},{9,8},{10,11},{13,12},{14,15},{17,16},{18,... | collective-permute-start | bytes 1769480 | tf_op jit(solution)/shard_map/ppermute | solution.py:598
  570.5 46.9 %collective-permute-start.22 = (bf16[192,1536]{1,0:T(8,128)(2,1)S(1)}, bf16[192,1536]{1,0:T(8,128)(2,1)S(1)}, u32[]{:S(2)}, u32[]{:S(2)}) collective-permute-start(bf16[192,1536]{1,0:T(8,128)(2,1)S(1)} %add_convert_fusion.14), channel_id=1, source_target_pairs={{1,0},{2,3},{5,4},{6,7},{9,8},{10,11},{13,12},{14,15},{17,16},{18,... | collective-permute-start | bytes 1769480 | tf_op jit(solution)/shard_map/ppermute | solution.py:598
  572.0 58.1 %collective-permute-start.14 = (bf16[192,1536]{1,0:T(8,128)(2,1)S(1)}, bf16[192,1536]{1,0:T(8,128)(2,1)S(1)}, u32[]{:S(2)}, u32[]{:S(2)}) collective-permute-start(bf16[192,1536]{1,0:T(8,128)(2,1)S(1)} %add_convert_fusion.16), channel_id=1, source_target_pairs={{1,0},{2,3},{5,4},{6,7},{9,8},{10,11},{13,12},{14,15},{17,16},{18,... | collective-permute-start | bytes 1769480 | tf_op jit(solution)/shard_map/ppermute | solution.py:598
  573.4 65.0 %collective-permute-start.39 = (bf16[192,1536]{1,0:T(8,128)(2,1)S(1)}, bf16[192,1536]{1,0:T(8,128)(2,1)S(1)}, u32[]{:S(2)}, u32[]{:S(2)}) collective-permute-start(bf16[192,1536]{1,0:T(8,128)(2,1)S(1)} %add_convert_fusion.10), channel_id=1, source_target_pairs={{1,0},{2,3},{5,4},{6,7},{9,8},{10,11},{13,12},{14,15},{17,16},{18,... | collective-permute-start | bytes 1769480 | tf_op jit(solution)/shard_map/ppermute | solution.py:598
  617.4 27.4 %collective-permute-start.31 = (bf16[192,1536]{1,0:T(8,128)(2,1)S(1)}, bf16[192,1536]{1,0:T(8,128)(2,1)S(1)}, u32[]{:S(2)}, u32[]{:S(2)}) collective-permute-start(bf16[192,1536]{1,0:T(8,128)(2,1)S(1)} %add_convert_fusion.12), channel_id=1, source_target_pairs={{1,0},{2,3},{5,4},{6,7},{9,8},{10,11},{13,12},{14,15},{17,16},{18,... | collective-permute-start | bytes 1769480 | tf_op jit(solution)/shard_map/ppermute | solution.py:598
  630.1 14.8 %collective-permute-start.23 = (bf16[192,1536]{1,0:T(8,128)(2,1)S(1)}, bf16[192,1536]{1,0:T(8,128)(2,1)S(1)}, u32[]{:S(2)}, u32[]{:S(2)}) collective-permute-start(bf16[192,1536]{1,0:T(8,128)(2,1)S(1)} %get-tuple-element.156), channel_id=1, source_target_pairs={{0,16},{16,0},{1,17},{17,1},{2,18},{18,2},{3,19},{19,3},{4,20},{20... | collective-permute-start | bytes 1769480 | tf_op jit(solution)/shard_map/ppermute | solution.py:561
  630.4 16.1 %collective-permute-start.57 = (bf16[384,768]{1,0:T(8,128)(2,1)S(1)}, bf16[384,768]{1,0:T(8,128)(2,1)S(1)}, u32[]{:S(2)}, u32[]{:S(2)}) collective-permute-start(bf16[384,768]{1,0:T(8,128)(2,1)S(1)} %get-tuple-element.150), channel_id=1, source_target_pairs={{0,16},{16,0},{1,17},{17,1},{2,18},{18,2},{3,19},{19,3},{4,20},{20... | collective-permute-start | bytes 1769480 | tf_op jit(solution)/shard_map/ppermute | solution.py:561
  644.9 3.4 collective-permute-start.40
  (27 other events, 293.3 us)
Sparse Core Ops, SparseCore 0:
  214.3 121.1 all-reduce.1

commit v2 on v0

v2 whole, which is shorter than its diff:
```python
import functools

import jax
import jax.numpy as jnp
from jax import lax
from jax.experimental import pallas as pl
from jax.experimental.pallas import tpu as pltpu
from jax.sharding import PartitionSpec as P

HEADS = 12
CAP = 28
EPS = 1e-12
SCALE = 0.125
VMEM = 30 * 1024 * 1024
F32 = jnp.float32
BF16 = jnp.bfloat16
B_Q, B_V, B_OUT, GAIN_ONE, GAIN_TWO, OFFSET_ONE, OFFSET_TWO, B_DOWN, B_UP = range(9)


def dot(left, right):
    return jnp.dot(left, right, preferred_element_type=F32)


def dot_t(left, right):
    return lax.dot_general(left, right, (((1,), (1,)), ((), ())), preferred_element_type=F32)


def t_dot(left, right):
    return lax.dot_general(left, right, (((0,), (0,)), ((), ())), preferred_element_type=F32)


def column_sum(values):
    return jnp.sum(values, axis=0, keepdims=True)


def standardize(summed):
    centre = jnp.mean(summed, axis=-1, keepdims=True)
    shifted = summed - centre
    spread = jnp.mean(shifted * shifted, axis=-1, keepdims=True)
    scale = lax.rsqrt(spread + EPS)
    return shifted * scale, scale


def norm_back(grad, hat, scale, gain):
    scaled = grad * gain
    return scale * (
        scaled
        - jnp.mean(scaled, axis=-1, keepdims=True)
        - hat * jnp.mean(scaled * hat, axis=-1, keepdims=True)
    )


def gauss_share(value):
    bell = jnp.exp2(value * value * -0.7213475204444817)
    part = 1.0 / (1.0 + 0.2316418882 * jnp.abs(value))
    tail = 0.5307027145
    for item in (-0.7265760135, 0.7107068705, -0.142248368, 0.127414796):
        tail = tail * part + item
    tail = tail * part * bell
    return jnp.where(value < 0.0, tail, 1.0 - tail), bell


def lane_halves():
    lane = lax.broadcasted_iota(jnp.int32, (1, 128), 1)
    lower = jnp.where(lane < 64, 1.0, 0.0)
    return lower.astype(BF16), (1.0 - lower).astype(BF16)


def two_heads(block, halves):
    return jnp.concatenate([block * halves[0], block * halves[1]], axis=0)


def sds(shape, dtype):
    return jax.ShapeDtypeStruct(shape, dtype)


class Mover:
    def __init__(self, sems):
        self.sems, self.used, self.outs = sems, 0, []

    def copy(self, source, target):
        self.used += 1
        return pltpu.make_async_copy(source, target, self.sems.at[self.used - 1])

    def load(self, source, target):
        self.last = self.copy(source, target)
        self.last.start()

    def choose(self, first, one, two, target):
        copy = self.copy(one, target)
        other = pltpu.make_async_copy(two, target, self.sems.at[self.used - 1])
        pl.when(first)(copy.start)
        pl.when(jnp.logical_not(first))(other.start)
        return copy

    def store(self, source, target):
        copy = self.copy(source, target)
        copy.start()
        self.outs.append(copy)

    def finish(self):
        for copy in self.outs:
            copy.wait()


class Operand:
    def __init__(self, ref, buffer, far):
        self.ref, self.buffer, self.far = ref, buffer, far

    def fetch(self, move, *index):
        if self.far:
            move.load(*(ref.at[index] if index else ref for ref in (self.ref, self.buffer)))
            return [move.last]
        return []

    def flush(self, move, *index):
        if self.far:
            move.store(*(ref.at[index] if index else ref for ref in (self.buffer, self.ref)))


NEAR, FAR, RAW = "near", "far", "raw"


def ready(waits):
    for item in waits:
        item.wait()


def call(kernel, ids, ins, outs, scratch, name, flops, nbytes):
    space = lambda kind: pl.BlockSpec(memory_space=pltpu.VMEM if kind == NEAR else pltpu.HBM)
    kinds = [kind for _, kind in ins] + [kind for _, kind in outs]
    shapes = [array for array, _ in ins] + [shape for shape, _ in outs]
    buffers = [pltpu.VMEM(shape.shape, shape.dtype) for shape, kind in zip(shapes, kinds) if kind == FAR]

    def body(ids_ref, *refs):
        count = len(kinds)
        spare = list(refs[count : count + len(buffers)])
        operands = []
        for ref, kind in zip(refs[:count], kinds):
            buffer = spare.pop(0) if kind == FAR else ref
            operands.append(Operand(ref, buffer, kind == FAR))
        kernel(ids_ref, *operands, *refs[count + len(buffers) :])

    return pl.pallas_call(
        body,
        in_specs=[pl.BlockSpec(memory_space=pltpu.SMEM)] + [space(kind) for _, kind in ins],
        out_specs=[space(kind) for _, kind in outs],
        out_shape=[shape for shape, _ in outs],
        scratch_shapes=buffers + [pltpu.VMEM(*item) for item in scratch] + [pltpu.SemaphoreType.DMA((64,))],
        compiler_params=pltpu.CompilerParams(vmem_limit_bytes=VMEM),
        cost_estimate=pl.CostEstimate(flops=flops, bytes_accessed=nbytes, transcendentals=0),
        name=name,
    )(ids, *(array for array, _ in ins))


def attend_phase(q, k, v, probs, ctx, mask, pairs):
    seqs = mask.shape[1]
    halves = lane_halves()
    feature = lax.broadcasted_iota(jnp.int32, (128, 128), 0)
    first_half = jnp.where(feature < 64, 1.0, 0.0).astype(BF16)
    second_half = jnp.where(feature < 64, 0.0, 1.0).astype(BF16)

    @pl.loop(*pairs)
    def _(pair):
        lanes = pl.ds(pl.multiple_of(pair * 128, 128), 128)
        for seq in range(seqs):
            rows = slice(seq * 128, seq * 128 + 128)
            seen = jnp.broadcast_to(mask[:, seq : seq + 1], (256, 128)) > 0.5
            scores = dot_t(two_heads(k[rows, lanes], halves), q[rows, lanes] * SCALE)
            scores = jnp.where(seen, scores, -1e30)
            parts = []
            for part in (scores[:128], scores[128:]):
                e = jnp.exp(part - jnp.max(part, axis=0, keepdims=True))
                parts.append(e * (1.0 / jnp.sum(e, axis=0, keepdims=True)))
            parts = jnp.concatenate(parts, axis=0)
            probs[seq, pair] = parts
            turned = v[rows, lanes].T
            turned = jnp.concatenate([turned * first_half, turned * second_half], axis=1)
            ctx[lanes, rows] = dot(turned, parts.astype(BF16)).astype(BF16)


def attend_kernel(layer, sec, x, w_a, w_b, small, mask, q, k, v, probs, ctx, w, sems):
    move = Mover(sems)
    mine = sec[0] == layer
    rows, width = x.buffer.shape
    waits = x.fetch(move) + small.fetch(move) + mask.fetch(move)
    parts = [
        move.choose(mine, w_a.ref.at[:, pl.ds(i * width, width)], w_b.ref.at[:, pl.ds(i * width, width)], w.at[i])
        for i in (1, 0, 2)
    ]
    ready(waits)
    x, small = x.buffer, small.buffer
    parts[0].wait()
    k.buffer[...] = dot(x[...], w[1]).astype(BF16)
    k.flush(move)
    parts[1].wait()
    q.buffer[...] = (dot(x[...], w[0]) + small[B_Q : B_Q + 1]).astype(BF16)
    q.flush(move)
    parts[2].wait()
    v.buffer[...] = (dot(x[...], w[2]) + small[B_V : B_V + 1]).astype(BF16)
    v.flush(move)
    half = width // 128 // 2
    for i in range(2):
        attend_phase(
            q.buffer, k.buffer, v.buffer, probs.buffer, ctx.buffer, mask.buffer, (i * half, i * half + half)
        )
        probs.flush(move, slice(None), pl.ds(i * half, half))
    ctx.flush(move)
    move.finish()


def attend_forward(layer, sec, x, x_kind, w_own, w_other, small, mask):
    rows, width = x.shape
    seqs = mask.shape[1]
    pairs = width // 128
    wide = sds((rows, width), BF16)
    return call(
        functools.partial(attend_kernel, layer),
        sec,
        [(x, x_kind), (w_own, RAW), (w_other, RAW), (small, FAR), (mask, FAR)],
        [(wide, FAR)] * 3 + [(sds((seqs, pairs, 256, 128), F32), FAR), (sds((width, rows), BF16), NEAR)],
        [((3, width, width), BF16)],
        "attend_forward",
        2 * rows * width * width * 4,
        12 << 20,
    )


def up_kernel(layer, sec, x, ctx, wo_a, wo_b, wu_a, wu_b, small, hat, scale, turned, act, slope, wo, wu, low, sems):
    move = Mover(sems)
    mine = sec[0] == layer
    blocks, _, wide = wu.shape
    waits = ctx.fetch(move) + [move.choose(mine, wo_a.ref, wo_b.ref, wo)] + small.fetch(move) + x.fetch(move)
    span = lambda i: pl.ds(i * wide, wide)
    parts = [move.choose(mine, wu_a.ref.at[:, span(i)], wu_b.ref.at[:, span(i)], wu.at[i]) for i in range(blocks)]
    ready(waits)
    small = small.buffer
    summed = x.buffer[...].astype(F32) + t_dot(ctx.buffer[...], wo[...]) + small[B_OUT : B_OUT + 1]
    unit, root = standardize(summed)
    hat.buffer[...] = unit
    hat.flush(move)
    scale.buffer[...] = jnp.broadcast_to(root, scale.buffer.shape)
    scale.flush(move)
    low[...] = (unit * small[GAIN_ONE : GAIN_ONE + 1] + small[OFFSET_ONE : OFFSET_ONE + 1]).astype(BF16)
    turned.buffer[...] = low[...].T
    turned.flush(move)
    for i in range(blocks):
        parts[i].wait()
        pre = dot(low[...], wu[i]) + small[B_UP + i : B_UP + i + 1]
        share, bell = gauss_share(pre)
        act.buffer[i] = (pre * share).astype(BF16)
        slope.buffer[i] = share + pre * 0.3989422804014327 * bell
        act.flush(move, i)
        slope.flush(move, i)
    move.finish()


def up_forward(layer, sec, x, x_kind, ctx, wo, wo_other, wu, wu_other, small):
    rows, width = x.shape
    blocks = wu.shape[1] // width
    wide = (rows, width)
    return call(
        functools.partial(up_kernel, layer),
        sec,
        [(x, x_kind), (ctx, NEAR), (wo, RAW), (wo_other, RAW), (wu, RAW), (wu_other, RAW), (small, FAR)],
        [
            (sds(wide, F32), NEAR),
            (sds((rows, 128), F32), FAR),
            (sds((width, rows), BF16), FAR),
            (sds((blocks,) + wide, BF16), NEAR),
            (sds((blocks,) + wide, F32), FAR),
        ],
        [((width, width), BF16), ((blocks, width, width), BF16), (wide, BF16)],
        "up_forward",
        2 * rows * width * width * (blocks + 1),
        20 << 20,
    )


def down_kernel(layer, sec, act, wd_a, wd_b, hat, small, y, two, scale, wd, total, sems):
    move = Mover(sems)
    mine = sec[0] == layer
    blocks, wide, _ = wd.shape
    parts = []
    for i in range(blocks):
        span = pl.ds(i * wide, wide)
        parts.append(act.fetch(move, i) + [move.choose(mine, wd_a.ref.at[span], wd_b.ref.at[span], wd.at[i])])
        if i == 0:
            waits = small.fetch(move) + hat.fetch(move)
    for i in range(blocks):
        ready(parts[i])
        product = dot(act.buffer[i], wd[i])
        total[...] = product if i == 0 else total[...] + product
    ready(waits)
    small = small.buffer
    normed = hat.buffer[...] * small[GAIN_ONE : GAIN_ONE + 1] + small[OFFSET_ONE : OFFSET_ONE + 1]
    unit, root = standardize(total[...] + normed + small[B_DOWN : B_DOWN + 1])
    y.buffer[...] = (unit * small[GAIN_TWO : GAIN_TWO + 1] + small[OFFSET_TWO : OFFSET_TWO + 1]).astype(BF16)
    y.flush(move)
    two.buffer[...] = unit
    two.flush(move)
    scale.buffer[...] = jnp.broadcast_to(root, scale.buffer.shape)
    scale.flush(move)
    move.finish()


def down_forward(layer, sec, act, wd, wd_other, hat, small, y_kind, two_kind):
    blocks, rows, width = act.shape
    wide = (rows, width)
    return call(
        functools.partial(down_kernel, layer),
        sec,
        [(act, NEAR), (wd, RAW), (wd_other, RAW), (hat, NEAR), (small, FAR)],
        [(sds(wide, BF16), y_kind), (sds(wide, F32), two_kind), (sds((rows, 128), F32), two_kind)],
        [((blocks, width, width), BF16), (wide, F32)],
        "down_forward",
        2 * rows * width * width * blocks,
        12 << 20,
    )


def down_grad_kernel(sec, gy, hat, scale, small, act, second, branch, sums, send, keep, turned, sems):
    move = Mover(sems)
    blocks = act.buffer.shape[0]
    tall = send.buffer.shape[1]
    waits = gy.fetch(move) + small.fetch(move) + scale.fetch(move) + hat.fetch(move)
    parts = [act.fetch(move, i) for i in range(blocks)]
    ready(waits)
    grad = gy.buffer[...].astype(F32)
    sums.buffer[0:1] = column_sum(grad * hat.buffer[...])
    sums.buffer[1:2] = column_sum(grad)
    unit = norm_back(grad, hat.buffer[...], scale.buffer[:, 0:1], small.buffer[GAIN_TWO : GAIN_TWO + 1])
    second.buffer[...] = unit
    second.flush(move)
    low = unit.astype(BF16)
    branch.buffer[...] = low
    branch.flush(move)
    sums.buffer[2:3] = column_sum(low.astype(F32))
    sums.buffer[3:] = jnp.zeros_like(sums.buffer[3:])
    sums.flush(move)
    turned[...] = branch.buffer[...].T
    for half, out in ((1 - sec[0], send), (sec[0], keep)):
        left = pl.ds(pl.multiple_of(half * tall, tall), tall)
        for i in range(blocks):
            if out is send:
                ready(parts[i])
            out.buffer[i] = dot(turned[left, :], act.buffer[i]).astype(BF16)
            out.flush(move, i)
    move.finish()


def down_grad(sec, gy, gy_kind, hat, scale, small, act, kind):
    rows, width = gy.shape
    blocks = act.shape[0]
    wide = (rows, width)
    part = sds((blocks, width // 2, width), BF16)
    return call(
        down_grad_kernel,
        sec,
        [(gy, gy_kind), (hat, kind), (scale, kind), (small, FAR), (act, kind)],
        [(sds(wide, F32), NEAR), (sds(wide, BF16), NEAR), (sds((8, width), F32), NEAR), (part, FAR), (part, FAR)],
        [((width, rows), BF16)],
        "down_grad",
        2 * rows * width * width * blocks,
        14 << 20,
    )


def up_grad_kernel(
    layer, sec, branch, second, wd_a, wd_b, slope, low, wu_a, wu_b, hat, scale, small,
    first, attend, sums, send, keep, wd, wu, pre, send_buffer, keep_buffer, sems,
):
    move = Mover(sems)
    mine = sec[0] == layer
    blocks, wide, _ = wd.shape
    half = blocks // 2
    at = [lax.rem(i + half * (1 - sec[0]), blocks) for i in range(blocks)]
    span = [pl.ds(pl.multiple_of(place * wide, wide), wide) for place in at]
    parts = []
    early = branch.fetch(move)
    for i in range(blocks):
        parts.append(
            [move.choose(mine, wd_a.ref.at[span[i]], wd_b.ref.at[span[i]], wd.at[i])]
            + slope.fetch(move, at[i])
            + [move.choose(mine, wu_a.ref.at[:, span[i]], wu_b.ref.at[:, span[i]], wu.at[i])]
        )
        if i == 0:
            early += low.fetch(move)
    late = second.fetch(move) + hat.fetch(move) + scale.fetch(move) + small.fetch(move)
    ready(early)
    branch, low, total = branch.buffer, low.buffer, first.buffer
    for i in range(blocks):
        ready(parts[i])
        pre[...] = (dot_t(branch[...], wd[i]) * slope.buffer[at[i]]).astype(BF16)
        sums.buffer[pl.ds(3 + at[i], 1)] = column_sum(pre[...].astype(F32))
        out, out_h, place = (send_buffer, send, i) if i < half else (keep_buffer, keep, i - half)
        out[place] = dot(low[...], pre[...]).astype(BF16)
        move.store(out.at[place], out_h.ref.at[:, pl.ds(place * wide, wide)])
        if i == 0:
            ready(late)
            total[...] = second.buffer[...] + dot_t(pre[...], wu[i])
        else:
            total[...] += dot_t(pre[...], wu[i])
    grad = total[...]
    sums.buffer[0:1] = column_sum(grad * hat.buffer[...])
    sums.buffer[1:2] = column_sum(grad)
    unit = norm_back(grad, hat.buffer[...], scale.buffer[:, 0:1], small.buffer[GAIN_ONE : GAIN_ONE + 1])
    attend.buffer[...] = unit.astype(BF16)
    attend.flush(move)
    total[...] = unit
    first.flush(move)
    sums.buffer[2:3] = column_sum(attend.buffer[...].astype(F32))
    sums.buffer[3 + blocks :] = jnp.zeros_like(sums.buffer[3 + blocks :])
    sums.flush(move)
    move.finish()


def up_grad(layer, sec, branch, second, wd, wd_other, slope, low, wu, wu_other, hat, scale, small):
    blocks, rows, width = slope.shape
    wide = (rows, width)
    part = sds((width, blocks * width // 2), BF16)
    square = ((blocks, width, width), BF16)
    return call(
        functools.partial(up_grad_kernel, layer),
        sec,
        [
            (branch, NEAR),
            (second, NEAR),
            (wd, RAW),
            (wd_other, RAW),
            (slope, FAR),
            (low, FAR),
            (wu, RAW),
            (wu_other, RAW),
            (hat, FAR),
            (scale, FAR),
            (small, FAR),
        ],
        [(sds(wide, F32), NEAR), (sds(wide, BF16), NEAR), (sds((8, width), F32), NEAR), (part, RAW), (part, RAW)],
        [square, square, (wide, BF16)] + [((blocks // 2, width, width), BF16)] * 2,
        "up_grad",
        6 * rows * width * width * blocks,
        30 << 20,
    )


def attend_grad_kernel(
    layer, shards, sec, attend, ctx, first, x, q, k, v, probs, wo_a, wo_b, w_a, w_b, down, up,
    gx, gx_low, send, keep, turned, wo, w, gc, grads, sems,
):
    move = Mover(sems)
    mine = sec[0] == layer
    rows_all, width = x.buffer.shape
    seqs = probs.buffer.shape[0]
    wide = width // 2
    tall = width // shards
    pairs = wide // 128
    waits = attend.fetch(move) + [move.choose(mine, wo_a.ref, wo_b.ref, wo)]
    near = probs.fetch(move) + v.fetch(move) + k.fetch(move) + q.fetch(move)
    later = x.fetch(move) + ctx.fetch(move) + down.fetch(move) + up.fetch(move)
    last = [
        move.choose(mine, w_a.ref.at[:, pl.ds(i * width, width)], w_b.ref.at[:, pl.ds(i * width, width)], w.at[i])
        for i in range(3)
    ] + first.fetch(move)
    ready(waits)
    attend, q, k, v, probs = (item.buffer for item in (attend, q, k, v, probs))
    gc[...] = dot_t(attend[...], wo[...]).astype(BF16)
    ready(near)
    halves = lane_halves()
    lower = lax.broadcasted_iota(jnp.int32, (128, 128), 1) < 64

    def attention(first_pair):
        @pl.loop(0, pairs)
        def _(index):
            pair = first_pair + index
            lanes = pl.ds(pl.multiple_of(pair * 128, 128), 128)
            for seq in range(seqs):
                rows = slice(seq * 128, seq * 128 + 128)
                grad = gc[rows, lanes]
                p = probs[seq, pair]
                full = dot(p.astype(BF16), grad)
                grads[2, rows, lanes] = jnp.where(lower, full[:128], full[128:]).astype(BF16)
                gp = dot_t(two_heads(v[rows, lanes], halves), grad)
                parts = []
                for side in (slice(0, 128), slice(128, 256)):
                    g, pp = gp[side], p[side]
                    parts.append(pp * (g - jnp.sum(g * pp, axis=0, keepdims=True)))
                gs = jnp.concatenate(parts, axis=0).astype(BF16)
                grads[0, rows, lanes] = t_dot(gs, two_heads(k[rows, lanes] * SCALE, halves)).astype(BF16)
                full = dot(gs, q[rows, lanes] * SCALE)
                grads[1, rows, lanes] = jnp.where(lower, full[:128], full[128:]).astype(BF16)

    def products(half, out):
        lanes = pl.ds(pl.multiple_of(half * wide, wide), wide)
        for part in range(4):
            if part < 3:
                block = dot(turned[...], grads[part, :, lanes]).astype(BF16)
            else:
                block = dot(ctx.buffer[...], attend[:, lanes]).astype(BF16)
            for shard in range(shards):
                out.buffer[shard, :tall, part * wide : part * wide + wide] = block[shard * tall : shard * tall + tall]

    attention((1 - sec[0]) * pairs)
    ready(later)
    turned[...] = x.buffer[...].T
    products(1 - sec[0], send)
    attention(sec[0] * pairs)
    products(sec[0], keep)
    b_v = column_sum(grads[2].astype(F32))
    b_q = column_sum(grads[0].astype(F32))
    little = jnp.concatenate([down.buffer[0:3], b_v, down.buffer[4:8], up.buffer[0:7], b_q], axis=0).astype(BF16)
    little = jnp.concatenate([little, jnp.zeros_like(little)], axis=1)
    for shard in range(shards):
        send.buffer[shard, tall:] = little
        keep.buffer[shard, tall:] = little
    send.flush(move)
    keep.flush(move)
    ready(last)
    total = first.buffer[...] + dot_t(grads[0], w[0]) + dot_t(grads[1], w[1]) + dot_t(grads[2], w[2])
    gx.buffer[...] = total
    gx.flush(move)
    gx_low.buffer[...] = total.astype(BF16)
    gx_low.flush(move)
    move.finish()


def attend_grad(layer, sec, attend, ctx, first, x, q, k, v, probs, wo, wo_other, w, w_other, down, up, shards, low_kind):
    rows, width = x.shape
    wide = (rows, width)
    part = sds((shards, width // shards + 16, 2 * width), BF16)
    return call(
        functools.partial(attend_grad_kernel, layer, shards),
        sec,
        [(attend, NEAR), (ctx, FAR), (first, NEAR)]
        + [(item, FAR) for item in (x, q, k, v, probs)]
        + [(wo, RAW), (wo_other, RAW), (w, RAW), (w_other, RAW), (down, NEAR), (up, NEAR)],
        [(sds(wide, F32), FAR), (sds(wide, BF16), low_kind), (part, FAR), (part, FAR)],
        [((width, rows), BF16), ((width, width), BF16), ((3, width, width), BF16), (wide, BF16), ((3,) + wide, BF16)],
        "attend_grad",
        2 * rows * width * width * 10,
        30 << 20,
    )


def layer_forward(layer, sec, x, mask, big, other, small):
    w_qkv, w_out, w_up, w_down = big
    o_qkv, o_out, o_up, o_down = other
    x_kind = FAR if layer == 0 else NEAR
    q, k, v, probs, ctx = attend_forward(layer, sec, x, x_kind, w_qkv, o_qkv, small, mask)
    hat_one, scale_one, low, act, slope = up_forward(layer, sec, x, x_kind, ctx, w_out, o_out, w_up, o_up, small)
    kinds = (NEAR, FAR) if layer == 0 else (FAR, NEAR)
    y, hat_two, scale_two = down_forward(layer, sec, act, w_down, o_down, hat_one, small, *kinds)
    return y, (x, q, k, v, probs, ctx, hat_one, scale_one, low, act, slope, hat_two, scale_two)


def layer_backward(line, layer, sec, gy, cache, big, other, small, shards):
    w_qkv, w_out, w_up, w_down = big
    o_qkv, o_out, o_up, o_down = other
    x, q, k, v, probs, ctx, hat_one, scale_one, low, act, slope, hat_two, scale_two = cache
    kinds = (NEAR, FAR) if layer == 0 else (FAR, NEAR)
    second, branch, down, d_send, d_keep = line.advance(
        lambda: down_grad(sec, gy, kinds[0], hat_two, scale_two, small, act, kinds[1])
    )
    line.add(d_send, d_keep)
    first, attend, up, u_send, u_keep = line.advance(
        lambda: up_grad(
            layer, sec, branch, second, w_down, o_down, slope, low, w_up, o_up, hat_one, scale_one, small
        )
    )
    line.add(*(item.reshape(shards, item.shape[0] // shards, item.shape[1]) for item in (u_send, u_keep)))
    gx, gx_low, a_send, a_keep = line.advance(
        lambda: attend_grad(
            layer, sec, attend, ctx, first, x, q, k, v, probs, w_out, o_out, w_qkv, o_qkv, down, up, shards,
            FAR if layer == 0 else NEAR,
        )
    )
    line.add(a_send, a_keep)
    return gx, gx_low


def exchange(array, axis, bit):
    length = lax.axis_size(axis)
    return lax.ppermute(array, axis, [(i, i ^ bit) for i in range(length)])


def pick(array, index, axis):
    return lax.dynamic_index_in_dim(array, index, axis, keepdims=False)


def split_at(rows):
    return (rows // 2 + 15) // 16 * 16


def join_section(ids, ins, outs):
    kept, got = ins
    top_send, top_keep, bottom_send, bottom_keep = outs
    low_bit, high_bit = ids[1], ids[2]
    cut = top_send.shape[1]
    for i in range(2):
        for out, shard in ((top_send, 2 * i + 1 - low_bit), (top_keep, 2 * i + low_bit)):
            out[i] = kept[shard, :cut] + got[shard, :cut]
        for out, shard in ((bottom_send, 2 * (1 - high_bit) + i), (bottom_keep, 2 * high_bit + i)):
            out[i] = kept[shard, cut:] + got[shard, cut:]


def join_first(ids, ins, outs):
    top, top_got, bottom, bottom_got = ins
    top_send, top_keep, bottom_send, bottom_keep = outs
    low_bit, high_bit = ids[1], ids[2]
    top_send[...] = top[1 - high_bit] + top_got[1 - high_bit]
    top_keep[...] = top[high_bit] + top_got[high_bit]
    bottom_send[...] = bottom[1 - low_bit] + bottom_got[1 - low_bit]
    bottom_keep[...] = bottom[low_bit] + bottom_got[low_bit]


def join_second(ids, ins, outs):
    top, top_got, bottom, bottom_got = ins
    cut = top.shape[0]
    outs[0][:cut] = top[...] + top_got[...]
    outs[0][cut:] = bottom[...] + bottom_got[...]


def join_add(ids, ins, outs):
    outs[0][...] = ins[0][...] + ins[1][...]


def join_last(ids, ins, outs):
    @pl.when(ids[3] == 1)
    def _():
        outs[0][...] = ins[1][...]

    @pl.when(ids[3] == 0)
    def _():
        outs[0][...] = ins[0][...]


def join(ids, jobs):
    counts = [(len(ins), len(shapes)) for _, ins, shapes in jobs]
    n_in = sum(a for a, _ in counts)

    def kernel(ids_ref, *refs):
        at_in, at_out = 0, n_in
        for (function, _, _), (a, b) in zip(jobs, counts):
            function(ids_ref, refs[at_in : at_in + a], refs[at_out : at_out + b])
            at_in, at_out = at_in + a, at_out + b

    flat = [array for _, ins, _ in jobs for array in ins]
    shapes = [sds(shape, BF16) for _, _, shapes in jobs for shape in shapes]
    vmem = pl.BlockSpec(memory_space=pltpu.VMEM)
    outs = pl.pallas_call(
        kernel,
        in_specs=[pl.BlockSpec(memory_space=pltpu.SMEM)] + [vmem] * n_in,
        out_specs=[vmem] * len(shapes),
        out_shape=shapes,
        compiler_params=pltpu.CompilerParams(vmem_limit_bytes=VMEM),
        name="join_sums",
    )(ids, *flat)
    result = []
    for _, b in counts:
        result.append(outs[:b])
        outs = outs[b:]
    return result


def move_section(parts):
    send, keep = parts
    shards = lax.axis_size("inner")
    if shards != 4:
        got = lax.psum_scatter(send.astype(BF16), "inner", scatter_dimension=0, tiled=False)
        own = lax.psum_scatter(keep.astype(BF16), "inner", scatter_dimension=0, tiled=False)
        got = exchange(got, "section", 1)
        return [own, got], join_add, [own.shape]
    got = exchange(send, "section", 1)
    _, rows, columns = keep.shape
    cut = split_at(rows)
    return [keep, got], join_section, [(2, cut, columns)] * 2 + [(2, rows - cut, columns)] * 2


def move_first(parts):
    top_send, top, bottom_send, bottom = parts
    top_got = exchange(top_send, "inner", 1)
    bottom_got = exchange(bottom_send, "inner", 2)
    return [top, top_got, bottom, bottom_got], join_first, [top.shape[1:]] * 2 + [bottom.shape[1:]] * 2


def move_second(parts):
    top_send, top, bottom_send, bottom = parts
    top_got = exchange(top_send, "inner", 2)
    bottom_got = exchange(bottom_send, "inner", 1)
    rows = top.shape[0] + bottom.shape[0]
    return [top, top_got, bottom, bottom_got], join_second, [(rows, top.shape[1])]


def move_in(parts):
    return [parts[0], lax.ppermute(parts[0], "outer", [(0, 1), (3, 2)])], join_add, [parts[0].shape]


def move_across(parts):
    return [parts[0], lax.ppermute(parts[0], "outer", [(1, 2), (2, 1)])], join_add, [parts[0].shape]


def move_out(parts):
    return [parts[0], lax.ppermute(parts[0], "outer", [(1, 0), (2, 3)])], join_last, [parts[0].shape]


def move_any(parts):
    return [parts[0], lax.psum(parts[0], "outer")], lambda ids, ins, outs: join_last(ids, ins, outs), [parts[0].shape]


class Line:
    def __init__(self):
        inner = [move_section] + ([move_first, move_second] if lax.axis_size("inner") == 4 else [])
        place = lax.axis_index("outer")
        if lax.axis_size("outer") == 4:
            outer = [move_in, move_across, move_out]
            outside = ((place == 0) | (place == 3)).astype(jnp.int32)
        else:
            outer = [move_any]
            outside = jnp.ones((), jnp.int32)
        spot = lax.axis_index("inner")
        self.ids = jnp.stack([lax.axis_index("section"), spot % 2, spot // 2, outside]).astype(jnp.int32)
        self.moves = inner + outer
        self.running = []

    def add(self, send, keep):
        self.running.append({"at": 0, "parts": [send, keep], "pending": None})

    def settle(self):
        active = [item for item in self.running if item["pending"] is not None]
        if active:
            for item, parts in zip(active, join(self.ids, [item["pending"] for item in active])):
                item["parts"], item["pending"] = parts, None

    def advance(self, work=None):
        self.settle()
        active = [item for item in self.running if item["at"] < len(self.moves)]
        started = [self.moves[item["at"]](item["parts"]) for item in active]
        beside = work() if work is not None else ()
        beside, tied = lax.optimization_barrier((beside, [ins for ins, _, _ in started]))
        for item, ins, (_, function, shapes) in zip(active, tied, started):
            item["at"] += 1
            item["pending"] = (function, ins, shapes)
        return beside

    def done(self):
        return all(item["at"] == len(self.moves) for item in self.running)


def local(
    hidden_in, caption_len, region_len, cotangent, w_qkv, b_qv, w_out, b_out, ln_gain, ln_bias, w_up, b_up, w_down, b_down
):
    section = lax.axis_index("section")
    shards = lax.axis_size("inner")
    sec = section.astype(jnp.int32)[None]
    seqs_local, length, width = hidden_in.shape
    seqs = seqs_local // 2
    rows = seqs * length
    positions = jnp.arange(length, dtype=jnp.int32)[None, :]
    mine = lambda array: lax.dynamic_slice_in_dim(array, section * seqs, seqs, 0)
    caption, region = mine(caption_len)[:, None], mine(region_len)[:, None]
    valid = (positions < caption) | (positions >= CAP) & (positions < CAP + region)
    mask = jnp.concatenate([valid, valid], axis=1).astype(F32).T
    x = mine(hidden_in).reshape(rows, width)
    gy = jnp.where(valid[:, :, None], mine(cotangent), jnp.zeros((), BF16)).reshape(rows, width)

    blocks = w_up.shape[2] // width
    little = jnp.concatenate(
        [b_qv[0], b_out, ln_gain[0], ln_bias[0], b_down, b_up.reshape(blocks, width), jnp.zeros((8 - blocks, width), F32)]
    )
    little_other = exchange(little, "section", 1)
    big = (w_qkv[0], w_out[0], w_up[0], w_down[0])
    o_qkv = exchange(big[0], "section", 1)
    o_qkv, late_out, late_up = lax.optimization_barrier((o_qkv, big[1], big[2]))
    o_out, o_up = exchange(late_out, "section", 1), exchange(late_up, "section", 1)
    o_up, late_down = lax.optimization_barrier((o_up, big[3]))
    other = (o_qkv, o_out, o_up, exchange(late_down, "section", 1))

    smalls = [jnp.where(section == layer, little, little_other) for layer in (0, 1)]
    y_one, cache_one = layer_forward(0, sec, x, mask, big, other, smalls[0])
    y_two, cache_two = layer_forward(1, sec, y_one, mask, big, other, smalls[1])
    line = Line()
    gx_two, gx_two_low = layer_backward(line, 1, sec, gy, cache_two, big, other, smalls[1], shards)
    gx_one, gx_one_low = layer_backward(line, 0, sec, gx_two_low, cache_one, big, other, smalls[0], shards)

    def gather(for_zero, for_one):
        kept = jnp.where(section == 0, for_zero, for_one)
        got = exchange(jnp.where(section == 0, for_one, for_zero), "section", 1)
        return jnp.where(section == 0, kept, got), jnp.where(section == 0, got, kept)

    activations, input_grads = line.advance(
        lambda: (
            jnp.concatenate(gather(y_one, y_two), axis=0).reshape(seqs_local, length, width),
            jnp.concatenate(gather(gx_one, gx_two_low.astype(F32)), axis=0).reshape(seqs_local, length, width),
        )
    )
    while not line.done():
        line.advance()
    line.settle()
    sums = [item["parts"][0] for item in line.running]
    down, up, attend = [gather(one, two) for one, two in zip(sums[3:], sums[:3])]
    g_w_down = jnp.concatenate(down, axis=0).T.astype(F32)
    g_w_up = jnp.concatenate(up, axis=1).astype(F32)
    part = width // 2
    tall = width // shards
    matrix = [side[:tall] for side in attend]
    g_w_qkv = jnp.concatenate(
        [side[:, i * part : (i + 1) * part] for i in range(3) for side in matrix], axis=1
    ).astype(F32)
    g_w_out = jnp.concatenate([side[:, 3 * part :] for side in matrix], axis=1).astype(F32)
    rows = jnp.where(section == 0, sums[5][tall:, :width], sums[2][tall:, :width])
    place = lax.axis_index("inner")
    mine = lax.dynamic_slice_in_dim(rows, place * tall, tall, 1).astype(F32)
    up_row = pick(rows[11 : 11 + blocks].reshape(shards, width * blocks // shards), place, 0).astype(F32)
    return (
        activations[None],
        input_grads[None],
        g_w_qkv[None],
        jnp.stack([mine[15], mine[3]])[None],
        g_w_out[None],
        mine[10][None],
        jnp.stack([mine[8], mine[0]])[None],
        jnp.stack([mine[9], mine[1]])[None],
        g_w_up[None],
        up_row[None],
        g_w_down[None],
        mine[2][None],
    )


def solution(mesh):
    rows = ("inner", "outer")
    return jax.shard_map(
        local,
        mesh=mesh,
        in_specs=(
            P(rows, None, None),
            P(rows),
            P(rows),
            P(rows, None, None),
            P("section", None, None),
            P("section", None, None),
            P("section", None, None),
            P("section", None),
            P("section", None, None),
            P("section", None, None),
            P("section", None, None),
            P("section", None),
            P("section", None, None),
            P("section", None),
        ),
        out_specs=(
            P("section", rows, None, None),
            P("section", rows, None, None),
            P("section", "inner", None),
            P("section", None, "inner"),
            P("section", "inner", None),
            P("section", "inner"),
            P("section", None, "inner"),
            P("section", None, "inner"),
            P("section", "inner", None),
            P("section", "inner"),
            P("section", "inner", None),
            P("section", "inner"),
        ),
        check_vma=False,
    )
```

time: 905 us -> 427 us (0.47)
  matrix products: 271 us -> 0 us
  waiting for transfers between devices: 367 us -> 101 us
  Pallas kernels: 0 us -> 145 us
  other arithmetic: 85.6 us -> 21.6 us
  starting transfers between devices: 10.2 us -> 73.1 us
  local copies, waits for them, and re-layouts: 131 us -> 77.9 us
  between operations: 16.6 us -> 2.11 us
  blocking collectives: 12.8 us -> 0 us
    dot_general x57 -> x0, matrix products: 271 us -> none  [the longest x12 85.1 us: back_project(): lax.dot_general(grad_rows, matrix, (((1,), (1,)), ((), ())), preferred_el...]
    pallas_call x0 -> x23, Pallas kernels: none -> 145 us  [the longest x12 131 us: call(): pl.pallas_call(body, in_specs=[pl.BlockSpec(memory_space=pltpu.SMEM)] + [...]
    unnamed x17 -> x0, waiting for transfers between devices: 145 us -> none
    psum x1 -> x0, waiting for transfers between devices: 116 us -> none  [local(): lax.psum(shards[0].astype(jnp.bfloat16), 'outer').astype(jnp.float32)]
    reduce_scatter x4 -> x0, waiting for transfers between devices: 105 us -> none  [the longest x1 60 us: local(): lax.psum_scatter(g_w_down.astype(jnp.bfloat16), 'inner', scatter_dimensio...]
    ppermute x4 -> x58, waiting for transfers between devices: 1.84 us -> 101 us  [the longest x40 54.9 us: exchange(): return lax.ppermute(array, axis, [(i, i ^ bit) for i in range(length)])]
    ppermute x4 -> x58, starting transfers between devices: 8.91 us -> 73.1 us  [the longest x6 31.4 us: move_in(): lax.ppermute(parts[0], 'outer', [(0, 1), (3, 2)])]
    reshape x11 -> x1, local copies, waits for them, and re-layouts: 35.3 us -> 0.01 us  [local(): b_up.reshape(blocks, width)]
  transfers between devices with their start and end apart: 15 -> 58, of which waited for: 10 -> 19; matrix products, arithmetic and copies ran while one was open for 18% -> 6% of each run, Pallas kernels for 0% -> 24%
where the time goes in v2:
time: 427 us; the launch traced here: 421 us
  Pallas kernels  145 us (34%)
  waiting for transfers between devices  101 us (24%)
  local copies, waits for them, and re-layouts  77.9 us (18%)
  starting transfers between devices  73.1 us (17%)
  other arithmetic  21.6 us (5%)
    pallas_call x12, Pallas kernels, call(): pl.pallas_call(body, in_specs=[pl.BlockSpec(memory_space=pltpu.SMEM)] + [...  131 us
    unnamed x237, local copies, waits for them, and re-layouts  75.5 us
    ppermute x40, waiting for transfers between devices, exchange(): return lax.ppermute(array, axis, [(i, i ^ bit) for i in range(length)])  54.9 us
    ppermute x6, waiting for transfers between devices, move_out(): lax.ppermute(parts[0], 'outer', [(1, 0), (2, 3)])  44.7 us
    ppermute x6, starting transfers between devices, move_in(): lax.ppermute(parts[0], 'outer', [(0, 1), (3, 2)])  31.4 us
    ppermute x40, starting transfers between devices, exchange(): return lax.ppermute(array, axis, [(i, i ^ bit) for i in range(length)])  29.8 us
    pallas_call x11, Pallas kernels, join(): pl.pallas_call(kernel, in_specs=[pl.BlockSpec(memory_space=pltpu.SMEM)] +...  14.6 us
  transfers between devices with their start and end apart: 58, of which 19 were waited for; matrix products, arithmetic and copies ran while one was open for 6% of the time, Pallas kernels for 24%

profile of v2, /device:TPU:0, one launch (start us, length us, event | category | flops | bytes accessed | tf_op | source)
XLA Modules:
  0.0 421.4 jit_solution(17199611205617034630)
XLA Ops:
  1.2 6.1 %collective-permute-done.refs_2_.refs_11_ = bf16[768,2304]{1,0:T(8,128)(2,1)S(1)} collective-permute-done((bf16[768,2304]{1,0:T(8,128)(2,1)}, bf16[768,2304]{1,0:T(8,128)(2,1)S(1)}, u32[]{:S(2)}, u32[]{:S(2)}) %collective-permute-start) | collective-permute-done | bytes 3538976 | tf_op jit(solution)/shard_map/ppermute | solution.py:583
  7.2 1.8 copy-done.74
  9.4 7.7 %collective-permute-done.3.refs_5_.refs_7_ = bf16[768,3072]{1,0:T(8,128)(2,1)S(1)} collective-permute-done((bf16[768,3072]{1,0:T(8,128)(2,1)}, bf16[768,3072]{1,0:T(8,128)(2,1)S(1)}, u32[]{:S(2)}, u32[]{:S(2)}) %collective-permute-start.3) | collective-permute-done | bytes 4718624 | tf_op jit(solution)/shard_map/ppermute | solution.py:583
  17.1 2.1 copy-done.2
  24.6 2.4 dynamic-slice_select_fusion
  27.4 2.1 copy-done.70
  29.5 2.2 copy-done.75
  31.7 8.6 %attend_forward.2 = (bf16[512,768]{1,0:T(8,128)(2,1)S(1)}, bf16[512,768]{1,0:T(8,128)(2,1)S(1)}, bf16[512,768]{1,0:T(8,128)(2,1)S(1)}, f32[4,6,256,128]{3,2,1,0:T(8,128)S(1)}, bf16[768,512]{1,0:T(8,128)(2,1)S(1)}) custom-call(s32[1]{0:T(128)} %bitcast.ids_ref, bf16[512,768]{1,0:T(8,128)(2,1)S(1)} %bitcast.85, bf16[768,2304]{1,0:T(8,128)(2,1)S(1)} %bitcast.94, ...), custom_call_target="tpu_custom_call" | custom-call | flops 2415919104 | bytes 12582912 | tf_op jit(solution)/shard_map/attend_forward/pallas_call | solution.py:144
  42.1 4.1 copy-done.3
  46.2 1.4 copy-done.13
  47.6 12.1 %up_forward.2 = (f32[512,768]{1,0:T(8,128)S(1)}, f32[512,128]{1,0:T(8,128)S(1)}, bf16[768,512]{1,0:T(8,128)(2,1)S(1)}, bf16[4,512,768]{2,1,0:T(8,128)(2,1)S(1)}, f32[4,512,768]{2,1,0:T(8,128)}) custom-call(s32[1]{0:T(128)} %bitcast.ids_ref, bf16[512,768]{1,0:T(8,128)(2,1)S(1)} %bitcast.86, bf16[768,512]{1,0:T(8,128)(2,1)S(1)} %get-tuple-element.260.refs_1_, ...), custom_call_target="tpu_custom_call" | custom-call | flops 3019898880 | bytes 20971520 | tf_op jit(solution)/shard_map/up_forward/pallas_call | solution.py:144
  61.5 6.5 %down_forward.2 = (bf16[512,768]{1,0:T(8,128)(2,1)S(1)}, f32[512,768]{1,0:T(8,128)S(1)}, f32[512,128]{1,0:T(8,128)S(1)}) custom-call(s32[1]{0:T(128)} %bitcast.ids_ref, bf16[4,512,768]{2,1,0:T(8,128)(2,1)S(1)} %get-tuple-element.264.refs_0_.refs_4_, bf16[3072,768]{1,0:T(8,128)(2,1)S(1)} %bitcast.67, ...), custom_call_target="tpu_custom_call" | custom-call | flops 2415919104 | bytes 12582912 | tf_op jit(solution)/shard_map/down_forward/pallas_call | solution.py:144
  68.1 8.7 %attend_forward.3 = (bf16[512,768]{1,0:T(8,128)(2,1)S(1)}, bf16[512,768]{1,0:T(8,128)(2,1)S(1)}, bf16[512,768]{1,0:T(8,128)(2,1)S(1)}, f32[4,6,256,128]{3,2,1,0:T(8,128)S(1)}, bf16[768,512]{1,0:T(8,128)(2,1)S(1)}) custom-call(s32[1]{0:T(128)} %bitcast.ids_ref, bf16[512,768]{1,0:T(8,128)(2,1)S(1)} %get-tuple-element.267.refs_0_.refs_3_, ...), custom_call_target="tpu_custom_call" | custom-call | flops 2415919104 | bytes 12582912 | tf_op jit(solution)/shard_map/attend_forward/pallas_call | solution.py:144
  76.8 1.7 copy-done.93
  78.5 3.5 copy-done.4
  82.0 11.8 %up_forward.3 = (f32[512,768]{1,0:T(8,128)S(1)}, f32[512,128]{1,0:T(8,128)S(1)}, bf16[768,512]{1,0:T(8,128)(2,1)S(1)}, bf16[4,512,768]{2,1,0:T(8,128)(2,1)S(1)}, f32[4,512,768]{2,1,0:T(8,128)}) custom-call(s32[1]{0:T(128)} %bitcast.ids_ref, bf16[512,768]{1,0:T(8,128)(2,1)S(1)} %get-tuple-element.267.refs_0_.refs_3_, ...), custom_call_target="tpu_custom_call" | custom-call | flops 3019898880 | bytes 20971520 | tf_op jit(solution)/shard_map/up_forward/pallas_call | solution.py:144
  93.8 7.4 %down_forward.3 = (bf16[512,768]{1,0:T(8,128)(2,1)S(1)}, f32[512,768]{1,0:T(8,128)S(1)}, f32[512,128]{1,0:T(8,128)S(1)}) custom-call(s32[1]{0:T(128)} %bitcast.ids_ref, bf16[4,512,768]{2,1,0:T(8,128)(2,1)S(1)} %get-tuple-element.269.refs_0_.refs_4_, bf16[3072,768]{1,0:T(8,128)(2,1)S(1)} %bitcast.68, ...), custom_call_target="tpu_custom_call" | custom-call | flops 2415919104 | bytes 12582912 | tf_op jit(solution)/shard_map/down_forward/pallas_call | solution.py:144
  101.3 6.0 %down_grad.2 = (f32[512,768]{1,0:T(8,128)S(1)}, bf16[512,768]{1,0:T(8,128)(2,1)S(1)}, f32[8,768]{1,0:T(8,128)S(1)}, bf16[4,384,768]{2,1,0:T(8,128)(2,1)}, bf16[4,384,768]{2,1,0:T(8,128)(2,1)S(1)}) custom-call(s32[1]{0:T(128)} %bitcast.ids_ref, bf16[512,768]{1,0:T(8,128)(2,1)S(1)} %bitcast.90, f32[512,768]{1,0:T(8,128)S(1)} %get-tuple-element.272.refs_1_, ...), custom_call_target="tpu_custom_call" | custom-call | flops 2415919104 | bytes 14680064 | tf_op jit(solution)/shard_map/down_grad/pallas_call | solution.py:144
  108.1 14.0 %up_grad.2 = (f32[512,768]{1,0:T(8,128)S(1)}, bf16[512,768]{1,0:T(8,128)(2,1)S(1)}, f32[8,768]{1,0:T(8,128)S(1)}, bf16[768,1536]{1,0:T(8,128)(2,1)}, bf16[768,1536]{1,0:T(8,128)(2,1)S(1)}) custom-call(s32[1]{0:T(128)} %bitcast.ids_ref, bf16[512,768]{1,0:T(8,128)(2,1)S(1)} %get-tuple-element.274.refs_0_, f32[512,768]{1,0:T(8,128)S(1)} %get-tuple-element.275.refs_1_, ...), custom_call_target="tpu_custom_call" | custom-call | flops 7247757312 | bytes 31457280 | tf_op jit(solution)/shard_map/up_grad/pallas_call | solution.py:144
  126.1 1.4 copy-done.19
  127.9 1.7 copy-done.18
  129.5 1.7 copy-done.20
  132.1 2.7 collective-permute-start.7
  134.8 1.5 collective-permute-start.8
  138.9 1.9 copy-done.94
  144.2 17.3 %attend_grad.2 = (f32[512,768]{1,0:T(8,128)}, bf16[512,768]{1,0:T(8,128)(2,1)S(1)}, bf16[4,208,1536]{2,1,0:T(8,128)(2,1)}, bf16[4,208,1536]{2,1,0:T(8,128)(2,1)S(1)}) custom-call(s32[1]{0:T(128)} %bitcast.ids_ref, bf16[512,768]{1,0:T(8,128)(2,1)S(1)} %copy-done.84, bf16[768,512]{1,0:T(8,128)(2,1)S(1)} %copy-done.31, f32[512,768]{1,0:T(8,128)S(1)} %copy-done.80, ...), custom_call_target="tpu_custom_call" | custom-call | flops 6039797760 | bytes 31457280 | tf_op jit(solution)/shard_map/attend_grad/pallas_call | solution.py:144
  161.6 2.3 join_sums.12
  168.1 1.5 collective-permute-start.11
  169.7 7.1 %down_grad.3 = (f32[512,768]{1,0:T(8,128)S(1)}, bf16[512,768]{1,0:T(8,128)(2,1)S(1)}, f32[8,768]{1,0:T(8,128)S(1)}, bf16[4,384,768]{2,1,0:T(8,128)(2,1)}, bf16[4,384,768]{2,1,0:T(8,128)(2,1)S(1)}) custom-call(s32[1]{0:T(128)} %bitcast.ids_ref, bf16[512,768]{1,0:T(8,128)(2,1)S(1)} %get-tuple-element.305.refs_0_, f32[512,768]{1,0:T(8,128)S(1)} %copy-done.78, ...), custom_call_target="tpu_custom_call" | custom-call | flops 2415919104 | bytes 14680064 | tf_op jit(solution)/shard_map/down_grad/pallas_call | solution.py:144
  176.8 11.2 %collective-permute-done.10.refs_1_ = bf16[192,768]{1,0:T(8,128)(2,1)S(1)} collective-permute-done((bf16[192,768]{1,0:T(8,128)(2,1)S(1)}, bf16[192,768]{1,0:T(8,128)(2,1)S(1)}, u32[]{:S(2)}, u32[]{:S(2)}) %collective-permute-start.10) | collective-permute-done | bytes 294944 | tf_op jit(solution)/shard_map/ppermute | solution.py:583
  188.2 1.9 join_sums.13
  193.8 3.5 collective-permute-start.15
  197.3 1.6 collective-permute-start.19
  198.9 2.7 collective-permute-done.16.refs_3_
  201.6 1.5 collective-permute-start.17
  205.2 13.9 %up_grad.3 = (f32[512,768]{1,0:T(8,128)S(1)}, bf16[512,768]{1,0:T(8,128)(2,1)S(1)}, f32[8,768]{1,0:T(8,128)S(1)}, bf16[768,1536]{1,0:T(8,128)(2,1)}, bf16[768,1536]{1,0:T(8,128)(2,1)S(1)}) custom-call(s32[1]{0:T(128)} %bitcast.ids_ref, bf16[512,768]{1,0:T(8,128)(2,1)S(1)} %copy-done.33, f32[512,768]{1,0:T(8,128)S(1)} %get-tuple-element.330.refs_1_, ...), custom_call_target="tpu_custom_call" | custom-call | flops 7247757312 | bytes 31457280 | tf_op jit(solution)/shard_map/up_grad/pallas_call | solution.py:144
  227.9 3.3 join_sums.14
  233.9 6.3 %collective-permute-start.22 = (bf16[192,1536]{1,0:T(8,128)(2,1)S(1)}, bf16[192,1536]{1,0:T(8,128)(2,1)S(1)}, u32[]{:S(2)}, u32[]{:S(2)}) collective-permute-start(bf16[192,1536]{1,0:T(8,128)(2,1)S(1)} %get-tuple-element.398.refs_2_), channel_id=1, source_target_pairs={{0,1},{3,2},{4,5},{7,6},{8,9},{11,10},{12,13},{15,14},{16,17},{19,... | collective-permute-start | bytes 1769480 | tf_op jit(solution)/shard_map/ppermute | solution.py:695
  245.0 2.0 copy-done.73
  247.0 1.4 copy-done.82
  248.4 1.9 copy-done.92
  253.7 17.4 %attend_grad.3 = (f32[512,768]{1,0:T(8,128)S(1)}, bf16[512,768]{1,0:T(8,128)(2,1)}, bf16[4,208,1536]{2,1,0:T(8,128)(2,1)S(1)}, bf16[4,208,1536]{2,1,0:T(8,128)(2,1)S(1)}) custom-call(s32[1]{0:T(128)} %bitcast.ids_ref, bf16[512,768]{1,0:T(8,128)(2,1)S(1)} %copy-done.86, bf16[768,512]{1,0:T(8,128)(2,1)S(1)} %copy-done.27, f32[512,768]{1,0:T(8,128)S(1)} %copy-done.82, ...), custom_call_target="tpu_custom_call" | custom-call | flops 6039797760 | bytes 31457280 | tf_op jit(solution)/shard_map/attend_grad/pallas_call | solution.py:144
  283.7 1.5 collective-permute-start.33
  285.4 4.5 %collective-permute-done.32.refs_7_ = bf16[192,768]{1,0:T(8,128)(2,1)S(1)} collective-permute-done((bf16[192,768]{1,0:T(8,128)(2,1)S(1)}, bf16[192,768]{1,0:T(8,128)(2,1)S(1)}, u32[]{:S(2)}, u32[]{:S(2)}) %collective-permute-start.32) | collective-permute-done | bytes 294944 | tf_op jit(solution)/shard_map/ppermute | solution.py:583
  289.9 4.3 %collective-permute-start.31 = (bf16[208,1536]{1,0:T(8,128)(2,1)S(1)}, bf16[208,1536]{1,0:T(8,128)(2,1)S(1)}, u32[]{:S(2)}, u32[]{:S(2)}) collective-permute-start(bf16[208,1536]{1,0:T(8,128)(2,1)S(1)} %get-tuple-element.429.refs_4_), channel_id=1, source_target_pairs={{0,1},{3,2},{4,5},{7,6},{8,9},{11,10},{12,13},{15,14},{16,17},{19,... | collective-permute-start | bytes 1916936 | tf_op jit(solution)/shard_map/ppermute | solution.py:695
  296.7 1.5 collective-permute-start.34
  298.7 1.7 fusion.1
  300.5 1.9 pad_maximum_fusion
  302.4 7.8 %collective-permute-done.34.refs_11_ = bf16[2,96,1536]{2,1,0:T(8,128)(2,1)S(1)} collective-permute-done((bf16[2,96,1536]{2,1,0:T(8,128)(2,1)S(1)}, bf16[2,96,1536]{2,1,0:T(8,128)(2,1)S(1)}, u32[]{:S(2)}, u32[]{:S(2)}) %collective-permute-start.34) | collective-permute-done | bytes 589856 | tf_op jit(solution)/shard_map/ppermute | solution.py:583
  317.2 2.2 collective-permute-done.40.refs_7_
  319.4 4.8 %collective-permute-start.39 = (bf16[384,768]{1,0:T(8,128)(2,1)S(1)}, bf16[384,768]{1,0:T(8,128)(2,1)S(1)}, u32[]{:S(2)}, u32[]{:S(2)}) collective-permute-start(bf16[384,768]{1,0:T(8,128)(2,1)S(1)} %get-tuple-element.456.refs_4_), channel_id=1, source_target_pairs={{0,1},{3,2},{4,5},{7,6},{8,9},{11,10},{12,13},{15,14},{16,17},{19,... | collective-permute-start | bytes 1769480 | tf_op jit(solution)/shard_map/ppermute | solution.py:695
  324.6 5.3 %collective-permute-done.37.refs_1_ = bf16[192,1536]{1,0:T(8,128)(2,1)S(1)} collective-permute-done((bf16[192,1536]{1,0:T(8,128)(2,1)S(1)}, bf16[192,1536]{1,0:T(8,128)(2,1)S(1)}, u32[]{:S(2)}, u32[]{:S(2)}) %collective-permute-start.37) | collective-permute-done | bytes 589856 | tf_op jit(solution)/shard_map/ppermute | solution.py:703
  330.0 1.6 collective-permute-done.39.refs_5_
  331.6 2.6 collective-permute-done.43.refs_13_
  337.1 7.9 %collective-permute-start.46 = (bf16[192,1536]{1,0:T(8,128)(2,1)S(1)}, bf16[192,1536]{1,0:T(8,128)(2,1)S(1)}, u32[]{:S(2)}, u32[]{:S(2)}) collective-permute-start(bf16[192,1536]{1,0:T(8,128)(2,1)S(1)} %get-tuple-element.477.refs_4_), channel_id=1, source_target_pairs={{0,1},{3,2},{4,5},{7,6},{8,9},{11,10},{12,13},{15,14},{16,17},{19,... | collective-permute-start | bytes 1769480 | tf_op jit(solution)/shard_map/ppermute | solution.py:695
  345.0 1.6 collective-permute-start.47
  347.2 6.1 %collective-permute-done.48.refs_9_ = bf16[96,1536]{1,0:T(8,128)(2,1)S(1)} collective-permute-done((bf16[96,1536]{1,0:T(8,128)(2,1)S(1)}, bf16[96,1536]{1,0:T(8,128)(2,1)S(1)}, u32[]{:S(2)}, u32[]{:S(2)}) %collective-permute-start.48) | collective-permute-done | bytes 294944 | tf_op jit(solution)/shard_map/ppermute | solution.py:583
  354.2 4.5 %collective-permute-start.51 = (bf16[208,1536]{1,0:T(8,128)(2,1)S(1)}, bf16[208,1536]{1,0:T(8,128)(2,1)S(1)}, u32[]{:S(2)}, u32[]{:S(2)}) collective-permute-start(bf16[208,1536]{1,0:T(8,128)(2,1)S(1)} %get-tuple-element.490.refs_4_), channel_id=1, source_target_pairs={{0,1},{3,2},{4,5},{7,6},{8,9},{11,10},{12,13},{15,14},{16,17},{19,... | collective-permute-start | bytes 1916936 | tf_op jit(solution)/shard_map/ppermute | solution.py:695
  360.7 9.8 %collective-permute-done.49.refs_1_ = bf16[384,768]{1,0:T(8,128)(2,1)S(1)} collective-permute-done((bf16[384,768]{1,0:T(8,128)(2,1)S(1)}, bf16[384,768]{1,0:T(8,128)(2,1)S(1)}, u32[]{:S(2)}, u32[]{:S(2)}) %collective-permute-start.49) | collective-permute-done | bytes 589856 | tf_op jit(solution)/shard_map/ppermute | solution.py:703
  374.1 14.3 %collective-permute-done.52.refs_1_ = bf16[192,1536]{1,0:T(8,128)(2,1)S(1)} collective-permute-done((bf16[192,1536]{1,0:T(8,128)(2,1)S(1)}, bf16[192,1536]{1,0:T(8,128)(2,1)S(1)}, u32[]{:S(2)}, u32[]{:S(2)}) %collective-permute-start.52) | collective-permute-done | bytes 589856 | tf_op jit(solution)/shard_map/ppermute | solution.py:703
  392.0 1.6 convert_bitcast_fusion
  393.5 3.0 copy.29
  399.1 1.7 maximum_convert_fusion
  400.7 14.7 %collective-permute-done.54.refs_1_ = bf16[208,1536]{1,0:T(8,128)(2,1)S(1)} collective-permute-done((bf16[208,1536]{1,0:T(8,128)(2,1)}, bf16[208,1536]{1,0:T(8,128)(2,1)S(1)}, u32[]{:S(2)}, u32[]{:S(2)}) %collective-permute-start.54) | collective-permute-done | bytes 639008 | tf_op jit(solution)/shard_map/ppermute | solution.py:703
  (354 shorter events, 96.5 us)
Async XLA Ops:
  0.6 23.8 %copy-start = (bf16[8,128,768]{2,1,0:T(8,128)(2,1)S(1)}, bf16[8,128,768]{2,1,0:T(8,128)(2,1)}, u32[]{:S(2)}) copy-start(bf16[8,128,768]{2,1,0:T(8,128)(2,1)} %param.14) | copy-start | bytes 4718596
  0.7 6.6 %collective-permute-start = (bf16[768,2304]{1,0:T(8,128)(2,1)}, bf16[768,2304]{1,0:T(8,128)(2,1)S(1)}, u32[]{:S(2)}, u32[]{:S(2)}) collective-permute-start(bf16[768,2304]{1,0:T(8,128)(2,1)} %bitcast.93), channel_id=1, source_target_pairs={{0,16},{16,0},{1,17},{17,1},{2,18},{18,2},{3,19},{19,3},{4,20},{20... | collective-permute-start | bytes 10616840 | tf_op jit(solution)/shard_map/ppermute | solution.py:583
  9.0 8.1 %collective-permute-start.3 = (bf16[768,3072]{1,0:T(8,128)(2,1)}, bf16[768,3072]{1,0:T(8,128)(2,1)S(1)}, u32[]{:S(2)}, u32[]{:S(2)}) collective-permute-start(bf16[768,3072]{1,0:T(8,128)(2,1)} %bitcast.73), channel_id=1, source_target_pairs={{0,16},{16,0},{1,17},{17,1},{2,18},{18,2},{3,19},{19,3},{4,20},{20... | collective-permute-start | bytes 14155784 | tf_op jit(solution)/shard_map/ppermute | solution.py:583
  19.3 42.2 %collective-permute-start.4 = (bf16[3072,768]{1,0:T(8,128)(2,1)}, bf16[3072,768]{1,0:T(8,128)(2,1)}, u32[]{:S(2)}, u32[]{:S(2)}) collective-permute-start(bf16[3072,768]{1,0:T(8,128)(2,1)} %bitcast.64), channel_id=1, source_target_pairs={{0,16},{16,0},{1,17},{17,1},{2,18},{18,2},{3,19},{19,3},{4,20},{20... | collective-permute-start | bytes 14155784 | tf_op jit(solution)/shard_map/ppermute | solution.py:583
  22.4 4.9 %collective-permute-start.1 = (f32[16,768]{1,0:T(8,128)S(1)}, f32[16,768]{1,0:T(8,128)S(1)}, u32[]{:S(2)}, u32[]{:S(2)}) collective-permute-start(f32[16,768]{1,0:T(8,128)S(1)} %concatenate.65), channel_id=1, source_target_pairs={{0,16},{16,0},{1,17},{17,1},{2,18},{18,2},{3,19},{19,3},{4,20},{20... | collective-permute-start | bytes 147464 | tf_op jit(solution)/shard_map/ppermute | solution.py:583
  22.6 19.5 %collective-permute-start.2 = (bf16[768,768]{1,0:T(8,128)(2,1)}, bf16[768,768]{1,0:T(8,128)(2,1)}, u32[]{:S(2)}, u32[]{:S(2)}) collective-permute-start(bf16[768,768]{1,0:T(8,128)(2,1)} %bitcast.80), channel_id=1, source_target_pairs={{0,16},{16,0},{1,17},{17,1},{2,18},{18,2},{3,19},{19,3},{4,20},{20... | collective-permute-start | bytes 3538952 | tf_op jit(solution)/shard_map/ppermute | solution.py:583
  27.3 34.1 %copy-start.23 = (f32[16,768]{1,0:T(8,128)}, f32[16,768]{1,0:T(8,128)S(1)}, u32[]{:S(2)}) copy-start(f32[16,768]{1,0:T(8,128)S(1)} %get-tuple-element.541.refs_3_.refs_6_.refs_4_.refs_10_) | copy-start | bytes 147460
  42.1 19.4 %slice-start = ((s8[4718592]{0:T(1024)(128)(4,1)}), s8[4194304]{0:T(1024)(128)(4,1)S(1)}, s32[]{:S(2)}) async-start(s8[4718592]{0:T(1024)(128)(4,1)} %bitcast.65), calls=%async_computation | async-start | bytes 8388608
  107.4 18.7 %collective-permute-start.6 = (bf16[4,384,768]{2,1,0:T(8,128)(2,1)}, bf16[4,384,768]{2,1,0:T(8,128)(2,1)S(1)}, u32[]{:S(2)}, u32[]{:S(2)}) collective-permute-start(bf16[4,384,768]{2,1,0:T(8,128)(2,1)} %get-tuple-element.285), channel_id=1, source_target_pairs={{0,16},{16,0},{1,17},{17,1},{2,18},{18,2},{3,19},{19,3},{4,20},{20... | collective-permute-start | bytes 7077896 | tf_op jit(solution)/shard_map/ppermute | solution.py:583
  127.5 34.0 %collective-permute-start.9 = (bf16[4,192,1536]{2,1,0:T(8,128)(2,1)}, bf16[4,192,1536]{2,1,0:T(8,128)(2,1)}, u32[]{:S(2)}, u32[]{:S(2)}) collective-permute-start(bf16[4,192,1536]{2,1,0:T(8,128)(2,1)} %bitcast.16), channel_id=1, source_target_pairs={{0,16},{16,0},{1,17},{17,1},{2,18},{18,2},{3,19},{19,3},{4,20},{20... | collective-permute-start | bytes 7077896 | tf_op jit(solution)/shard_map/ppermute | solution.py:583
  132.1 29.4 %collective-permute-start.7 = (bf16[2,192,768]{2,1,0:T(8,128)(2,1)S(1)}, bf16[2,192,768]{2,1,0:T(8,128)(2,1)S(1)}, u32[]{:S(2)}, u32[]{:S(2)}) collective-permute-start(bf16[2,192,768]{2,1,0:T(8,128)(2,1)S(1)} %get-tuple-element.300), channel_id=1, source_target_pairs={{0,4},{4,0},{8,12},{12,8},{1,5},{5,1},{9,13},{13,9},{2,6},{6,2},{1... | collective-permute-start | bytes 1769480 | tf_op jit(solution)/shard_map/ppermute | solution.py:583
  134.8 26.7 %collective-permute-start.8 = (bf16[2,192,768]{2,1,0:T(8,128)(2,1)S(1)}, bf16[2,192,768]{2,1,0:T(8,128)(2,1)S(1)}, u32[]{:S(2)}, u32[]{:S(2)}) collective-permute-start(bf16[2,192,768]{2,1,0:T(8,128)(2,1)S(1)} %get-tuple-element.302), channel_id=1, source_target_pairs={{0,8},{4,12},{8,0},{12,4},{1,9},{5,13},{9,1},{13,5},{2,10},{6,14},... | collective-permute-start | bytes 1769480 | tf_op jit(solution)/shard_map/ppermute | solution.py:583
  161.5 26.5 %collective-permute-start.14 = (bf16[4,208,1536]{2,1,0:T(8,128)(2,1)}, bf16[4,208,1536]{2,1,0:T(8,128)(2,1)S(1)}, u32[]{:S(2)}, u32[]{:S(2)}) collective-permute-start(bf16[4,208,1536]{2,1,0:T(8,128)(2,1)} %get-tuple-element.328), channel_id=1, source_target_pairs={{0,16},{16,0},{1,17},{17,1},{2,18},{18,2},{3,19},{19,3},{4,20},{20... | collective-permute-start | bytes 7667720 | tf_op jit(solution)/shard_map/ppermute | solution.py:583
  165.5 22.5 %collective-permute-start.12 = (bf16[2,96,1536]{2,1,0:T(8,128)(2,1)S(1)}, bf16[2,96,1536]{2,1,0:T(8,128)(2,1)S(1)}, u32[]{:S(2)}, u32[]{:S(2)}) collective-permute-start(bf16[2,96,1536]{2,1,0:T(8,128)(2,1)S(1)} %get-tuple-element.324), channel_id=1, source_target_pairs={{0,4},{4,0},{8,12},{12,8},{1,5},{5,1},{9,13},{13,9},{2,6},{6,2},{1... | collective-permute-start | bytes 1769480 | tf_op jit(solution)/shard_map/ppermute | solution.py:583
  166.1 21.9 %collective-permute-start.13 = (bf16[2,96,1536]{2,1,0:T(8,128)(2,1)S(1)}, bf16[2,96,1536]{2,1,0:T(8,128)(2,1)S(1)}, u32[]{:S(2)}, u32[]{:S(2)}) collective-permute-start(bf16[2,96,1536]{2,1,0:T(8,128)(2,1)S(1)} %get-tuple-element.326), channel_id=1, source_target_pairs={{0,8},{4,12},{8,0},{12,4},{1,9},{5,13},{9,1},{13,5},{2,10},{6,14},... | collective-permute-start | bytes 1769480 | tf_op jit(solution)/shard_map/ppermute | solution.py:583
  166.8 21.2 %collective-permute-start.10 = (bf16[192,768]{1,0:T(8,128)(2,1)S(1)}, bf16[192,768]{1,0:T(8,128)(2,1)S(1)}, u32[]{:S(2)}, u32[]{:S(2)}) collective-permute-start(bf16[192,768]{1,0:T(8,128)(2,1)S(1)} %get-tuple-element.320), channel_id=1, source_target_pairs={{0,8},{4,12},{8,0},{12,4},{1,9},{5,13},{9,1},{13,5},{2,10},{6,14},... | collective-permute-start | bytes 884744 | tf_op jit(solution)/shard_map/ppermute | solution.py:583
  168.1 19.9 %collective-permute-start.11 = (bf16[192,768]{1,0:T(8,128)(2,1)S(1)}, bf16[192,768]{1,0:T(8,128)(2,1)S(1)}, u32[]{:S(2)}, u32[]{:S(2)}) collective-permute-start(bf16[192,768]{1,0:T(8,128)(2,1)S(1)} %get-tuple-element.322), channel_id=1, source_target_pairs={{0,4},{4,0},{8,12},{12,8},{1,5},{5,1},{9,13},{13,9},{2,6},{6,2},{1... | collective-permute-start | bytes 884744 | tf_op jit(solution)/shard_map/ppermute | solution.py:583
  188.1 35.5 %collective-permute-start.20 = (bf16[4,384,768]{2,1,0:T(8,128)(2,1)}, bf16[4,384,768]{2,1,0:T(8,128)(2,1)}, u32[]{:S(2)}, u32[]{:S(2)}) collective-permute-start(bf16[4,384,768]{2,1,0:T(8,128)(2,1)} %get-tuple-element.359), channel_id=1, source_target_pairs={{0,16},{16,0},{1,17},{17,1},{2,18},{18,2},{3,19},{19,3},{4,20},{20... | collective-permute-start | bytes 7077896 | tf_op jit(solution)/shard_map/ppermute | solution.py:583
  191.8 27.3 %copy-start.40 = (bf16[384,768]{1,0:T(8,128)(2,1)}, bf16[384,768]{1,0:T(8,128)(2,1)S(1)}, u32[]{:S(2)}) copy-start(bf16[384,768]{1,0:T(8,128)(2,1)S(1)} %get-tuple-element.371.refs_0_) | copy-start | bytes 1769476
  191.8 9.8 %collective-permute-start.16 = (bf16[96,1536]{1,0:T(8,128)(2,1)S(1)}, bf16[96,1536]{1,0:T(8,128)(2,1)S(1)}, u32[]{:S(2)}, u32[]{:S(2)}) collective-permute-start(bf16[96,1536]{1,0:T(8,128)(2,1)S(1)} %get-tuple-element.351), channel_id=1, source_target_pairs={{0,8},{4,12},{8,0},{12,4},{1,9},{5,13},{9,1},{13,5},{2,10},{6,14},... | collective-permute-start | bytes 884744 | tf_op jit(solution)/shard_map/ppermute | solution.py:583
  192.5 30.2 %collective-permute-start.18 = (bf16[2,112,1536]{2,1,0:T(8,128)(2,1)}, bf16[2,112,1536]{2,1,0:T(8,128)(2,1)S(1)}, u32[]{:S(2)}, u32[]{:S(2)}) collective-permute-start(bf16[2,112,1536]{2,1,0:T(8,128)(2,1)} %get-tuple-element.355), channel_id=1, source_target_pairs={{0,4},{4,0},{8,12},{12,8},{1,5},{5,1},{9,13},{13,9},{2,6},{6,2},{1... | collective-permute-start | bytes 2064392 | tf_op jit(solution)/shard_map/ppermute | solution.py:583
  193.8 28.0 %collective-permute-start.15 = (bf16[384,768]{1,0:T(8,128)(2,1)S(1)}, bf16[384,768]{1,0:T(8,128)(2,1)S(1)}, u32[]{:S(2)}, u32[]{:S(2)}) collective-permute-start(bf16[384,768]{1,0:T(8,128)(2,1)S(1)} %get-tuple-element.371.refs_0_), channel_id=1, source_target_pairs={{0,1},{3,2},{4,5},{7,6},{8,9},{11,10},{12,13},{15,14},{16,17},{19,... | collective-permute-start | bytes 1769480 | tf_op jit(solution)/shard_map/ppermute | solution.py:695
  197.3 24.5 %collective-permute-start.19 = (bf16[2,96,1536]{2,1,0:T(8,128)(2,1)}, bf16[2,96,1536]{2,1,0:T(8,128)(2,1)S(1)}, u32[]{:S(2)}, u32[]{:S(2)}) collective-permute-start(bf16[2,96,1536]{2,1,0:T(8,128)(2,1)} %get-tuple-element.357), channel_id=1, source_target_pairs={{0,8},{4,12},{8,0},{12,4},{1,9},{5,13},{9,1},{13,5},{2,10},{6,14},... | collective-permute-start | bytes 1769480 | tf_op jit(solution)/shard_map/ppermute | solution.py:583
  201.6 19.5 %collective-permute-start.17 = (bf16[96,1536]{1,0:T(8,128)(2,1)}, bf16[96,1536]{1,0:T(8,128)(2,1)S(1)}, u32[]{:S(2)}, u32[]{:S(2)}) collective-permute-start(bf16[96,1536]{1,0:T(8,128)(2,1)} %get-tuple-element.353), channel_id=1, source_target_pairs={{0,4},{4,0},{8,12},{12,8},{1,5},{5,1},{9,13},{13,9},{2,6},{6,2},{1... | collective-permute-start | bytes 884744 | tf_op jit(solution)/shard_map/ppermute | solution.py:583
  223.5 21.5 %copy-start.14 = (bf16[4,128,768]{2,1,0:T(8,128)(2,1)S(1)}, bf16[4,128,768]{2,1,0:T(8,128)(2,1)}, u32[]{:S(2)}) copy-start(bf16[4,128,768]{2,1,0:T(8,128)(2,1)} %copy-done.12) | copy-start | bytes 2359300
  223.5 21.5 %copy-start.27 = (bf16[768,512]{1,0:T(8,128)(2,1)S(1)}, bf16[768,512]{1,0:T(8,128)(2,1)}, u32[]{:S(2)}) copy-start(bf16[768,512]{1,0:T(8,128)(2,1)} %copy-done.26) | copy-start | bytes 2359300
  223.5 50.9 %collective-permute-start.27 = (bf16[4,192,1536]{2,1,0:T(8,128)(2,1)}, bf16[4,192,1536]{2,1,0:T(8,128)(2,1)S(1)}, u32[]{:S(2)}, u32[]{:S(2)}) collective-permute-start(bf16[4,192,1536]{2,1,0:T(8,128)(2,1)} %bitcast.18), channel_id=1, source_target_pairs={{0,16},{16,0},{1,17},{17,1},{2,18},{18,2},{3,19},{19,3},{4,20},{20... | collective-permute-start | bytes 7077896 | tf_op jit(solution)/shard_map/ppermute | solution.py:583
  231.9 11.0 %collective-permute-start.23 = (bf16[112,1536]{1,0:T(8,128)(2,1)S(1)}, bf16[112,1536]{1,0:T(8,128)(2,1)S(1)}, u32[]{:S(2)}, u32[]{:S(2)}) collective-permute-start(bf16[112,1536]{1,0:T(8,128)(2,1)S(1)} %get-tuple-element.386), channel_id=1, source_target_pairs={{0,8},{4,12},{8,0},{12,4},{1,9},{5,13},{9,1},{13,5},{2,10},{6,14},... | collective-permute-start | bytes 1032200 | tf_op jit(solution)/shard_map/ppermute | solution.py:583
  232.5 9.0 %collective-permute-start.24 = (bf16[96,1536]{1,0:T(8,128)(2,1)S(1)}, bf16[96,1536]{1,0:T(8,128)(2,1)S(1)}, u32[]{:S(2)}, u32[]{:S(2)}) collective-permute-start(bf16[96,1536]{1,0:T(8,128)(2,1)S(1)} %get-tuple-element.388), channel_id=1, source_target_pairs={{0,4},{4,0},{8,12},{12,8},{1,5},{5,1},{9,13},{13,9},{2,6},{6,2},{1... | collective-permute-start | bytes 884744 | tf_op jit(solution)/shard_map/ppermute | solution.py:583
  233.2 37.9 %collective-permute-start.21 = (bf16[384,768]{1,0:T(8,128)(2,1)S(1)}, bf16[384,768]{1,0:T(8,128)(2,1)S(1)}, u32[]{:S(2)}, u32[]{:S(2)}) collective-permute-start(bf16[384,768]{1,0:T(8,128)(2,1)S(1)} %get-tuple-element.396.refs_0_), channel_id=1, source_target_pairs={{1,2},{2,1},{5,6},{6,5},{9,10},{10,9},{13,14},{14,13},{17,18},{18,... | collective-permute-start | bytes 1769480 | tf_op jit(solution)/shard_map/ppermute | solution.py:699
  233.9 38.0 %collective-permute-start.22 = (bf16[192,1536]{1,0:T(8,128)(2,1)S(1)}, bf16[192,1536]{1,0:T(8,128)(2,1)S(1)}, u32[]{:S(2)}, u32[]{:S(2)}) collective-permute-start(bf16[192,1536]{1,0:T(8,128)(2,1)S(1)} %get-tuple-element.398.refs_2_), channel_id=1, source_target_pairs={{0,1},{3,2},{4,5},{7,6},{8,9},{11,10},{12,13},{15,14},{16,17},{19,... | collective-permute-start | bytes 1769480 | tf_op jit(solution)/shard_map/ppermute | solution.py:695
  242.2 30.6 %collective-permute-start.25 = (bf16[2,192,768]{2,1,0:T(8,128)(2,1)}, bf16[2,192,768]{2,1,0:T(8,128)(2,1)S(1)}, u32[]{:S(2)}, u32[]{:S(2)}) collective-permute-start(bf16[2,192,768]{2,1,0:T(8,128)(2,1)} %get-tuple-element.390), channel_id=1, source_target_pairs={{0,4},{4,0},{8,12},{12,8},{1,5},{5,1},{9,13},{13,9},{2,6},{6,2},{1... | collective-permute-start | bytes 1769480 | tf_op jit(solution)/shard_map/ppermute | solution.py:583
  243.7 29.9 %collective-permute-start.26 = (bf16[2,192,768]{2,1,0:T(8,128)(2,1)}, bf16[2,192,768]{2,1,0:T(8,128)(2,1)S(1)}, u32[]{:S(2)}, u32[]{:S(2)}) collective-permute-start(bf16[2,192,768]{2,1,0:T(8,128)(2,1)} %get-tuple-element.392), channel_id=1, source_target_pairs={{0,8},{4,12},{8,0},{12,4},{1,9},{5,13},{9,1},{13,5},{2,10},{6,14},... | collective-permute-start | bytes 1769480 | tf_op jit(solution)/shard_map/ppermute | solution.py:583
  275.9 35.5 %collective-permute-start.36 = (bf16[4,208,1536]{2,1,0:T(8,128)(2,1)S(1)}, bf16[4,208,1536]{2,1,0:T(8,128)(2,1)S(1)}, u32[]{:S(2)}, u32[]{:S(2)}) collective-permute-start(bf16[4,208,1536]{2,1,0:T(8,128)(2,1)S(1)} %get-tuple-element.422), channel_id=1, source_target_pairs={{0,16},{16,0},{1,17},{17,1},{2,18},{18,2},{3,19},{19,3},{4,20},{20... | collective-permute-start | bytes 7667720 | tf_op jit(solution)/shard_map/ppermute | solution.py:583
  276.1 22.1 %collective-permute-start.28 = (f32[512,768]{1,0:T(8,128)S(1)}, f32[512,768]{1,0:T(8,128)}, u32[]{:S(2)}, u32[]{:S(2)}) collective-permute-start(f32[512,768]{1,0:T(8,128)S(1)} %convert_select_fusion), channel_id=1, source_target_pairs={{0,16},{16,0},{1,17},{17,1},{2,18},{18,2},{3,19},{19,3},{4,20},{20... | collective-permute-start | bytes 4718600 | tf_op jit(solution)/shard_map/ppermute | solution.py:583
  276.8 6.9 %collective-permute-start.5 = (bf16[512,768]{1,0:T(8,128)(2,1)S(1)}, bf16[512,768]{1,0:T(8,128)(2,1)S(1)}, u32[]{:S(2)}, u32[]{:S(2)}) collective-permute-start(bf16[512,768]{1,0:T(8,128)(2,1)S(1)} %broadcast_select_fusion.2), channel_id=1, source_target_pairs={{0,16},{16,0},{1,17},{17,1},{2,18},{18,2},{3,19},{19,3},{4,20},{20... | collective-permute-start | bytes 2359304 | tf_op jit(solution)/shard_map/ppermute | solution.py:583
  280.5 16.2 %collective-permute-start.29 = (bf16[384,768]{1,0:T(8,128)(2,1)S(1)}, bf16[384,768]{1,0:T(8,128)(2,1)S(1)}, u32[]{:S(2)}, u32[]{:S(2)}) collective-permute-start(bf16[384,768]{1,0:T(8,128)(2,1)S(1)} %get-tuple-element.425.refs_0_), channel_id=1, source_target_pairs={{1,0},{2,3},{5,4},{6,7},{9,8},{10,11},{13,12},{14,15},{17,16},{18,... | collective-permute-start | bytes 1769480 | tf_op jit(solution)/shard_map/ppermute | solution.py:703
  281.8 8.1 %collective-permute-start.32 = (bf16[192,768]{1,0:T(8,128)(2,1)S(1)}, bf16[192,768]{1,0:T(8,128)(2,1)S(1)}, u32[]{:S(2)}, u32[]{:S(2)}) collective-permute-start(bf16[192,768]{1,0:T(8,128)(2,1)S(1)} %get-tuple-element.414), channel_id=1, source_target_pairs={{0,8},{4,12},{8,0},{12,4},{1,9},{5,13},{9,1},{13,5},{2,10},{6,14},... | collective-permute-start | bytes 884744 | tf_op jit(solution)/shard_map/ppermute | solution.py:583
  283.7 11.8 %collective-permute-start.33 = (bf16[192,768]{1,0:T(8,128)(2,1)S(1)}, bf16[192,768]{1,0:T(8,128)(2,1)S(1)}, u32[]{:S(2)}, u32[]{:S(2)}) collective-permute-start(bf16[192,768]{1,0:T(8,128)(2,1)S(1)} %get-tuple-element.416), channel_id=1, source_target_pairs={{0,4},{4,0},{8,12},{12,8},{1,5},{5,1},{9,13},{13,9},{2,6},{6,2},{1... | collective-permute-start | bytes 884744 | tf_op jit(solution)/shard_map/ppermute | solution.py:583
  289.9 21.5 %collective-permute-start.31 = (bf16[208,1536]{1,0:T(8,128)(2,1)S(1)}, bf16[208,1536]{1,0:T(8,128)(2,1)S(1)}, u32[]{:S(2)}, u32[]{:S(2)}) collective-permute-start(bf16[208,1536]{1,0:T(8,128)(2,1)S(1)} %get-tuple-element.429.refs_4_), channel_id=1, source_target_pairs={{0,1},{3,2},{4,5},{7,6},{8,9},{11,10},{12,13},{15,14},{16,17},{19,... | collective-permute-start | bytes 1916936 | tf_op jit(solution)/shard_map/ppermute | solution.py:695
  295.5 6.9 %collective-permute-start.30 = (bf16[192,1536]{1,0:T(8,128)(2,1)S(1)}, bf16[192,1536]{1,0:T(8,128)(2,1)S(1)}, u32[]{:S(2)}, u32[]{:S(2)}) collective-permute-start(bf16[192,1536]{1,0:T(8,128)(2,1)S(1)} %get-tuple-element.427.refs_2_), channel_id=1, source_target_pairs={{1,2},{2,1},{5,6},{6,5},{9,10},{10,9},{13,14},{14,13},{17,18},{18,... | collective-permute-start | bytes 1769480 | tf_op jit(solution)/shard_map/ppermute | solution.py:699
  296.7 13.4 %collective-permute-start.34 = (bf16[2,96,1536]{2,1,0:T(8,128)(2,1)S(1)}, bf16[2,96,1536]{2,1,0:T(8,128)(2,1)S(1)}, u32[]{:S(2)}, u32[]{:S(2)}) collective-permute-start(bf16[2,96,1536]{2,1,0:T(8,128)(2,1)S(1)} %get-tuple-element.418), channel_id=1, source_target_pairs={{0,4},{4,0},{8,12},{12,8},{1,5},{5,1},{9,13},{13,9},{2,6},{6,2},{1... | collective-permute-start | bytes 1769480 | tf_op jit(solution)/shard_map/ppermute | solution.py:583
  298.2 13.1 %collective-permute-start.35 = (bf16[2,96,1536]{2,1,0:T(8,128)(2,1)S(1)}, bf16[2,96,1536]{2,1,0:T(8,128)(2,1)S(1)}, u32[]{:S(2)}, u32[]{:S(2)}) collective-permute-start(bf16[2,96,1536]{2,1,0:T(8,128)(2,1)S(1)} %get-tuple-element.420), channel_id=1, source_target_pairs={{0,8},{4,12},{8,0},{12,4},{1,9},{5,13},{9,1},{13,5},{2,10},{6,14},... | collective-permute-start | bytes 1769480 | tf_op jit(solution)/shard_map/ppermute | solution.py:583
  312.6 6.8 %collective-permute-start.40 = (bf16[96,1536]{1,0:T(8,128)(2,1)S(1)}, bf16[96,1536]{1,0:T(8,128)(2,1)S(1)}, u32[]{:S(2)}, u32[]{:S(2)}) collective-permute-start(bf16[96,1536]{1,0:T(8,128)(2,1)S(1)} %get-tuple-element.445), channel_id=1, source_target_pairs={{0,8},{4,12},{8,0},{12,4},{1,9},{5,13},{9,1},{13,5},{2,10},{6,14},... | collective-permute-start | bytes 884744 | tf_op jit(solution)/shard_map/ppermute | solution.py:583
  313.2 11.1 %collective-permute-start.41 = (bf16[96,1536]{1,0:T(8,128)(2,1)S(1)}, bf16[96,1536]{1,0:T(8,128)(2,1)S(1)}, u32[]{:S(2)}, u32[]{:S(2)}) collective-permute-start(bf16[96,1536]{1,0:T(8,128)(2,1)S(1)} %get-tuple-element.447), channel_id=1, source_target_pairs={{0,4},{4,0},{8,12},{12,8},{1,5},{5,1},{9,13},{13,9},{2,6},{6,2},{1... | collective-permute-start | bytes 884744 | tf_op jit(solution)/shard_map/ppermute | solution.py:583
  313.9 20.3 %collective-permute-start.42 = (bf16[2,112,1536]{2,1,0:T(8,128)(2,1)S(1)}, bf16[2,112,1536]{2,1,0:T(8,128)(2,1)S(1)}, u32[]{:S(2)}, u32[]{:S(2)}) collective-permute-start(bf16[2,112,1536]{2,1,0:T(8,128)(2,1)S(1)} %get-tuple-element.449), channel_id=1, source_target_pairs={{0,4},{4,0},{8,12},{12,8},{1,5},{5,1},{9,13},{13,9},{2,6},{6,2},{1... | collective-permute-start | bytes 2064392 | tf_op jit(solution)/shard_map/ppermute | solution.py:583
  315.2 19.0 %collective-permute-start.38 = (bf16[208,1536]{1,0:T(8,128)(2,1)S(1)}, bf16[208,1536]{1,0:T(8,128)(2,1)S(1)}, u32[]{:S(2)}, u32[]{:S(2)}) collective-permute-start(bf16[208,1536]{1,0:T(8,128)(2,1)S(1)} %get-tuple-element.454.refs_2_), channel_id=1, source_target_pairs={{1,2},{2,1},{5,6},{6,5},{9,10},{10,9},{13,14},{14,13},{17,18},{18,... | collective-permute-start | bytes 1916936 | tf_op jit(solution)/shard_map/ppermute | solution.py:699
  315.9 14.1 %collective-permute-start.37 = (bf16[192,1536]{1,0:T(8,128)(2,1)S(1)}, bf16[192,1536]{1,0:T(8,128)(2,1)S(1)}, u32[]{:S(2)}, u32[]{:S(2)}) collective-permute-start(bf16[192,1536]{1,0:T(8,128)(2,1)S(1)} %get-tuple-element.452.refs_0_), channel_id=1, source_target_pairs={{1,0},{2,3},{5,4},{6,7},{9,8},{10,11},{13,12},{14,15},{17,16},{18,... | collective-permute-start | bytes 1769480 | tf_op jit(solution)/shard_map/ppermute | solution.py:703
  319.4 12.2 %collective-permute-start.39 = (bf16[384,768]{1,0:T(8,128)(2,1)S(1)}, bf16[384,768]{1,0:T(8,128)(2,1)S(1)}, u32[]{:S(2)}, u32[]{:S(2)}) collective-permute-start(bf16[384,768]{1,0:T(8,128)(2,1)S(1)} %get-tuple-element.456.refs_4_), channel_id=1, source_target_pairs={{0,1},{3,2},{4,5},{7,6},{8,9},{11,10},{12,13},{15,14},{16,17},{19,... | collective-permute-start | bytes 1769480 | tf_op jit(solution)/shard_map/ppermute | solution.py:695
  324.3 9.9 %collective-permute-start.43 = (bf16[2,96,1536]{2,1,0:T(8,128)(2,1)S(1)}, bf16[2,96,1536]{2,1,0:T(8,128)(2,1)S(1)}, u32[]{:S(2)}, u32[]{:S(2)}) collective-permute-start(bf16[2,96,1536]{2,1,0:T(8,128)(2,1)S(1)} %get-tuple-element.451), channel_id=1, source_target_pairs={{0,8},{4,12},{8,0},{12,4},{1,9},{5,13},{9,1},{13,5},{2,10},{6,14},... | collective-permute-start | bytes 1769480 | tf_op jit(solution)/shard_map/ppermute | solution.py:583
  335.1 18.2 %collective-permute-start.44 = (bf16[208,1536]{1,0:T(8,128)(2,1)S(1)}, bf16[208,1536]{1,0:T(8,128)(2,1)S(1)}, u32[]{:S(2)}, u32[]{:S(2)}) collective-permute-start(bf16[208,1536]{1,0:T(8,128)(2,1)S(1)} %get-tuple-element.473.refs_0_), channel_id=1, source_target_pairs={{1,0},{2,3},{5,4},{6,7},{9,8},{10,11},{13,12},{14,15},{17,16},{18,... | collective-permute-start | bytes 1916936 | tf_op jit(solution)/shard_map/ppermute | solution.py:703
  336.4 16.9 %collective-permute-start.45 = (bf16[384,768]{1,0:T(8,128)(2,1)S(1)}, bf16[384,768]{1,0:T(8,128)(2,1)S(1)}, u32[]{:S(2)}, u32[]{:S(2)}) collective-permute-start(bf16[384,768]{1,0:T(8,128)(2,1)S(1)} %get-tuple-element.475.refs_2_), channel_id=1, source_target_pairs={{1,2},{2,1},{5,6},{6,5},{9,10},{10,9},{13,14},{14,13},{17,18},{18,... | collective-permute-start | bytes 1769480 | tf_op jit(solution)/shard_map/ppermute | solution.py:699
  337.1 16.2 %collective-permute-start.46 = (bf16[192,1536]{1,0:T(8,128)(2,1)S(1)}, bf16[192,1536]{1,0:T(8,128)(2,1)S(1)}, u32[]{:S(2)}, u32[]{:S(2)}) collective-permute-start(bf16[192,1536]{1,0:T(8,128)(2,1)S(1)} %get-tuple-element.477.refs_4_), channel_id=1, source_target_pairs={{0,1},{3,2},{4,5},{7,6},{8,9},{11,10},{12,13},{15,14},{16,17},{19,... | collective-permute-start | bytes 1769480 | tf_op jit(solution)/shard_map/ppermute | solution.py:695
  345.0 8.3 %collective-permute-start.47 = (bf16[112,1536]{1,0:T(8,128)(2,1)S(1)}, bf16[112,1536]{1,0:T(8,128)(2,1)S(1)}, u32[]{:S(2)}, u32[]{:S(2)}) collective-permute-start(bf16[112,1536]{1,0:T(8,128)(2,1)S(1)} %get-tuple-element.470), channel_id=1, source_target_pairs={{0,8},{4,12},{8,0},{12,4},{1,9},{5,13},{9,1},{13,5},{2,10},{6,14},... | collective-permute-start | bytes 1032200 | tf_op jit(solution)/shard_map/ppermute | solution.py:583
  346.6 6.7 %collective-permute-start.48 = (bf16[96,1536]{1,0:T(8,128)(2,1)S(1)}, bf16[96,1536]{1,0:T(8,128)(2,1)S(1)}, u32[]{:S(2)}, u32[]{:S(2)}) collective-permute-start(bf16[96,1536]{1,0:T(8,128)(2,1)S(1)} %get-tuple-element.472), channel_id=1, source_target_pairs={{0,4},{4,0},{8,12},{12,8},{1,5},{5,1},{9,13},{13,9},{2,6},{6,2},{1... | collective-permute-start | bytes 884744 | tf_op jit(solution)/shard_map/ppermute | solution.py:583
  354.2 16.3 %collective-permute-start.51 = (bf16[208,1536]{1,0:T(8,128)(2,1)S(1)}, bf16[208,1536]{1,0:T(8,128)(2,1)S(1)}, u32[]{:S(2)}, u32[]{:S(2)}) collective-permute-start(bf16[208,1536]{1,0:T(8,128)(2,1)S(1)} %get-tuple-element.490.refs_4_), channel_id=1, source_target_pairs={{0,1},{3,2},{4,5},{7,6},{8,9},{11,10},{12,13},{15,14},{16,17},{19,... | collective-permute-start | bytes 1916936 | tf_op jit(solution)/shard_map/ppermute | solution.py:695
  358.7 11.8 %collective-permute-start.49 = (bf16[384,768]{1,0:T(8,128)(2,1)S(1)}, bf16[384,768]{1,0:T(8,128)(2,1)S(1)}, u32[]{:S(2)}, u32[]{:S(2)}) collective-permute-start(bf16[384,768]{1,0:T(8,128)(2,1)S(1)} %get-tuple-element.486.refs_0_), channel_id=1, source_target_pairs={{1,0},{2,3},{5,4},{6,7},{9,8},{10,11},{13,12},{14,15},{17,16},{18,... | collective-permute-start | bytes 1769480 | tf_op jit(solution)/shard_map/ppermute | solution.py:703
  360.0 10.5 %collective-permute-start.50 = (bf16[192,1536]{1,0:T(8,128)(2,1)S(1)}, bf16[192,1536]{1,0:T(8,128)(2,1)S(1)}, u32[]{:S(2)}, u32[]{:S(2)}) collective-permute-start(bf16[192,1536]{1,0:T(8,128)(2,1)S(1)} %get-tuple-element.488.refs_2_), channel_id=1, source_target_pairs={{1,2},{2,1},{5,6},{6,5},{9,10},{10,9},{13,14},{14,13},{17,18},{18,... | collective-permute-start | bytes 1769480 | tf_op jit(solution)/shard_map/ppermute | solution.py:699
  371.2 17.2 %collective-permute-start.53 = (bf16[208,1536]{1,0:T(8,128)(2,1)S(1)}, bf16[208,1536]{1,0:T(8,128)(2,1)S(1)}, u32[]{:S(2)}, u32[]{:S(2)}) collective-permute-start(bf16[208,1536]{1,0:T(8,128)(2,1)S(1)} %get-tuple-element.496.refs_2_), channel_id=1, source_target_pairs={{1,2},{2,1},{5,6},{6,5},{9,10},{10,9},{13,14},{14,13},{17,18},{18,... | collective-permute-start | bytes 1916936 | tf_op jit(solution)/shard_map/ppermute | solution.py:699
  371.9 16.5 %collective-permute-start.52 = (bf16[192,1536]{1,0:T(8,128)(2,1)S(1)}, bf16[192,1536]{1,0:T(8,128)(2,1)S(1)}, u32[]{:S(2)}, u32[]{:S(2)}) collective-permute-start(bf16[192,1536]{1,0:T(8,128)(2,1)S(1)} %get-tuple-element.494.refs_0_), channel_id=1, source_target_pairs={{1,0},{2,3},{5,4},{6,7},{9,8},{10,11},{13,12},{14,15},{17,16},{18,... | collective-permute-start | bytes 1769480 | tf_op jit(solution)/shard_map/ppermute | solution.py:703
  374.1 16.7 %collective-permute-start.57 = (bf16[384,768]{1,0:T(8,128)(2,1)}, bf16[384,768]{1,0:T(8,128)(2,1)}, u32[]{:S(2)}, u32[]{:S(2)}) collective-permute-start(bf16[384,768]{1,0:T(8,128)(2,1)} %broadcast_select_fusion.10), channel_id=1, source_target_pairs={{0,16},{16,0},{1,17},{17,1},{2,18},{18,2},{3,19},{19,3},{4,20},{20... | collective-permute-start | bytes 1769480 | tf_op jit(solution)/shard_map/ppermute | solution.py:583
  390.8 7.1 %collective-permute-start.56 = (bf16[192,1536]{1,0:T(8,128)(2,1)}, bf16[192,1536]{1,0:T(8,128)(2,1)}, u32[]{:S(2)}, u32[]{:S(2)}) collective-permute-start(bf16[192,1536]{1,0:T(8,128)(2,1)} %broadcast_select_fusion.12), channel_id=1, source_target_pairs={{0,16},{16,0},{1,17},{17,1},{2,18},{18,2},{3,19},{19,3},{4,20},{20... | collective-permute-start | bytes 1769480 | tf_op jit(solution)/shard_map/ppermute | solution.py:583
  396.6 18.9 %collective-permute-start.54 = (bf16[208,1536]{1,0:T(8,128)(2,1)}, bf16[208,1536]{1,0:T(8,128)(2,1)S(1)}, u32[]{:S(2)}, u32[]{:S(2)}) collective-permute-start(bf16[208,1536]{1,0:T(8,128)(2,1)} %copy-done.38), channel_id=1, source_target_pairs={{1,0},{2,3},{5,4},{6,7},{9,8},{10,11},{13,12},{14,15},{17,16},{18,... | collective-permute-start | bytes 1916936 | tf_op jit(solution)/shard_map/ppermute | solution.py:703
  416.2 2.5 collective-permute-start.55
  (109 other events, 622.9 us)

commit v3 on v2

--- a/solution.py
+++ b/solution.py
@@ -118,7 +118,7 @@
             move.store(*(ref.at[index] if index else ref for ref in (self.buffer, self.ref)))
 
 
-NEAR, FAR, RAW = "near", "far", "raw"
+NEAR, FAR, RAW, BOTH = "near", "far", "raw", "both"
 
 
 def ready(waits):
@@ -127,30 +127,38 @@
 
 
 def call(kernel, ids, ins, outs, scratch, name, flops, nbytes):
-    space = lambda kind: pl.BlockSpec(memory_space=pltpu.VMEM if kind == NEAR else pltpu.HBM)
-    kinds = [kind for _, kind in ins] + [kind for _, kind in outs]
-    shapes = [array for array, _ in ins] + [shape for shape, _ in outs]
+    space = lambda kind: pltpu.VMEM if kind == NEAR else pltpu.HBM
+    spread = [(shape, part) for shape, kind in outs for part in ((NEAR, RAW) if kind == BOTH else (kind,))]
+    kinds = [kind for _, kind in ins] + [kind for _, kind in spread]
+    shapes = [array for array, _ in ins] + [shape for shape, _ in spread]
     buffers = [pltpu.VMEM(shape.shape, shape.dtype) for shape, kind in zip(shapes, kinds) if kind == FAR]
 
     def body(ids_ref, *refs):
         count = len(kinds)
         spare = list(refs[count : count + len(buffers)])
+        left = list(refs[:count])
         operands = []
-        for ref, kind in zip(refs[:count], kinds):
-            buffer = spare.pop(0) if kind == FAR else ref
-            operands.append(Operand(ref, buffer, kind == FAR))
+        for _, kind in list(ins) + list(outs):
+            ref = left.pop(0)
+            if kind == BOTH:
+                operands.append(Operand(left.pop(0), ref, True))
+            else:
+                operands.append(Operand(ref, spare.pop(0) if kind == FAR else ref, kind == FAR))
         kernel(ids_ref, *operands, *refs[count + len(buffers) :])
 
-    return pl.pallas_call(
+    results = pl.pallas_call(
         body,
-        in_specs=[pl.BlockSpec(memory_space=pltpu.SMEM)] + [space(kind) for _, kind in ins],
-        out_specs=[space(kind) for _, kind in outs],
-        out_shape=[shape for shape, _ in outs],
+        in_specs=[pl.BlockSpec(memory_space=pltpu.SMEM)]
+        + [pl.BlockSpec(memory_space=space(kind)) for _, kind in ins],
+        out_specs=[pl.BlockSpec(memory_space=space(kind)) for _, kind in spread],
+        out_shape=[space(kind)(shape.shape, shape.dtype) for shape, kind in spread],
         scratch_shapes=buffers + [pltpu.VMEM(*item) for item in scratch] + [pltpu.SemaphoreType.DMA((64,))],
         compiler_params=pltpu.CompilerParams(vmem_limit_bytes=VMEM),
         cost_estimate=pl.CostEstimate(flops=flops, bytes_accessed=nbytes, transcendentals=0),
         name=name,
-    )(ids, *(array for array, _ in ins))
+    )(ids, *(pltpu.with_memory_space_constraint(array, space(kind)) for array, kind in ins))
+    results = list(results)
+    return [(results.pop(0), results.pop(0)) if kind == BOTH else results.pop(0) for _, kind in outs]
 
 
 def attend_phase(q, k, v, probs, ctx, mask, pairs):
@@ -218,7 +226,7 @@
         functools.partial(attend_kernel, layer),
         sec,
         [(x, x_kind), (w_own, RAW), (w_other, RAW), (small, FAR), (mask, FAR)],
-        [(wide, FAR)] * 3 + [(sds((seqs, pairs, 256, 128), F32), FAR), (sds((width, rows), BF16), NEAR)],
+        [(wide, FAR)] * 3 + [(sds((seqs, pairs, 256, 128), F32), FAR), (sds((width, rows), BF16), BOTH)],
         [((3, width, width), BF16)],
         "attend_forward",
         2 * rows * width * width * 4,
@@ -264,10 +272,10 @@
         sec,
         [(x, x_kind), (ctx, NEAR), (wo, RAW), (wo_other, RAW), (wu, RAW), (wu_other, RAW), (small, FAR)],
         [
-            (sds(wide, F32), NEAR),
+            (sds(wide, F32), BOTH),
             (sds((rows, 128), F32), FAR),
             (sds((width, rows), BF16), FAR),
-            (sds((blocks,) + wide, BF16), NEAR),
+            (sds((blocks,) + wide, BF16), BOTH if layer == 0 else NEAR),
             (sds((blocks,) + wide, F32), FAR),
         ],
         [((width, width), BF16), ((blocks, width, width), BF16), (wide, BF16)],
@@ -358,7 +366,7 @@
         down_grad_kernel,
         sec,
         [(gy, gy_kind), (hat, kind), (scale, kind), (small, FAR), (act, kind)],
-        [(sds(wide, F32), NEAR), (sds(wide, BF16), NEAR), (sds((8, width), F32), NEAR), (part, FAR), (part, FAR)],
+        [(sds(wide, F32), NEAR), (sds(wide, BF16), NEAR), (sds((8, width), F32), NEAR), (part, NEAR), (part, NEAR)],
         [((width, rows), BF16)],
         "down_grad",
         2 * rows * width * width * blocks,
@@ -366,190 +374,239 @@
     )
 
 
-def up_grad_kernel(
-    layer, sec, branch, second, wd_a, wd_b, slope, low, wu_a, wu_b, hat, scale, small,
-    first, attend, sums, send, keep, wd, wu, pre, send_buffer, keep_buffer, sems,
-):
+def up_grad_kernel(layer, last, sec, *refs):
+    refs = list(refs)
+    take = lambda count: [refs.pop(0) for _ in range(count)]
+    branch, base, wd_a, wd_b, slope_h, low, wu_a, wu_b = take(8)
+    if last:
+        hat, scale, small, sums_in = take(4)
+        first, attend, sums, out = take(4)
+    else:
+        first, sums, out = take(3)
+    wd, wu, slope, pre, sems = refs
     move = Mover(sems)
     mine = sec[0] == layer
-    blocks, wide, _ = wd.shape
-    half = blocks // 2
-    at = [lax.rem(i + half * (1 - sec[0]), blocks) for i in range(blocks)]
+    half, wide, _ = wd.shape
+    side = sec[0] if last else 1 - sec[0]
+    at = [side * half + i for i in range(half)]
     span = [pl.ds(pl.multiple_of(place * wide, wide), wide) for place in at]
     parts = []
     early = branch.fetch(move)
-    for i in range(blocks):
+    for i in range(half):
+        move.load(slope_h.ref.at[at[i]], slope.at[i])
         parts.append(
-            [move.choose(mine, wd_a.ref.at[span[i]], wd_b.ref.at[span[i]], wd.at[i])]
-            + slope.fetch(move, at[i])
-            + [move.choose(mine, wu_a.ref.at[:, span[i]], wu_b.ref.at[:, span[i]], wu.at[i])]
+            [
+                move.last,
+                move.choose(mine, wd_a.ref.at[span[i]], wd_b.ref.at[span[i]], wd.at[i]),
+                move.choose(mine, wu_a.ref.at[:, span[i]], wu_b.ref.at[:, span[i]], wu.at[i]),
+            ]
         )
         if i == 0:
             early += low.fetch(move)
-    late = second.fetch(move) + hat.fetch(move) + scale.fetch(move) + small.fetch(move)
+    late = base.fetch(move)
+    if last:
+        late += hat.fetch(move) + scale.fetch(move) + small.fetch(move)
+        sums.buffer[...] = sums_in.buffer[...]
+    else:
+        sums.buffer[...] = jnp.zeros_like(sums.buffer)
     ready(early)
-    branch, low, total = branch.buffer, low.buffer, first.buffer
-    for i in range(blocks):
+    total = first.buffer
+    shards, tall, _ = out.buffer.shape
+    for i in range(half):
         ready(parts[i])
-        pre[...] = (dot_t(branch[...], wd[i]) * slope.buffer[at[i]]).astype(BF16)
+        pre[...] = (dot_t(branch.buffer[...], wd[i]) * slope[i]).astype(BF16)
         sums.buffer[pl.ds(3 + at[i], 1)] = column_sum(pre[...].astype(F32))
-        out, out_h, place = (send_buffer, send, i) if i < half else (keep_buffer, keep, i - half)
-        out[place] = dot(low[...], pre[...]).astype(BF16)
-        move.store(out.at[place], out_h.ref.at[:, pl.ds(place * wide, wide)])
+        block = dot(low.buffer[...], pre[...]).astype(BF16)
+        for shard in range(shards):
+            out.buffer[shard, :, i * wide : i * wide + wide] = block[shard * tall : shard * tall + tall]
         if i == 0:
             ready(late)
-            total[...] = second.buffer[...] + dot_t(pre[...], wu[i])
+            total[...] = base.buffer[...] + dot_t(pre[...], wu[i])
         else:
             total[...] += dot_t(pre[...], wu[i])
-    grad = total[...]
-    sums.buffer[0:1] = column_sum(grad * hat.buffer[...])
-    sums.buffer[1:2] = column_sum(grad)
-    unit = norm_back(grad, hat.buffer[...], scale.buffer[:, 0:1], small.buffer[GAIN_ONE : GAIN_ONE + 1])
-    attend.buffer[...] = unit.astype(BF16)
-    attend.flush(move)
-    total[...] = unit
-    first.flush(move)
-    sums.buffer[2:3] = column_sum(attend.buffer[...].astype(F32))
-    sums.buffer[3 + blocks :] = jnp.zeros_like(sums.buffer[3 + blocks :])
-    sums.flush(move)
+    if last:
+        grad = total[...]
+        sums.buffer[0:1] = column_sum(grad * hat.buffer[...])
+        sums.buffer[1:2] = column_sum(grad)
+        unit = norm_back(grad, hat.buffer[...], scale.buffer[:, 0:1], small.buffer[GAIN_ONE : GAIN_ONE + 1])
+        attend.buffer[...] = unit.astype(BF16)
+        total[...] = unit
+        sums.buffer[2:3] = column_sum(attend.buffer[...].astype(F32))
     move.finish()
 
 
-def up_grad(layer, sec, branch, second, wd, wd_other, slope, low, wu, wu_other, hat, scale, small):
+def up_grad(layer, last, sec, branch, base, wd, wd_other, slope, low, wu, wu_other, shards, more=()):
     blocks, rows, width = slope.shape
+    half = blocks // 2
     wide = (rows, width)
-    part = sds((width, blocks * width // 2), BF16)
-    square = ((blocks, width, width), BF16)
+    part = sds((shards, width // shards, half * width), BF16)
+    square = ((half, width, width), BF16)
+    near = lambda *shapes: [(shape, NEAR) for shape in shapes]
+    ins = [
+        (branch, NEAR),
+        (base, NEAR),
+        (wd, RAW),
+        (wd_other, RAW),
+        (slope, RAW),
+        (low, FAR),
+        (wu, RAW),
+        (wu_other, RAW),
+    ]
+    if last:
+        hat, scale, small, sums = more
+        ins += [(hat, FAR), (scale, FAR), (small, FAR), (sums, NEAR)]
+        outs = near(sds(wide, F32), sds(wide, BF16), sds((8, width), F32), part)
+    else:
+        outs = near(sds(wide, F32), sds((8, width), F32), part)
     return call(
-        functools.partial(up_grad_kernel, layer),
+        functools.partial(up_grad_kernel, layer, last),
         sec,
-        [
-            (branch, NEAR),
-            (second, NEAR),
-            (wd, RAW),
-            (wd_other, RAW),
-            (slope, FAR),
-            (low, FAR),
-            (wu, RAW),
-            (wu_other, RAW),
-            (hat, FAR),
-            (scale, FAR),
-            (small, FAR),
-        ],
-        [(sds(wide, F32), NEAR), (sds(wide, BF16), NEAR), (sds((8, width), F32), NEAR), (part, RAW), (part, RAW)],
-        [square, square, (wide, BF16)] + [((blocks // 2, width, width), BF16)] * 2,
-        "up_grad",
-        6 * rows * width * width * blocks,
-        30 << 20,
-    )
-
-
-def attend_grad_kernel(
-    layer, shards, sec, attend, ctx, first, x, q, k, v, probs, wo_a, wo_b, w_a, w_b, down, up,
-    gx, gx_low, send, keep, turned, wo, w, gc, grads, sems,
-):
+        ins,
+        outs,
+        [square, square, ((half,) + wide, F32), (wide, BF16)],
+        "up_grad_last" if last else "up_grad_first",
+        3 * rows * width * width * blocks,
+        15 << 20,
+    )
+
+
+def attend_grad_kernel(layer, last, sec, *refs):
+    refs = list(refs)
+    take = lambda count: [refs.pop(0) for _ in range(count)]
+    attend, ctx, base, x, q_h, k_h, v_h, p_h, wo_a, wo_b, w_a, w_b, down, up = take(14)
+    if last:
+        gx, gx_low, out = take(3)
+    else:
+        total, turned, out = take(3)
+    q, k, v, probs, wo, w, gc, grads, sems = refs
     move = Mover(sems)
     mine = sec[0] == layer
-    rows_all, width = x.buffer.shape
-    seqs = probs.buffer.shape[0]
-    wide = width // 2
+    rows_all, wide = q.shape
+    width = 2 * wide
+    seqs = probs.shape[0]
+    shards = out.buffer.shape[0]
     tall = width // shards
     pairs = wide // 128
-    waits = attend.fetch(move) + [move.choose(mine, wo_a.ref, wo_b.ref, wo)]
-    near = probs.fetch(move) + v.fetch(move) + k.fetch(move) + q.fetch(move)
+    side = sec[0] if last else 1 - sec[0]
+    lanes_half = pl.ds(pl.multiple_of(side * wide, wide), wide)
+    waits = attend.fetch(move) + [move.choose(mine, wo_a.ref.at[lanes_half], wo_b.ref.at[lanes_half], wo)]
+    near = []
+    for source, target in (
+        (p_h.ref.at[:, pl.ds(side * pairs, pairs)], probs),
+        (v_h.ref.at[:, lanes_half], v),
+        (k_h.ref.at[:, lanes_half], k),
+        (q_h.ref.at[:, lanes_half], q),
+    ):
+        move.load(source, target)
+        near.append(move.last)
     later = x.fetch(move) + ctx.fetch(move) + down.fetch(move) + up.fetch(move)
-    last = [
-        move.choose(mine, w_a.ref.at[:, pl.ds(i * width, width)], w_b.ref.at[:, pl.ds(i * width, width)], w.at[i])
-        for i in range(3)
-    ] + first.fetch(move)
+    finals = base.fetch(move)
+    for i in range(3):
+        there = pl.ds(pl.multiple_of(i * width + side * wide, wide), wide)
+        finals.append(move.choose(mine, w_a.ref.at[:, there], w_b.ref.at[:, there], w.at[:, pl.ds(i * wide, wide)]))
     ready(waits)
-    attend, q, k, v, probs = (item.buffer for item in (attend, q, k, v, probs))
-    gc[...] = dot_t(attend[...], wo[...]).astype(BF16)
+    gc[...] = dot_t(attend.buffer[...], wo[...]).astype(BF16)
     ready(near)
     halves = lane_halves()
     lower = lax.broadcasted_iota(jnp.int32, (128, 128), 1) < 64
 
-    def attention(first_pair):
-        @pl.loop(0, pairs)
-        def _(index):
-            pair = first_pair + index
-            lanes = pl.ds(pl.multiple_of(pair * 128, 128), 128)
-            for seq in range(seqs):
-                rows = slice(seq * 128, seq * 128 + 128)
-                grad = gc[rows, lanes]
-                p = probs[seq, pair]
-                full = dot(p.astype(BF16), grad)
-                grads[2, rows, lanes] = jnp.where(lower, full[:128], full[128:]).astype(BF16)
-                gp = dot_t(two_heads(v[rows, lanes], halves), grad)
-                parts = []
-                for side in (slice(0, 128), slice(128, 256)):
-                    g, pp = gp[side], p[side]
-                    parts.append(pp * (g - jnp.sum(g * pp, axis=0, keepdims=True)))
-                gs = jnp.concatenate(parts, axis=0).astype(BF16)
-                grads[0, rows, lanes] = t_dot(gs, two_heads(k[rows, lanes] * SCALE, halves)).astype(BF16)
-                full = dot(gs, q[rows, lanes] * SCALE)
-                grads[1, rows, lanes] = jnp.where(lower, full[:128], full[128:]).astype(BF16)
-
-    def products(half, out):
-        lanes = pl.ds(pl.multiple_of(half * wide, wide), wide)
-        for part in range(4):
-            if part < 3:
-                block = dot(turned[...], grads[part, :, lanes]).astype(BF16)
-            else:
-                block = dot(ctx.buffer[...], attend[:, lanes]).astype(BF16)
-            for shard in range(shards):
-                out.buffer[shard, :tall, part * wide : part * wide + wide] = block[shard * tall : shard * tall + tall]
-
-    attention((1 - sec[0]) * pairs)
+    for pair in range(pairs):
+        lanes = slice(pair * 128, pair * 128 + 128)
+        for seq in range(seqs):
+            rows = slice(seq * 128, seq * 128 + 128)
+
+            def put(part, value):
+                grads[rows, part * wide + pair * 128 : part * wide + pair * 128 + 128] = value.astype(BF16)
+
+            grad = gc[rows, lanes]
+            p = probs[seq, pair]
+            full = dot(p.astype(BF16), grad)
+            put(2, jnp.where(lower, full[:128], full[128:]))
+            gp = dot_t(two_heads(v[rows, lanes], halves), grad)
+            parts = []
+            for part in (slice(0, 128), slice(128, 256)):
+                g, pp = gp[part], p[part]
+                parts.append(pp * (g - jnp.sum(g * pp, axis=0, keepdims=True)))
+            gs = jnp.concatenate(parts, axis=0).astype(BF16)
+            put(0, t_dot(gs, two_heads(k[rows, lanes] * SCALE, halves)))
+            full = dot(gs, q[rows, lanes] * SCALE)
+            put(1, jnp.where(lower, full[:128], full[128:]))
     ready(later)
-    turned[...] = x.buffer[...].T
-    products(1 - sec[0], send)
-    attention(sec[0] * pairs)
-    products(sec[0], keep)
-    b_v = column_sum(grads[2].astype(F32))
-    b_q = column_sum(grads[0].astype(F32))
-    little = jnp.concatenate([down.buffer[0:3], b_v, down.buffer[4:8], up.buffer[0:7], b_q], axis=0).astype(BF16)
-    little = jnp.concatenate([little, jnp.zeros_like(little)], axis=1)
+    if last:
+        turned = x
+    else:
+        turned.buffer[...] = x.buffer[...].T
+    left = dot(turned.buffer[...], grads[...]).astype(BF16)
+    right = dot(ctx.buffer[...], attend.buffer[:, lanes_half]).astype(BF16)
+    little = jnp.concatenate([down.buffer[...], up.buffer[...]], axis=0).astype(BF16)
+    zeros = jnp.zeros_like(little)
+    b_q = column_sum(grads[:, 0:wide].astype(F32)).astype(BF16)
+    b_v = column_sum(grads[:, 2 * wide :].astype(F32)).astype(BF16)
+    pad = jnp.concatenate([b_q, b_v], axis=1)
+    pad = jnp.concatenate([pad, jnp.zeros((15, width), BF16)], axis=0)
     for shard in range(shards):
-        send.buffer[shard, tall:] = little
-        keep.buffer[shard, tall:] = little
-    send.flush(move)
-    keep.flush(move)
-    ready(last)
-    total = first.buffer[...] + dot_t(grads[0], w[0]) + dot_t(grads[1], w[1]) + dot_t(grads[2], w[2])
-    gx.buffer[...] = total
-    gx.flush(move)
-    gx_low.buffer[...] = total.astype(BF16)
-    gx_low.flush(move)
+        out.buffer[shard, :tall, 0 : 3 * wide] = left[shard * tall : shard * tall + tall]
+        out.buffer[shard, :tall, 3 * wide :] = right[shard * tall : shard * tall + tall]
+        out.buffer[shard, tall:, 0:width] = little
+        out.buffer[shard, tall:, width:] = pad
+    ready(finals)
+    sum_all = base.buffer[...] + dot_t(grads[...], w[...])
+    if last:
+        gx.buffer[...] = sum_all
+        gx.flush(move)
+        gx_low.buffer[...] = sum_all.astype(BF16)
+        gx_low.flush(move)
+    else:
+        total.buffer[...] = sum_all
     move.finish()
 
 
-def attend_grad(layer, sec, attend, ctx, first, x, q, k, v, probs, wo, wo_other, w, w_other, down, up, shards, low_kind):
-    rows, width = x.shape
-    wide = (rows, width)
-    part = sds((shards, width // shards + 16, 2 * width), BF16)
+def attend_grad(layer, last, sec, attend, ctx, base, x, q, k, v, probs, wo, wo_other, w, w_other, down, up, shards, low_kind):
+    rows, width = attend.shape
+    seqs = probs.shape[0]
+    wide = width // 2
+    flat = (rows, width)
+    part = (sds((shards, width // shards + 16, 2 * width), BF16), NEAR)
+    if last:
+        outs = [(sds(flat, F32), FAR), (sds(flat, BF16), low_kind), part]
+    else:
+        outs = [(sds(flat, F32), NEAR), (sds((width, rows), BF16), NEAR), part]
+    half = ((rows, wide), BF16)
     return call(
-        functools.partial(attend_grad_kernel, layer, shards),
+        functools.partial(attend_grad_kernel, layer, last),
         sec,
-        [(attend, NEAR), (ctx, FAR), (first, NEAR)]
-        + [(item, FAR) for item in (x, q, k, v, probs)]
-        + [(wo, RAW), (wo_other, RAW), (w, RAW), (w_other, RAW), (down, NEAR), (up, NEAR)],
-        [(sds(wide, F32), FAR), (sds(wide, BF16), low_kind), (part, FAR), (part, FAR)],
-        [((width, rows), BF16), ((width, width), BF16), ((3, width, width), BF16), (wide, BF16), ((3,) + wide, BF16)],
-        "attend_grad",
-        2 * rows * width * width * 10,
-        30 << 20,
-    )
-
-
-def layer_forward(layer, sec, x, mask, big, other, small):
+        [(attend, NEAR), (ctx, FAR), (base, NEAR), (x, NEAR if last else FAR)]
+        + [(item, RAW) for item in (q, k, v, probs, wo, wo_other, w, w_other)]
+        + [(down, NEAR), (up, NEAR)],
+        outs,
+        [
+            half,
+            half,
+            half,
+            ((seqs, wide // 128) + probs.shape[2:], F32),
+            ((wide, width), BF16),
+            ((width, 3 * wide), BF16),
+            half,
+            ((rows, 3 * wide), BF16),
+        ],
+        "attend_grad_last" if last else "attend_grad_first",
+        rows * width * width * 10,
+        15 << 20,
+    )
+
+
+def layer_forward(layer, sec, x, front, big, other, small, far=None):
     w_qkv, w_out, w_up, w_down = big
     o_qkv, o_out, o_up, o_down = other
     x_kind = FAR if layer == 0 else NEAR
-    q, k, v, probs, ctx = attend_forward(layer, sec, x, x_kind, w_qkv, o_qkv, small, mask)
-    hat_one, scale_one, low, act, slope = up_forward(layer, sec, x, x_kind, ctx, w_out, o_out, w_up, o_up, small)
-    kinds = (NEAR, FAR) if layer == 0 else (FAR, NEAR)
-    y, hat_two, scale_two = down_forward(layer, sec, act, w_down, o_down, hat_one, small, *kinds)
+    q, k, v, probs, (ctx_near, ctx) = front
+    (hat_near, hat_one), scale_one, low, act, slope = up_forward(
+        layer, sec, x, x_kind, ctx_near, w_out, o_out, w_up, o_up, small
+    )
+    act_near, act = act if layer == 0 else (act, act)
+    kinds = (BOTH, FAR) if layer == 0 else (FAR, NEAR)
+    y, hat_two, scale_two = down_forward(layer, sec, act_near, w_down, o_down, hat_near, small, *kinds)
+    x = x if far is None else far
     return y, (x, q, k, v, probs, ctx, hat_one, scale_one, low, act, slope, hat_two, scale_two)
 
 
@@ -562,19 +619,22 @@
         lambda: down_grad(sec, gy, kinds[0], hat_two, scale_two, small, act, kinds[1])
     )
     line.add(d_send, d_keep)
-    first, attend, up, u_send, u_keep = line.advance(
-        lambda: up_grad(
-            layer, sec, branch, second, w_down, o_down, slope, low, w_up, o_up, hat_one, scale_one, small
-        )
-    )
-    line.add(*(item.reshape(shards, item.shape[0] // shards, item.shape[1]) for item in (u_send, u_keep)))
-    gx, gx_low, a_send, a_keep = line.advance(
-        lambda: attend_grad(
-            layer, sec, attend, ctx, first, x, q, k, v, probs, w_out, o_out, w_qkv, o_qkv, down, up, shards,
-            FAR if layer == 0 else NEAR,
-        )
-    )
-    line.add(a_send, a_keep)
+    up_ins = (w_down, o_down, slope, low, w_up, o_up, shards)
+    part, up, u_send = line.advance(lambda: up_grad(layer, False, sec, branch, second, *up_ins))
+    more = (hat_one, scale_one, small, up)
+    line.add(u_send, None, layer == 0)
+    first, attend, up, u_keep = line.advance(lambda: up_grad(layer, True, sec, branch, part, *up_ins, more))
+    line.keep(u_keep)
+    heads = (q, k, v, probs, w_out, o_out, w_qkv, o_qkv, down, up, shards)
+    low_kind = FAR if layer == 0 else BOTH
+    part, turned, a_send = line.advance(
+        lambda: attend_grad(layer, False, sec, attend, ctx, first, x, *heads, low_kind)
+    )
+    line.add(a_send, None, layer == 0)
+    gx, gx_low, a_keep = line.advance(
+        lambda: attend_grad(layer, True, sec, attend, ctx, part, turned, *heads, low_kind)
+    )
+    line.keep(a_keep)
     return gx, gx_low
 
 
@@ -624,14 +684,44 @@
     outs[0][...] = ins[0][...] + ins[1][...]
 
 
+def join_split(ids, ins, outs):
+    top, top_got, bottom, bottom_got = ins
+    send, keep = outs
+    cut, wide = top.shape[0], send.shape[1]
+    for out, half in ((send, 1 - ids[3]), (keep, ids[3])):
+        lanes = pl.ds(pl.multiple_of(half * wide, wide), wide)
+        out[:cut] = top[:, lanes] + top_got[:, lanes]
+        out[cut:] = bottom[:, lanes] + bottom_got[:, lanes]
+
+
+def join_half(ids, ins, outs):
+    kept, got = ins
+    send, keep = outs
+    wide = send.shape[1]
+    for out, half in ((send, 1 - ids[4]), (keep, ids[4])):
+        lanes = pl.ds(pl.multiple_of(half * wide, wide), wide)
+        out[...] = kept[:, lanes] + got[:, lanes]
+
+
 def join_last(ids, ins, outs):
-    @pl.when(ids[3] == 1)
+    edge = ids[3] == ids[4]
+
+    @pl.when(edge)
     def _():
         outs[0][...] = ins[1][...]
 
-    @pl.when(ids[3] == 0)
+    @pl.when(jnp.logical_not(edge))
     def _():
         outs[0][...] = ins[0][...]
+
+
+def join_sides(bit):
+    def function(ids, ins, outs):
+        wide = ins[0].shape[1]
+        for part, half in ((ins[0], ids[bit]), (ins[1], 1 - ids[bit])):
+            outs[0][:, pl.ds(pl.multiple_of(half * wide, wide), wide)] = part[...]
+
+    return function
 
 
 def join(ids, jobs):
@@ -662,88 +752,114 @@
     return result
 
 
-def move_section(parts):
-    send, keep = parts
-    shards = lax.axis_size("inner")
-    if shards != 4:
-        got = lax.psum_scatter(send.astype(BF16), "inner", scatter_dimension=0, tiled=False)
-        own = lax.psum_scatter(keep.astype(BF16), "inner", scatter_dimension=0, tiled=False)
-        got = exchange(got, "section", 1)
-        return [own, got], join_add, [own.shape]
-    got = exchange(send, "section", 1)
-    _, rows, columns = keep.shape
-    cut = split_at(rows)
-    return [keep, got], join_section, [(2, cut, columns)] * 2 + [(2, rows - cut, columns)] * 2
-
-
-def move_first(parts):
-    top_send, top, bottom_send, bottom = parts
-    top_got = exchange(top_send, "inner", 1)
-    bottom_got = exchange(bottom_send, "inner", 2)
-    return [top, top_got, bottom, bottom_got], join_first, [top.shape[1:]] * 2 + [bottom.shape[1:]] * 2
-
-
-def move_second(parts):
-    top_send, top, bottom_send, bottom = parts
-    top_got = exchange(top_send, "inner", 2)
-    bottom_got = exchange(bottom_send, "inner", 1)
-    rows = top.shape[0] + bottom.shape[0]
-    return [top, top_got, bottom, bottom_got], join_second, [(rows, top.shape[1])]
-
-
-def move_in(parts):
-    return [parts[0], lax.ppermute(parts[0], "outer", [(0, 1), (3, 2)])], join_add, [parts[0].shape]
-
-
-def move_across(parts):
-    return [parts[0], lax.ppermute(parts[0], "outer", [(1, 2), (2, 1)])], join_add, [parts[0].shape]
-
-
-def move_out(parts):
-    return [parts[0], lax.ppermute(parts[0], "outer", [(1, 0), (2, 3)])], join_last, [parts[0].shape]
-
-
-def move_any(parts):
-    return [parts[0], lax.psum(parts[0], "outer")], lambda ids, ins, outs: join_last(ids, ins, outs), [parts[0].shape]
+TIMES = (1, 2, 2, 1, 1, 1, 1)
 
 
 class Line:
     def __init__(self):
-        inner = [move_section] + ([move_first, move_second] if lax.axis_size("inner") == 4 else [])
-        place = lax.axis_index("outer")
-        if lax.axis_size("outer") == 4:
-            outer = [move_in, move_across, move_out]
-            outside = ((place == 0) | (place == 3)).astype(jnp.int32)
-        else:
-            outer = [move_any]
-            outside = jnp.ones((), jnp.int32)
-        spot = lax.axis_index("inner")
-        self.ids = jnp.stack([lax.axis_index("section"), spot % 2, spot // 2, outside]).astype(jnp.int32)
-        self.moves = inner + outer
+        self.plain = lax.axis_size("inner") != 4
+        self.short = lax.axis_size("outer") == 4
+        spot, place = lax.axis_index("inner"), lax.axis_index("outer")
+        self.ids = jnp.stack([lax.axis_index("section"), spot % 2, spot // 2, place % 2, place // 2]).astype(jnp.int32)
         self.running = []
 
-    def add(self, send, keep):
-        self.running.append({"at": 0, "parts": [send, keep], "pending": None})
-
-    def settle(self):
-        active = [item for item in self.running if item["pending"] is not None]
-        if active:
-            for item, parts in zip(active, join(self.ids, [item["pending"] for item in active])):
+    def add(self, send, keep, late=False):
+        self.running.append({"at": 0, "parts": [send, keep], "pending": None, "keep": keep, "late": late, "done": None, "flight": None})
+
+    def keep(self, keep):
+        self.running[-1]["keep"] = keep
+
+    def start(self, item):
+        at, parts = item["at"], item["parts"]
+        item["at"] += 1
+        if at == 0:
+            got = exchange(parts[0], "section", 1)
+            if self.plain:
+                return [got], lambda tied: (join_add, [item["keep"], tied[0]], [item["keep"].shape])
+            _, rows, columns = parts[0].shape
+            cut = split_at(rows)
+            shapes = [(2, cut, columns)] * 2 + [(2, rows - cut, columns)] * 2
+            return [got], lambda tied: (join_section, [item["keep"], tied[0]], shapes)
+        if self.plain:
+            total = lax.psum_scatter(parts[0], "inner", scatter_dimension=0, tiled=False)
+            item["done"] = lax.psum(total, "outer")
+            return None
+        if at == 1:
+            top_send, top, bottom_send, bottom = parts
+            gots = [exchange(top_send, "inner", 1), exchange(bottom_send, "inner", 2)]
+            shapes = [top.shape[1:]] * 2 + [bottom.shape[1:]] * 2
+            return gots, lambda tied: (join_first, [top, tied[0], bottom, tied[1]], shapes)
+        halves = self.short and item["late"]
+        if at == 2:
+            top_send, top, bottom_send, bottom = parts
+            gots = [exchange(top_send, "inner", 2), exchange(bottom_send, "inner", 1)]
+            rows, columns = top.shape[0] + bottom.shape[0], top.shape[1]
+            if halves:
+                return gots, lambda tied: (
+                    join_split, [top, tied[0], bottom, tied[1]], [(rows, columns // 2)] * 2
+                )
+            return gots, lambda tied: (join_second, [top, tied[0], bottom, tied[1]], [(rows, columns)])
+        if not self.short:
+            item["done"] = lax.psum(parts[0], "outer")
+            return None
+        rows, columns = parts[0].shape
+        if not halves and at in (3, 4, 5):
+            pairs = ([(0, 1), (3, 2)], [(1, 2), (2, 1)], [(1, 0), (2, 3)])[at - 3]
+            got = lax.ppermute(parts[0], "outer", pairs)
+            function = join_last if at == 5 else join_add
+            return [got], lambda tied: (function, [parts[0], tied[0]], [(rows, columns)])
+        if at == 3:
+            send, keep = parts
+            got = exchange(send, "outer", 1)
+            return [got], lambda tied: (join_half, [keep, tied[0]], [(rows, columns // 2)] * 2)
+        if at == 4:
+            send, keep = parts
+            got = exchange(send, "outer", 2)
+            return [got], lambda tied: (join_add, [keep, tied[0]], [(rows, columns)])
+        if halves and at in (5, 6):
+            bit = 7 - at
+            got = exchange(parts[0], "outer", bit)
+            return [got], lambda tied: (join_sides(2 + bit), [parts[0], tied[0]], [(rows, 2 * columns)])
+        item["done"] = parts[0]
+        return None
+
+    def settle(self, items):
+        if items:
+            for item, parts in zip(items, join(self.ids, [item["pending"]() for item in items])):
                 item["parts"], item["pending"] = parts, None
 
-    def advance(self, work=None):
-        self.settle()
-        active = [item for item in self.running if item["at"] < len(self.moves)]
-        started = [self.moves[item["at"]](item["parts"]) for item in active]
-        beside = work() if work is not None else ()
-        beside, tied = lax.optimization_barrier((beside, [ins for ins, _, _ in started]))
-        for item, ins, (_, function, shapes) in zip(active, tied, started):
-            item["at"] += 1
-            item["pending"] = (function, ins, shapes)
+    def advance(self, work):
+        self.settle([item for item in self.running if item["pending"] is not None])
+        for item in self.running:
+            if item["done"] is None and item["flight"] is None:
+                move = self.start(item)
+                if move is not None:
+                    item["flight"], item["left"] = move, TIMES[item["at"] - 1]
+        flying = [item for item in self.running if item["flight"] is not None]
+        for item in flying:
+            item["left"] -= 1
+        due = [item for item in flying if item["left"] == 0]
+        beside, tied = lax.optimization_barrier((work(), [item["flight"][0] for item in due]))
+        for item, gots in zip(due, tied):
+            item["pending"], item["flight"] = functools.partial(item["flight"][1], gots), None
         return beside
 
-    def done(self):
-        return all(item["at"] == len(self.moves) for item in self.running)
+    def finish(self):
+        if not self.short or self.plain:
+            for item in self.running:
+                while item["done"] is None:
+                    if item["flight"] is not None:
+                        gots, after = item["flight"]
+                        item["pending"], item["flight"] = functools.partial(after, gots), None
+                    if item["pending"] is not None:
+                        self.settle([item])
+                    item["flight"] = self.start(item)
+        while any(item["done"] is None for item in self.running):
+            self.advance(lambda: ())
+            for item in self.running:
+                if item["flight"] is not None and item is self.running[-1]:
+                    item["left"] = 1
+        return [item["done"] for item in self.running]
 
 
 def local(
@@ -770,33 +886,33 @@
     little_other = exchange(little, "section", 1)
     big = (w_qkv[0], w_out[0], w_up[0], w_down[0])
     o_qkv = exchange(big[0], "section", 1)
-    o_qkv, late_out, late_up = lax.optimization_barrier((o_qkv, big[1], big[2]))
+
+    smalls = [jnp.where(section == layer, little, little_other) for layer in (0, 1)]
+    o_qkv, smalls, mask, x, late_out, late_up = lax.optimization_barrier(
+        (o_qkv, smalls, mask, x, big[1], big[2])
+    )
     o_out, o_up = exchange(late_out, "section", 1), exchange(late_up, "section", 1)
-    o_up, late_down = lax.optimization_barrier((o_up, big[3]))
+    front = attend_forward(0, sec, x, FAR, big[0], o_qkv, smalls[0], mask)
+    front, o_out, o_up, late_down = lax.optimization_barrier((front, o_out, o_up, big[3]))
     other = (o_qkv, o_out, o_up, exchange(late_down, "section", 1))
-
-    smalls = [jnp.where(section == layer, little, little_other) for layer in (0, 1)]
-    y_one, cache_one = layer_forward(0, sec, x, mask, big, other, smalls[0])
-    y_two, cache_two = layer_forward(1, sec, y_one, mask, big, other, smalls[1])
+    y_one, cache_one = layer_forward(0, sec, x, front, big, other, smalls[0])
+    y_near, y_one = y_one
+    front = attend_forward(1, sec, y_near, NEAR, big[0], o_qkv, smalls[1], mask)
+    y_two, cache_two = layer_forward(1, sec, y_near, front, big, other, smalls[1], y_one)
     line = Line()
-    gx_two, gx_two_low = layer_backward(line, 1, sec, gy, cache_two, big, other, smalls[1], shards)
-    gx_one, gx_one_low = layer_backward(line, 0, sec, gx_two_low, cache_one, big, other, smalls[0], shards)
+    gx_two, (gx_two_near, gx_two_low) = layer_backward(line, 1, sec, gy, cache_two, big, other, smalls[1], shards)
+    gx_one, gx_one_low = layer_backward(line, 0, sec, gx_two_near, cache_one, big, other, smalls[0], shards)
 
     def gather(for_zero, for_one):
         kept = jnp.where(section == 0, for_zero, for_one)
         got = exchange(jnp.where(section == 0, for_one, for_zero), "section", 1)
         return jnp.where(section == 0, kept, got), jnp.where(section == 0, got, kept)
 
-    activations, input_grads = line.advance(
-        lambda: (
-            jnp.concatenate(gather(y_one, y_two), axis=0).reshape(seqs_local, length, width),
-            jnp.concatenate(gather(gx_one, gx_two_low.astype(F32)), axis=0).reshape(seqs_local, length, width),
-        )
-    )
-    while not line.done():
-        line.advance()
-    line.settle()
-    sums = [item["parts"][0] for item in line.running]
+    activations = jnp.concatenate(gather(y_one, y_two), axis=0).reshape(seqs_local, length, width)
+    input_grads = jnp.concatenate(gather(gx_one, gx_two_low.astype(F32)), axis=0).reshape(
+        seqs_local, length, width
+    )
+    sums = line.finish()
     down, up, attend = [gather(one, two) for one, two in zip(sums[3:], sums[:3])]
     g_w_down = jnp.concatenate(down, axis=0).T.astype(F32)
     g_w_up = jnp.concatenate(up, axis=1).astype(F32)
@@ -807,7 +923,11 @@
         [side[:, i * part : (i + 1) * part] for i in range(3) for side in matrix], axis=1
     ).astype(F32)
     g_w_out = jnp.concatenate([side[:, 3 * part :] for side in matrix], axis=1).astype(F32)
-    rows = jnp.where(section == 0, sums[5][tall:, :width], sums[2][tall:, :width])
+    rows = attend[0][tall:, :width]
+    b_q, b_v = [
+        jnp.concatenate([side[tall, width + i * part : width + (i + 1) * part] for side in attend]) for i in range(2)
+    ]
+    rows = jnp.concatenate([rows, b_q[None], b_v[None]], axis=0)
     place = lax.axis_index("inner")
     mine = lax.dynamic_slice_in_dim(rows, place * tall, tall, 1).astype(F32)
     up_row = pick(rows[11 : 11 + blocks].reshape(shards, width * blocks // shards), place, 0).astype(F32)
@@ -815,7 +935,7 @@
         activations[None],
         input_grads[None],
         g_w_qkv[None],
-        jnp.stack([mine[15], mine[3]])[None],
+        mine[16:18][None],
         g_w_out[None],
         mine[10][None],
         jnp.stack([mine[8], mine[0]])[None],

time: 427 us -> 360 us (0.84)
  local copies, waits for them, and re-layouts: 77.9 us -> 17.8 us
  waiting for transfers between devices: 101 us -> 82.5 us
  Pallas kernels: 145 us -> 158 us
    unnamed x237 -> x55, local copies, waits for them, and re-layouts: 75.5 us -> 13.2 us
    ppermute x18 -> x12, waiting for transfers between devices: 46.4 us -> 12.4 us  [start(): got = lax.ppermute(parts[0], 'outer', pairs)]
    ppermute x40 -> x48, starting transfers between devices: 29.8 us -> 45.8 us  [exchange(): return lax.ppermute(array, axis, [(i, i ^ bit) for i in range(length)])]
    ppermute x40 -> x48, waiting for transfers between devices: 54.9 us -> 70.1 us  [exchange(): return lax.ppermute(array, axis, [(i, i ^ bit) for i in range(length)])]
    ppermute x18 -> x12, starting transfers between devices: 43.3 us -> 28.2 us  [start(): got = lax.ppermute(parts[0], 'outer', pairs)]
    pallas_call x12 -> x16, Pallas kernels: 131 us -> 144 us  [call(): pl.pallas_call(body, in_specs=[pl.BlockSpec(memory_space=pltpu.SMEM)] + [...]
    pallas_call x11 -> x17, Pallas kernels: 14.6 us -> 14.2 us  [join(): pl.pallas_call(kernel, in_specs=[pl.BlockSpec(memory_space=pltpu.SMEM)] +...]
  transfers between devices with their start and end apart: 58 -> 60, of which waited for: 19 -> 25; matrix products, arithmetic and copies ran while one was open for 6% -> 7% of each run, Pallas kernels for 24% -> 32%
where the time goes in v3:
time: 360 us; the launch traced here: 357 us
  Pallas kernels  158 us (44%)
  waiting for transfers between devices  82.5 us (23%)
  starting transfers between devices  73.9 us (21%)
  other arithmetic  22.6 us (6%)
  local copies, waits for them, and re-layouts  17.8 us (5%)
    pallas_call x16, Pallas kernels, call(): pl.pallas_call(body, in_specs=[pl.BlockSpec(memory_space=pltpu.SMEM)] + [...  144 us
    ppermute x48, waiting for transfers between devices, exchange(): return lax.ppermute(array, axis, [(i, i ^ bit) for i in range(length)])  70.1 us
    ppermute x48, starting transfers between devices, exchange(): return lax.ppermute(array, axis, [(i, i ^ bit) for i in range(length)])  45.8 us
    ppermute x12, starting transfers between devices, start(): got = lax.ppermute(parts[0], 'outer', pairs)  28.2 us
    pallas_call x17, Pallas kernels, join(): pl.pallas_call(kernel, in_specs=[pl.BlockSpec(memory_space=pltpu.SMEM)] +...  14.2 us
    unnamed x55, local copies, waits for them, and re-layouts  13.2 us
    ppermute x12, waiting for transfers between devices, start(): got = lax.ppermute(parts[0], 'outer', pairs)  12.4 us
  transfers between devices with their start and end apart: 60, of which 25 were waited for; matrix products, arithmetic and copies ran while one was open for 7% of the time, Pallas kernels for 32%

profile of v3, /device:TPU:0, one launch (start us, length us, event | category | flops | bytes accessed | tf_op | source)
XLA Modules:
  0.0 356.6 jit_solution(10030935060848560287)
XLA Ops:
  8.5 10.7 %attend_forward.2 = (bf16[512,768]{1,0:T(8,128)(2,1)}, bf16[512,768]{1,0:T(8,128)(2,1)}, bf16[512,768]{1,0:T(8,128)(2,1)}, f32[4,6,256,128]{3,2,1,0:T(8,128)}, b...) custom-call(s32[1]{0:T(128)} %bitcast.ids_ref, bf16[512,768]{1,0:T(8,128)(2,1)} %bitcast.89, ...), custom_call_target="tpu_custom_call" | custom-call | flops 2415919104 | bytes 12582912 | tf_op jit(solution)/shard_map/attend_forward/pallas_call | solution.py:149
  22.0 12.1 %up_forward.2 = (f32[512,768]{1,0:T(8,128)S(1)}, f32[512,768]{1,0:T(8,128)}, f32[512,128]{1,0:T(8,128)}, bf16[768,512]{1,0:T(8,128)(2,1)}, bf16[4,512,768]{2,1,0...) custom-call(s32[1]{0:T(128)} %bitcast.ids_ref, bf16[512,768]{1,0:T(8,128)(2,1)} %bitcast.90, ...), custom_call_target="tpu_custom_call" | custom-call | flops 3019898880 | bytes 20971520 | tf_op jit(solution)/shard_map/up_forward/pallas_call | solution.py:149
  34.1 2.2 copy-done.12
  36.3 8.1 %down_forward.2 = (bf16[512,768]{1,0:T(8,128)(2,1)S(1)}, bf16[512,768]{1,0:T(8,128)(2,1)}, f32[512,768]{1,0:T(8,128)}, f32[512,128]{1,0:T(8,128)}) custom-call(s32[1]{0:T(128)} %bitcast.ids_ref, bf16[4,512,768]{2,1,0:T(8,128)(2,1)S(1)} %get-tuple-element.263.refs_0_, bf16[3072,768]{1,0:T(8,128)(2,1)} %bitcast.59, bf16[3072,768]{1,0:T(8,128)(2,1)} %copy-done.12, ...), custom_call_target="tpu_custom_call" | custom-call | flops 2415919104 | bytes 12582912 | tf_op jit(solution)/shard_map/down_forward/pallas_call | solution.py:149
  44.4 11.0 %attend_forward.3 = (bf16[512,768]{1,0:T(8,128)(2,1)}, bf16[512,768]{1,0:T(8,128)(2,1)}, bf16[512,768]{1,0:T(8,128)(2,1)}, f32[4,6,256,128]{3,2,1,0:T(8,128)}, b...) custom-call(s32[1]{0:T(128)} %bitcast.ids_ref, bf16[512,768]{1,0:T(8,128)(2,1)S(1)} %get-tuple-element.267.refs_0_, ...), custom_call_target="tpu_custom_call" | custom-call | flops 2415919104 | bytes 12582912 | tf_op jit(solution)/shard_map/attend_forward/pallas_call | solution.py:149
  55.4 11.6 %up_forward.3 = (f32[512,768]{1,0:T(8,128)S(1)}, f32[512,768]{1,0:T(8,128)}, f32[512,128]{1,0:T(8,128)}, bf16[768,512]{1,0:T(8,128)(2,1)}, bf16[4,512,768]{2,1,0:T(8,128)(2,1)S(1)}, /*index=5*/f32[4,512,768]{2,1,0:T(8,128)}) custom-call(s32[1]{0:T(128)} %bitcast.ids_ref, bf16[512,768]{1,0:T(8,128)(2,1)S(1)} %get-tuple-element.267.refs_0_, ...), custom_call_target="tpu_custom_call" | custom-call | flops 3019898880 | bytes 20971520 | tf_op jit(solution)/shard_map/up_forward/pallas_call | solution.py:149
  67.0 7.5 %down_forward.3 = (bf16[512,768]{1,0:T(8,128)(2,1)}, f32[512,768]{1,0:T(8,128)S(1)}, f32[512,128]{1,0:T(8,128)S(1)}) custom-call(s32[1]{0:T(128)} %bitcast.ids_ref, bf16[4,512,768]{2,1,0:T(8,128)(2,1)S(1)} %get-tuple-element.270.refs_0_.refs_4_, bf16[3072,768]{1,0:T(8,128)(2,1)} %bitcast.60, bf16[3072,768]{1,0:T(8,128)(2,1)} %copy-done.12, ...), custom_call_target="tpu_custom_call" | custom-call | flops 2415919104 | bytes 12582912 | tf_op jit(solution)/shard_map/down_forward/pallas_call | solution.py:149
  74.6 5.8 %down_grad.2 = (f32[512,768]{1,0:T(8,128)S(1)}, bf16[512,768]{1,0:T(8,128)(2,1)S(1)}, f32[8,768]{1,0:T(8,128)S(1)}, bf16[4,384,768]{2,1,0:T(8,128)(2,1)S(1)}, bf16[4,384,768]{2,1,0:T(8,128)(2,1)S(1)}) custom-call(s32[1]{0:T(128)} %bitcast.ids_ref, bf16[512,768]{1,0:T(8,128)(2,1)} %bitcast.94, f32[512,768]{1,0:T(8,128)S(1)} %get-tuple-element.273.refs_1_, ...), custom_call_target="tpu_custom_call" | custom-call | flops 2415919104 | bytes 14680064 | tf_op jit(solution)/shard_map/down_grad/pallas_call | solution.py:149
  80.9 8.6 %up_grad_first.2 = (f32[512,768]{1,0:T(8,128)S(1)}, f32[8,768]{1,0:T(8,128)S(1)}, bf16[4,192,1536]{2,1,0:T(8,128)(2,1)}) custom-call(s32[1]{0:T(128)} %bitcast.ids_ref, bf16[512,768]{1,0:T(8,128)(2,1)S(1)} %get-tuple-element.275.refs_0_, f32[512,768]{1,0:T(8,128)S(1)} %get-tuple-element.276.refs_1_, bf16[3072,768]{1,0:T(8,128)(2,1)} %bitcast.61, ...), custom_call_target="tpu_custom_call" | custom-call | flops 3623878656 | bytes 15728640 | tf_op jit(solution)/shard_map/up_grad_first/pallas_call | solution.py:149
  92.5 1.7 copy-done.3
  94.2 1.7 copy-done.5
  96.8 2.6 collective-permute-start.8
  99.4 1.5 collective-permute-start.9
  100.9 8.6 %up_grad_last.2 = (f32[512,768]{1,0:T(8,128)S(1)}, bf16[512,768]{1,0:T(8,128)(2,1)S(1)}, f32[8,768]{1,0:T(8,128)S(1)}, bf16[4,192,1536]{2,1,0:T(8,128)(2,1)S(1)}) custom-call(s32[1]{0:T(128)} %bitcast.ids_ref, bf16[512,768]{1,0:T(8,128)(2,1)S(1)} %get-tuple-element.275.refs_0_, f32[512,768]{1,0:T(8,128)S(1)} %copy-done.7, bf16[3072,768]{1,0:T(8,128)(2,1)} %bitcast.62, ...), custom_call_target="tpu_custom_call" | custom-call | flops 3623878656 | bytes 15728640 | tf_op jit(solution)/shard_map/up_grad_last/pallas_call | solution.py:149
  109.5 8.6 %attend_grad_first.2 = (f32[512,768]{1,0:T(8,128)S(1)}, bf16[768,512]{1,0:T(8,128)(2,1)S(1)}, bf16[4,208,1536]{2,1,0:T(8,128)(2,1)S(1)}) custom-call(s32[1]{0:T(128)} %bitcast.ids_ref, bf16[512,768]{1,0:T(8,128)(2,1)S(1)} %get-tuple-element.292.refs_0_, bf16[768,512]{1,0:T(8,128)(2,1)} %get-tuple-element.293.refs_1_, ...), custom_call_target="tpu_custom_call" | custom-call | flops 3019898880 | bytes 15728640 | tf_op jit(solution)/shard_map/attend_grad_first/pallas_call | solution.py:149
  120.6 1.7 collective-permute-start.13
  123.8 9.8 %attend_grad_last.2 = (f32[512,768]{1,0:T(8,128)}, bf16[512,768]{1,0:T(8,128)(2,1)S(1)}, bf16[512,768]{1,0:T(8,128)(2,1)}, bf16[4,208,1536]{2,1,0:T(8,128)(2,1)S(1)}) custom-call(s32[1]{0:T(128)} %bitcast.ids_ref, bf16[512,768]{1,0:T(8,128)(2,1)S(1)} %get-tuple-element.292.refs_0_, bf16[768,512]{1,0:T(8,128)(2,1)} %get-tuple-element.293.refs_1_, ...), custom_call_target="tpu_custom_call" | custom-call | flops 3019898880 | bytes 15728640 | tf_op jit(solution)/shard_map/attend_grad_last/pallas_call | solution.py:149
  133.6 1.6 collective-permute-done.10.refs_1_
  135.8 7.3 %down_grad.3 = (f32[512,768]{1,0:T(8,128)S(1)}, bf16[512,768]{1,0:T(8,128)(2,1)S(1)}, f32[8,768]{1,0:T(8,128)S(1)}, bf16[4,384,768]{2,1,0:T(8,128)(2,1)S(1)}, bf16[4,384,768]{2,1,0:T(8,128)(2,1)S(1)}) custom-call(s32[1]{0:T(128)} %bitcast.ids_ref, bf16[512,768]{1,0:T(8,128)(2,1)S(1)} %get-tuple-element.318.refs_0_, f32[512,768]{1,0:T(8,128)} %get-tuple-element.319.refs_1_, ...), custom_call_target="tpu_custom_call" | custom-call | flops 2415919104 | bytes 14680064 | tf_op jit(solution)/shard_map/down_grad/pallas_call | solution.py:149
  144.1 1.5 collective-permute-start.18
  146.1 1.5 collective-permute-start.19
  148.2 3.5 collective-permute-start.15
  151.8 3.7 %collective-permute-done.16.refs_3_ = bf16[96,1536]{1,0:T(8,128)(2,1)S(1)} collective-permute-done((bf16[96,1536]{1,0:T(8,128)(2,1)S(1)}, bf16[96,1536]{1,0:T(8,128)(2,1)S(1)}, u32[]{:S(2)}, u32[]{:S(2)}) %collective-permute-start.16) | collective-permute-done | bytes 294944 | tf_op jit(solution)/shard_map/ppermute | solution.py:643
  156.0 7.5 %up_grad_first.3 = (f32[512,768]{1,0:T(8,128)S(1)}, f32[8,768]{1,0:T(8,128)S(1)}, bf16[4,192,1536]{2,1,0:T(8,128)(2,1)S(1)}) custom-call(s32[1]{0:T(128)} %bitcast.ids_ref, bf16[512,768]{1,0:T(8,128)(2,1)S(1)} %get-tuple-element.333.refs_0_, f32[512,768]{1,0:T(8,128)S(1)} %get-tuple-element.334.refs_1_, bf16[3072,768]{1,0:T(8,128)(2,1)} %bitcast.63, ...), custom_call_target="tpu_custom_call" | custom-call | flops 3623878656 | bytes 15728640 | tf_op jit(solution)/shard_map/up_grad_first/pallas_call | solution.py:149
  163.5 4.8 %collective-permute-done.17.refs_5_ = bf16[96,1536]{1,0:T(8,128)(2,1)S(1)} collective-permute-done((bf16[96,1536]{1,0:T(8,128)(2,1)S(1)}, bf16[96,1536]{1,0:T(8,128)(2,1)S(1)}, u32[]{:S(2)}, u32[]{:S(2)}) %collective-permute-start.17) | collective-permute-done | bytes 294944 | tf_op jit(solution)/shard_map/ppermute | solution.py:643
  170.1 6.3 %collective-permute-start.22 = (bf16[192,1536]{1,0:T(8,128)(2,1)S(1)}, bf16[192,1536]{1,0:T(8,128)(2,1)S(1)}, u32[]{:S(2)}, u32[]{:S(2)}) collective-permute-start(bf16[192,1536]{1,0:T(8,128)(2,1)S(1)} %get-tuple-element.375.refs_2_), channel_id=1, source_target_pairs={{0,1},{3,2},{4,5},{7,6},{8,9},{11,10},{12,13},{15,14},{16,17},{19,... | collective-permute-start | bytes 1769480 | tf_op jit(solution)/shard_map/ppermute | solution.py:808
  176.4 1.6 collective-permute-start.28
  178.5 8.6 %up_grad_last.3 = (f32[512,768]{1,0:T(8,128)S(1)}, bf16[512,768]{1,0:T(8,128)(2,1)S(1)}, f32[8,768]{1,0:T(8,128)S(1)}, bf16[4,192,1536]{2,1,0:T(8,128)(2,1)S(1)}) custom-call(s32[1]{0:T(128)} %bitcast.ids_ref, bf16[512,768]{1,0:T(8,128)(2,1)S(1)} %get-tuple-element.333.refs_0_, f32[512,768]{1,0:T(8,128)S(1)} %get-tuple-element.355.refs_1_, ...), custom_call_target="tpu_custom_call" | custom-call | flops 3623878656 | bytes 15728640 | tf_op jit(solution)/shard_map/up_grad_last/pallas_call | solution.py:149
  187.7 1.6 collective-permute-done.22.refs_3_
  192.4 5.6 %collective-permute-done.27.refs_7_ = bf16[96,1536]{1,0:T(8,128)(2,1)S(1)} collective-permute-done((bf16[96,1536]{1,0:T(8,128)(2,1)S(1)}, bf16[96,1536]{1,0:T(8,128)(2,1)S(1)}, u32[]{:S(2)}, u32[]{:S(2)}) %collective-permute-start.27) | collective-permute-done | bytes 294944 | tf_op jit(solution)/shard_map/ppermute | solution.py:643
  198.5 8.4 %attend_grad_first.3 = (f32[512,768]{1,0:T(8,128)S(1)}, bf16[768,512]{1,0:T(8,128)(2,1)S(1)}, bf16[4,208,1536]{2,1,0:T(8,128)(2,1)S(1)}) custom-call(s32[1]{0:T(128)} %bitcast.ids_ref, bf16[512,768]{1,0:T(8,128)(2,1)S(1)} %get-tuple-element.377.refs_0_, bf16[768,512]{1,0:T(8,128)(2,1)} %get-tuple-element.378.refs_1_, ...), custom_call_target="tpu_custom_call" | custom-call | flops 3019898880 | bytes 15728640 | tf_op jit(solution)/shard_map/attend_grad_first/pallas_call | solution.py:149
  206.9 2.3 collective-permute-done.26.refs_5_
  210.1 3.7 %collective-permute-start.31 = (bf16[208,1536]{1,0:T(8,128)(2,1)S(1)}, bf16[208,1536]{1,0:T(8,128)(2,1)S(1)}, u32[]{:S(2)}, u32[]{:S(2)}) collective-permute-start(bf16[208,1536]{1,0:T(8,128)(2,1)S(1)} %get-tuple-element.414.refs_2_), channel_id=1, source_target_pairs={{0,1},{3,2},{4,5},{7,6},{8,9},{11,10},{12,13},{15,14},{16,17},{19,... | collective-permute-start | bytes 1916936 | tf_op jit(solution)/shard_map/ppermute | solution.py:808
  213.8 1.6 collective-permute-start.32
  217.2 9.8 %attend_grad_last.3 = (f32[512,768]{1,0:T(8,128)}, bf16[512,768]{1,0:T(8,128)(2,1)}, bf16[4,208,1536]{2,1,0:T(8,128)(2,1)S(1)}) custom-call(s32[1]{0:T(128)} %bitcast.ids_ref, bf16[512,768]{1,0:T(8,128)(2,1)S(1)} %get-tuple-element.377.refs_0_, bf16[768,512]{1,0:T(8,128)(2,1)} %get-tuple-element.378.refs_1_, f32[512,768]{1,0:T(8,128)S(1)} %get-tuple-element.399.refs_2_, ...), custom_call_target="tpu_custom_call" | custom-call | flops 3019898880 | bytes 15728640 | tf_op jit(solution)/shard_map/attend_grad_last/pallas_call | solution.py:149
  227.0 2.4 collective-permute-done.32.refs_5_
  230.6 2.1 collective-permute-done.30.refs_1_
  234.6 1.6 collective-permute-start.37
  236.7 1.5 collective-permute-start.43
  238.2 4.1 %collective-permute-done.37.refs_3_ = bf16[192,768]{1,0:T(8,128)(2,1)S(1)} collective-permute-done((bf16[192,768]{1,0:T(8,128)(2,1)S(1)}, bf16[192,768]{1,0:T(8,128)(2,1)S(1)}, u32[]{:S(2)}, u32[]{:S(2)}) %collective-permute-start.37) | collective-permute-done | bytes 294944 | tf_op jit(solution)/shard_map/ppermute | solution.py:643
  242.3 3.8 %collective-permute-done.38.refs_5_ = bf16[192,768]{1,0:T(8,128)(2,1)S(1)} collective-permute-done((bf16[192,768]{1,0:T(8,128)(2,1)S(1)}, bf16[192,768]{1,0:T(8,128)(2,1)S(1)}, u32[]{:S(2)}, u32[]{:S(2)}) %collective-permute-start.38) | collective-permute-done | bytes 294944 | tf_op jit(solution)/shard_map/ppermute | solution.py:643
  248.7 1.5 collective-permute-start.44
  250.2 6.4 %collective-permute-start.40 = (bf16[384,768]{1,0:T(8,128)(2,1)S(1)}, bf16[384,768]{1,0:T(8,128)(2,1)S(1)}, u32[]{:S(2)}, u32[]{:S(2)}) collective-permute-start(bf16[384,768]{1,0:T(8,128)(2,1)S(1)} %get-tuple-element.437.refs_2_), channel_id=1, source_target_pairs={{0,1},{3,2},{4,5},{7,6},{8,9},{11,10},{12,13},{15,14},{16,17},{19,... | collective-permute-start | bytes 1769480 | tf_op jit(solution)/shard_map/ppermute | solution.py:808
  256.6 1.5 collective-permute-done.41.refs_5_
  259.9 4.9 %collective-permute-done.42.refs_7_ = bf16[96,1536]{1,0:T(8,128)(2,1)S(1)} collective-permute-done((bf16[96,1536]{1,0:T(8,128)(2,1)S(1)}, bf16[96,1536]{1,0:T(8,128)(2,1)S(1)}, u32[]{:S(2)}, u32[]{:S(2)}) %collective-permute-start.42) | collective-permute-done | bytes 294944 | tf_op jit(solution)/shard_map/ppermute | solution.py:643
  264.8 1.5 collective-permute-done.40.refs_3_
  266.4 1.6 join_sums.27
  269.6 8.3 %collective-permute-start.46 = (bf16[192,768]{1,0:T(8,128)(2,1)S(1)}, bf16[192,768]{1,0:T(8,128)(2,1)S(1)}, u32[]{:S(2)}, u32[]{:S(2)}) collective-permute-start(bf16[192,768]{1,0:T(8,128)(2,1)S(1)} %get-tuple-element.453), channel_id=1, source_target_pairs={{0,1},{1,0},{2,3},{3,2},{4,5},{5,4},{6,7},{7,6},{8,9},{9,8},{10,11... | collective-permute-start | bytes 884744 | tf_op jit(solution)/shard_map/ppermute | solution.py:643
  277.9 7.7 %collective-permute-done.46.refs_3_ = bf16[192,768]{1,0:T(8,128)(2,1)S(1)} collective-permute-done((bf16[192,768]{1,0:T(8,128)(2,1)S(1)}, bf16[192,768]{1,0:T(8,128)(2,1)S(1)}, u32[]{:S(2)}, u32[]{:S(2)}) %collective-permute-start.46) | collective-permute-done | bytes 294944 | tf_op jit(solution)/shard_map/ppermute | solution.py:643
  288.2 1.6 collective-permute-start.49
  290.3 3.8 %collective-permute-start.48 = (bf16[192,384]{1,0:T(8,128)(2,1)}, bf16[192,384]{1,0:T(8,128)(2,1)S(1)}, u32[]{:S(2)}, u32[]{:S(2)}) collective-permute-start(bf16[192,384]{1,0:T(8,128)(2,1)} %copy-done.11), channel_id=1, source_target_pairs={{0,2},{1,3},{2,0},{3,1},{4,6},{5,7},{6,4},{7,5},{8,10},{9,11},{10,... | collective-permute-start | bytes 442376 | tf_op jit(solution)/shard_map/ppermute | solution.py:643
  294.1 1.5 broadcast_select_fusion.1
  295.6 2.9 collective-permute-done.50.refs_7_
  300.0 7.0 %collective-permute-done.47.refs_1_ = bf16[384,768]{1,0:T(8,128)(2,1)S(1)} collective-permute-done((bf16[384,768]{1,0:T(8,128)(2,1)S(1)}, bf16[384,768]{1,0:T(8,128)(2,1)S(1)}, u32[]{:S(2)}, u32[]{:S(2)}) %collective-permute-start.47) | collective-permute-done | bytes 589856 | tf_op jit(solution)/shard_map/ppermute | solution.py:808
  309.6 1.9 collective-permute-start.51
  311.6 6.0 %collective-permute-done.51.refs_1_ = bf16[192,384]{1,0:T(8,128)(2,1)S(1)} collective-permute-done((bf16[192,384]{1,0:T(8,128)(2,1)S(1)}, bf16[192,384]{1,0:T(8,128)(2,1)S(1)}, u32[]{:S(2)}, u32[]{:S(2)}) %collective-permute-start.51) | collective-permute-done | bytes 147488 | tf_op jit(solution)/shard_map/ppermute | solution.py:643
  317.6 2.2 collective-permute-done.52.refs_3_
  320.5 1.7 fusion.1
  323.5 1.9 pad_maximum_fusion
  325.3 4.0 %collective-permute-done.54.refs_3_ = bf16[208,384]{1,0:T(8,128)(2,1)S(1)} collective-permute-done((bf16[208,384]{1,0:T(8,128)(2,1)S(1)}, bf16[208,384]{1,0:T(8,128)(2,1)S(1)}, u32[]{:S(2)}, u32[]{:S(2)}) %collective-permute-start.54) | collective-permute-done | bytes 159776 | tf_op jit(solution)/shard_map/ppermute | solution.py:643
  332.9 6.6 %collective-permute-done.55.refs_1_ = bf16[208,384]{1,0:T(8,128)(2,1)S(1)} collective-permute-done((bf16[208,384]{1,0:T(8,128)(2,1)S(1)}, bf16[208,384]{1,0:T(8,128)(2,1)S(1)}, u32[]{:S(2)}, u32[]{:S(2)}) %collective-permute-start.55) | collective-permute-done | bytes 159776 | tf_op jit(solution)/shard_map/ppermute | solution.py:643
  341.0 1.6 convert_bitcast_fusion
  342.6 3.0 copy.29
  349.1 1.7 maximum_convert_fusion
  (190 shorter events, 64.3 us)
Async XLA Ops:
  0.7 7.3 %collective-permute-start = (bf16[768,2304]{1,0:T(8,128)(2,1)}, bf16[768,2304]{1,0:T(8,128)(2,1)}, u32[]{:S(2)}, u32[]{:S(2)}) collective-permute-start(bf16[768,2304]{1,0:T(8,128)(2,1)} %bitcast.75), channel_id=1, source_target_pairs={{0,16},{16,0},{1,17},{17,1},{2,18},{18,2},{3,19},{19,3},{4,20},{20... | collective-permute-start | bytes 10616840 | tf_op jit(solution)/shard_map/ppermute | solution.py:643
  3.9 3.4 collective-permute-start.1
  8.0 11.2 %collective-permute-start.3 = (bf16[768,3072]{1,0:T(8,128)(2,1)}, bf16[768,3072]{1,0:T(8,128)(2,1)S(1)}, u32[]{:S(2)}, u32[]{:S(2)}) collective-permute-start(bf16[768,3072]{1,0:T(8,128)(2,1)} %bitcast.68), channel_id=1, source_target_pairs={{0,16},{16,0},{1,17},{17,1},{2,18},{18,2},{3,19},{19,3},{4,20},{20... | collective-permute-start | bytes 14155784 | tf_op jit(solution)/shard_map/ppermute | solution.py:643
  8.4 10.8 %collective-permute-start.2 = (bf16[768,768]{1,0:T(8,128)(2,1)}, bf16[768,768]{1,0:T(8,128)(2,1)S(1)}, u32[]{:S(2)}, u32[]{:S(2)}) collective-permute-start(bf16[768,768]{1,0:T(8,128)(2,1)} %bitcast.82), channel_id=1, source_target_pairs={{0,16},{16,0},{1,17},{17,1},{2,18},{18,2},{3,19},{19,3},{4,20},{20... | collective-permute-start | bytes 3538952 | tf_op jit(solution)/shard_map/ppermute | solution.py:643
  19.3 14.8 %collective-permute-start.4 = (bf16[3072,768]{1,0:T(8,128)(2,1)S(1)}, bf16[3072,768]{1,0:T(8,128)(2,1)S(1)}, u32[]{:S(2)}, u32[]{:S(2)}) collective-permute-start(bf16[3072,768]{1,0:T(8,128)(2,1)S(1)} %bitcast.67), channel_id=1, source_target_pairs={{0,16},{16,0},{1,17},{17,1},{2,18},{18,2},{3,19},{19,3},{4,20},{20... | collective-permute-start | bytes 14155784 | tf_op jit(solution)/shard_map/ppermute | solution.py:643
  80.4 10.3 %collective-permute-start.6 = (bf16[4,384,768]{2,1,0:T(8,128)(2,1)S(1)}, bf16[4,384,768]{2,1,0:T(8,128)(2,1)S(1)}, u32[]{:S(2)}, u32[]{:S(2)}) collective-permute-start(bf16[4,384,768]{2,1,0:T(8,128)(2,1)S(1)} %get-tuple-element.282), channel_id=1, source_target_pairs={{0,16},{16,0},{1,17},{17,1},{2,18},{18,2},{3,19},{19,3},{4,20},{20... | collective-permute-start | bytes 7077896 | tf_op jit(solution)/shard_map/ppermute | solution.py:643
  92.0 17.4 %collective-permute-start.7 = (bf16[4,192,1536]{2,1,0:T(8,128)(2,1)}, bf16[4,192,1536]{2,1,0:T(8,128)(2,1)S(1)}, u32[]{:S(2)}, u32[]{:S(2)}) collective-permute-start(bf16[4,192,1536]{2,1,0:T(8,128)(2,1)} %get-tuple-element.291), channel_id=1, source_target_pairs={{0,16},{16,0},{1,17},{17,1},{2,18},{18,2},{3,19},{19,3},{4,20},{20... | collective-permute-start | bytes 7077896 | tf_op jit(solution)/shard_map/ppermute | solution.py:643
  96.8 21.3 %collective-permute-start.8 = (bf16[2,192,768]{2,1,0:T(8,128)(2,1)S(1)}, bf16[2,192,768]{2,1,0:T(8,128)(2,1)S(1)}, u32[]{:S(2)}, u32[]{:S(2)}) collective-permute-start(bf16[2,192,768]{2,1,0:T(8,128)(2,1)S(1)} %get-tuple-element.306), channel_id=1, source_target_pairs={{0,4},{4,0},{8,12},{12,8},{1,5},{5,1},{9,13},{13,9},{2,6},{6,2},{1... | collective-permute-start | bytes 1769480 | tf_op jit(solution)/shard_map/ppermute | solution.py:643
  99.4 18.7 %collective-permute-start.9 = (bf16[2,192,768]{2,1,0:T(8,128)(2,1)S(1)}, bf16[2,192,768]{2,1,0:T(8,128)(2,1)S(1)}, u32[]{:S(2)}, u32[]{:S(2)}) collective-permute-start(bf16[2,192,768]{2,1,0:T(8,128)(2,1)S(1)} %get-tuple-element.307), channel_id=1, source_target_pairs={{0,8},{4,12},{8,0},{12,4},{1,9},{5,13},{9,1},{13,5},{2,10},{6,14},... | collective-permute-start | bytes 1769480 | tf_op jit(solution)/shard_map/ppermute | solution.py:643
  118.1 17.7 %collective-permute-start.12 = (bf16[4,208,1536]{2,1,0:T(8,128)(2,1)S(1)}, bf16[4,208,1536]{2,1,0:T(8,128)(2,1)S(1)}, u32[]{:S(2)}, u32[]{:S(2)}) collective-permute-start(bf16[4,208,1536]{2,1,0:T(8,128)(2,1)S(1)} %get-tuple-element.317), channel_id=1, source_target_pairs={{0,16},{16,0},{1,17},{17,1},{2,18},{18,2},{3,19},{19,3},{4,20},{20... | collective-permute-start | bytes 7667720 | tf_op jit(solution)/shard_map/ppermute | solution.py:643
  119.0 16.2 %collective-permute-start.10 = (bf16[2,96,1536]{2,1,0:T(8,128)(2,1)S(1)}, bf16[2,96,1536]{2,1,0:T(8,128)(2,1)S(1)}, u32[]{:S(2)}, u32[]{:S(2)}) collective-permute-start(bf16[2,96,1536]{2,1,0:T(8,128)(2,1)S(1)} %get-tuple-element.315), channel_id=1, source_target_pairs={{0,4},{4,0},{8,12},{12,8},{1,5},{5,1},{9,13},{13,9},{2,6},{6,2},{1... | collective-permute-start | bytes 1769480 | tf_op jit(solution)/shard_map/ppermute | solution.py:643
  119.6 16.2 %collective-permute-start.11 = (bf16[2,96,1536]{2,1,0:T(8,128)(2,1)S(1)}, bf16[2,96,1536]{2,1,0:T(8,128)(2,1)S(1)}, u32[]{:S(2)}, u32[]{:S(2)}) collective-permute-start(bf16[2,96,1536]{2,1,0:T(8,128)(2,1)S(1)} %get-tuple-element.316), channel_id=1, source_target_pairs={{0,8},{4,12},{8,0},{12,4},{1,9},{5,13},{9,1},{13,5},{2,10},{6,14},... | collective-permute-start | bytes 1769480 | tf_op jit(solution)/shard_map/ppermute | solution.py:643
  120.6 22.4 %collective-permute-start.13 = (bf16[192,768]{1,0:T(8,128)(2,1)S(1)}, bf16[192,768]{1,0:T(8,128)(2,1)S(1)}, u32[]{:S(2)}, u32[]{:S(2)}) collective-permute-start(bf16[192,768]{1,0:T(8,128)(2,1)S(1)} %get-tuple-element.331), channel_id=1, source_target_pairs={{0,8},{4,12},{8,0},{12,4},{1,9},{5,13},{9,1},{13,5},{2,10},{6,14},... | collective-permute-start | bytes 884744 | tf_op jit(solution)/shard_map/ppermute | solution.py:643
  122.4 20.7 %collective-permute-start.14 = (bf16[192,768]{1,0:T(8,128)(2,1)S(1)}, bf16[192,768]{1,0:T(8,128)(2,1)S(1)}, u32[]{:S(2)}, u32[]{:S(2)}) collective-permute-start(bf16[192,768]{1,0:T(8,128)(2,1)S(1)} %get-tuple-element.332), channel_id=1, source_target_pairs={{0,4},{4,0},{8,12},{12,8},{1,5},{5,1},{9,13},{13,9},{2,6},{6,2},{1... | collective-permute-start | bytes 884744 | tf_op jit(solution)/shard_map/ppermute | solution.py:643
  143.1 25.3 %collective-permute-start.20 = (bf16[4,384,768]{2,1,0:T(8,128)(2,1)S(1)}, bf16[4,384,768]{2,1,0:T(8,128)(2,1)S(1)}, u32[]{:S(2)}, u32[]{:S(2)}) collective-permute-start(bf16[4,384,768]{2,1,0:T(8,128)(2,1)S(1)} %get-tuple-element.354), channel_id=1, source_target_pairs={{0,16},{16,0},{1,17},{17,1},{2,18},{18,2},{3,19},{19,3},{4,20},{20... | collective-permute-start | bytes 7077896 | tf_op jit(solution)/shard_map/ppermute | solution.py:643
  144.1 24.2 %collective-permute-start.18 = (bf16[2,112,1536]{2,1,0:T(8,128)(2,1)S(1)}, bf16[2,112,1536]{2,1,0:T(8,128)(2,1)S(1)}, u32[]{:S(2)}, u32[]{:S(2)}) collective-permute-start(bf16[2,112,1536]{2,1,0:T(8,128)(2,1)S(1)} %get-tuple-element.352), channel_id=1, source_target_pairs={{0,4},{4,0},{8,12},{12,8},{1,5},{5,1},{9,13},{13,9},{2,6},{6,2},{1... | collective-permute-start | bytes 2064392 | tf_op jit(solution)/shard_map/ppermute | solution.py:643
  145.6 9.8 %collective-permute-start.16 = (bf16[96,1536]{1,0:T(8,128)(2,1)S(1)}, bf16[96,1536]{1,0:T(8,128)(2,1)S(1)}, u32[]{:S(2)}, u32[]{:S(2)}) collective-permute-start(bf16[96,1536]{1,0:T(8,128)(2,1)S(1)} %get-tuple-element.350), channel_id=1, source_target_pairs={{0,8},{4,12},{8,0},{12,4},{1,9},{5,13},{9,1},{13,5},{2,10},{6,14},... | collective-permute-start | bytes 884744 | tf_op jit(solution)/shard_map/ppermute | solution.py:643
  146.1 22.2 %collective-permute-start.19 = (bf16[2,96,1536]{2,1,0:T(8,128)(2,1)S(1)}, bf16[2,96,1536]{2,1,0:T(8,128)(2,1)S(1)}, u32[]{:S(2)}, u32[]{:S(2)}) collective-permute-start(bf16[2,96,1536]{2,1,0:T(8,128)(2,1)S(1)} %get-tuple-element.353), channel_id=1, source_target_pairs={{0,8},{4,12},{8,0},{12,4},{1,9},{5,13},{9,1},{13,5},{2,10},{6,14},... | collective-permute-start | bytes 1769480 | tf_op jit(solution)/shard_map/ppermute | solution.py:643
  148.2 20.1 %collective-permute-start.15 = (bf16[384,768]{1,0:T(8,128)(2,1)S(1)}, bf16[384,768]{1,0:T(8,128)(2,1)S(1)}, u32[]{:S(2)}, u32[]{:S(2)}) collective-permute-start(bf16[384,768]{1,0:T(8,128)(2,1)S(1)} %join_sums.20.refs_0_), channel_id=1, source_target_pairs={{0,1},{3,2},{4,5},{7,6},{8,9},{11,10},{12,13},{15,14},{16,17},{19,... | collective-permute-start | bytes 1769480 | tf_op jit(solution)/shard_map/ppermute | solution.py:808
  155.4 12.8 %collective-permute-start.17 = (bf16[96,1536]{1,0:T(8,128)(2,1)S(1)}, bf16[96,1536]{1,0:T(8,128)(2,1)S(1)}, u32[]{:S(2)}, u32[]{:S(2)}) collective-permute-start(bf16[96,1536]{1,0:T(8,128)(2,1)S(1)} %get-tuple-element.351), channel_id=1, source_target_pairs={{0,4},{4,0},{8,12},{12,8},{1,5},{5,1},{9,13},{13,9},{2,6},{6,2},{1... | collective-permute-start | bytes 884744 | tf_op jit(solution)/shard_map/ppermute | solution.py:643
  168.3 21.0 %collective-permute-start.23 = (bf16[4,192,1536]{2,1,0:T(8,128)(2,1)S(1)}, bf16[4,192,1536]{2,1,0:T(8,128)(2,1)S(1)}, u32[]{:S(2)}, u32[]{:S(2)}) collective-permute-start(bf16[4,192,1536]{2,1,0:T(8,128)(2,1)S(1)} %get-tuple-element.376), channel_id=1, source_target_pairs={{0,16},{16,0},{1,17},{17,1},{2,18},{18,2},{3,19},{19,3},{4,20},{20... | collective-permute-start | bytes 7077896 | tf_op jit(solution)/shard_map/ppermute | solution.py:643
  169.4 17.7 %collective-permute-start.21 = (bf16[384,768]{1,0:T(8,128)(2,1)S(1)}, bf16[384,768]{1,0:T(8,128)(2,1)S(1)}, u32[]{:S(2)}, u32[]{:S(2)}) collective-permute-start(bf16[384,768]{1,0:T(8,128)(2,1)S(1)} %get-tuple-element.374.refs_0_), channel_id=1, source_target_pairs={{1,2},{2,1},{5,6},{6,5},{9,10},{10,9},{13,14},{14,13},{17,18},{18,... | collective-permute-start | bytes 1769480 | tf_op jit(solution)/shard_map/ppermute | solution.py:808
  170.1 19.2 %collective-permute-start.22 = (bf16[192,1536]{1,0:T(8,128)(2,1)S(1)}, bf16[192,1536]{1,0:T(8,128)(2,1)S(1)}, u32[]{:S(2)}, u32[]{:S(2)}) collective-permute-start(bf16[192,1536]{1,0:T(8,128)(2,1)S(1)} %get-tuple-element.375.refs_2_), channel_id=1, source_target_pairs={{0,1},{3,2},{4,5},{7,6},{8,9},{11,10},{12,13},{15,14},{16,17},{19,... | collective-permute-start | bytes 1769480 | tf_op jit(solution)/shard_map/ppermute | solution.py:808
  176.4 32.7 %collective-permute-start.28 = (bf16[2,192,768]{2,1,0:T(8,128)(2,1)S(1)}, bf16[2,192,768]{2,1,0:T(8,128)(2,1)S(1)}, u32[]{:S(2)}, u32[]{:S(2)}) collective-permute-start(bf16[2,192,768]{2,1,0:T(8,128)(2,1)S(1)} %get-tuple-element.397), channel_id=1, source_target_pairs={{0,4},{4,0},{8,12},{12,8},{1,5},{5,1},{9,13},{13,9},{2,6},{6,2},{1... | collective-permute-start | bytes 1769480 | tf_op jit(solution)/shard_map/ppermute | solution.py:643
  178.0 20.0 %collective-permute-start.27 = (bf16[96,1536]{1,0:T(8,128)(2,1)S(1)}, bf16[96,1536]{1,0:T(8,128)(2,1)S(1)}, u32[]{:S(2)}, u32[]{:S(2)}) collective-permute-start(bf16[96,1536]{1,0:T(8,128)(2,1)S(1)} %get-tuple-element.396), channel_id=1, source_target_pairs={{0,4},{4,0},{8,12},{12,8},{1,5},{5,1},{9,13},{13,9},{2,6},{6,2},{1... | collective-permute-start | bytes 884744 | tf_op jit(solution)/shard_map/ppermute | solution.py:643
  187.1 22.0 %collective-permute-start.29 = (bf16[2,192,768]{2,1,0:T(8,128)(2,1)S(1)}, bf16[2,192,768]{2,1,0:T(8,128)(2,1)S(1)}, u32[]{:S(2)}, u32[]{:S(2)}) collective-permute-start(bf16[2,192,768]{2,1,0:T(8,128)(2,1)S(1)} %get-tuple-element.398), channel_id=1, source_target_pairs={{0,8},{4,12},{8,0},{12,4},{1,9},{5,13},{9,1},{13,5},{2,10},{6,14},... | collective-permute-start | bytes 1769480 | tf_op jit(solution)/shard_map/ppermute | solution.py:643
  190.2 18.9 %collective-permute-start.24 = (bf16[384,768]{1,0:T(8,128)(2,1)S(1)}, bf16[384,768]{1,0:T(8,128)(2,1)S(1)}, u32[]{:S(2)}, u32[]{:S(2)}) collective-permute-start(bf16[384,768]{1,0:T(8,128)(2,1)S(1)} %get-tuple-element.393.refs_0_), channel_id=1, source_target_pairs={{1,0},{2,3},{5,4},{6,7},{9,8},{10,11},{13,12},{14,15},{17,16},{18,... | collective-permute-start | bytes 1769480 | tf_op jit(solution)/shard_map/ppermute | solution.py:808
  191.5 17.6 %collective-permute-start.25 = (bf16[192,1536]{1,0:T(8,128)(2,1)S(1)}, bf16[192,1536]{1,0:T(8,128)(2,1)S(1)}, u32[]{:S(2)}, u32[]{:S(2)}) collective-permute-start(bf16[192,1536]{1,0:T(8,128)(2,1)S(1)} %get-tuple-element.394.refs_2_), channel_id=1, source_target_pairs={{1,2},{2,1},{5,6},{6,5},{9,10},{10,9},{13,14},{14,13},{17,18},{18,... | collective-permute-start | bytes 1769480 | tf_op jit(solution)/shard_map/ppermute | solution.py:808
  198.0 11.2 %collective-permute-start.26 = (bf16[112,1536]{1,0:T(8,128)(2,1)S(1)}, bf16[112,1536]{1,0:T(8,128)(2,1)S(1)}, u32[]{:S(2)}, u32[]{:S(2)}) collective-permute-start(bf16[112,1536]{1,0:T(8,128)(2,1)S(1)} %get-tuple-element.395), channel_id=1, source_target_pairs={{0,8},{4,12},{8,0},{12,4},{1,9},{5,13},{9,1},{13,5},{2,10},{6,14},... | collective-permute-start | bytes 1032200 | tf_op jit(solution)/shard_map/ppermute | solution.py:643
  209.2 23.5 %collective-permute-start.34 = (bf16[4,208,1536]{2,1,0:T(8,128)(2,1)S(1)}, bf16[4,208,1536]{2,1,0:T(8,128)(2,1)S(1)}, u32[]{:S(2)}, u32[]{:S(2)}) collective-permute-start(bf16[4,208,1536]{2,1,0:T(8,128)(2,1)S(1)} %get-tuple-element.417), channel_id=1, source_target_pairs={{0,16},{16,0},{1,17},{17,1},{2,18},{18,2},{3,19},{19,3},{4,20},{20... | collective-permute-start | bytes 7667720 | tf_op jit(solution)/shard_map/ppermute | solution.py:643
  210.1 22.6 %collective-permute-start.31 = (bf16[208,1536]{1,0:T(8,128)(2,1)S(1)}, bf16[208,1536]{1,0:T(8,128)(2,1)S(1)}, u32[]{:S(2)}, u32[]{:S(2)}) collective-permute-start(bf16[208,1536]{1,0:T(8,128)(2,1)S(1)} %get-tuple-element.414.refs_2_), channel_id=1, source_target_pairs={{0,1},{3,2},{4,5},{7,6},{8,9},{11,10},{12,13},{15,14},{16,17},{19,... | collective-permute-start | bytes 1916936 | tf_op jit(solution)/shard_map/ppermute | solution.py:808
  213.8 15.5 %collective-permute-start.32 = (bf16[2,96,1536]{2,1,0:T(8,128)(2,1)S(1)}, bf16[2,96,1536]{2,1,0:T(8,128)(2,1)S(1)}, u32[]{:S(2)}, u32[]{:S(2)}) collective-permute-start(bf16[2,96,1536]{2,1,0:T(8,128)(2,1)S(1)} %get-tuple-element.415), channel_id=1, source_target_pairs={{0,4},{4,0},{8,12},{12,8},{1,5},{5,1},{9,13},{13,9},{2,6},{6,2},{1... | collective-permute-start | bytes 1769480 | tf_op jit(solution)/shard_map/ppermute | solution.py:643
  215.4 15.2 %collective-permute-start.33 = (bf16[2,96,1536]{2,1,0:T(8,128)(2,1)S(1)}, bf16[2,96,1536]{2,1,0:T(8,128)(2,1)S(1)}, u32[]{:S(2)}, u32[]{:S(2)}) collective-permute-start(bf16[2,96,1536]{2,1,0:T(8,128)(2,1)S(1)} %get-tuple-element.416), channel_id=1, source_target_pairs={{0,8},{4,12},{8,0},{12,4},{1,9},{5,13},{9,1},{13,5},{2,10},{6,14},... | collective-permute-start | bytes 1769480 | tf_op jit(solution)/shard_map/ppermute | solution.py:643
  215.9 16.8 %collective-permute-start.30 = (bf16[192,1536]{1,0:T(8,128)(2,1)S(1)}, bf16[192,1536]{1,0:T(8,128)(2,1)S(1)}, u32[]{:S(2)}, u32[]{:S(2)}) collective-permute-start(bf16[192,1536]{1,0:T(8,128)(2,1)S(1)} %get-tuple-element.413.refs_0_), channel_id=1, source_target_pairs={{1,0},{2,3},{5,4},{6,7},{9,8},{10,11},{13,12},{14,15},{17,16},{18,... | collective-permute-start | bytes 1769480 | tf_op jit(solution)/shard_map/ppermute | solution.py:808
  233.7 24.9 %copy-start.16 = (f32[512,768]{1,0:T(8,128)S(1)}, f32[512,768]{1,0:T(8,128)}, u32[]{:S(2)}) copy-start(f32[512,768]{1,0:T(8,128)} %get-tuple-element.418) | copy-start | bytes 4718596
  233.8 24.9 %copy-start.19 = (bf16[512,768]{1,0:T(8,128)(2,1)S(1)}, bf16[512,768]{1,0:T(8,128)(2,1)}, u32[]{:S(2)}) copy-start(bf16[512,768]{1,0:T(8,128)(2,1)} %get-tuple-element.419) | copy-start | bytes 2359300
  233.8 12.4 %collective-permute-start.36 = (bf16[208,1536]{1,0:T(8,128)(2,1)S(1)}, bf16[208,1536]{1,0:T(8,128)(2,1)S(1)}, u32[]{:S(2)}, u32[]{:S(2)}) collective-permute-start(bf16[208,1536]{1,0:T(8,128)(2,1)S(1)} %get-tuple-element.428.refs_0_), channel_id=1, source_target_pairs={{1,2},{2,1},{5,6},{6,5},{9,10},{10,9},{13,14},{14,13},{17,18},{18,... | collective-permute-start | bytes 1916936 | tf_op jit(solution)/shard_map/ppermute | solution.py:808
  234.6 7.7 %collective-permute-start.37 = (bf16[192,768]{1,0:T(8,128)(2,1)S(1)}, bf16[192,768]{1,0:T(8,128)(2,1)S(1)}, u32[]{:S(2)}, u32[]{:S(2)}) collective-permute-start(bf16[192,768]{1,0:T(8,128)(2,1)S(1)} %get-tuple-element.429), channel_id=1, source_target_pairs={{0,8},{4,12},{8,0},{12,4},{1,9},{5,13},{9,1},{13,5},{2,10},{6,14},... | collective-permute-start | bytes 884744 | tf_op jit(solution)/shard_map/ppermute | solution.py:643
  236.2 9.9 %collective-permute-start.38 = (bf16[192,768]{1,0:T(8,128)(2,1)S(1)}, bf16[192,768]{1,0:T(8,128)(2,1)S(1)}, u32[]{:S(2)}, u32[]{:S(2)}) collective-permute-start(bf16[192,768]{1,0:T(8,128)(2,1)S(1)} %get-tuple-element.430), channel_id=1, source_target_pairs={{0,4},{4,0},{8,12},{12,8},{1,5},{5,1},{9,13},{13,9},{2,6},{6,2},{1... | collective-permute-start | bytes 884744 | tf_op jit(solution)/shard_map/ppermute | solution.py:643
  236.7 28.1 %collective-permute-start.43 = (bf16[2,112,1536]{2,1,0:T(8,128)(2,1)S(1)}, bf16[2,112,1536]{2,1,0:T(8,128)(2,1)S(1)}, u32[]{:S(2)}, u32[]{:S(2)}) collective-permute-start(bf16[2,112,1536]{2,1,0:T(8,128)(2,1)S(1)} %get-tuple-element.440), channel_id=1, source_target_pairs={{0,4},{4,0},{8,12},{12,8},{1,5},{5,1},{9,13},{13,9},{2,6},{6,2},{1... | collective-permute-start | bytes 2064392 | tf_op jit(solution)/shard_map/ppermute | solution.py:643
  246.8 19.6 %collective-permute-start.39 = (bf16[208,1536]{1,0:T(8,128)(2,1)S(1)}, bf16[208,1536]{1,0:T(8,128)(2,1)S(1)}, u32[]{:S(2)}, u32[]{:S(2)}) collective-permute-start(bf16[208,1536]{1,0:T(8,128)(2,1)S(1)} %get-tuple-element.436.refs_0_), channel_id=1, source_target_pairs={{1,0},{2,3},{5,4},{6,7},{9,8},{10,11},{13,12},{14,15},{17,16},{18,... | collective-permute-start | bytes 1916936 | tf_op jit(solution)/shard_map/ppermute | solution.py:808
  248.1 10.0 %collective-permute-start.41 = (bf16[96,1536]{1,0:T(8,128)(2,1)S(1)}, bf16[96,1536]{1,0:T(8,128)(2,1)S(1)}, u32[]{:S(2)}, u32[]{:S(2)}) collective-permute-start(bf16[96,1536]{1,0:T(8,128)(2,1)S(1)} %get-tuple-element.438), channel_id=1, source_target_pairs={{0,8},{4,12},{8,0},{12,4},{1,9},{5,13},{9,1},{13,5},{2,10},{6,14},... | collective-permute-start | bytes 884744 | tf_op jit(solution)/shard_map/ppermute | solution.py:643
  248.7 16.1 %collective-permute-start.44 = (bf16[2,96,1536]{2,1,0:T(8,128)(2,1)S(1)}, bf16[2,96,1536]{2,1,0:T(8,128)(2,1)S(1)}, u32[]{:S(2)}, u32[]{:S(2)}) collective-permute-start(bf16[2,96,1536]{2,1,0:T(8,128)(2,1)S(1)} %get-tuple-element.441), channel_id=1, source_target_pairs={{0,8},{4,12},{8,0},{12,4},{1,9},{5,13},{9,1},{13,5},{2,10},{6,14},... | collective-permute-start | bytes 1769480 | tf_op jit(solution)/shard_map/ppermute | solution.py:643
  250.2 16.2 %collective-permute-start.40 = (bf16[384,768]{1,0:T(8,128)(2,1)S(1)}, bf16[384,768]{1,0:T(8,128)(2,1)S(1)}, u32[]{:S(2)}, u32[]{:S(2)}) collective-permute-start(bf16[384,768]{1,0:T(8,128)(2,1)S(1)} %get-tuple-element.437.refs_2_), channel_id=1, source_target_pairs={{0,1},{3,2},{4,5},{7,6},{8,9},{11,10},{12,13},{15,14},{16,17},{19,... | collective-permute-start | bytes 1769480 | tf_op jit(solution)/shard_map/ppermute | solution.py:808
  258.1 6.7 %collective-permute-start.42 = (bf16[96,1536]{1,0:T(8,128)(2,1)S(1)}, bf16[96,1536]{1,0:T(8,128)(2,1)S(1)}, u32[]{:S(2)}, u32[]{:S(2)}) collective-permute-start(bf16[96,1536]{1,0:T(8,128)(2,1)S(1)} %get-tuple-element.439), channel_id=1, source_target_pairs={{0,4},{4,0},{8,12},{12,8},{1,5},{5,1},{9,13},{13,9},{2,6},{6,2},{1... | collective-permute-start | bytes 884744 | tf_op jit(solution)/shard_map/ppermute | solution.py:643
  264.8 55.7 %collective-permute-start.35 = (f32[512,768]{1,0:T(8,128)}, f32[512,768]{1,0:T(8,128)}, u32[]{:S(2)}, u32[]{:S(2)}) collective-permute-start(f32[512,768]{1,0:T(8,128)} %convert_select_fusion), channel_id=1, source_target_pairs={{0,16},{16,0},{1,17},{17,1},{2,18},{18,2},{3,19},{19,3},{4,20},{20... | collective-permute-start | bytes 4718600 | tf_op jit(solution)/shard_map/ppermute | solution.py:643
  267.9 18.3 %copy-start.8 = (bf16[96,1536]{1,0:T(8,128)(2,1)}, bf16[96,1536]{1,0:T(8,128)(2,1)S(1)}, u32[]{:S(2)}) copy-start(bf16[96,1536]{1,0:T(8,128)(2,1)S(1)} %get-tuple-element.466.refs_6_) | copy-start | bytes 884740
  268.0 18.9 %copy-start.10 = (bf16[96,1536]{1,0:T(8,128)(2,1)}, bf16[96,1536]{1,0:T(8,128)(2,1)S(1)}, u32[]{:S(2)}) copy-start(bf16[96,1536]{1,0:T(8,128)(2,1)S(1)} %get-tuple-element.460) | copy-start | bytes 884740
  268.0 17.6 %collective-permute-start.45 = (bf16[384,768]{1,0:T(8,128)(2,1)S(1)}, bf16[384,768]{1,0:T(8,128)(2,1)S(1)}, u32[]{:S(2)}, u32[]{:S(2)}) collective-permute-start(bf16[384,768]{1,0:T(8,128)(2,1)S(1)} %get-tuple-element.452.refs_0_), channel_id=1, source_target_pairs={{1,2},{2,1},{5,6},{6,5},{9,10},{10,9},{13,14},{14,13},{17,18},{18,... | collective-permute-start | bytes 1769480 | tf_op jit(solution)/shard_map/ppermute | solution.py:808
  269.6 20.7 %collective-permute-start.5 = (bf16[512,768]{1,0:T(8,128)(2,1)}, bf16[512,768]{1,0:T(8,128)(2,1)}, u32[]{:S(2)}, u32[]{:S(2)}) collective-permute-start(bf16[512,768]{1,0:T(8,128)(2,1)} %broadcast_select_fusion.2), channel_id=1, source_target_pairs={{0,16},{16,0},{1,17},{17,1},{2,18},{18,2},{3,19},{19,3},{4,20},{20... | collective-permute-start | bytes 2359304 | tf_op jit(solution)/shard_map/ppermute | solution.py:643
  269.6 15.9 %collective-permute-start.46 = (bf16[192,768]{1,0:T(8,128)(2,1)S(1)}, bf16[192,768]{1,0:T(8,128)(2,1)S(1)}, u32[]{:S(2)}, u32[]{:S(2)}) collective-permute-start(bf16[192,768]{1,0:T(8,128)(2,1)S(1)} %get-tuple-element.453), channel_id=1, source_target_pairs={{0,1},{1,0},{2,3},{3,2},{4,5},{5,4},{6,7},{7,6},{8,9},{9,8},{10,11... | collective-permute-start | bytes 884744 | tf_op jit(solution)/shard_map/ppermute | solution.py:643
  286.9 20.2 %collective-permute-start.47 = (bf16[384,768]{1,0:T(8,128)(2,1)S(1)}, bf16[384,768]{1,0:T(8,128)(2,1)S(1)}, u32[]{:S(2)}, u32[]{:S(2)}) collective-permute-start(bf16[384,768]{1,0:T(8,128)(2,1)S(1)} %get-tuple-element.457.refs_0_), channel_id=1, source_target_pairs={{1,0},{2,3},{5,4},{6,7},{9,8},{10,11},{13,12},{14,15},{17,16},{18,... | collective-permute-start | bytes 1769480 | tf_op jit(solution)/shard_map/ppermute | solution.py:808
  288.2 10.4 %collective-permute-start.49 = (bf16[112,1536]{1,0:T(8,128)(2,1)}, bf16[112,1536]{1,0:T(8,128)(2,1)}, u32[]{:S(2)}, u32[]{:S(2)}) collective-permute-start(bf16[112,1536]{1,0:T(8,128)(2,1)} %get-tuple-element.459), channel_id=1, source_target_pairs={{0,8},{4,12},{8,0},{12,4},{1,9},{5,13},{9,1},{13,5},{2,10},{6,14},... | collective-permute-start | bytes 1032200 | tf_op jit(solution)/shard_map/ppermute | solution.py:643
  289.8 8.8 %collective-permute-start.50 = (bf16[96,1536]{1,0:T(8,128)(2,1)}, bf16[96,1536]{1,0:T(8,128)(2,1)S(1)}, u32[]{:S(2)}, u32[]{:S(2)}) collective-permute-start(bf16[96,1536]{1,0:T(8,128)(2,1)} %copy-done.10), channel_id=1, source_target_pairs={{0,4},{4,0},{8,12},{12,8},{1,5},{5,1},{9,13},{13,9},{2,6},{6,2},{1... | collective-permute-start | bytes 884744 | tf_op jit(solution)/shard_map/ppermute | solution.py:643
  290.3 9.7 %collective-permute-start.48 = (bf16[192,384]{1,0:T(8,128)(2,1)}, bf16[192,384]{1,0:T(8,128)(2,1)S(1)}, u32[]{:S(2)}, u32[]{:S(2)}) collective-permute-start(bf16[192,384]{1,0:T(8,128)(2,1)} %copy-done.11), channel_id=1, source_target_pairs={{0,2},{1,3},{2,0},{3,1},{4,6},{5,7},{6,4},{7,5},{8,10},{9,11},{10,... | collective-permute-start | bytes 442376 | tf_op jit(solution)/shard_map/ppermute | solution.py:643
  308.2 11.6 %collective-permute-start.52 = (bf16[208,768]{1,0:T(8,128)(2,1)S(1)}, bf16[208,768]{1,0:T(8,128)(2,1)S(1)}, u32[]{:S(2)}, u32[]{:S(2)}) collective-permute-start(bf16[208,768]{1,0:T(8,128)(2,1)S(1)} %get-tuple-element.469), channel_id=1, source_target_pairs={{0,1},{1,0},{2,3},{3,2},{4,5},{5,4},{6,7},{7,6},{8,9},{9,8},{10,11... | collective-permute-start | bytes 958472 | tf_op jit(solution)/shard_map/ppermute | solution.py:643
  309.6 8.0 %collective-permute-start.51 = (bf16[192,384]{1,0:T(8,128)(2,1)S(1)}, bf16[192,384]{1,0:T(8,128)(2,1)S(1)}, u32[]{:S(2)}, u32[]{:S(2)}) collective-permute-start(bf16[192,384]{1,0:T(8,128)(2,1)S(1)} %get-tuple-element.468.refs_0_), channel_id=1, source_target_pairs={{0,2},{1,3},{2,0},{3,1},{4,6},{5,7},{6,4},{7,5},{8,10},{9,11},{10,... | collective-permute-start | bytes 442376 | tf_op jit(solution)/shard_map/ppermute | solution.py:643
  311.6 21.2 %collective-permute-start.59 = (bf16[384,768]{1,0:T(8,128)(2,1)S(1)}, bf16[384,768]{1,0:T(8,128)(2,1)S(1)}, u32[]{:S(2)}, u32[]{:S(2)}) collective-permute-start(bf16[384,768]{1,0:T(8,128)(2,1)S(1)} %broadcast_select_fusion.10), channel_id=1, source_target_pairs={{0,16},{16,0},{1,17},{17,1},{2,18},{18,2},{3,19},{19,3},{4,20},{20... | collective-permute-start | bytes 1769480 | tf_op jit(solution)/shard_map/ppermute | solution.py:643
  320.4 10.4 %collective-permute-start.53 = (bf16[192,768]{1,0:T(8,128)(2,1)S(1)}, bf16[192,768]{1,0:T(8,128)(2,1)S(1)}, u32[]{:S(2)}, u32[]{:S(2)}) collective-permute-start(bf16[192,768]{1,0:T(8,128)(2,1)S(1)} %get-tuple-element.473.refs_0_), channel_id=1, source_target_pairs={{0,1},{1,0},{2,3},{3,2},{4,5},{5,4},{6,7},{7,6},{8,9},{9,8},{10,11... | collective-permute-start | bytes 884744 | tf_op jit(solution)/shard_map/ppermute | solution.py:643
  322.2 7.1 %collective-permute-start.54 = (bf16[208,384]{1,0:T(8,128)(2,1)S(1)}, bf16[208,384]{1,0:T(8,128)(2,1)S(1)}, u32[]{:S(2)}, u32[]{:S(2)}) collective-permute-start(bf16[208,384]{1,0:T(8,128)(2,1)S(1)} %get-tuple-element.474), channel_id=1, source_target_pairs={{0,2},{1,3},{2,0},{3,1},{4,6},{5,7},{6,4},{7,5},{8,10},{9,11},{10,... | collective-permute-start | bytes 479240 | tf_op jit(solution)/shard_map/ppermute | solution.py:643
  331.4 8.1 %collective-permute-start.55 = (bf16[208,384]{1,0:T(8,128)(2,1)S(1)}, bf16[208,384]{1,0:T(8,128)(2,1)S(1)}, u32[]{:S(2)}, u32[]{:S(2)}) collective-permute-start(bf16[208,384]{1,0:T(8,128)(2,1)S(1)} %get-tuple-element.478.refs_0_), channel_id=1, source_target_pairs={{0,2},{1,3},{2,0},{3,1},{4,6},{5,7},{6,4},{7,5},{8,10},{9,11},{10,... | collective-permute-start | bytes 479240 | tf_op jit(solution)/shard_map/ppermute | solution.py:643
  340.1 7.1 %collective-permute-start.56 = (bf16[208,768]{1,0:T(8,128)(2,1)S(1)}, bf16[208,768]{1,0:T(8,128)(2,1)S(1)}, u32[]{:S(2)}, u32[]{:S(2)}) collective-permute-start(bf16[208,768]{1,0:T(8,128)(2,1)S(1)} %join_sums.32.refs_0_), channel_id=1, source_target_pairs={{0,1},{1,0},{2,3},{3,2},{4,5},{5,4},{6,7},{7,6},{8,9},{9,8},{10,11... | collective-permute-start | bytes 958472 | tf_op jit(solution)/shard_map/ppermute | solution.py:643
  341.0 6.9 %collective-permute-start.58 = (bf16[192,1536]{1,0:T(8,128)(2,1)}, bf16[192,1536]{1,0:T(8,128)(2,1)}, u32[]{:S(2)}, u32[]{:S(2)}) collective-permute-start(bf16[192,1536]{1,0:T(8,128)(2,1)} %broadcast_select_fusion.12), channel_id=1, source_target_pairs={{0,16},{16,0},{1,17},{17,1},{2,18},{18,2},{3,19},{19,3},{4,20},{20... | collective-permute-start | bytes 1769480 | tf_op jit(solution)/shard_map/ppermute | solution.py:643
  347.8 2.9 collective-permute-start.57
  (20 other events, 116.8 us)

commit v4 on v3

--- a/solution.py
+++ b/solution.py
@@ -330,7 +330,8 @@
 def down_grad_kernel(sec, gy, hat, scale, small, act, second, branch, sums, send, keep, turned, sems):
     move = Mover(sems)
     blocks = act.buffer.shape[0]
-    tall = send.buffer.shape[1]
+    low_rows, wide = send.buffer.shape[1], act.buffer.shape[2]
+    tall = 2 * low_rows
     waits = gy.fetch(move) + small.fetch(move) + scale.fetch(move) + hat.fetch(move)
     parts = [act.fetch(move, i) for i in range(blocks)]
     ready(waits)
@@ -352,8 +353,9 @@
         for i in range(blocks):
             if out is send:
                 ready(parts[i])
-            out.buffer[i] = dot(turned[left, :], act.buffer[i]).astype(BF16)
-            out.flush(move, i)
+            block = dot(turned[left, :], act.buffer[i]).astype(BF16)
+            out.buffer[i, :, :wide] = block[:low_rows]
+            out.buffer[i, :, wide:] = block[low_rows:]
     move.finish()
 
 
@@ -361,7 +363,7 @@
     rows, width = gy.shape
     blocks = act.shape[0]
     wide = (rows, width)
-    part = sds((blocks, width // 2, width), BF16)
+    part = sds((blocks, width // 4, 2 * width), BF16)
     return call(
         down_grad_kernel,
         sec,
@@ -595,6 +597,183 @@
     )
 
 
+def up_whole_kernel(
+    layer, sec, branch, second, wd_a, wd_b, slope, low, wu_a, wu_b, hat, scale, small,
+    first, attend, sums, send, keep, wd, wu, pre, sems,
+):
+    move = Mover(sems)
+    mine = sec[0] == layer
+    blocks, wide, _ = wd.shape
+    half = blocks // 2
+    at = [lax.rem(i + half * (1 - sec[0]), blocks) for i in range(blocks)]
+    span = [pl.ds(pl.multiple_of(place * wide, wide), wide) for place in at]
+    parts = []
+    early = branch.fetch(move)
+    for i in range(blocks):
+        parts.append(
+            [move.choose(mine, wd_a.ref.at[span[i]], wd_b.ref.at[span[i]], wd.at[i])]
+            + slope.fetch(move, at[i])
+            + [move.choose(mine, wu_a.ref.at[:, span[i]], wu_b.ref.at[:, span[i]], wu.at[i])]
+        )
+        if i == 0:
+            early += low.fetch(move)
+    late = second.fetch(move) + hat.fetch(move) + scale.fetch(move) + small.fetch(move)
+    ready(early)
+    branch, low, total = branch.buffer, low.buffer, first.buffer
+    for i in range(blocks):
+        ready(parts[i])
+        pre[...] = (dot_t(branch[...], wd[i]) * slope.buffer[at[i]]).astype(BF16)
+        sums.buffer[pl.ds(3 + at[i], 1)] = column_sum(pre[...].astype(F32))
+        out, place = (send, i) if i < half else (keep, i - half)
+        block = dot(low[...], pre[...]).astype(BF16)
+        shards, tall, _ = out.buffer.shape
+        for shard in range(shards):
+            out.buffer[shard, :, place * wide : place * wide + wide] = block[shard * tall : shard * tall + tall]
+        if i == 0:
+            ready(late)
+            total[...] = second.buffer[...] + dot_t(pre[...], wu[i])
+        else:
+            total[...] += dot_t(pre[...], wu[i])
+    grad = total[...]
+    sums.buffer[0:1] = column_sum(grad * hat.buffer[...])
+    sums.buffer[1:2] = column_sum(grad)
+    unit = norm_back(grad, hat.buffer[...], scale.buffer[:, 0:1], small.buffer[GAIN_ONE : GAIN_ONE + 1])
+    attend.buffer[...] = unit.astype(BF16)
+    attend.flush(move)
+    total[...] = unit
+    first.flush(move)
+    sums.buffer[2:3] = column_sum(attend.buffer[...].astype(F32))
+    sums.buffer[3 + blocks :] = jnp.zeros_like(sums.buffer[3 + blocks :])
+    sums.flush(move)
+    move.finish()
+
+
+def up_whole(layer, sec, branch, second, wd, wd_other, slope, low, wu, wu_other, hat, scale, small, shards):
+    blocks, rows, width = slope.shape
+    wide = (rows, width)
+    part = sds((shards, width // shards, blocks * width // 2), BF16)
+    square = ((blocks, width, width), BF16)
+    return call(
+        functools.partial(up_whole_kernel, layer),
+        sec,
+        [
+            (branch, NEAR),
+            (second, NEAR),
+            (wd, RAW),
+            (wd_other, RAW),
+            (slope, FAR),
+            (low, FAR),
+            (wu, RAW),
+            (wu_other, RAW),
+            (hat, FAR),
+            (scale, FAR),
+            (small, FAR),
+        ],
+        [(sds(wide, F32), NEAR), (sds(wide, BF16), NEAR), (sds((8, width), F32), NEAR), (part, NEAR), (part, NEAR)],
+        [square, square, (wide, BF16)],
+        "up_grad",
+        6 * rows * width * width * blocks,
+        30 << 20,
+    )
+
+
+def attend_whole_kernel(
+    layer, shards, sec, attend, ctx, first, x, q, k, v, probs, wo_a, wo_b, w_a, w_b, down, up,
+    gx, gx_low, send, keep, turned, wo, w, gc, grads, sems,
+):
+    move = Mover(sems)
+    mine = sec[0] == layer
+    rows_all, width = x.buffer.shape
+    seqs = probs.buffer.shape[0]
+    wide = width // 2
+    tall = width // shards
+    pairs = wide // 128
+    waits = attend.fetch(move) + [move.choose(mine, wo_a.ref, wo_b.ref, wo)]
+    near = probs.fetch(move) + v.fetch(move) + k.fetch(move) + q.fetch(move)
+    later = x.fetch(move) + ctx.fetch(move) + down.fetch(move) + up.fetch(move)
+    last = [
+        move.choose(mine, w_a.ref.at[:, pl.ds(i * width, width)], w_b.ref.at[:, pl.ds(i * width, width)], w.at[i])
+        for i in range(3)
+    ] + first.fetch(move)
+    ready(waits)
+    attend, q, k, v, probs = (item.buffer for item in (attend, q, k, v, probs))
+    gc[...] = dot_t(attend[...], wo[...]).astype(BF16)
+    ready(near)
+    halves = lane_halves()
+    lower = lax.broadcasted_iota(jnp.int32, (128, 128), 1) < 64
+
+    def attention(first_pair):
+        @pl.loop(0, pairs)
+        def _(index):
+            pair = first_pair + index
+            lanes = pl.ds(pl.multiple_of(pair * 128, 128), 128)
+            for seq in range(seqs):
+                rows = slice(seq * 128, seq * 128 + 128)
+                grad = gc[rows, lanes]
+                p = probs[seq, pair]
+                full = dot(p.astype(BF16), grad)
+                grads[2, rows, lanes] = jnp.where(lower, full[:128], full[128:]).astype(BF16)
+                gp = dot_t(two_heads(v[rows, lanes], halves), grad)
+                parts = []
+                for side in (slice(0, 128), slice(128, 256)):
+                    g, pp = gp[side], p[side]
+                    parts.append(pp * (g - jnp.sum(g * pp, axis=0, keepdims=True)))
+                gs = jnp.concatenate(parts, axis=0).astype(BF16)
+                grads[0, rows, lanes] = t_dot(gs, two_heads(k[rows, lanes] * SCALE, halves)).astype(BF16)
+                full = dot(gs, q[rows, lanes] * SCALE)
+                grads[1, rows, lanes] = jnp.where(lower, full[:128], full[128:]).astype(BF16)
+
+    def products(half, out):
+        lanes = pl.ds(pl.multiple_of(half * wide, wide), wide)
+        for part in range(4):
+            if part < 3:
+                block = dot(turned[...], grads[part, :, lanes]).astype(BF16)
+            else:
+                block = dot(ctx.buffer[...], attend[:, lanes]).astype(BF16)
+            for shard in range(shards):
+                out.buffer[shard, :tall, part * wide : part * wide + wide] = block[shard * tall : shard * tall + tall]
+
+    attention((1 - sec[0]) * pairs)
+    ready(later)
+    turned[...] = x.buffer[...].T
+    products(1 - sec[0], send)
+    attention(sec[0] * pairs)
+    products(sec[0], keep)
+    little = jnp.concatenate([down.buffer[...], up.buffer[...]], axis=0).astype(BF16)
+    for half, out in ((1 - sec[0], send), (sec[0], keep)):
+        lanes = pl.ds(pl.multiple_of(half * wide, wide), wide)
+        pad = [column_sum(grads[part, :, lanes].astype(F32)).astype(BF16) for part in (0, 2)]
+        pad = jnp.concatenate([jnp.concatenate(pad, axis=1), jnp.zeros((15, width), BF16)], axis=0)
+        for shard in range(shards):
+            out.buffer[shard, tall:, 0:width] = little
+            out.buffer[shard, tall:, width:] = pad
+    ready(last)
+    total = first.buffer[...] + dot_t(grads[0], w[0]) + dot_t(grads[1], w[1]) + dot_t(grads[2], w[2])
+    gx.buffer[...] = total
+    gx.flush(move)
+    gx_low.buffer[...] = total.astype(BF16)
+    gx_low.flush(move)
+    move.finish()
+
+
+def attend_whole(layer, sec, attend, ctx, first, x, q, k, v, probs, wo, wo_other, w, w_other, down, up, shards, low_kind):
+    rows, width = x.shape
+    wide = (rows, width)
+    part = sds((shards, width // shards + 16, 2 * width), BF16)
+    return call(
+        functools.partial(attend_whole_kernel, layer, shards),
+        sec,
+        [(attend, NEAR), (ctx, FAR), (first, NEAR)]
+        + [(item, FAR) for item in (x, q, k, v, probs)]
+        + [(wo, RAW), (wo_other, RAW), (w, RAW), (w_other, RAW), (down, NEAR), (up, NEAR)],
+        [(sds(wide, F32), FAR), (sds(wide, BF16), low_kind), (part, NEAR), (part, NEAR)],
+        [((width, rows), BF16), ((width, width), BF16), ((3, width, width), BF16), (wide, BF16), ((3,) + wide, BF16)],
+        "attend_grad",
+        2 * rows * width * width * 10,
+        30 << 20,
+    )
+
+
 def layer_forward(layer, sec, x, front, big, other, small, far=None):
     w_qkv, w_out, w_up, w_down = big
     o_qkv, o_out, o_up, o_down = other
@@ -610,32 +789,75 @@
     return y, (x, q, k, v, probs, ctx, hat_one, scale_one, low, act, slope, hat_two, scale_two)
 
 
-def layer_backward(line, layer, sec, gy, cache, big, other, small, shards):
-    w_qkv, w_out, w_up, w_down = big
-    o_qkv, o_out, o_up, o_down = other
-    x, q, k, v, probs, ctx, hat_one, scale_one, low, act, slope, hat_two, scale_two = cache
-    kinds = (NEAR, FAR) if layer == 0 else (FAR, NEAR)
-    second, branch, down, d_send, d_keep = line.advance(
-        lambda: down_grad(sec, gy, kinds[0], hat_two, scale_two, small, act, kinds[1])
-    )
-    line.add(d_send, d_keep)
-    up_ins = (w_down, o_down, slope, low, w_up, o_up, shards)
-    part, up, u_send = line.advance(lambda: up_grad(layer, False, sec, branch, second, *up_ins))
-    more = (hat_one, scale_one, small, up)
-    line.add(u_send, None, layer == 0)
-    first, attend, up, u_keep = line.advance(lambda: up_grad(layer, True, sec, branch, part, *up_ins, more))
-    line.keep(u_keep)
-    heads = (q, k, v, probs, w_out, o_out, w_qkv, o_qkv, down, up, shards)
-    low_kind = FAR if layer == 0 else BOTH
-    part, turned, a_send = line.advance(
-        lambda: attend_grad(layer, False, sec, attend, ctx, first, x, *heads, low_kind)
-    )
-    line.add(a_send, None, layer == 0)
-    gx, gx_low, a_keep = line.advance(
-        lambda: attend_grad(layer, True, sec, attend, ctx, part, turned, *heads, low_kind)
-    )
-    line.keep(a_keep)
-    return gx, gx_low
+class Backward:
+    def __init__(self, line, layer, sec, cache, big, other, small, shards):
+        self.line, self.layer, self.sec, self.small, self.shards = line, layer, sec, small, shards
+        self.cache, self.weights, self.made = cache, tuple(zip(big, other)), {}
+
+    def down(self, gy):
+        act, _, hat_two, scale_two = self.cache[-4:]
+        kinds = (NEAR, FAR) if self.layer == 0 else (FAR, NEAR)
+        second, branch, sums, send, keep = down_grad(
+            self.line.sec, gy, kinds[0], hat_two, scale_two, self.small, act, kinds[1]
+        )
+        self.made.update(second=second, branch=branch, down_sums=sums)
+        self.line.add(send, keep)
+
+    def up_inputs(self):
+        (w_up, o_up), (w_down, o_down) = self.weights[2:]
+        low, _, slope = self.cache[-5:-2]
+        return w_down, o_down, slope, low, w_up, o_up, self.shards
+
+    def up_first(self):
+        made = self.made
+        made["part"], made["up_sums"], send = up_grad(
+            self.layer, False, self.line.sec, made["branch"], made["second"], *self.up_inputs()
+        )
+        self.up_chunk = self.line.add(send, None)
+
+    def up_last(self):
+        made = self.made
+        hat_one, scale_one = self.cache[-7:-5]
+        more = (hat_one, scale_one, self.small, made["up_sums"])
+        made["first"], made["attend"], made["up_sums"], self.up_chunk.keep = up_grad(
+            self.layer, True, self.line.sec, made["branch"], made["part"], *self.up_inputs(), more
+        )
+
+    def up(self):
+        made = self.made
+        hat_one, scale_one = self.cache[-7:-5]
+        ins = self.up_inputs()
+        made["first"], made["attend"], made["up_sums"], send, keep = up_whole(
+            self.layer, self.line.sec, made["branch"], made["second"], *ins[:-1], hat_one, scale_one, self.small, ins[-1]
+        )
+        self.line.add(send, keep)
+
+    def attention(self):
+        made = self.made
+        made["gx"], made["gx_low"], send, keep = attend_whole(
+            self.layer, self.line.sec, made["attend"], self.cache[5], made["first"], self.cache[0], *self.heads()
+        )
+        self.line.add(send, keep)
+
+    def heads(self):
+        q, k, v, probs = self.cache[1:5]
+        (w_qkv, o_qkv), (w_out, o_out) = self.weights[:2]
+        low_kind = FAR if self.layer == 0 else BOTH
+        sums = (self.made["down_sums"], self.made["up_sums"])
+        return (q, k, v, probs, w_out, o_out, w_qkv, o_qkv) + sums + (self.shards, low_kind)
+
+    def attend_first(self):
+        made = self.made
+        made["part"], made["turned"], send = attend_grad(
+            self.layer, False, self.line.sec, made["attend"], self.cache[5], made["first"], self.cache[0], *self.heads()
+        )
+        self.attend_chunk = self.line.add(send, None)
+
+    def attend_last(self):
+        made = self.made
+        made["gx"], made["gx_low"], self.attend_chunk.keep = attend_grad(
+            self.layer, True, self.line.sec, made["attend"], self.cache[5], made["part"], made["turned"], *self.heads()
+        )
 
 
 def exchange(array, axis, bit):
@@ -651,215 +873,241 @@
     return (rows // 2 + 15) // 16 * 16
 
 
-def join_section(ids, ins, outs):
-    kept, got = ins
-    top_send, top_keep, bottom_send, bottom_keep = outs
-    low_bit, high_bit = ids[1], ids[2]
-    cut = top_send.shape[1]
-    for i in range(2):
-        for out, shard in ((top_send, 2 * i + 1 - low_bit), (top_keep, 2 * i + low_bit)):
-            out[i] = kept[shard, :cut] + got[shard, :cut]
-        for out, shard in ((bottom_send, 2 * (1 - high_bit) + i), (bottom_keep, 2 * high_bit + i)):
-            out[i] = kept[shard, cut:] + got[shard, cut:]
-
-
-def join_first(ids, ins, outs):
-    top, top_got, bottom, bottom_got = ins
-    top_send, top_keep, bottom_send, bottom_keep = outs
-    low_bit, high_bit = ids[1], ids[2]
-    top_send[...] = top[1 - high_bit] + top_got[1 - high_bit]
-    top_keep[...] = top[high_bit] + top_got[high_bit]
-    bottom_send[...] = bottom[1 - low_bit] + bottom_got[1 - low_bit]
-    bottom_keep[...] = bottom[low_bit] + bottom_got[low_bit]
-
-
-def join_second(ids, ins, outs):
-    top, top_got, bottom, bottom_got = ins
-    cut = top.shape[0]
-    outs[0][:cut] = top[...] + top_got[...]
-    outs[0][cut:] = bottom[...] + bottom_got[...]
-
-
-def join_add(ids, ins, outs):
-    outs[0][...] = ins[0][...] + ins[1][...]
-
-
-def join_split(ids, ins, outs):
-    top, top_got, bottom, bottom_got = ins
-    send, keep = outs
-    cut, wide = top.shape[0], send.shape[1]
-    for out, half in ((send, 1 - ids[3]), (keep, ids[3])):
-        lanes = pl.ds(pl.multiple_of(half * wide, wide), wide)
-        out[:cut] = top[:, lanes] + top_got[:, lanes]
-        out[cut:] = bottom[:, lanes] + bottom_got[:, lanes]
-
-
-def join_half(ids, ins, outs):
-    kept, got = ins
-    send, keep = outs
-    wide = send.shape[1]
-    for out, half in ((send, 1 - ids[4]), (keep, ids[4])):
-        lanes = pl.ds(pl.multiple_of(half * wide, wide), wide)
-        out[...] = kept[:, lanes] + got[:, lanes]
-
-
-def join_last(ids, ins, outs):
-    edge = ids[3] == ids[4]
-
-    @pl.when(edge)
-    def _():
-        outs[0][...] = ins[1][...]
-
-    @pl.when(jnp.logical_not(edge))
-    def _():
-        outs[0][...] = ins[0][...]
-
-
-def join_sides(bit):
-    def function(ids, ins, outs):
-        wide = ins[0].shape[1]
-        for part, half in ((ins[0], ids[bit]), (ins[1], 1 - ids[bit])):
-            outs[0][:, pl.ds(pl.multiple_of(half * wide, wide), wide)] = part[...]
-
-    return function
-
-
-def join(ids, jobs):
-    counts = [(len(ins), len(shapes)) for _, ins, shapes in jobs]
-    n_in = sum(a for a, _ in counts)
-
-    def kernel(ids_ref, *refs):
-        at_in, at_out = 0, n_in
-        for (function, _, _), (a, b) in zip(jobs, counts):
-            function(ids_ref, refs[at_in : at_in + a], refs[at_out : at_out + b])
-            at_in, at_out = at_in + a, at_out + b
-
-    flat = [array for _, ins, _ in jobs for array in ins]
-    shapes = [sds(shape, BF16) for _, _, shapes in jobs for shape in shapes]
-    vmem = pl.BlockSpec(memory_space=pltpu.VMEM)
-    outs = pl.pallas_call(
-        kernel,
-        in_specs=[pl.BlockSpec(memory_space=pltpu.SMEM)] + [vmem] * n_in,
-        out_specs=[vmem] * len(shapes),
-        out_shape=shapes,
-        compiler_params=pltpu.CompilerParams(vmem_limit_bytes=VMEM),
-        name="join_sums",
-    )(ids, *flat)
-    result = []
-    for _, b in counts:
-        result.append(outs[:b])
-        outs = outs[b:]
-    return result
-
-
-TIMES = (1, 2, 2, 1, 1, 1, 1)
+class Sums:
+    def __init__(self, columns):
+        self.columns, self.ins, self.outs, self.code = columns, [], [], []
+        self.rows = {}
+
+    def use(self, array):
+        for index, known in enumerate(self.ins):
+            if known is array:
+                return index
+        self.ins.append(array)
+        return len(self.ins) - 1
+
+    def result(self, shape):
+        self.outs.append(sds(tuple(shape) + (self.columns,), BF16))
+        return len(self.outs) - 1
+
+    def region(self, way, rows):
+        first = self.rows.get(way, 0)
+        self.rows[way] = first + rows
+        return first
+
+    def run(self, ids):
+        ways = sorted(self.rows)
+        shapes = self.outs + [sds((self.rows[way], self.columns), BF16) for way in ways]
+        n_in, n_out = len(self.ins), len(self.outs)
+
+        def kernel(ids_ref, *refs):
+            sends = dict(zip(ways, refs[n_in + n_out :]))
+            for code in self.code:
+                code(ids_ref, refs[:n_in], refs[n_in : n_in + n_out], sends)
+
+        vmem = pl.BlockSpec(memory_space=pltpu.VMEM)
+        results = pl.pallas_call(
+            kernel,
+            in_specs=[pl.BlockSpec(memory_space=pltpu.SMEM)] + [vmem] * n_in,
+            out_specs=[vmem] * len(shapes),
+            out_shape=shapes,
+            compiler_params=pltpu.CompilerParams(vmem_limit_bytes=VMEM),
+            name="join_sums",
+        )(ids, *self.ins)
+        return results[:n_out], dict(zip(ways, results[n_out:]))
+
+
+def at_rows(first, index, count):
+    return pl.ds(pl.multiple_of(first + index * count, 16), count)
+
+
+def sum_section(sums, chunk):
+    kept, got = sums.use(chunk.keep), sums.use(chunk.got["section"])
+    _, rows, _ = chunk.keep.shape
+    cut = chunk.cut
+    rest = rows - cut
+    top, bottom = sums.result((2, cut)), sums.result((2, rest))
+    chunk.first = {"x": sums.region("x", 2 * cut), "y": sums.region("y", 2 * rest)}
+    to_x, to_y = chunk.first["x"], chunk.first["y"]
+
+    def code(ids, ins, outs, sends):
+        low, high = ids[1], ids[2]
+        for i in range(2):
+            add = lambda shard, lines: ins[kept][shard, lines] + ins[got][shard, lines]
+            sends["x"][to_x + i * cut : to_x + i * cut + cut] = add(2 * i + 1 - low, slice(0, cut))
+            outs[top][i] = add(2 * i + low, slice(0, cut))
+            sends["y"][to_y + i * rest : to_y + i * rest + rest] = add(2 * (1 - high) + i, slice(cut, rows))
+            outs[bottom][i] = add(2 * high + i, slice(cut, rows))
+
+    sums.code.append(code)
+    return [top, bottom]
+
+
+def sum_first(sums, chunk):
+    top, bottom = (sums.use(item) for item in chunk.kept)
+    got_x, got_y = sums.use(chunk.got["x"]), sums.use(chunk.got["y"])
+    at_x, at_y = chunk.first["x"], chunk.first["y"]
+    cut, rest = chunk.kept[0].shape[1], chunk.kept[1].shape[1]
+    new_top, new_bottom = sums.result((cut,)), sums.result((rest,))
+    chunk.first = {"y": sums.region("y", cut), "x": sums.region("x", rest)}
+    to_x, to_y = chunk.first["x"], chunk.first["y"]
+
+    def code(ids, ins, outs, sends):
+        low, high = ids[1], ids[2]
+        upper = lambda i: ins[top][i] + ins[got_x][at_rows(at_x, i, cut)]
+        lower = lambda i: ins[bottom][i] + ins[got_y][at_rows(at_y, i, rest)]
+        sends["y"][to_y : to_y + cut] = upper(1 - high)
+        outs[new_top][...] = upper(high)
+        sends["x"][to_x : to_x + rest] = lower(1 - low)
+        outs[new_bottom][...] = lower(low)
+
+    sums.code.append(code)
+    return [new_top, new_bottom]
+
+
+def sum_second(sums, chunk):
+    top, bottom = (sums.use(item) for item in chunk.kept)
+    got_x, got_y = sums.use(chunk.got["x"]), sums.use(chunk.got["y"])
+    at_x, at_y = chunk.first["x"], chunk.first["y"]
+    cut, rest = chunk.kept[0].shape[0], chunk.kept[1].shape[0]
+    part = sums.result((cut + rest,))
+    onward = chunk.line.short
+    if onward:
+        sums.rows["ends"] = max(sums.rows.get("ends", 0), cut + rest)
+
+    def code(ids, ins, outs, sends):
+        outs[part][:cut] = ins[top][...] + ins[got_y][at_y : at_y + cut]
+        outs[part][cut:] = ins[bottom][...] + ins[got_x][at_x : at_x + rest]
+        if onward:
+
+            @pl.when(ids[3] == 1)
+            def _():
+                sends["ends"][: cut + rest] = outs[part][...]
+
+    sums.code.append(code)
+    return [part]
+
+
+def sum_ends(sums, chunk):
+    part, got = sums.use(chunk.kept[0]), sums.use(chunk.got["ends"])
+    rows = chunk.kept[0].shape[0]
+    chunk.first = {"middle": sums.region("middle", rows)}
+    to = chunk.first["middle"]
+
+    def code(ids, ins, outs, sends):
+        sends["middle"][to : to + rows] = ins[part][...] + ins[got][:rows]
+
+    sums.code.append(code)
+    return []
+
+
+def sum_middle(sums, chunk):
+    sent, got = sums.use(chunk.sent["middle"]), sums.use(chunk.got["middle"])
+    at, rows = chunk.first["middle"], chunk.rows
+    whole = sums.result((rows,))
+    sums.rows["ends"] = max(sums.rows.get("ends", 0), rows)
+
+    def code(ids, ins, outs, sends):
+        outs[whole][...] = ins[sent][at : at + rows] + ins[got][at : at + rows]
+
+        @pl.when(ids[3] == 0)
+        def _():
+            sends["ends"][:rows] = outs[whole][...]
+
+    sums.code.append(code)
+    return [whole]
+
+
+def sum_last(sums, chunk):
+    whole, got = sums.use(chunk.kept[0]), sums.use(chunk.got["ends"])
+    rows = chunk.rows
+    result = sums.result((rows,))
+
+    def code(ids, ins, outs, sends):
+        @pl.when(ids[3] == 1)
+        def _():
+            outs[result][...] = ins[got][:rows]
+
+        @pl.when(ids[3] == 0)
+        def _():
+            outs[result][...] = ins[whole][...]
+
+    sums.code.append(code)
+    return [result]
+
+
+class Chunk:
+    def __init__(self, line, send, keep):
+        self.line, self.send, self.keep = line, send, keep
+        self.at, self.kept, self.got, self.sent, self.done = 0, [], {}, {}, None
+        self.rows = send.shape[1]
+        self.cut = split_at(self.rows)
 
 
 class Line:
-    def __init__(self):
-        self.plain = lax.axis_size("inner") != 4
+    def __init__(self, sec):
+        self.sec = sec
+        self.square = lax.axis_size("inner") == 4
         self.short = lax.axis_size("outer") == 4
         spot, place = lax.axis_index("inner"), lax.axis_index("outer")
-        self.ids = jnp.stack([lax.axis_index("section"), spot % 2, spot // 2, place % 2, place // 2]).astype(jnp.int32)
-        self.running = []
-
-    def add(self, send, keep, late=False):
-        self.running.append({"at": 0, "parts": [send, keep], "pending": None, "keep": keep, "late": late, "done": None, "flight": None})
-
-    def keep(self, keep):
-        self.running[-1]["keep"] = keep
-
-    def start(self, item):
-        at, parts = item["at"], item["parts"]
-        item["at"] += 1
-        if at == 0:
-            got = exchange(parts[0], "section", 1)
-            if self.plain:
-                return [got], lambda tied: (join_add, [item["keep"], tied[0]], [item["keep"].shape])
-            _, rows, columns = parts[0].shape
-            cut = split_at(rows)
-            shapes = [(2, cut, columns)] * 2 + [(2, rows - cut, columns)] * 2
-            return [got], lambda tied: (join_section, [item["keep"], tied[0]], shapes)
-        if self.plain:
-            total = lax.psum_scatter(parts[0], "inner", scatter_dimension=0, tiled=False)
-            item["done"] = lax.psum(total, "outer")
-            return None
-        if at == 1:
-            top_send, top, bottom_send, bottom = parts
-            gots = [exchange(top_send, "inner", 1), exchange(bottom_send, "inner", 2)]
-            shapes = [top.shape[1:]] * 2 + [bottom.shape[1:]] * 2
-            return gots, lambda tied: (join_first, [top, tied[0], bottom, tied[1]], shapes)
-        halves = self.short and item["late"]
-        if at == 2:
-            top_send, top, bottom_send, bottom = parts
-            gots = [exchange(top_send, "inner", 2), exchange(bottom_send, "inner", 1)]
-            rows, columns = top.shape[0] + bottom.shape[0], top.shape[1]
-            if halves:
-                return gots, lambda tied: (
-                    join_split, [top, tied[0], bottom, tied[1]], [(rows, columns // 2)] * 2
-                )
-            return gots, lambda tied: (join_second, [top, tied[0], bottom, tied[1]], [(rows, columns)])
-        if not self.short:
-            item["done"] = lax.psum(parts[0], "outer")
-            return None
-        rows, columns = parts[0].shape
-        if not halves and at in (3, 4, 5):
-            pairs = ([(0, 1), (3, 2)], [(1, 2), (2, 1)], [(1, 0), (2, 3)])[at - 3]
-            got = lax.ppermute(parts[0], "outer", pairs)
-            function = join_last if at == 5 else join_add
-            return [got], lambda tied: (function, [parts[0], tied[0]], [(rows, columns)])
-        if at == 3:
-            send, keep = parts
-            got = exchange(send, "outer", 1)
-            return [got], lambda tied: (join_half, [keep, tied[0]], [(rows, columns // 2)] * 2)
-        if at == 4:
-            send, keep = parts
-            got = exchange(send, "outer", 2)
-            return [got], lambda tied: (join_add, [keep, tied[0]], [(rows, columns)])
-        if halves and at in (5, 6):
-            bit = 7 - at
-            got = exchange(parts[0], "outer", bit)
-            return [got], lambda tied: (join_sides(2 + bit), [parts[0], tied[0]], [(rows, 2 * columns)])
-        item["done"] = parts[0]
-        return None
-
-    def settle(self, items):
-        if items:
-            for item, parts in zip(items, join(self.ids, [item["pending"]() for item in items])):
-                item["parts"], item["pending"] = parts, None
-
-    def advance(self, work):
-        self.settle([item for item in self.running if item["pending"] is not None])
-        for item in self.running:
-            if item["done"] is None and item["flight"] is None:
-                move = self.start(item)
-                if move is not None:
-                    item["flight"], item["left"] = move, TIMES[item["at"] - 1]
-        flying = [item for item in self.running if item["flight"] is not None]
-        for item in flying:
-            item["left"] -= 1
-        due = [item for item in flying if item["left"] == 0]
-        beside, tied = lax.optimization_barrier((work(), [item["flight"][0] for item in due]))
-        for item, gots in zip(due, tied):
-            item["pending"], item["flight"] = functools.partial(item["flight"][1], gots), None
-        return beside
+        outside = (place == 0) | (place == lax.axis_size("outer") - 1)
+        self.ids = jnp.stack([lax.axis_index("section"), spot % 2, spot // 2, outside]).astype(jnp.int32)
+        self.chunks, self.made = [], {}
+        self.sums = (sum_section, sum_first, sum_second, sum_ends, sum_middle, sum_last)
+
+    def add(self, send, keep):
+        chunk = Chunk(self, send, keep)
+        self.chunks.append(chunk)
+        return chunk
+
+    def move(self, way, array):
+        if way == "section":
+            return exchange(array, "section", 1)
+        if way in ("x", "y"):
+            return exchange(array, "inner", 1 if way == "x" else 2)
+        return lax.ppermute(array, "outer", [(0, 1), (1, 0), (2, 3), (3, 2)] if way == "ends" else [(1, 2), (2, 1)])
+
+    def advance(self, owner, *works):
+        moving = [chunk for chunk in self.chunks if chunk.done is None and chunk.at > 0]
+        sends = {}
+        if moving and self.square:
+            sums = Sums(moving[0].send.shape[-1])
+            places = [self.sums[chunk.at - 1](sums, chunk) for chunk in moving]
+            outs, sends = sums.run(self.ids)
+            for chunk, place in zip(moving, places):
+                chunk.kept, chunk.sent = [outs[index] for index in place], sends
+        for chunk in moving:
+            chunk.at += 1
+            if not self.square:
+                half = chunk.keep.astype(F32) + chunk.got["section"].astype(F32)
+                half = lax.psum_scatter(half.astype(BF16), "inner", scatter_dimension=0, tiled=False)
+                chunk.done = lax.psum(half, "outer")
+            elif chunk.at == 4 and not self.short:
+                chunk.done = lax.psum(chunk.kept[0], "outer")
+            elif chunk.at == 7:
+                chunk.done = chunk.kept[0]
+        new = [chunk for chunk in self.chunks if chunk.at == 0]
+        gots = {way: self.move(way, array) for way, array in sends.items()}
+        arrived = [self.move("section", chunk.send) for chunk in new]
+        for work in works:
+            work()
+        fresh = [chunk for chunk in self.chunks if chunk not in new and chunk.at == 0]
+        late = [chunk for chunk in self.chunks if chunk.keep is not None and chunk.at == 0]
+        owner.made, parts, keeps, gots, arrived = lax.optimization_barrier(
+            (owner.made, [chunk.send for chunk in fresh], [chunk.keep for chunk in late], gots, arrived)
+        )
+        for chunk, part in zip(fresh, parts):
+            chunk.send = part
+        for chunk, part in zip(late, keeps):
+            chunk.keep = part
+        for chunk in moving:
+            chunk.got = gots
+        for chunk, part in zip(new, arrived):
+            chunk.at, chunk.got = 1, {"section": part}
 
     def finish(self):
-        if not self.short or self.plain:
-            for item in self.running:
-                while item["done"] is None:
-                    if item["flight"] is not None:
-                        gots, after = item["flight"]
-                        item["pending"], item["flight"] = functools.partial(after, gots), None
-                    if item["pending"] is not None:
-                        self.settle([item])
-                    item["flight"] = self.start(item)
-        while any(item["done"] is None for item in self.running):
-            self.advance(lambda: ())
-            for item in self.running:
-                if item["flight"] is not None and item is self.running[-1]:
-                    item["left"] = 1
-        return [item["done"] for item in self.running]
+        while any(chunk.done is None for chunk in self.chunks):
+            self.advance(self)
+        return [chunk.done for chunk in self.chunks]
 
 
 def local(
@@ -899,9 +1147,18 @@
     y_near, y_one = y_one
     front = attend_forward(1, sec, y_near, NEAR, big[0], o_qkv, smalls[1], mask)
     y_two, cache_two = layer_forward(1, sec, y_near, front, big, other, smalls[1], y_one)
-    line = Line()
-    gx_two, (gx_two_near, gx_two_low) = layer_backward(line, 1, sec, gy, cache_two, big, other, smalls[1], shards)
-    gx_one, gx_one_low = layer_backward(line, 0, sec, gx_two_near, cache_one, big, other, smalls[0], shards)
+    line = Line(sec)
+    two = Backward(line, 1, sec, cache_two, big, other, smalls[1], shards)
+    one = Backward(line, 0, sec, cache_one, big, other, smalls[0], shards)
+    line.advance(two, lambda: two.down(gy))
+    line.advance(two, two.up_first)
+    line.advance(two, two.up_last)
+    line.advance(two, two.attention)
+    gx_two_near, gx_two_low = two.made["gx_low"]
+    line.advance(one, lambda: one.down(gx_two_near))
+    line.advance(one, one.up)
+    line.advance(one, one.attention)
+    gx_one = one.made["gx"]
 
     def gather(for_zero, for_one):
         kept = jnp.where(section == 0, for_zero, for_one)
@@ -914,7 +1171,9 @@
     )
     sums = line.finish()
     down, up, attend = [gather(one, two) for one, two in zip(sums[3:], sums[:3])]
-    g_w_down = jnp.concatenate(down, axis=0).T.astype(F32)
+    g_w_down = jnp.concatenate(
+        [side[:, i * width : (i + 1) * width] for side in down for i in range(2)], axis=0
+    ).T.astype(F32)
     g_w_up = jnp.concatenate(up, axis=1).astype(F32)
     part = width // 2
     tall = width // shards

time: 360 us -> 340 us (0.944)
  starting transfers between devices: 73.9 us -> 54.5 us
    ppermute x12 -> x15, waiting for transfers between devices: 12.4 us -> 58.8 us  [move(): lax.ppermute(array, 'outer', [(0, 1), (1, 0), (2, 3), (3, 2)] if way == '...]
    ppermute x48 -> x32, waiting for transfers between devices: 70.1 us -> 26.3 us  [exchange(): return lax.ppermute(array, axis, [(i, i ^ bit) for i in range(length)])]
    ppermute x48 -> x32, starting transfers between devices: 45.8 us -> 23.6 us  [exchange(): return lax.ppermute(array, axis, [(i, i ^ bit) for i in range(length)])]
    pallas_call x16 -> x13, Pallas kernels: 144 us -> 141 us  [call(): pl.pallas_call(body, in_specs=[pl.BlockSpec(memory_space=pltpu.SMEM)] + [...]
    ppermute x12 -> x15, starting transfers between devices: 28.2 us -> 30.9 us  [move(): lax.ppermute(array, 'outer', [(0, 1), (1, 0), (2, 3), (3, 2)] if way == '...]
    pallas_call x17 -> x12, Pallas kernels: 14.2 us -> 13.5 us  [run(): pl.pallas_call(kernel, in_specs=[pl.BlockSpec(memory_space=pltpu.SMEM)] +...]
    unnamed x55 -> x51, local copies, waits for them, and re-layouts: 13.2 us -> 13.3 us
  transfers between devices with their start and end apart: 60 -> 47, of which waited for: 25 -> 17; matrix products, arithmetic and copies ran while one was open for 7% -> 8% of each run, Pallas kernels for 32% -> 32%
where the time goes in v4:
time: 340 us; the launch traced here: 337 us
  Pallas kernels  155 us (46%)
  waiting for transfers between devices  85.2 us (25%)
  starting transfers between devices  54.5 us (16%)
  other arithmetic  22.7 us (7%)
  local copies, waits for them, and re-layouts  18 us (5%)
    pallas_call x13, Pallas kernels, call(): pl.pallas_call(body, in_specs=[pl.BlockSpec(memory_space=pltpu.SMEM)] + [...  141 us
    ppermute x15, waiting for transfers between devices, move(): lax.ppermute(array, 'outer', [(0, 1), (1, 0), (2, 3), (3, 2)] if way == '...  58.8 us
    ppermute x15, starting transfers between devices, move(): lax.ppermute(array, 'outer', [(0, 1), (1, 0), (2, 3), (3, 2)] if way == '...  30.9 us
    ppermute x32, waiting for transfers between devices, exchange(): return lax.ppermute(array, axis, [(i, i ^ bit) for i in range(length)])  26.3 us
    ppermute x32, starting transfers between devices, exchange(): return lax.ppermute(array, axis, [(i, i ^ bit) for i in range(length)])  23.6 us
    pallas_call x12, Pallas kernels, run(): pl.pallas_call(kernel, in_specs=[pl.BlockSpec(memory_space=pltpu.SMEM)] +...  13.5 us
    unnamed x51, local copies, waits for them, and re-layouts  13.3 us
  transfers between devices with their start and end apart: 47, of which 17 were waited for; matrix products, arithmetic and copies ran while one was open for 8% of the time, Pallas kernels for 32%

profile of v4, /device:TPU:0, one launch (start us, length us, event | category | flops | bytes accessed | tf_op | source)
XLA Modules:
  0.0 336.5 jit_solution(9744045936152137145)
XLA Ops:
  1.7 1.4 reduce.11
  8.6 10.7 %attend_forward.2 = (bf16[512,768]{1,0:T(8,128)(2,1)}, bf16[512,768]{1,0:T(8,128)(2,1)}, bf16[512,768]{1,0:T(8,128)(2,1)}, f32[4,6,256,128]{3,2,1,0:T(8,128)}, b...) custom-call(s32[1]{0:T(128)} %bitcast.ids_ref, bf16[512,768]{1,0:T(8,128)(2,1)} %bitcast.78, ...), custom_call_target="tpu_custom_call" | custom-call | flops 2415919104 | bytes 12582912 | tf_op jit(solution)/shard_map/attend_forward/pallas_call | solution.py:149
  19.8 1.5 dynamic-slice_select_fusion
  22.0 12.1 %up_forward.2 = (f32[512,768]{1,0:T(8,128)S(1)}, f32[512,768]{1,0:T(8,128)}, f32[512,128]{1,0:T(8,128)}, bf16[768,512]{1,0:T(8,128)(2,1)}, bf16[4,512,768]{2,1,0...) custom-call(s32[1]{0:T(128)} %bitcast.ids_ref, bf16[512,768]{1,0:T(8,128)(2,1)} %bitcast.79, ...), custom_call_target="tpu_custom_call" | custom-call | flops 3019898880 | bytes 20971520 | tf_op jit(solution)/shard_map/up_forward/pallas_call | solution.py:149
  34.2 2.2 copy-done.10
  36.3 8.1 %down_forward.2 = (bf16[512,768]{1,0:T(8,128)(2,1)S(1)}, bf16[512,768]{1,0:T(8,128)(2,1)}, f32[512,768]{1,0:T(8,128)}, f32[512,128]{1,0:T(8,128)}) custom-call(s32[1]{0:T(128)} %bitcast.ids_ref, bf16[4,512,768]{2,1,0:T(8,128)(2,1)S(1)} %get-tuple-element.250.refs_0_, bf16[3072,768]{1,0:T(8,128)(2,1)} %bitcast.58, bf16[3072,768]{1,0:T(8,128)(2,1)} %copy-done.10, ...), custom_call_target="tpu_custom_call" | custom-call | flops 2415919104 | bytes 12582912 | tf_op jit(solution)/shard_map/down_forward/pallas_call | solution.py:149
  44.4 10.8 %attend_forward.3 = (bf16[512,768]{1,0:T(8,128)(2,1)}, bf16[512,768]{1,0:T(8,128)(2,1)}, bf16[512,768]{1,0:T(8,128)(2,1)}, f32[4,6,256,128]{3,2,1,0:T(8,128)}, b...) custom-call(s32[1]{0:T(128)} %bitcast.ids_ref, bf16[512,768]{1,0:T(8,128)(2,1)S(1)} %get-tuple-element.254.refs_0_, ...), custom_call_target="tpu_custom_call" | custom-call | flops 2415919104 | bytes 12582912 | tf_op jit(solution)/shard_map/attend_forward/pallas_call | solution.py:149
  55.2 11.7 %up_forward.3 = (f32[512,768]{1,0:T(8,128)S(1)}, f32[512,768]{1,0:T(8,128)}, f32[512,128]{1,0:T(8,128)}, bf16[768,512]{1,0:T(8,128)(2,1)}, bf16[4,512,768]{2,1,0:T(8,128)(2,1)S(1)}, /*index=5*/f32[4,512,768]{2,1,0:T(8,128)}) custom-call(s32[1]{0:T(128)} %bitcast.ids_ref, bf16[512,768]{1,0:T(8,128)(2,1)S(1)} %get-tuple-element.254.refs_0_, ...), custom_call_target="tpu_custom_call" | custom-call | flops 3019898880 | bytes 20971520 | tf_op jit(solution)/shard_map/up_forward/pallas_call | solution.py:149
  67.0 7.5 %down_forward.3 = (bf16[512,768]{1,0:T(8,128)(2,1)}, f32[512,768]{1,0:T(8,128)S(1)}, f32[512,128]{1,0:T(8,128)S(1)}) custom-call(s32[1]{0:T(128)} %bitcast.ids_ref, bf16[4,512,768]{2,1,0:T(8,128)(2,1)S(1)} %get-tuple-element.257.refs_0_.refs_4_, bf16[3072,768]{1,0:T(8,128)(2,1)} %bitcast.59, bf16[3072,768]{1,0:T(8,128)(2,1)} %copy-done.10, ...), custom_call_target="tpu_custom_call" | custom-call | flops 2415919104 | bytes 12582912 | tf_op jit(solution)/shard_map/down_forward/pallas_call | solution.py:149
  74.5 5.8 %down_grad.2 = (f32[512,768]{1,0:T(8,128)S(1)}, bf16[512,768]{1,0:T(8,128)(2,1)S(1)}, f32[8,768]{1,0:T(8,128)S(1)}, bf16[4,192,1536]{2,1,0:T(8,128)(2,1)S(1)}, bf16[4,192,1536]{2,1,0:T(8,128)(2,1)S(1)}) custom-call(s32[1]{0:T(128)} %bitcast.ids_ref, bf16[512,768]{1,0:T(8,128)(2,1)} %bitcast.82, f32[512,768]{1,0:T(8,128)S(1)} %get-tuple-element.260.refs_1_, ...), custom_call_target="tpu_custom_call" | custom-call | flops 2415919104 | bytes 14680064 | tf_op jit(solution)/shard_map/down_grad/pallas_call | solution.py:149
  80.8 8.6 %up_grad_first.1 = (f32[512,768]{1,0:T(8,128)S(1)}, f32[8,768]{1,0:T(8,128)S(1)}, bf16[4,192,1536]{2,1,0:T(8,128)(2,1)}) custom-call(s32[1]{0:T(128)} %bitcast.ids_ref, bf16[512,768]{1,0:T(8,128)(2,1)S(1)} %get-tuple-element.277.refs_0_, f32[512,768]{1,0:T(8,128)S(1)} %get-tuple-element.269.refs_1_, bf16[3072,768]{1,0:T(8,128)(2,1)} %bitcast.60, ...), custom_call_target="tpu_custom_call" | custom-call | flops 3623878656 | bytes 15728640 | tf_op jit(solution)/shard_map/up_grad_first/pallas_call | solution.py:149
  90.6 1.4 copy-done.4
  92.5 1.7 copy-done.3
  94.2 1.7 copy-done.5
  96.7 2.6 collective-permute-start.7
  99.3 1.5 collective-permute-start.8
  100.8 8.6 %up_grad_last.1 = (f32[512,768]{1,0:T(8,128)S(1)}, bf16[512,768]{1,0:T(8,128)(2,1)S(1)}, f32[8,768]{1,0:T(8,128)S(1)}, bf16[4,192,1536]{2,1,0:T(8,128)(2,1)S(1)}) custom-call(s32[1]{0:T(128)} %bitcast.ids_ref, bf16[512,768]{1,0:T(8,128)(2,1)S(1)} %get-tuple-element.277.refs_0_, f32[512,768]{1,0:T(8,128)S(1)} %copy-done.7, bf16[3072,768]{1,0:T(8,128)(2,1)} %bitcast.61, ...), custom_call_target="tpu_custom_call" | custom-call | flops 3623878656 | bytes 15728640 | tf_op jit(solution)/shard_map/up_grad_last/pallas_call | solution.py:149
  109.4 3.9 %collective-permute-done.7.refs_2_ = bf16[192,1536]{1,0:T(8,128)(2,1)S(1)} collective-permute-done((bf16[192,1536]{1,0:T(8,128)(2,1)S(1)}, bf16[192,1536]{1,0:T(8,128)(2,1)S(1)}, u32[]{:S(2)}, u32[]{:S(2)}) %collective-permute-start.7) | collective-permute-done | bytes 589856 | tf_op jit(solution)/shard_map/ppermute | solution.py:865
  113.3 1.5 collective-permute-done.8.refs_3_
  116.1 1.7 collective-permute-start.11
  117.8 17.6 %attend_grad.2 = (f32[512,768]{1,0:T(8,128)}, bf16[512,768]{1,0:T(8,128)(2,1)S(1)}, bf16[512,768]{1,0:T(8,128)(2,1)}, bf16[4,208,1536]{2,1,0:T(8,128)(2,1)S(1)}, bf16[4,208,1536]{2,1,0:T(8,128)(2,1)S(1)}) custom-call(s32[1]{0:T(128)} %bitcast.ids_ref, bf16[512,768]{1,0:T(8,128)(2,1)S(1)} %get-tuple-element.292.refs_0_, ...), custom_call_target="tpu_custom_call" | custom-call | flops 6039797760 | bytes 31457280 | tf_op jit(solution)/shard_map/attend_grad/pallas_call | solution.py:149
  135.4 1.3 collective-permute-done.10.refs_2_
  137.8 1.5 collective-permute-start.12
  139.4 1.4 collective-permute-start.13
  140.8 1.5 collective-permute-start.14
  142.3 6.8 %down_grad.3 = (f32[512,768]{1,0:T(8,128)S(1)}, bf16[512,768]{1,0:T(8,128)(2,1)S(1)}, f32[8,768]{1,0:T(8,128)S(1)}, bf16[4,192,1536]{2,1,0:T(8,128)(2,1)S(1)}, bf16[4,192,1536]{2,1,0:T(8,128)(2,1)S(1)}) custom-call(s32[1]{0:T(128)} %bitcast.ids_ref, bf16[512,768]{1,0:T(8,128)(2,1)S(1)} %get-tuple-element.313.refs_0_, f32[512,768]{1,0:T(8,128)} %get-tuple-element.314.refs_1_, ...), custom_call_target="tpu_custom_call" | custom-call | flops 2415919104 | bytes 14680064 | tf_op jit(solution)/shard_map/down_grad/pallas_call | solution.py:149
  149.7 4.0 %collective-permute-done.12.refs_1_ = bf16[192,1536]{1,0:T(8,128)(2,1)S(1)} collective-permute-done((bf16[192,1536]{1,0:T(8,128)(2,1)S(1)}, bf16[192,1536]{1,0:T(8,128)(2,1)S(1)}, u32[]{:S(2)}, u32[]{:S(2)}) %collective-permute-start.12) | collective-permute-done | bytes 589856 | tf_op jit(solution)/shard_map/ppermute | solution.py:1067
  154.6 1.4 collective-permute-start.18
  156.0 1.5 collective-permute-start.16
  158.6 1.6 collective-permute-start.19
  160.2 15.2 %up_grad.1 = (f32[512,768]{1,0:T(8,128)S(1)}, bf16[512,768]{1,0:T(8,128)(2,1)S(1)}, f32[8,768]{1,0:T(8,128)S(1)}, bf16[4,192,1536]{2,1,0:T(8,128)(2,1)S(1)}, bf16[4,192,1536]{2,1,0:T(8,128)(2,1)S(1)}) custom-call(s32[1]{0:T(128)} %bitcast.ids_ref, bf16[512,768]{1,0:T(8,128)(2,1)S(1)} %get-tuple-element.333.refs_0_, ...), custom_call_target="tpu_custom_call" | custom-call | flops 7247757312 | bytes 31457280 | tf_op jit(solution)/shard_map/up_grad/pallas_call | solution.py:149
  177.8 4.5 %collective-permute-start.21 = (bf16[192,1536]{1,0:T(8,128)(2,1)S(1)}, bf16[192,1536]{1,0:T(8,128)(2,1)S(1)}, u32[]{:S(2)}, u32[]{:S(2)}) collective-permute-start(bf16[192,1536]{1,0:T(8,128)(2,1)S(1)} %get-tuple-element.381), channel_id=1, source_target_pairs={{0,1},{1,0},{2,3},{3,2},{4,5},{5,4},{6,7},{7,6},{8,9},{9,8},{10,11... | collective-permute-start | bytes 1769480 | tf_op jit(solution)/shard_map/ppermute | solution.py:1067
  183.1 17.6 %attend_grad.3 = (f32[512,768]{1,0:T(8,128)}, bf16[512,768]{1,0:T(8,128)(2,1)}, bf16[4,208,1536]{2,1,0:T(8,128)(2,1)S(1)}, bf16[4,208,1536]{2,1,0:T(8,128)(2,1)S(1)}) custom-call(s32[1]{0:T(128)} %bitcast.ids_ref, bf16[512,768]{1,0:T(8,128)(2,1)S(1)} %get-tuple-element.359.refs_0_, bf16[768,512]{1,0:T(8,128)(2,1)} %get-tuple-element.362.refs_1_, ...), custom_call_target="tpu_custom_call" | custom-call | flops 6039797760 | bytes 31457280 | tf_op jit(solution)/shard_map/attend_grad/pallas_call | solution.py:149
  202.0 1.5 collective-permute-start.28
  203.5 1.5 collective-permute-start.29
  205.0 1.7 collective-permute-start.27
  206.8 14.5 %collective-permute-done.27.refs_1_ = bf16[208,1536]{1,0:T(8,128)(2,1)S(1)} collective-permute-done((bf16[208,1536]{1,0:T(8,128)(2,1)S(1)}, bf16[208,1536]{1,0:T(8,128)(2,1)S(1)}, u32[]{:S(2)}, u32[]{:S(2)}) %collective-permute-start.27) | collective-permute-done | bytes 639008 | tf_op jit(solution)/shard_map/ppermute | solution.py:1067
  221.2 2.9 collective-permute-done.28.refs_5_
  227.1 1.5 collective-permute-start.34
  229.3 4.5 %collective-permute-start.31 = (bf16[192,1536]{1,0:T(8,128)(2,1)S(1)}, bf16[192,1536]{1,0:T(8,128)(2,1)S(1)}, u32[]{:S(2)}, u32[]{:S(2)}) collective-permute-start(bf16[192,1536]{1,0:T(8,128)(2,1)S(1)} %get-tuple-element.416), channel_id=1, source_target_pairs={{0,1},{1,0},{2,3},{3,2},{4,5},{5,4},{6,7},{7,6},{8,9},{9,8},{10,11... | collective-permute-start | bytes 1769480 | tf_op jit(solution)/shard_map/ppermute | solution.py:1067
  234.8 11.1 %collective-permute-done.31.refs_3_ = bf16[192,1536]{1,0:T(8,128)(2,1)S(1)} collective-permute-done((bf16[192,1536]{1,0:T(8,128)(2,1)S(1)}, bf16[192,1536]{1,0:T(8,128)(2,1)S(1)}, u32[]{:S(2)}, u32[]{:S(2)}) %collective-permute-start.31) | collective-permute-done | bytes 589856 | tf_op jit(solution)/shard_map/ppermute | solution.py:1067
  245.8 1.9 collective-permute-done.34.refs_7_
  247.8 1.8 collective-permute-done.33.refs_6_
  250.5 2.6 collective-permute-start.35
  253.8 1.5 collective-permute-start.37
  256.6 4.4 %collective-permute-done.37.refs_7_ = bf16[96,1536]{1,0:T(8,128)(2,1)S(1)} collective-permute-done((bf16[96,1536]{1,0:T(8,128)(2,1)S(1)}, bf16[96,1536]{1,0:T(8,128)(2,1)S(1)}, u32[]{:S(2)}, u32[]{:S(2)}) %collective-permute-start.37) | collective-permute-done | bytes 294944 | tf_op jit(solution)/shard_map/ppermute | solution.py:865
  261.6 6.6 %collective-permute-done.38.refs_8_ = bf16[112,1536]{1,0:T(8,128)(2,1)S(1)} collective-permute-done((bf16[112,1536]{1,0:T(8,128)(2,1)S(1)}, bf16[112,1536]{1,0:T(8,128)(2,1)S(1)}, u32[]{:S(2)}, u32[]{:S(2)}) %collective-permute-start.38) | collective-permute-done | bytes 344096 | tf_op jit(solution)/shard_map/ppermute | solution.py:865
  268.2 1.8 join_sums.20
  270.9 1.8 collective-permute-start.39
  272.7 1.5 collective-permute-start.40
  274.2 1.5 broadcast_select_fusion.1
  277.0 6.9 %collective-permute-done.39.refs_1_ = bf16[208,1536]{1,0:T(8,128)(2,1)S(1)} collective-permute-done((bf16[208,1536]{1,0:T(8,128)(2,1)}, bf16[208,1536]{1,0:T(8,128)(2,1)S(1)}, u32[]{:S(2)}, u32[]{:S(2)}) %collective-permute-start.39) | collective-permute-done | bytes 639008 | tf_op jit(solution)/shard_map/ppermute | solution.py:1067
  283.9 1.8 join_sums.21
  285.9 1.7 fusion.1
  287.6 1.9 pad_maximum_fusion
  290.1 5.5 %collective-permute-start.41 = (bf16[192,1536]{1,0:T(8,128)(2,1)S(1)}, bf16[192,1536]{1,0:T(8,128)(2,1)S(1)}, u32[]{:S(2)}, u32[]{:S(2)}) collective-permute-start(bf16[192,1536]{1,0:T(8,128)(2,1)S(1)} %get-tuple-element.447), channel_id=1, source_target_pairs={{0,1},{1,0},{2,3},{3,2},{4,5},{5,4},{6,7},{7,6},{8,9},{9,8},{10,11... | collective-permute-start | bytes 1769480 | tf_op jit(solution)/shard_map/ppermute | solution.py:1067
  295.8 13.5 %collective-permute-done.41.refs_1_ = bf16[192,1536]{1,0:T(8,128)(2,1)S(1)} collective-permute-done((bf16[192,1536]{1,0:T(8,128)(2,1)S(1)}, bf16[192,1536]{1,0:T(8,128)(2,1)S(1)}, u32[]{:S(2)}, u32[]{:S(2)}) %collective-permute-start.41) | collective-permute-done | bytes 589856 | tf_op jit(solution)/shard_map/ppermute | solution.py:1067
  309.3 1.5 join_sums.22
  310.8 1.8 collective-permute-start.43
  313.5 1.6 convert_bitcast_fusion
  315.0 3.0 copy.29
  318.1 8.9 %collective-permute-done.43.refs_1_ = bf16[208,1536]{1,0:T(8,128)(2,1)S(1)} collective-permute-done((bf16[208,1536]{1,0:T(8,128)(2,1)}, bf16[208,1536]{1,0:T(8,128)(2,1)S(1)}, u32[]{:S(2)}, u32[]{:S(2)}) %collective-permute-start.43) | collective-permute-done | bytes 639008 | tf_op jit(solution)/shard_map/ppermute | solution.py:1067
  328.9 1.7 maximum_convert_fusion
  332.4 1.3 convert_element_type.47
  (153 shorter events, 38.6 us)
Async XLA Ops:
  0.6 4.9 %copy-start = (bf16[8,128,768]{2,1,0:T(8,128)(2,1)S(1)}, bf16[8,128,768]{2,1,0:T(8,128)(2,1)}, u32[]{:S(2)}) copy-start(bf16[8,128,768]{2,1,0:T(8,128)(2,1)} %param.14) | copy-start | bytes 4718596
  0.7 7.4 %collective-permute-start = (bf16[768,2304]{1,0:T(8,128)(2,1)}, bf16[768,2304]{1,0:T(8,128)(2,1)}, u32[]{:S(2)}, u32[]{:S(2)}) collective-permute-start(bf16[768,2304]{1,0:T(8,128)(2,1)} %bitcast.88), channel_id=1, source_target_pairs={{0,16},{16,0},{1,17},{17,1},{2,18},{18,2},{3,19},{19,3},{4,20},{20... | collective-permute-start | bytes 10616840 | tf_op jit(solution)/shard_map/ppermute | solution.py:865
  3.9 3.5 %collective-permute-start.1 = (f32[16,768]{1,0:T(8,128)S(1)}, f32[16,768]{1,0:T(8,128)S(1)}, u32[]{:S(2)}, u32[]{:S(2)}) collective-permute-start(f32[16,768]{1,0:T(8,128)S(1)} %concatenate.74), channel_id=1, source_target_pairs={{0,16},{16,0},{1,17},{17,1},{2,18},{18,2},{3,19},{19,3},{4,20},{20... | collective-permute-start | bytes 147464 | tf_op jit(solution)/shard_map/ppermute | solution.py:865
  7.4 11.9 %slice-start = ((s8[4718592]{0:T(1024)(128)(4,1)}), s8[4194304]{0:T(1024)(128)(4,1)S(1)}, s32[]{:S(2)}) async-start(s8[4718592]{0:T(1024)(128)(4,1)} %bitcast.63), calls=%async_computation | async-start | bytes 8388608
  8.0 11.2 %collective-permute-start.3 = (bf16[768,3072]{1,0:T(8,128)(2,1)}, bf16[768,3072]{1,0:T(8,128)(2,1)S(1)}, u32[]{:S(2)}, u32[]{:S(2)}) collective-permute-start(bf16[768,3072]{1,0:T(8,128)(2,1)} %bitcast.66), channel_id=1, source_target_pairs={{0,16},{16,0},{1,17},{17,1},{2,18},{18,2},{3,19},{19,3},{4,20},{20... | collective-permute-start | bytes 14155784 | tf_op jit(solution)/shard_map/ppermute | solution.py:865
  8.5 10.8 %collective-permute-start.2 = (bf16[768,768]{1,0:T(8,128)(2,1)}, bf16[768,768]{1,0:T(8,128)(2,1)S(1)}, u32[]{:S(2)}, u32[]{:S(2)}) collective-permute-start(bf16[768,768]{1,0:T(8,128)(2,1)} %bitcast.72), channel_id=1, source_target_pairs={{0,16},{16,0},{1,17},{17,1},{2,18},{18,2},{3,19},{19,3},{4,20},{20... | collective-permute-start | bytes 3538952 | tf_op jit(solution)/shard_map/ppermute | solution.py:865
  8.6 10.7 %slice-start.1 = ((s8[4718592]{0:T(1024)(128)(4,1)}), s8[524288]{0:T(1024)(128)(4,1)S(1)}, s32[]{:S(2)}) async-start(s8[4718592]{0:T(1024)(128)(4,1)} %bitcast.63), calls=%async_computation.1 | async-start | bytes 1048576
  8.6 11.3 %copy-start.19 = (bf16[8,128,768]{2,1,0:T(8,128)(2,1)S(1)}, bf16[8,128,768]{2,1,0:T(8,128)(2,1)}, u32[]{:S(2)}) copy-start(bf16[8,128,768]{2,1,0:T(8,128)(2,1)} %param.17) | copy-start | bytes 4718596
  19.3 2.0 copy-start.14
  19.3 2.7 copy-start.11
  19.3 14.8 %collective-permute-start.4 = (bf16[3072,768]{1,0:T(8,128)(2,1)S(1)}, bf16[3072,768]{1,0:T(8,128)(2,1)S(1)}, u32[]{:S(2)}, u32[]{:S(2)}) collective-permute-start(bf16[3072,768]{1,0:T(8,128)(2,1)S(1)} %bitcast.65), channel_id=1, source_target_pairs={{0,16},{16,0},{1,17},{17,1},{2,18},{18,2},{3,19},{19,3},{4,20},{20... | collective-permute-start | bytes 14155784 | tf_op jit(solution)/shard_map/ppermute | solution.py:865
  34.2 2.2 copy-start.10
  80.3 9.1 %copy-start.2 = (bf16[4,192,1536]{2,1,0:T(8,128)(2,1)}, bf16[4,192,1536]{2,1,0:T(8,128)(2,1)S(1)}, u32[]{:S(2)}) copy-start(bf16[4,192,1536]{2,1,0:T(8,128)(2,1)S(1)} %get-tuple-element.287.refs_0_) | copy-start | bytes 7077892
  80.3 10.3 %collective-permute-start.6 = (bf16[4,192,1536]{2,1,0:T(8,128)(2,1)S(1)}, bf16[4,192,1536]{2,1,0:T(8,128)(2,1)S(1)}, u32[]{:S(2)}, u32[]{:S(2)}) collective-permute-start(bf16[4,192,1536]{2,1,0:T(8,128)(2,1)S(1)} %get-tuple-element.276), channel_id=1, source_target_pairs={{0,16},{16,0},{1,17},{17,1},{2,18},{18,2},{3,19},{19,3},{4,20},{20... | collective-permute-start | bytes 7077896 | tf_op jit(solution)/shard_map/ppermute | solution.py:865
  92.0 22.8 %collective-permute-start.9 = (bf16[4,192,1536]{2,1,0:T(8,128)(2,1)}, bf16[4,192,1536]{2,1,0:T(8,128)(2,1)S(1)}, u32[]{:S(2)}, u32[]{:S(2)}) collective-permute-start(bf16[4,192,1536]{2,1,0:T(8,128)(2,1)} %get-tuple-element.291), channel_id=1, source_target_pairs={{0,16},{16,0},{1,17},{17,1},{2,18},{18,2},{3,19},{19,3},{4,20},{20... | collective-permute-start | bytes 7077896 | tf_op jit(solution)/shard_map/ppermute | solution.py:865
  95.8 5.0 %copy-start.7 = (f32[512,768]{1,0:T(8,128)S(1)}, f32[512,768]{1,0:T(8,128)}, u32[]{:S(2)}) copy-start(f32[512,768]{1,0:T(8,128)} %copy-done.6) | copy-start | bytes 4718596
  96.7 16.6 %collective-permute-start.7 = (bf16[192,1536]{1,0:T(8,128)(2,1)S(1)}, bf16[192,1536]{1,0:T(8,128)(2,1)S(1)}, u32[]{:S(2)}, u32[]{:S(2)}) collective-permute-start(bf16[192,1536]{1,0:T(8,128)(2,1)S(1)} %get-tuple-element.289), channel_id=1, source_target_pairs={{0,4},{4,0},{8,12},{12,8},{1,5},{5,1},{9,13},{13,9},{2,6},{6,2},{1... | collective-permute-start | bytes 1769480 | tf_op jit(solution)/shard_map/ppermute | solution.py:865
  99.3 15.4 %collective-permute-start.8 = (bf16[192,1536]{1,0:T(8,128)(2,1)S(1)}, bf16[192,1536]{1,0:T(8,128)(2,1)S(1)}, u32[]{:S(2)}, u32[]{:S(2)}) collective-permute-start(bf16[192,1536]{1,0:T(8,128)(2,1)S(1)} %get-tuple-element.290), channel_id=1, source_target_pairs={{0,8},{4,12},{8,0},{12,4},{1,9},{5,13},{9,1},{13,5},{2,10},{6,14},... | collective-permute-start | bytes 1769480 | tf_op jit(solution)/shard_map/ppermute | solution.py:865
  115.7 21.0 %collective-permute-start.10 = (bf16[288,1536]{1,0:T(8,128)(2,1)S(1)}, bf16[288,1536]{1,0:T(8,128)(2,1)S(1)}, u32[]{:S(2)}, u32[]{:S(2)}) collective-permute-start(bf16[288,1536]{1,0:T(8,128)(2,1)S(1)} %get-tuple-element.311), channel_id=1, source_target_pairs={{0,4},{4,0},{8,12},{12,8},{1,5},{5,1},{9,13},{13,9},{2,6},{6,2},{1... | collective-permute-start | bytes 2654216 | tf_op jit(solution)/shard_map/ppermute | solution.py:865
  116.1 21.0 %collective-permute-start.11 = (bf16[288,1536]{1,0:T(8,128)(2,1)S(1)}, bf16[288,1536]{1,0:T(8,128)(2,1)S(1)}, u32[]{:S(2)}, u32[]{:S(2)}) collective-permute-start(bf16[288,1536]{1,0:T(8,128)(2,1)S(1)} %get-tuple-element.312), channel_id=1, source_target_pairs={{0,8},{4,12},{8,0},{12,4},{1,9},{5,13},{9,1},{13,5},{2,10},{6,14},... | collective-permute-start | bytes 2654216 | tf_op jit(solution)/shard_map/ppermute | solution.py:865
  137.1 16.6 %collective-permute-start.15 = (bf16[4,208,1536]{2,1,0:T(8,128)(2,1)S(1)}, bf16[4,208,1536]{2,1,0:T(8,128)(2,1)S(1)}, u32[]{:S(2)}, u32[]{:S(2)}) collective-permute-start(bf16[4,208,1536]{2,1,0:T(8,128)(2,1)S(1)} %get-tuple-element.332), channel_id=1, source_target_pairs={{0,16},{16,0},{1,17},{17,1},{2,18},{18,2},{3,19},{19,3},{4,20},{20... | collective-permute-start | bytes 7667720 | tf_op jit(solution)/shard_map/ppermute | solution.py:865
  137.8 15.8 %collective-permute-start.12 = (bf16[192,1536]{1,0:T(8,128)(2,1)S(1)}, bf16[192,1536]{1,0:T(8,128)(2,1)S(1)}, u32[]{:S(2)}, u32[]{:S(2)}) collective-permute-start(bf16[192,1536]{1,0:T(8,128)(2,1)S(1)} %get-tuple-element.329), channel_id=1, source_target_pairs={{0,1},{1,0},{2,3},{3,2},{4,5},{5,4},{6,7},{7,6},{8,9},{9,8},{10,11... | collective-permute-start | bytes 1769480 | tf_op jit(solution)/shard_map/ppermute | solution.py:1067
  139.4 9.8 %collective-permute-start.13 = (bf16[96,1536]{1,0:T(8,128)(2,1)S(1)}, bf16[96,1536]{1,0:T(8,128)(2,1)S(1)}, u32[]{:S(2)}, u32[]{:S(2)}) collective-permute-start(bf16[96,1536]{1,0:T(8,128)(2,1)S(1)} %get-tuple-element.330), channel_id=1, source_target_pairs={{0,4},{4,0},{8,12},{12,8},{1,5},{5,1},{9,13},{13,9},{2,6},{6,2},{1... | collective-permute-start | bytes 884744 | tf_op jit(solution)/shard_map/ppermute | solution.py:865
  140.8 8.9 %collective-permute-start.14 = (bf16[96,1536]{1,0:T(8,128)(2,1)S(1)}, bf16[96,1536]{1,0:T(8,128)(2,1)S(1)}, u32[]{:S(2)}, u32[]{:S(2)}) collective-permute-start(bf16[96,1536]{1,0:T(8,128)(2,1)S(1)} %get-tuple-element.331), channel_id=1, source_target_pairs={{0,8},{4,12},{8,0},{12,4},{1,9},{5,13},{9,1},{13,5},{2,10},{6,14},... | collective-permute-start | bytes 884744 | tf_op jit(solution)/shard_map/ppermute | solution.py:865
  153.7 21.8 %collective-permute-start.20 = (bf16[4,192,1536]{2,1,0:T(8,128)(2,1)S(1)}, bf16[4,192,1536]{2,1,0:T(8,128)(2,1)S(1)}, u32[]{:S(2)}, u32[]{:S(2)}) collective-permute-start(bf16[4,192,1536]{2,1,0:T(8,128)(2,1)S(1)} %get-tuple-element.358), channel_id=1, source_target_pairs={{0,16},{16,0},{1,17},{17,1},{2,18},{18,2},{3,19},{19,3},{4,20},{20... | collective-permute-start | bytes 7077896 | tf_op jit(solution)/shard_map/ppermute | solution.py:865
  154.6 20.8 %collective-permute-start.18 = (bf16[224,1536]{1,0:T(8,128)(2,1)S(1)}, bf16[224,1536]{1,0:T(8,128)(2,1)S(1)}, u32[]{:S(2)}, u32[]{:S(2)}) collective-permute-start(bf16[224,1536]{1,0:T(8,128)(2,1)S(1)} %get-tuple-element.356), channel_id=1, source_target_pairs={{0,4},{4,0},{8,12},{12,8},{1,5},{5,1},{9,13},{13,9},{2,6},{6,2},{1... | collective-permute-start | bytes 2064392 | tf_op jit(solution)/shard_map/ppermute | solution.py:865
  156.0 19.4 %collective-permute-start.16 = (bf16[192,1536]{1,0:T(8,128)(2,1)S(1)}, bf16[192,1536]{1,0:T(8,128)(2,1)S(1)}, u32[]{:S(2)}, u32[]{:S(2)}) collective-permute-start(bf16[192,1536]{1,0:T(8,128)(2,1)S(1)} %get-tuple-element.354), channel_id=1, source_target_pairs={{0,1},{1,0},{2,3},{3,2},{4,5},{5,4},{6,7},{7,6},{8,9},{9,8},{10,11... | collective-permute-start | bytes 1769480 | tf_op jit(solution)/shard_map/ppermute | solution.py:1067
  157.5 17.9 %collective-permute-start.17 = (bf16[192,1536]{1,0:T(8,128)(2,1)S(1)}, bf16[192,1536]{1,0:T(8,128)(2,1)S(1)}, u32[]{:S(2)}, u32[]{:S(2)}) collective-permute-start(bf16[192,1536]{1,0:T(8,128)(2,1)S(1)} %get-tuple-element.355.refs_0_), channel_id=1, source_target_pairs={{1,2},{2,1},{5,6},{6,5},{9,10},{10,9},{13,14},{14,13},{17,18},{18,... | collective-permute-start | bytes 1769480 | tf_op jit(solution)/shard_map/ppermute | solution.py:1067
  158.6 16.8 %collective-permute-start.19 = (bf16[192,1536]{1,0:T(8,128)(2,1)S(1)}, bf16[192,1536]{1,0:T(8,128)(2,1)S(1)}, u32[]{:S(2)}, u32[]{:S(2)}) collective-permute-start(bf16[192,1536]{1,0:T(8,128)(2,1)S(1)} %get-tuple-element.357), channel_id=1, source_target_pairs={{0,8},{4,12},{8,0},{12,4},{1,9},{5,13},{9,1},{13,5},{2,10},{6,14},... | collective-permute-start | bytes 1769480 | tf_op jit(solution)/shard_map/ppermute | solution.py:865
  175.5 25.3 %collective-permute-start.25 = (bf16[4,192,1536]{2,1,0:T(8,128)(2,1)S(1)}, bf16[4,192,1536]{2,1,0:T(8,128)(2,1)S(1)}, u32[]{:S(2)}, u32[]{:S(2)}) collective-permute-start(bf16[4,192,1536]{2,1,0:T(8,128)(2,1)S(1)} %get-tuple-element.385), channel_id=1, source_target_pairs={{0,16},{16,0},{1,17},{17,1},{2,18},{18,2},{3,19},{19,3},{4,20},{20... | collective-permute-start | bytes 7077896 | tf_op jit(solution)/shard_map/ppermute | solution.py:865
  176.6 24.2 %collective-permute-start.24 = (bf16[304,1536]{1,0:T(8,128)(2,1)S(1)}, bf16[304,1536]{1,0:T(8,128)(2,1)S(1)}, u32[]{:S(2)}, u32[]{:S(2)}) collective-permute-start(bf16[304,1536]{1,0:T(8,128)(2,1)S(1)} %get-tuple-element.384), channel_id=1, source_target_pairs={{0,8},{4,12},{8,0},{12,4},{1,9},{5,13},{9,1},{13,5},{2,10},{6,14},... | collective-permute-start | bytes 2801672 | tf_op jit(solution)/shard_map/ppermute | solution.py:865
  177.2 23.6 %collective-permute-start.23 = (bf16[288,1536]{1,0:T(8,128)(2,1)S(1)}, bf16[288,1536]{1,0:T(8,128)(2,1)S(1)}, u32[]{:S(2)}, u32[]{:S(2)}) collective-permute-start(bf16[288,1536]{1,0:T(8,128)(2,1)S(1)} %get-tuple-element.383), channel_id=1, source_target_pairs={{0,4},{4,0},{8,12},{12,8},{1,5},{5,1},{9,13},{13,9},{2,6},{6,2},{1... | collective-permute-start | bytes 2654216 | tf_op jit(solution)/shard_map/ppermute | solution.py:865
  177.8 23.0 %collective-permute-start.21 = (bf16[192,1536]{1,0:T(8,128)(2,1)S(1)}, bf16[192,1536]{1,0:T(8,128)(2,1)S(1)}, u32[]{:S(2)}, u32[]{:S(2)}) collective-permute-start(bf16[192,1536]{1,0:T(8,128)(2,1)S(1)} %get-tuple-element.381), channel_id=1, source_target_pairs={{0,1},{1,0},{2,3},{3,2},{4,5},{5,4},{6,7},{7,6},{8,9},{9,8},{10,11... | collective-permute-start | bytes 1769480 | tf_op jit(solution)/shard_map/ppermute | solution.py:1067
  182.3 18.5 %collective-permute-start.22 = (bf16[192,1536]{1,0:T(8,128)(2,1)S(1)}, bf16[192,1536]{1,0:T(8,128)(2,1)S(1)}, u32[]{:S(2)}, u32[]{:S(2)}) collective-permute-start(bf16[192,1536]{1,0:T(8,128)(2,1)S(1)} %get-tuple-element.382.refs_2_), channel_id=1, source_target_pairs={{1,2},{2,1},{5,6},{6,5},{9,10},{10,9},{13,14},{14,13},{17,18},{18,... | collective-permute-start | bytes 1769480 | tf_op jit(solution)/shard_map/ppermute | solution.py:1067
  200.8 24.5 %collective-permute-start.30 = (bf16[4,208,1536]{2,1,0:T(8,128)(2,1)S(1)}, bf16[4,208,1536]{2,1,0:T(8,128)(2,1)S(1)}, u32[]{:S(2)}, u32[]{:S(2)}) collective-permute-start(bf16[4,208,1536]{2,1,0:T(8,128)(2,1)S(1)} %get-tuple-element.404), channel_id=1, source_target_pairs={{0,16},{16,0},{1,17},{17,1},{2,18},{18,2},{3,19},{19,3},{4,20},{20... | collective-permute-start | bytes 7667720 | tf_op jit(solution)/shard_map/ppermute | solution.py:865
  202.0 22.1 %collective-permute-start.28 = (bf16[288,1536]{1,0:T(8,128)(2,1)S(1)}, bf16[288,1536]{1,0:T(8,128)(2,1)S(1)}, u32[]{:S(2)}, u32[]{:S(2)}) collective-permute-start(bf16[288,1536]{1,0:T(8,128)(2,1)S(1)} %get-tuple-element.402), channel_id=1, source_target_pairs={{0,4},{4,0},{8,12},{12,8},{1,5},{5,1},{9,13},{13,9},{2,6},{6,2},{1... | collective-permute-start | bytes 2654216 | tf_op jit(solution)/shard_map/ppermute | solution.py:865
  203.5 21.8 %collective-permute-start.29 = (bf16[288,1536]{1,0:T(8,128)(2,1)S(1)}, bf16[288,1536]{1,0:T(8,128)(2,1)S(1)}, u32[]{:S(2)}, u32[]{:S(2)}) collective-permute-start(bf16[288,1536]{1,0:T(8,128)(2,1)S(1)} %get-tuple-element.403), channel_id=1, source_target_pairs={{0,8},{4,12},{8,0},{12,4},{1,9},{5,13},{9,1},{13,5},{2,10},{6,14},... | collective-permute-start | bytes 2654216 | tf_op jit(solution)/shard_map/ppermute | solution.py:865
  205.0 16.2 %collective-permute-start.27 = (bf16[208,1536]{1,0:T(8,128)(2,1)S(1)}, bf16[208,1536]{1,0:T(8,128)(2,1)S(1)}, u32[]{:S(2)}, u32[]{:S(2)}) collective-permute-start(bf16[208,1536]{1,0:T(8,128)(2,1)S(1)} %get-tuple-element.401), channel_id=1, source_target_pairs={{0,1},{1,0},{2,3},{3,2},{4,5},{5,4},{6,7},{7,6},{8,9},{9,8},{10,11... | collective-permute-start | bytes 1916936 | tf_op jit(solution)/shard_map/ppermute | solution.py:1067
  225.3 8.5 %copy-start.15 = (bf16[512,768]{1,0:T(8,128)(2,1)S(1)}, bf16[512,768]{1,0:T(8,128)(2,1)}, u32[]{:S(2)}) copy-start(bf16[512,768]{1,0:T(8,128)(2,1)} %get-tuple-element.253.refs_3_) | copy-start | bytes 2359300
  225.3 8.5 %copy-start.16 = (bf16[512,768]{1,0:T(8,128)(2,1)S(1)}, bf16[512,768]{1,0:T(8,128)(2,1)}, u32[]{:S(2)}) copy-start(bf16[512,768]{1,0:T(8,128)(2,1)} %get-tuple-element.259) | copy-start | bytes 2359300
  226.4 23.1 %collective-permute-start.33 = (bf16[320,1536]{1,0:T(8,128)(2,1)S(1)}, bf16[320,1536]{1,0:T(8,128)(2,1)S(1)}, u32[]{:S(2)}, u32[]{:S(2)}) collective-permute-start(bf16[320,1536]{1,0:T(8,128)(2,1)S(1)} %get-tuple-element.417), channel_id=1, source_target_pairs={{0,4},{4,0},{8,12},{12,8},{1,5},{5,1},{9,13},{13,9},{2,6},{6,2},{1... | collective-permute-start | bytes 2949128 | tf_op jit(solution)/shard_map/ppermute | solution.py:865
  227.1 20.7 %collective-permute-start.34 = (bf16[288,1536]{1,0:T(8,128)(2,1)S(1)}, bf16[288,1536]{1,0:T(8,128)(2,1)S(1)}, u32[]{:S(2)}, u32[]{:S(2)}) collective-permute-start(bf16[288,1536]{1,0:T(8,128)(2,1)S(1)} %get-tuple-element.418), channel_id=1, source_target_pairs={{0,8},{4,12},{8,0},{12,4},{1,9},{5,13},{9,1},{13,5},{2,10},{6,14},... | collective-permute-start | bytes 2654216 | tf_op jit(solution)/shard_map/ppermute | solution.py:865
  228.6 17.2 %collective-permute-start.32 = (bf16[208,1536]{1,0:T(8,128)(2,1)S(1)}, bf16[208,1536]{1,0:T(8,128)(2,1)S(1)}, u32[]{:S(2)}, u32[]{:S(2)}) collective-permute-start(bf16[208,1536]{1,0:T(8,128)(2,1)S(1)} %get-tuple-element.415.refs_0_), channel_id=1, source_target_pairs={{1,2},{2,1},{5,6},{6,5},{9,10},{10,9},{13,14},{14,13},{17,18},{18,... | collective-permute-start | bytes 1916936 | tf_op jit(solution)/shard_map/ppermute | solution.py:1067
  229.3 16.5 %collective-permute-start.31 = (bf16[192,1536]{1,0:T(8,128)(2,1)S(1)}, bf16[192,1536]{1,0:T(8,128)(2,1)S(1)}, u32[]{:S(2)}, u32[]{:S(2)}) collective-permute-start(bf16[192,1536]{1,0:T(8,128)(2,1)S(1)} %get-tuple-element.416), channel_id=1, source_target_pairs={{0,1},{1,0},{2,3},{3,2},{4,5},{5,4},{6,7},{7,6},{8,9},{9,8},{10,11... | collective-permute-start | bytes 1769480 | tf_op jit(solution)/shard_map/ppermute | solution.py:1067
  234.8 39.5 %collective-permute-start.5 = (bf16[512,768]{1,0:T(8,128)(2,1)}, bf16[512,768]{1,0:T(8,128)(2,1)}, u32[]{:S(2)}, u32[]{:S(2)}) collective-permute-start(bf16[512,768]{1,0:T(8,128)(2,1)} %broadcast_select_fusion.2), channel_id=1, source_target_pairs={{0,16},{16,0},{1,17},{17,1},{2,18},{18,2},{3,19},{19,3},{4,20},{20... | collective-permute-start | bytes 2359304 | tf_op jit(solution)/shard_map/ppermute | solution.py:865
  249.5 5.7 %copy-start.12 = (f32[512,768]{1,0:T(8,128)S(1)}, f32[512,768]{1,0:T(8,128)}, u32[]{:S(2)}) copy-start(f32[512,768]{1,0:T(8,128)} %get-tuple-element.386) | copy-start | bytes 4718596
  249.5 5.7 %copy-start.17 = (bf16[512,768]{1,0:T(8,128)(2,1)S(1)}, bf16[512,768]{1,0:T(8,128)(2,1)}, u32[]{:S(2)}) copy-start(bf16[512,768]{1,0:T(8,128)(2,1)} %get-tuple-element.387) | copy-start | bytes 2359300
  250.5 17.8 %collective-permute-start.35 = (bf16[208,1536]{1,0:T(8,128)(2,1)S(1)}, bf16[208,1536]{1,0:T(8,128)(2,1)S(1)}, u32[]{:S(2)}, u32[]{:S(2)}) collective-permute-start(bf16[208,1536]{1,0:T(8,128)(2,1)S(1)} %get-tuple-element.429), channel_id=1, source_target_pairs={{0,1},{1,0},{2,3},{3,2},{4,5},{5,4},{6,7},{7,6},{8,9},{9,8},{10,11... | collective-permute-start | bytes 1916936 | tf_op jit(solution)/shard_map/ppermute | solution.py:1067
  253.1 15.2 %collective-permute-start.36 = (bf16[192,1536]{1,0:T(8,128)(2,1)S(1)}, bf16[192,1536]{1,0:T(8,128)(2,1)S(1)}, u32[]{:S(2)}, u32[]{:S(2)}) collective-permute-start(bf16[192,1536]{1,0:T(8,128)(2,1)S(1)} %get-tuple-element.430.refs_2_), channel_id=1, source_target_pairs={{1,2},{2,1},{5,6},{6,5},{9,10},{10,9},{13,14},{14,13},{17,18},{18,... | collective-permute-start | bytes 1769480 | tf_op jit(solution)/shard_map/ppermute | solution.py:1067
  253.8 7.2 %collective-permute-start.37 = (bf16[96,1536]{1,0:T(8,128)(2,1)S(1)}, bf16[96,1536]{1,0:T(8,128)(2,1)S(1)}, u32[]{:S(2)}, u32[]{:S(2)}) collective-permute-start(bf16[96,1536]{1,0:T(8,128)(2,1)S(1)} %get-tuple-element.431), channel_id=1, source_target_pairs={{0,4},{4,0},{8,12},{12,8},{1,5},{5,1},{9,13},{13,9},{2,6},{6,2},{1... | collective-permute-start | bytes 884744 | tf_op jit(solution)/shard_map/ppermute | solution.py:865
  256.6 29.3 %collective-permute-start.26 = (f32[512,768]{1,0:T(8,128)}, f32[512,768]{1,0:T(8,128)}, u32[]{:S(2)}, u32[]{:S(2)}) collective-permute-start(f32[512,768]{1,0:T(8,128)} %convert_select_fusion), channel_id=1, source_target_pairs={{0,16},{16,0},{1,17},{17,1},{2,18},{18,2},{3,19},{19,3},{4,20},{20... | collective-permute-start | bytes 4718600 | tf_op jit(solution)/shard_map/ppermute | solution.py:865
  261.0 7.3 %collective-permute-start.38 = (bf16[112,1536]{1,0:T(8,128)(2,1)S(1)}, bf16[112,1536]{1,0:T(8,128)(2,1)S(1)}, u32[]{:S(2)}, u32[]{:S(2)}) collective-permute-start(bf16[112,1536]{1,0:T(8,128)(2,1)S(1)} %get-tuple-element.432), channel_id=1, source_target_pairs={{0,8},{4,12},{8,0},{12,4},{1,9},{5,13},{9,1},{13,5},{2,10},{6,14},... | collective-permute-start | bytes 1032200 | tf_op jit(solution)/shard_map/ppermute | solution.py:865
  270.9 13.0 %collective-permute-start.39 = (bf16[208,1536]{1,0:T(8,128)(2,1)}, bf16[208,1536]{1,0:T(8,128)(2,1)S(1)}, u32[]{:S(2)}, u32[]{:S(2)}) collective-permute-start(bf16[208,1536]{1,0:T(8,128)(2,1)} %get-tuple-element.441), channel_id=1, source_target_pairs={{0,1},{1,0},{2,3},{3,2},{4,5},{5,4},{6,7},{7,6},{8,9},{9,8},{10,11... | collective-permute-start | bytes 1916936 | tf_op jit(solution)/shard_map/ppermute | solution.py:1067
  272.7 4.3 %collective-permute-start.40 = (bf16[192,1536]{1,0:T(8,128)(2,1)}, bf16[192,1536]{1,0:T(8,128)(2,1)}, u32[]{:S(2)}, u32[]{:S(2)}) collective-permute-start(bf16[192,1536]{1,0:T(8,128)(2,1)} %get-tuple-element.442.refs_2_), channel_id=1, source_target_pairs={{1,2},{2,1},{5,6},{6,5},{9,10},{10,9},{13,14},{14,13},{17,18},{18,... | collective-permute-start | bytes 1769480 | tf_op jit(solution)/shard_map/ppermute | solution.py:1067
  275.7 8.2 %copy-start.9 = (bf16[192,1536]{1,0:T(8,128)(2,1)S(1)}, bf16[192,1536]{1,0:T(8,128)(2,1)}, u32[]{:S(2)}) copy-start(bf16[192,1536]{1,0:T(8,128)(2,1)} %copy-done.8) | copy-start | bytes 1769476
  283.9 2.0 copy-start.13
  283.9 2.0 copy-start.18
  285.8 9.9 %collective-permute-start.46 = (bf16[192,1536]{1,0:T(8,128)(2,1)S(1)}, bf16[192,1536]{1,0:T(8,128)(2,1)S(1)}, u32[]{:S(2)}, u32[]{:S(2)}) collective-permute-start(bf16[192,1536]{1,0:T(8,128)(2,1)S(1)} %broadcast_select_fusion.10), channel_id=1, source_target_pairs={{0,16},{16,0},{1,17},{17,1},{2,18},{18,2},{3,19},{19,3},{4,20},{20... | collective-permute-start | bytes 1769480 | tf_op jit(solution)/shard_map/ppermute | solution.py:865
  289.4 19.9 %collective-permute-start.42 = (bf16[208,1536]{1,0:T(8,128)(2,1)S(1)}, bf16[208,1536]{1,0:T(8,128)(2,1)S(1)}, u32[]{:S(2)}, u32[]{:S(2)}) collective-permute-start(bf16[208,1536]{1,0:T(8,128)(2,1)S(1)} %get-tuple-element.448.refs_2_), channel_id=1, source_target_pairs={{1,2},{2,1},{5,6},{6,5},{9,10},{10,9},{13,14},{14,13},{17,18},{18,... | collective-permute-start | bytes 1916936 | tf_op jit(solution)/shard_map/ppermute | solution.py:1067
  290.1 19.2 %collective-permute-start.41 = (bf16[192,1536]{1,0:T(8,128)(2,1)S(1)}, bf16[192,1536]{1,0:T(8,128)(2,1)S(1)}, u32[]{:S(2)}, u32[]{:S(2)}) collective-permute-start(bf16[192,1536]{1,0:T(8,128)(2,1)S(1)} %get-tuple-element.447), channel_id=1, source_target_pairs={{0,1},{1,0},{2,3},{3,2},{4,5},{5,4},{6,7},{7,6},{8,9},{9,8},{10,11... | collective-permute-start | bytes 1769480 | tf_op jit(solution)/shard_map/ppermute | solution.py:1067
  310.8 16.2 %collective-permute-start.43 = (bf16[208,1536]{1,0:T(8,128)(2,1)}, bf16[208,1536]{1,0:T(8,128)(2,1)S(1)}, u32[]{:S(2)}, u32[]{:S(2)}) collective-permute-start(bf16[208,1536]{1,0:T(8,128)(2,1)} %get-tuple-element.452), channel_id=1, source_target_pairs={{0,1},{1,0},{2,3},{3,2},{4,5},{5,4},{6,7},{7,6},{8,9},{9,8},{10,11... | collective-permute-start | bytes 1916936 | tf_op jit(solution)/shard_map/ppermute | solution.py:1067
  313.5 14.3 %collective-permute-start.45 = (bf16[192,1536]{1,0:T(8,128)(2,1)}, bf16[192,1536]{1,0:T(8,128)(2,1)}, u32[]{:S(2)}, u32[]{:S(2)}) collective-permute-start(bf16[192,1536]{1,0:T(8,128)(2,1)} %broadcast_select_fusion.12), channel_id=1, source_target_pairs={{0,16},{16,0},{1,17},{17,1},{2,18},{18,2},{3,19},{19,3},{4,20},{20... | collective-permute-start | bytes 1769480 | tf_op jit(solution)/shard_map/ppermute | solution.py:865
  327.7 2.9 collective-permute-start.44
  332.2 4.1 %copy-start.1 = (bf16[8,128,768]{2,1,0:T(8,128)(2,1)S(1)}, bf16[8,128,768]{2,1,0:T(8,128)(2,1)}, u32[]{:S(2)}) copy-start(bf16[8,128,768]{2,1,0:T(8,128)(2,1)} %param.14) | copy-start | bytes 4718596
  (5 other events, 6.7 us)

commit v5 on v4

--- a/solution.py
+++ b/solution.py
@@ -1,4 +1,5 @@
 import functools
+import math
 
 import jax
 import jax.numpy as jnp
@@ -11,7 +12,7 @@
 CAP = 28
 EPS = 1e-12
 SCALE = 0.125
-VMEM = 30 * 1024 * 1024
+SPARE = 8 * 1024 * 1024
 F32 = jnp.float32
 BF16 = jnp.bfloat16
 B_Q, B_V, B_OUT, GAIN_ONE, GAIN_TWO, OFFSET_ONE, OFFSET_TWO, B_DOWN, B_UP = range(9)
@@ -118,7 +119,7 @@
             move.store(*(ref.at[index] if index else ref for ref in (self.buffer, self.ref)))
 
 
-NEAR, FAR, RAW, BOTH = "near", "far", "raw", "both"
+NEAR, FAR, RAW, BOTH, FREE = "near", "far", "raw", "both", "free"
 
 
 def ready(waits):
@@ -127,7 +128,7 @@
 
 
 def call(kernel, ids, ins, outs, scratch, name, flops, nbytes):
-    space = lambda kind: pltpu.VMEM if kind == NEAR else pltpu.HBM
+    space = lambda kind: {NEAR: pltpu.VMEM, FREE: pl.ANY}.get(kind, pltpu.HBM)
     spread = [(shape, part) for shape, kind in outs for part in ((NEAR, RAW) if kind == BOTH else (kind,))]
     kinds = [kind for _, kind in ins] + [kind for _, kind in spread]
     shapes = [array for array, _ in ins] + [shape for shape, _ in spread]
@@ -146,6 +147,9 @@
                 operands.append(Operand(ref, spare.pop(0) if kind == FAR else ref, kind == FAR))
         kernel(ids_ref, *operands, *refs[count + len(buffers) :])
 
+    size = lambda shape, dtype: math.prod(shape) * jnp.dtype(dtype).itemsize
+    limit = SPARE + sum(size(*item) for item in scratch)
+    limit += sum(size(shape.shape, shape.dtype) for shape, kind in zip(shapes, kinds) if kind == FAR)
     results = pl.pallas_call(
         body,
         in_specs=[pl.BlockSpec(memory_space=pltpu.SMEM)]
@@ -153,7 +157,7 @@
         out_specs=[pl.BlockSpec(memory_space=space(kind)) for _, kind in spread],
         out_shape=[space(kind)(shape.shape, shape.dtype) for shape, kind in spread],
         scratch_shapes=buffers + [pltpu.VMEM(*item) for item in scratch] + [pltpu.SemaphoreType.DMA((64,))],
-        compiler_params=pltpu.CompilerParams(vmem_limit_bytes=VMEM),
+        compiler_params=pltpu.CompilerParams(vmem_limit_bytes=limit),
         cost_estimate=pl.CostEstimate(flops=flops, bytes_accessed=nbytes, transcendentals=0),
         name=name,
     )(ids, *(pltpu.with_memory_space_constraint(array, space(kind)) for array, kind in ins))
@@ -168,12 +172,11 @@
     first_half = jnp.where(feature < 64, 1.0, 0.0).astype(BF16)
     second_half = jnp.where(feature < 64, 0.0, 1.0).astype(BF16)
 
-    @pl.loop(*pairs)
-    def _(pair):
-        lanes = pl.ds(pl.multiple_of(pair * 128, 128), 128)
-        for seq in range(seqs):
-            rows = slice(seq * 128, seq * 128 + 128)
-            seen = jnp.broadcast_to(mask[:, seq : seq + 1], (256, 128)) > 0.5
+    for seq in range(seqs):
+        rows = slice(seq * 128, seq * 128 + 128)
+        seen = jnp.broadcast_to(mask[:, seq : seq + 1], (256, 128)) > 0.5
+        for pair in range(*pairs):
+            lanes = slice(pair * 128, pair * 128 + 128)
             scores = dot_t(two_heads(k[rows, lanes], halves), q[rows, lanes] * SCALE)
             scores = jnp.where(seen, scores, -1e30)
             parts = []
@@ -267,10 +270,11 @@
     rows, width = x.shape
     blocks = wu.shape[1] // width
     wide = (rows, width)
+    other_kind = FREE if layer == 0 else RAW
     return call(
         functools.partial(up_kernel, layer),
         sec,
-        [(x, x_kind), (ctx, NEAR), (wo, RAW), (wo_other, RAW), (wu, RAW), (wu_other, RAW), (small, FAR)],
+        [(x, x_kind), (ctx, NEAR), (wo, RAW), (wo_other, other_kind), (wu, RAW), (wu_other, other_kind), (small, FAR)],
         [
             (sds(wide, F32), BOTH),
             (sds((rows, 128), F32), FAR),
@@ -318,7 +322,7 @@
     return call(
         functools.partial(down_kernel, layer),
         sec,
-        [(act, NEAR), (wd, RAW), (wd_other, RAW), (hat, NEAR), (small, FAR)],
+        [(act, NEAR), (wd, RAW), (wd_other, FREE if layer == 0 else RAW), (hat, NEAR), (small, FAR)],
         [(sds(wide, BF16), y_kind), (sds(wide, F32), two_kind), (sds((rows, 128), F32), two_kind)],
         [((blocks, width, width), BF16), (wide, F32)],
         "down_forward",
@@ -910,7 +914,7 @@
             in_specs=[pl.BlockSpec(memory_space=pltpu.SMEM)] + [vmem] * n_in,
             out_specs=[vmem] * len(shapes),
             out_shape=shapes,
-            compiler_params=pltpu.CompilerParams(vmem_limit_bytes=VMEM),
+            compiler_params=pltpu.CompilerParams(vmem_limit_bytes=SPARE),
             name="join_sums",
         )(ids, *self.ins)
         return results[:n_out], dict(zip(ways, results[n_out:]))
@@ -1020,24 +1024,37 @@
 def sum_last(sums, chunk):
     whole, got = sums.use(chunk.kept[0]), sums.use(chunk.got["ends"])
     rows = chunk.rows
-    result = sums.result((rows,))
+    results = [sums.result((rows,))]
+    if chunk.partner is not None:
+        other = sums.use(chunk.partner.done[0])
+        results.append(sums.result((rows,)))
 
     def code(ids, ins, outs, sends):
-        @pl.when(ids[3] == 1)
-        def _():
-            outs[result][...] = ins[got][:rows]
-
-        @pl.when(ids[3] == 0)
-        def _():
-            outs[result][...] = ins[whole][...]
+        def put(value, outer):
+            if chunk.partner is None:
+                outs[results[0]][...] = value(slice(None))
+                return
+            for first, (to_value, to_other) in ((0, results), (1, results[::-1])):
+
+                @pl.when((ids[0] == first) & (ids[3] == outer))
+                def _():
+                    outs[to_value][...] = value(slice(None))
+                    outs[to_other][...] = ins[other][...]
+
+        if chunk.partner is None:
+            pl.when(ids[3] == 1)(lambda: put(lambda _: ins[got][:rows], 1))
+            pl.when(ids[3] == 0)(lambda: put(lambda _: ins[whole][...], 0))
+        else:
+            put(lambda _: ins[got][:rows], 1)
+            put(lambda _: ins[whole][...], 0)
 
     sums.code.append(code)
-    return [result]
+    return results
 
 
 class Chunk:
-    def __init__(self, line, send, keep):
-        self.line, self.send, self.keep = line, send, keep
+    def __init__(self, line, send, keep, partner):
+        self.line, self.send, self.keep, self.partner = line, send, keep, partner
         self.at, self.kept, self.got, self.sent, self.done = 0, [], {}, {}, None
         self.rows = send.shape[1]
         self.cut = split_at(self.rows)
@@ -1050,12 +1067,13 @@
         self.short = lax.axis_size("outer") == 4
         spot, place = lax.axis_index("inner"), lax.axis_index("outer")
         outside = (place == 0) | (place == lax.axis_size("outer") - 1)
-        self.ids = jnp.stack([lax.axis_index("section"), spot % 2, spot // 2, outside]).astype(jnp.int32)
+        self.ids = jnp.stack([lax.axis_index("section"), spot % 2, spot // 2, outside, spot]).astype(jnp.int32)
         self.chunks, self.made = [], {}
         self.sums = (sum_section, sum_first, sum_second, sum_ends, sum_middle, sum_last)
 
     def add(self, send, keep):
-        chunk = Chunk(self, send, keep)
+        count = len(self.chunks)
+        chunk = Chunk(self, send, keep, self.chunks[count - 3] if count >= 3 else None)
         self.chunks.append(chunk)
         return chunk
 
@@ -1080,11 +1098,11 @@
             if not self.square:
                 half = chunk.keep.astype(F32) + chunk.got["section"].astype(F32)
                 half = lax.psum_scatter(half.astype(BF16), "inner", scatter_dimension=0, tiled=False)
-                chunk.done = lax.psum(half, "outer")
+                chunk.done = [lax.psum(half, "outer")]
             elif chunk.at == 4 and not self.short:
-                chunk.done = lax.psum(chunk.kept[0], "outer")
+                chunk.done = [lax.psum(chunk.kept[0], "outer")]
             elif chunk.at == 7:
-                chunk.done = chunk.kept[0]
+                chunk.done = chunk.kept
         new = [chunk for chunk in self.chunks if chunk.at == 0]
         gots = {way: self.move(way, array) for way, array in sends.items()}
         arrived = [self.move("section", chunk.send) for chunk in new]
@@ -1107,7 +1125,122 @@
     def finish(self):
         while any(chunk.done is None for chunk in self.chunks):
             self.advance(self)
-        return [chunk.done for chunk in self.chunks]
+        pairs = []
+        for chunk in self.chunks[3:]:
+            if len(chunk.done) == 1:
+                two, one = chunk.partner.done[0], chunk.done[0]
+                mine, send = (jnp.where(self.ids[0] == 0, *item) for item in ((one, two), (two, one)))
+            else:
+                mine, send = chunk.done
+            pairs.append((mine, exchange(send, "section", 1)))
+        return pairs
+
+
+def assemble_kernel(sec, y_one, y_two, y_got, one, two_low, got, y_out, g_out, y, low, wide, sems):
+    move = Mover(sems)
+    first = sec[0] == 0
+    loads = [
+        move.choose(first, y_one.ref, y_got.ref, y.at[0]),
+        move.choose(first, y_got.ref, y_two.ref, y.at[1]),
+        move.choose(first, one.ref, got.ref, wide.at[0]),
+    ]
+    move.load(two_low.ref, low)
+    loads.append(move.last)
+    pl.when(first)(lambda: move.choose(first, got.ref, got.ref, wide.at[1]).wait())
+    ready(loads)
+    move.used += 1
+
+    @pl.when(jnp.logical_not(first))
+    def _():
+        wide[1] = low[...].astype(F32)
+
+    move.store(y, y_out.ref)
+    move.store(wide, g_out.ref)
+    move.finish()
+
+
+def assemble(sec, y_one, y_two, y_got, one, two_low, got):
+    flat = one.shape
+    return call(
+        assemble_kernel,
+        sec,
+        [(item, RAW) for item in (y_one, y_two, y_got, one, two_low, got)],
+        [(sds((2,) + flat, BF16), RAW), (sds((2,) + flat, F32), RAW)],
+        [((2,) + flat, BF16), (flat, BF16), ((2,) + flat, F32)],
+        "assemble",
+        1000,
+        10 << 20,
+    )
+
+
+class Rest:
+    def __init__(self, sec):
+        self.sec, self.made = sec, {}
+
+    def send(self, one, two_low):
+        low = two_low.astype(F32)
+        self.made["got"] = exchange(jnp.where(self.sec[0] == 0, low, one), "section", 1)
+
+    def assemble(self, y_one, y_two, one, two_low):
+        self.made["outs"] = assemble(self.sec, y_one, y_two, self.made["y"], one, two_low, self.made["got"])
+
+
+def last_kernel(ids, up_mine, up_got, mine, got, qkv, out, b_qv, b_out, gain, offset, b_up, b_down, w_up, sems):
+    move = Mover(sems)
+    up_wide = w_up.buffer.shape[1] // 2
+    for half, side in ((ids[0], up_mine), (1 - ids[0], up_got)):
+        w_up.buffer[:, pl.ds(pl.multiple_of(half * up_wide, up_wide), up_wide)] = side.buffer[...].astype(F32)
+    w_up.flush(move)
+    mine, got = mine.buffer, got.buffer
+    tall, wide = qkv.buffer.shape[0], out.buffer.shape[1] // 2
+    for half, side in ((ids[0], mine), (1 - ids[0], got)):
+        for part in range(4):
+            block = side[:tall, part * wide : part * wide + wide].astype(F32)
+            target, first = (qkv, 2 * part * wide) if part < 3 else (out, 0)
+            lanes = pl.ds(pl.multiple_of(first + half * wide, wide), wide)
+            target.buffer[:, lanes] = block
+    qkv.flush(move)
+    out.flush(move)
+    rows = mine[tall:, : 2 * wide].astype(F32)
+    own, other = (side[tall : tall + 1, 2 * wide :].astype(F32) for side in (mine, got))
+
+    def write(first_half, place):
+        left, right = (own, other) if first_half else (other, own)
+        span = slice(place * tall, place * tall + tall)
+        for row in range(2):
+            bias = jnp.concatenate([side[:, row * wide : row * wide + wide] for side in (left, right)], axis=1)
+            b_qv.buffer[row : row + 1, :] = bias[:, span]
+        b_out.buffer[...] = rows[10:11, span]
+        gain.buffer[0:1, :] = rows[8:9, span]
+        gain.buffer[1:2, :] = rows[0:1, span]
+        offset.buffer[0:1, :] = rows[9:10, span]
+        offset.buffer[1:2, :] = rows[1:2, span]
+        b_up.buffer[...] = rows[11 + place : 12 + place]
+        b_down.buffer[...] = rows[2:3, span]
+
+    for first_half in (True, False):
+        for place in range(2 * wide // tall):
+            here = (ids[0] == (0 if first_half else 1)) & (ids[4] == place)
+            pl.when(here)(functools.partial(write, first_half, place))
+    for item in (b_qv, b_out, gain, offset, b_up, b_down):
+        item.flush(move)
+    move.finish()
+
+
+def last(ids, up, attend, width, shards):
+    tall = width // shards
+    shapes = [(tall, 3 * width), (tall, width), (2, tall), (1, tall), (2, tall), (2, tall), (1, width), (1, tall)]
+    shapes.append((tall, 2 * up[0].shape[1]))
+    return call(
+        last_kernel,
+        ids,
+        [(item, NEAR) for item in (*up, *attend)],
+        [(sds(shape, F32), FAR) for shape in shapes],
+        [],
+        "last",
+        1000,
+        5 << 20,
+    )
 
 
 def local(
@@ -1150,6 +1283,7 @@
     line = Line(sec)
     two = Backward(line, 1, sec, cache_two, big, other, smalls[1], shards)
     one = Backward(line, 0, sec, cache_one, big, other, smalls[0], shards)
+    exchanged_y = exchange(jnp.where(section == 0, y_two, y_one), "section", 1)
     line.advance(two, lambda: two.down(gy))
     line.advance(two, two.up_first)
     line.advance(two, two.up_last)
@@ -1160,49 +1294,37 @@
     line.advance(one, one.attention)
     gx_one = one.made["gx"]
 
-    def gather(for_zero, for_one):
-        kept = jnp.where(section == 0, for_zero, for_one)
-        got = exchange(jnp.where(section == 0, for_one, for_zero), "section", 1)
-        return jnp.where(section == 0, kept, got), jnp.where(section == 0, got, kept)
-
-    activations = jnp.concatenate(gather(y_one, y_two), axis=0).reshape(seqs_local, length, width)
-    input_grads = jnp.concatenate(gather(gx_one, gx_two_low.astype(F32)), axis=0).reshape(
-        seqs_local, length, width
-    )
-    sums = line.finish()
-    down, up, attend = [gather(one, two) for one, two in zip(sums[3:], sums[:3])]
+    rest = Rest(sec)
+    rest.made["y"] = exchanged_y
+    for _ in range(3):
+        line.advance(line)
+    line.advance(rest, lambda: rest.send(gx_one, gx_two_low))
+    line.advance(rest, lambda: rest.assemble(y_one, y_two, gx_one, gx_two_low))
+    activations, input_grads = rest.made["outs"]
+    activations = activations.reshape(seqs_local, length, width)
+    input_grads = input_grads.reshape(seqs_local, length, width)
+    down, up, attend = line.finish()
+    g_w_qkv, g_w_out, g_b_qv, g_b_out, g_gain, g_offset, g_b_up, g_b_down, g_w_up = last(
+        line.ids, up, attend, width, shards
+    )
+    mine, got = down
+    down = (jnp.where(section == 0, mine, got), jnp.where(section == 0, got, mine))
     g_w_down = jnp.concatenate(
         [side[:, i * width : (i + 1) * width] for side in down for i in range(2)], axis=0
     ).T.astype(F32)
-    g_w_up = jnp.concatenate(up, axis=1).astype(F32)
-    part = width // 2
-    tall = width // shards
-    matrix = [side[:tall] for side in attend]
-    g_w_qkv = jnp.concatenate(
-        [side[:, i * part : (i + 1) * part] for i in range(3) for side in matrix], axis=1
-    ).astype(F32)
-    g_w_out = jnp.concatenate([side[:, 3 * part :] for side in matrix], axis=1).astype(F32)
-    rows = attend[0][tall:, :width]
-    b_q, b_v = [
-        jnp.concatenate([side[tall, width + i * part : width + (i + 1) * part] for side in attend]) for i in range(2)
-    ]
-    rows = jnp.concatenate([rows, b_q[None], b_v[None]], axis=0)
-    place = lax.axis_index("inner")
-    mine = lax.dynamic_slice_in_dim(rows, place * tall, tall, 1).astype(F32)
-    up_row = pick(rows[11 : 11 + blocks].reshape(shards, width * blocks // shards), place, 0).astype(F32)
     return (
         activations[None],
         input_grads[None],
         g_w_qkv[None],
-        mine[16:18][None],
+        g_b_qv[None],
         g_w_out[None],
-        mine[10][None],
-        jnp.stack([mine[8], mine[0]])[None],
-        jnp.stack([mine[9], mine[1]])[None],
+        g_b_out,
+        g_gain[None],
+        g_offset[None],
         g_w_up[None],
-        up_row[None],
+        g_b_up,
         g_w_down[None],
-        mine[2][None],
+        g_b_down,
     )
 
 

time: 340 us -> 322 us (0.947)
  other arithmetic: 22.7 us -> 6.17 us
  Pallas kernels: 155 us -> 160 us
  local copies, waits for them, and re-layouts: 18 us -> 14.5 us
    select_n x9 -> x3, other arithmetic: 6.75 us -> 0.31 us  [the longest x1 0.15 us: send(): jnp.where(self.sec[0] == 0, low, one)]
    pallas_call x13 -> x15, Pallas kernels: 141 us -> 147 us  [call(): pl.pallas_call(body, in_specs=[pl.BlockSpec(memory_space=pltpu.SMEM)] + [...]
    convert_element_type x5 -> x0, other arithmetic: 4.52 us -> none  [the longest x1 1.67 us: local(): g_w_up = jnp.concatenate(up, axis=1).astype(F32)]
    concatenate x5 -> x0, other arithmetic: 4.3 us -> none  [the longest x1 1.87 us: local(): jnp.concatenate(gather(gx_one, gx_two_low.astype(F32)), axis=0)]
    ppermute x32, starting transfers between devices: 23.6 us -> 20 us  [exchange(): return lax.ppermute(array, axis, [(i, i ^ bit) for i in range(length)])]
    unnamed x51 -> x42, local copies, waits for them, and re-layouts: 13.3 us -> 11 us
  transfers between devices with their start and end apart: 47 -> 47, of which waited for: 17 -> 20; matrix products, arithmetic and copies ran while one was open for 8% -> 4% of each run, Pallas kernels for 32% -> 34%
where the time goes in v5:
time: 322 us; the launch traced here: 317 us
  Pallas kernels  160 us (50%)
  waiting for transfers between devices  83.3 us (26%)
  starting transfers between devices  52 us (16%)
  local copies, waits for them, and re-layouts  14.5 us (5%)
  other arithmetic  6.17 us (2%)
    pallas_call x15, Pallas kernels, call(): pl.pallas_call(body, in_specs=[pl.BlockSpec(memory_space=pltpu.SMEM)] + [...  147 us
    ppermute x15, waiting for transfers between devices, move(): lax.ppermute(array, 'outer', [(0, 1), (1, 0), (2, 3), (3, 2)] if way == '...  60.4 us
    ppermute x15, starting transfers between devices, move(): lax.ppermute(array, 'outer', [(0, 1), (1, 0), (2, 3), (3, 2)] if way == '...  32 us
    ppermute x32, waiting for transfers between devices, exchange(): return lax.ppermute(array, axis, [(i, i ^ bit) for i in range(length)])  22.9 us
    ppermute x32, starting transfers between devices, exchange(): return lax.ppermute(array, axis, [(i, i ^ bit) for i in range(length)])  20 us
    pallas_call x12, Pallas kernels, run(): pl.pallas_call(kernel, in_specs=[pl.BlockSpec(memory_space=pltpu.SMEM)] +...  12.5 us
    unnamed x42, local copies, waits for them, and re-layouts  11 us
  transfers between devices with their start and end apart: 47, of which 20 were waited for; matrix products, arithmetic and copies ran while one was open for 4% of the time, Pallas kernels for 34%

profile of v5, /device:TPU:0, one launch (start us, length us, event | category | flops | bytes accessed | tf_op | source)
XLA Modules:
  0.0 317.2 jit_solution(11702917700287643912)
XLA Ops:
  1.7 1.4 reduce.3
  5.5 1.0 constant_dynamic-slice_fusion
  8.5 8.5 %attend_forward.2 = (bf16[512,768]{1,0:T(8,128)(2,1)}, bf16[512,768]{1,0:T(8,128)(2,1)}, bf16[512,768]{1,0:T(8,128)(2,1)}, f32[4,6,256,128]{3,2,1,0:T(8,128)}, b...) custom-call(s32[1]{0:T(128)} %bitcast.ids_ref, bf16[512,768]{1,0:T(8,128)(2,1)} %bitcast.46, ...), custom_call_target="tpu_custom_call" | custom-call | flops 2415919104 | bytes 12582912 | tf_op jit(solution)/shard_map/attend_forward/pallas_call | solution.py:153
  18.4 1.4 dynamic-slice_select_fusion
  19.8 12.4 %up_forward.2 = (f32[512,768]{1,0:T(8,128)S(1)}, f32[512,768]{1,0:T(8,128)}, f32[512,128]{1,0:T(8,128)}, bf16[768,512]{1,0:T(8,128)(2,1)}, bf16[4,512,768]{2,1,0...) custom-call(s32[1]{0:T(128)} %bitcast.ids_ref, bf16[512,768]{1,0:T(8,128)(2,1)} %bitcast.47, ...), custom_call_target="tpu_custom_call" | custom-call | flops 3019898880 | bytes 20971520 | tf_op jit(solution)/shard_map/up_forward/pallas_call | solution.py:153
  32.3 9.0 %down_forward.2 = (bf16[512,768]{1,0:T(8,128)(2,1)S(1)}, bf16[512,768]{1,0:T(8,128)(2,1)}, f32[512,768]{1,0:T(8,128)}, f32[512,128]{1,0:T(8,128)}) custom-call(s32[1]{0:T(128)} %bitcast.ids_ref, bf16[4,512,768]{2,1,0:T(8,128)(2,1)S(1)} %get-tuple-element.269.refs_0_, bf16[3072,768]{1,0:T(8,128)(2,1)} %bitcast.27, ...), custom_call_target="tpu_custom_call" | custom-call | flops 2415919104 | bytes 12582912 | tf_op jit(solution)/shard_map/down_forward/pallas_call | solution.py:153
  41.3 8.1 %attend_forward.3 = (bf16[512,768]{1,0:T(8,128)(2,1)}, bf16[512,768]{1,0:T(8,128)(2,1)}, bf16[512,768]{1,0:T(8,128)(2,1)}, f32[4,6,256,128]{3,2,1,0:T(8,128)}, b...) custom-call(s32[1]{0:T(128)} %bitcast.ids_ref, bf16[512,768]{1,0:T(8,128)(2,1)S(1)} %get-tuple-element.272.refs_0_, ...), custom_call_target="tpu_custom_call" | custom-call | flops 2415919104 | bytes 12582912 | tf_op jit(solution)/shard_map/attend_forward/pallas_call | solution.py:153
  49.4 11.9 %up_forward.3 = (f32[512,768]{1,0:T(8,128)S(1)}, f32[512,768]{1,0:T(8,128)}, f32[512,128]{1,0:T(8,128)}, bf16[768,512]{1,0:T(8,128)(2,1)}, bf16[4,512,768]{2,1,0:T(8,128)(2,1)S(1)}, /*index=5*/f32[4,512,768]{2,1,0:T(8,128)}) custom-call(s32[1]{0:T(128)} %bitcast.ids_ref, bf16[512,768]{1,0:T(8,128)(2,1)S(1)} %get-tuple-element.272.refs_0_, ...), custom_call_target="tpu_custom_call" | custom-call | flops 3019898880 | bytes 20971520 | tf_op jit(solution)/shard_map/up_forward/pallas_call | solution.py:153
  61.3 7.5 %down_forward.3 = (bf16[512,768]{1,0:T(8,128)(2,1)}, f32[512,768]{1,0:T(8,128)S(1)}, f32[512,128]{1,0:T(8,128)S(1)}) custom-call(s32[1]{0:T(128)} %bitcast.ids_ref, bf16[4,512,768]{2,1,0:T(8,128)(2,1)S(1)} %get-tuple-element.275.refs_0_.refs_4_, bf16[3072,768]{1,0:T(8,128)(2,1)} %bitcast.28, bf16[3072,768]{1,0:T(8,128)(2,1)} %copy-done.2, ...), custom_call_target="tpu_custom_call" | custom-call | flops 2415919104 | bytes 12582912 | tf_op jit(solution)/shard_map/down_forward/pallas_call | solution.py:153
  68.8 5.6 %down_grad.2 = (f32[512,768]{1,0:T(8,128)S(1)}, bf16[512,768]{1,0:T(8,128)(2,1)S(1)}, f32[8,768]{1,0:T(8,128)S(1)}, bf16[4,192,1536]{2,1,0:T(8,128)(2,1)S(1)}, bf16[4,192,1536]{2,1,0:T(8,128)(2,1)S(1)}) custom-call(s32[1]{0:T(128)} %bitcast.ids_ref, bf16[512,768]{1,0:T(8,128)(2,1)} %bitcast.49, f32[512,768]{1,0:T(8,128)S(1)} %get-tuple-element.277.refs_1_, ...), custom_call_target="tpu_custom_call" | custom-call | flops 2415919104 | bytes 14680064 | tf_op jit(solution)/shard_map/down_grad/pallas_call | solution.py:153
  74.5 1.4 copy-done.5
  75.9 8.7 %up_grad_first.1 = (f32[512,768]{1,0:T(8,128)S(1)}, f32[8,768]{1,0:T(8,128)S(1)}, bf16[4,192,1536]{2,1,0:T(8,128)(2,1)}) custom-call(s32[1]{0:T(128)} %bitcast.ids_ref, bf16[512,768]{1,0:T(8,128)(2,1)S(1)} %get-tuple-element.294.refs_0_, f32[512,768]{1,0:T(8,128)S(1)} %get-tuple-element.286.refs_1_, bf16[3072,768]{1,0:T(8,128)(2,1)} %bitcast.29, ...), custom_call_target="tpu_custom_call" | custom-call | flops 3623878656 | bytes 15728640 | tf_op jit(solution)/shard_map/up_grad_first/pallas_call | solution.py:153
  84.6 1.1 copy-done.9
  85.7 1.4 copy-done.7
  87.8 1.7 copy-done.6
  89.4 1.7 copy-done.8
  92.0 3.0 collective-permute-start.6
  94.9 1.5 collective-permute-start.7
  96.5 8.6 %up_grad_last.1 = (f32[512,768]{1,0:T(8,128)S(1)}, bf16[512,768]{1,0:T(8,128)(2,1)S(1)}, f32[8,768]{1,0:T(8,128)S(1)}, bf16[4,192,1536]{2,1,0:T(8,128)(2,1)S(1)}) custom-call(s32[1]{0:T(128)} %bitcast.ids_ref, bf16[512,768]{1,0:T(8,128)(2,1)S(1)} %get-tuple-element.294.refs_0_, f32[512,768]{1,0:T(8,128)S(1)} %copy-done.10, bf16[3072,768]{1,0:T(8,128)(2,1)} %bitcast.30, ...), custom_call_target="tpu_custom_call" | custom-call | flops 3623878656 | bytes 15728640 | tf_op jit(solution)/shard_map/up_grad_last/pallas_call | solution.py:153
  105.0 3.4 %collective-permute-done.6.refs_2_ = bf16[192,1536]{1,0:T(8,128)(2,1)S(1)} collective-permute-done((bf16[192,1536]{1,0:T(8,128)(2,1)S(1)}, bf16[192,1536]{1,0:T(8,128)(2,1)S(1)}, u32[]{:S(2)}, u32[]{:S(2)}) %collective-permute-start.6) | collective-permute-done | bytes 589856 | tf_op jit(solution)/shard_map/ppermute | solution.py:869
  108.4 1.5 collective-permute-done.7.refs_3_
  110.8 1.6 collective-permute-start.10
  112.9 17.8 %attend_grad.2 = (f32[512,768]{1,0:T(8,128)}, bf16[512,768]{1,0:T(8,128)(2,1)S(1)}, bf16[512,768]{1,0:T(8,128)(2,1)}, bf16[4,208,1536]{2,1,0:T(8,128)(2,1)S(1)}, bf16[4,208,1536]{2,1,0:T(8,128)(2,1)S(1)}) custom-call(s32[1]{0:T(128)} %bitcast.ids_ref, bf16[512,768]{1,0:T(8,128)(2,1)S(1)} %get-tuple-element.309.refs_0_, ...), custom_call_target="tpu_custom_call" | custom-call | flops 6039797760 | bytes 31457280 | tf_op jit(solution)/shard_map/attend_grad/pallas_call | solution.py:153
  131.3 1.3 collective-permute-done.9.refs_2_
  133.3 1.6 collective-permute-start.11
  136.0 6.8 %down_grad.3 = (f32[512,768]{1,0:T(8,128)S(1)}, bf16[512,768]{1,0:T(8,128)(2,1)S(1)}, f32[8,768]{1,0:T(8,128)S(1)}, bf16[4,192,1536]{2,1,0:T(8,128)(2,1)S(1)}, bf16[4,192,1536]{2,1,0:T(8,128)(2,1)S(1)}) custom-call(s32[1]{0:T(128)} %bitcast.ids_ref, bf16[512,768]{1,0:T(8,128)(2,1)S(1)} %get-tuple-element.332.refs_0_, f32[512,768]{1,0:T(8,128)} %get-tuple-element.333.refs_1_, ...), custom_call_target="tpu_custom_call" | custom-call | flops 2415919104 | bytes 14680064 | tf_op jit(solution)/shard_map/down_grad/pallas_call | solution.py:153
  142.8 1.2 collective-permute-done.12.refs_4_
  144.3 4.8 %collective-permute-done.11.refs_1_ = bf16[192,1536]{1,0:T(8,128)(2,1)S(1)} collective-permute-done((bf16[192,1536]{1,0:T(8,128)(2,1)S(1)}, bf16[192,1536]{1,0:T(8,128)(2,1)S(1)}, u32[]{:S(2)}, u32[]{:S(2)}) %collective-permute-start.11) | collective-permute-done | bytes 589856 | tf_op jit(solution)/shard_map/ppermute | solution.py:1085
  149.1 1.0 join_sums.15
  150.8 1.5 collective-permute-start.15
  153.8 15.2 %up_grad.1 = (f32[512,768]{1,0:T(8,128)S(1)}, bf16[512,768]{1,0:T(8,128)(2,1)S(1)}, f32[8,768]{1,0:T(8,128)S(1)}, bf16[4,192,1536]{2,1,0:T(8,128)(2,1)S(1)}, bf16[4,192,1536]{2,1,0:T(8,128)(2,1)S(1)}) custom-call(s32[1]{0:T(128)} %bitcast.ids_ref, bf16[512,768]{1,0:T(8,128)(2,1)S(1)} %get-tuple-element.352.refs_0_, ...), custom_call_target="tpu_custom_call" | custom-call | flops 7247757312 | bytes 31457280 | tf_op jit(solution)/shard_map/up_grad/pallas_call | solution.py:153
  169.1 1.0 join_sums.16
  170.2 1.6 collective-permute-start.23
  171.7 1.4 collective-permute-start.22
  173.2 4.5 %collective-permute-start.20 = (bf16[192,1536]{1,0:T(8,128)(2,1)S(1)}, bf16[192,1536]{1,0:T(8,128)(2,1)S(1)}, u32[]{:S(2)}, u32[]{:S(2)}) collective-permute-start(bf16[192,1536]{1,0:T(8,128)(2,1)S(1)} %get-tuple-element.400), channel_id=1, source_target_pairs={{0,1},{1,0},{2,3},{3,2},{4,5},{5,4},{6,7},{7,6},{8,9},{9,8},{10,11... | collective-permute-start | bytes 1769480 | tf_op jit(solution)/shard_map/ppermute | solution.py:1085
  177.6 0.9 collective-permute-start.21
  178.6 17.6 %attend_grad.3 = (f32[512,768]{1,0:T(8,128)}, bf16[512,768]{1,0:T(8,128)(2,1)}, bf16[4,208,1536]{2,1,0:T(8,128)(2,1)S(1)}, bf16[4,208,1536]{2,1,0:T(8,128)(2,1)S(1)}) custom-call(s32[1]{0:T(128)} %bitcast.ids_ref, bf16[512,768]{1,0:T(8,128)(2,1)S(1)} %get-tuple-element.378.refs_0_, bf16[768,512]{1,0:T(8,128)(2,1)} %get-tuple-element.381.refs_1_, ...), custom_call_target="tpu_custom_call" | custom-call | flops 6039797760 | bytes 31457280 | tf_op jit(solution)/shard_map/attend_grad/pallas_call | solution.py:153
  196.3 1.1 join_sums.17
  198.7 3.3 %collective-permute-start.27 = (bf16[208,1536]{1,0:T(8,128)(2,1)S(1)}, bf16[208,1536]{1,0:T(8,128)(2,1)S(1)}, u32[]{:S(2)}, u32[]{:S(2)}) collective-permute-start(bf16[208,1536]{1,0:T(8,128)(2,1)S(1)} %get-tuple-element.420), channel_id=1, source_target_pairs={{0,1},{1,0},{2,3},{3,2},{4,5},{5,4},{6,7},{7,6},{8,9},{9,8},{10,11... | collective-permute-start | bytes 1916936 | tf_op jit(solution)/shard_map/ppermute | solution.py:1085
  201.9 14.5 %collective-permute-done.27.refs_1_ = bf16[208,1536]{1,0:T(8,128)(2,1)S(1)} collective-permute-done((bf16[208,1536]{1,0:T(8,128)(2,1)S(1)}, bf16[208,1536]{1,0:T(8,128)(2,1)S(1)}, u32[]{:S(2)}, u32[]{:S(2)}) %collective-permute-start.27) | collective-permute-done | bytes 639008 | tf_op jit(solution)/shard_map/ppermute | solution.py:1085
  216.4 3.2 collective-permute-done.28.refs_5_
  219.9 1.1 join_sums.18
  221.1 1.5 collective-permute-start.33
  223.8 4.5 %collective-permute-start.31 = (bf16[192,1536]{1,0:T(8,128)(2,1)S(1)}, bf16[192,1536]{1,0:T(8,128)(2,1)S(1)}, u32[]{:S(2)}, u32[]{:S(2)}) collective-permute-start(bf16[192,1536]{1,0:T(8,128)(2,1)S(1)} %get-tuple-element.435), channel_id=1, source_target_pairs={{0,1},{1,0},{2,3},{3,2},{4,5},{5,4},{6,7},{7,6},{8,9},{9,8},{10,11... | collective-permute-start | bytes 1769480 | tf_op jit(solution)/shard_map/ppermute | solution.py:1085
  228.5 11.8 %collective-permute-done.31.refs_3_ = bf16[192,1536]{1,0:T(8,128)(2,1)S(1)} collective-permute-done((bf16[192,1536]{1,0:T(8,128)(2,1)S(1)}, bf16[192,1536]{1,0:T(8,128)(2,1)S(1)}, u32[]{:S(2)}, u32[]{:S(2)}) %collective-permute-start.31) | collective-permute-done | bytes 589856 | tf_op jit(solution)/shard_map/ppermute | solution.py:1085
  240.3 2.9 collective-permute-done.34.refs_7_
  243.2 1.0 collective-permute-done.33.refs_6_
  245.1 2.5 collective-permute-start.35
  249.0 1.3 collective-permute-start.38
  250.4 5.0 %collective-permute-done.37.refs_7_ = bf16[96,1536]{1,0:T(8,128)(2,1)S(1)} collective-permute-done((bf16[96,1536]{1,0:T(8,128)(2,1)S(1)}, bf16[96,1536]{1,0:T(8,128)(2,1)S(1)}, u32[]{:S(2)}, u32[]{:S(2)}) %collective-permute-start.37) | collective-permute-done | bytes 294944 | tf_op jit(solution)/shard_map/ppermute | solution.py:869
  255.5 1.4 collective-permute-done.38.refs_8_
  256.9 3.7 %collective-permute-done.35.refs_1_ = bf16[208,1536]{1,0:T(8,128)(2,1)S(1)} collective-permute-done((bf16[208,1536]{1,0:T(8,128)(2,1)S(1)}, bf16[208,1536]{1,0:T(8,128)(2,1)S(1)}, u32[]{:S(2)}, u32[]{:S(2)}) %collective-permute-start.35) | collective-permute-done | bytes 639008 | tf_op jit(solution)/shard_map/ppermute | solution.py:1085
  261.5 2.7 collective-permute-start.39
  264.9 11.3 %collective-permute-done.39.refs_1_ = bf16[208,1536]{1,0:T(8,128)(2,1)S(1)} collective-permute-done((bf16[208,1536]{1,0:T(8,128)(2,1)S(1)}, bf16[208,1536]{1,0:T(8,128)(2,1)S(1)}, u32[]{:S(2)}, u32[]{:S(2)}) %collective-permute-start.39) | collective-permute-done | bytes 639008 | tf_op jit(solution)/shard_map/ppermute | solution.py:1085
  277.7 4.7 %collective-permute-start.41 = (bf16[192,1536]{1,0:T(8,128)(2,1)S(1)}, bf16[192,1536]{1,0:T(8,128)(2,1)S(1)}, u32[]{:S(2)}, u32[]{:S(2)}) collective-permute-start(bf16[192,1536]{1,0:T(8,128)(2,1)S(1)} %get-tuple-element.470), channel_id=1, source_target_pairs={{0,1},{1,0},{2,3},{3,2},{4,5},{5,4},{6,7},{7,6},{8,9},{9,8},{10,11... | collective-permute-start | bytes 1769480 | tf_op jit(solution)/shard_map/ppermute | solution.py:1085
  282.4 5.4 %assemble.1 = (bf16[2,512,768]{2,1,0:T(8,128)(2,1)}, f32[2,512,768]{2,1,0:T(8,128)}) custom-call(s32[1]{0:T(128)} %bitcast.ids_ref, bf16[512,768]{1,0:T(8,128)(2,1)} %get-tuple-element.313.refs_3_.refs_0_, bf16[512,768]{1,0:T(8,128)(2,1)} %get-tuple-element.406.refs_1_, bf16[512,768]{1,0:T(8,128)(2,1)} %copy-done.16, f32[512,768]{1,0:T(8,128)} %get-tuple-element.405.refs_3_, ...), custom_call_target="tpu_custom_call" | custom-call | flops 1000 | bytes 10485760 | tf_op jit(solution)/shard_map/assemble/pallas_call | solution.py:153
  287.8 4.5 %collective-permute-done.41.refs_1_ = bf16[192,1536]{1,0:T(8,128)(2,1)S(1)} collective-permute-done((bf16[192,1536]{1,0:T(8,128)(2,1)S(1)}, bf16[192,1536]{1,0:T(8,128)(2,1)S(1)}, u32[]{:S(2)}, u32[]{:S(2)}) %collective-permute-start.41) | collective-permute-done | bytes 589856 | tf_op jit(solution)/shard_map/ppermute | solution.py:1085
  292.3 1.5 join_sums.22
  293.8 2.2 collective-permute-start.44
  296.5 9.7 %collective-permute-done.44.refs_1_ = bf16[208,1536]{1,0:T(8,128)(2,1)S(1)} collective-permute-done((bf16[208,1536]{1,0:T(8,128)(2,1)S(1)}, bf16[208,1536]{1,0:T(8,128)(2,1)S(1)}, u32[]{:S(2)}, u32[]{:S(2)}) %collective-permute-start.44) | collective-permute-done | bytes 639008 | tf_op jit(solution)/shard_map/ppermute | solution.py:1085
  306.3 1.5 join_sums.23
  307.9 1.6 convert_bitcast_fusion
  309.5 3.2 copy.29
  312.7 4.1 %last.1 = (f32[192,2304]{1,0:T(8,128)}, f32[192,768]{1,0:T(8,128)}, f32[2,192]{1,0:T(2,128)}, f32[1,192]{1,0:T(1,128)}, f32[2,192]{1,0:T(2,128)}, /*index=5*/f32...) custom-call(s32[5]{0:T(128)S(1)} %stack.24.ids_ref, ...), custom_call_target="tpu_custom_call" | custom-call | flops 1000 | bytes 5242880 | tf_op jit(solution)/shard_map/last/pallas_call | solution.py:153
  (119 shorter events, 23.8 us)
Async XLA Ops:
  0.6 4.9 %copy-start = (bf16[8,128,768]{2,1,0:T(8,128)(2,1)S(1)}, bf16[8,128,768]{2,1,0:T(8,128)(2,1)}, u32[]{:S(2)}) copy-start(bf16[8,128,768]{2,1,0:T(8,128)(2,1)} %param.14) | copy-start | bytes 4718596
  0.7 7.4 %collective-permute-start = (bf16[768,2304]{1,0:T(8,128)(2,1)}, bf16[768,2304]{1,0:T(8,128)(2,1)}, u32[]{:S(2)}, u32[]{:S(2)}) collective-permute-start(bf16[768,2304]{1,0:T(8,128)(2,1)} %bitcast.55), channel_id=1, source_target_pairs={{0,16},{16,0},{1,17},{17,1},{2,18},{18,2},{3,19},{19,3},{4,20},{20... | collective-permute-start | bytes 10616840 | tf_op jit(solution)/shard_map/ppermute | solution.py:869
  3.9 3.5 %collective-permute-start.1 = (f32[16,768]{1,0:T(8,128)S(1)}, f32[16,768]{1,0:T(8,128)S(1)}, u32[]{:S(2)}, u32[]{:S(2)}) collective-permute-start(f32[16,768]{1,0:T(8,128)S(1)} %concatenate.9), channel_id=1, source_target_pairs={{0,16},{16,0},{1,17},{17,1},{2,18},{18,2},{3,19},{19,3},{4,20},{20... | collective-permute-start | bytes 147464 | tf_op jit(solution)/shard_map/ppermute | solution.py:869
  7.4 10.5 %slice-start = ((s8[4718592]{0:T(1024)(128)(4,1)}), s8[4194304]{0:T(1024)(128)(4,1)S(1)}, s32[]{:S(2)}) async-start(s8[4718592]{0:T(1024)(128)(4,1)} %bitcast.32), calls=%async_computation | async-start | bytes 8388608
  8.0 9.9 %collective-permute-start.3 = (bf16[768,3072]{1,0:T(8,128)(2,1)}, bf16[768,3072]{1,0:T(8,128)(2,1)S(1)}, u32[]{:S(2)}, u32[]{:S(2)}) collective-permute-start(bf16[768,3072]{1,0:T(8,128)(2,1)} %bitcast.35), channel_id=1, source_target_pairs={{0,16},{16,0},{1,17},{17,1},{2,18},{18,2},{3,19},{19,3},{4,20},{20... | collective-permute-start | bytes 14155784 | tf_op jit(solution)/shard_map/ppermute | solution.py:869
  8.5 9.4 %collective-permute-start.2 = (bf16[768,768]{1,0:T(8,128)(2,1)}, bf16[768,768]{1,0:T(8,128)(2,1)S(1)}, u32[]{:S(2)}, u32[]{:S(2)}) collective-permute-start(bf16[768,768]{1,0:T(8,128)(2,1)} %bitcast.41), channel_id=1, source_target_pairs={{0,16},{16,0},{1,17},{17,1},{2,18},{18,2},{3,19},{19,3},{4,20},{20... | collective-permute-start | bytes 3538952 | tf_op jit(solution)/shard_map/ppermute | solution.py:869
  8.5 9.4 %slice-start.1 = ((s8[4718592]{0:T(1024)(128)(4,1)}), s8[524288]{0:T(1024)(128)(4,1)S(1)}, s32[]{:S(2)}) async-start(s8[4718592]{0:T(1024)(128)(4,1)} %bitcast.32), calls=%async_computation.1 | async-start | bytes 1048576
  8.5 9.8 %copy-start.17 = (bf16[8,128,768]{2,1,0:T(8,128)(2,1)S(1)}, bf16[8,128,768]{2,1,0:T(8,128)(2,1)}, u32[]{:S(2)}) copy-start(bf16[8,128,768]{2,1,0:T(8,128)(2,1)} %param.17) | copy-start | bytes 4718596
  17.9 14.3 %copy-start.4 = (bf16[768,768]{1,0:T(8,128)(2,1)}, bf16[768,768]{1,0:T(8,128)(2,1)S(1)}, u32[]{:S(2)}) copy-start(bf16[768,768]{1,0:T(8,128)(2,1)S(1)} %collective-permute-done.2.refs_3_.refs_9_) | copy-start | bytes 3538948
  17.9 14.3 %copy-start.3 = (bf16[768,3072]{1,0:T(8,128)(2,1)}, bf16[768,3072]{1,0:T(8,128)(2,1)S(1)}, u32[]{:S(2)}) copy-start(bf16[768,3072]{1,0:T(8,128)(2,1)S(1)} %collective-permute-done.3.refs_5_.refs_7_) | copy-start | bytes 14155780
  17.9 14.3 %collective-permute-start.4 = (bf16[3072,768]{1,0:T(8,128)(2,1)S(1)}, bf16[3072,768]{1,0:T(8,128)(2,1)S(1)}, u32[]{:S(2)}, u32[]{:S(2)}) collective-permute-start(bf16[3072,768]{1,0:T(8,128)(2,1)S(1)} %bitcast.34), channel_id=1, source_target_pairs={{0,16},{16,0},{1,17},{17,1},{2,18},{18,2},{3,19},{19,3},{4,20},{20... | collective-permute-start | bytes 14155784 | tf_op jit(solution)/shard_map/ppermute | solution.py:869
  32.3 9.0 %copy-start.2 = (bf16[3072,768]{1,0:T(8,128)(2,1)}, bf16[3072,768]{1,0:T(8,128)(2,1)S(1)}, u32[]{:S(2)}) copy-start(bf16[3072,768]{1,0:T(8,128)(2,1)S(1)} %collective-permute-done.4.refs_2_.refs_3_) | copy-start | bytes 14155780
  75.9 9.8 %collective-permute-start.5 = (bf16[4,192,1536]{2,1,0:T(8,128)(2,1)S(1)}, bf16[4,192,1536]{2,1,0:T(8,128)(2,1)S(1)}, u32[]{:S(2)}, u32[]{:S(2)}) collective-permute-start(bf16[4,192,1536]{2,1,0:T(8,128)(2,1)S(1)} %get-tuple-element.293), channel_id=1, source_target_pairs={{0,16},{16,0},{1,17},{17,1},{2,18},{18,2},{3,19},{19,3},{4,20},{20... | collective-permute-start | bytes 7077896 | tf_op jit(solution)/shard_map/ppermute | solution.py:869
  87.2 22.7 %collective-permute-start.8 = (bf16[4,192,1536]{2,1,0:T(8,128)(2,1)}, bf16[4,192,1536]{2,1,0:T(8,128)(2,1)S(1)}, u32[]{:S(2)}, u32[]{:S(2)}) collective-permute-start(bf16[4,192,1536]{2,1,0:T(8,128)(2,1)} %get-tuple-element.308), channel_id=1, source_target_pairs={{0,16},{16,0},{1,17},{17,1},{2,18},{18,2},{3,19},{19,3},{4,20},{20... | collective-permute-start | bytes 7077896 | tf_op jit(solution)/shard_map/ppermute | solution.py:869
  87.8 1.7 copy-start.6
  89.4 1.7 copy-start.8
  91.1 5.4 %copy-start.10 = (f32[512,768]{1,0:T(8,128)S(1)}, f32[512,768]{1,0:T(8,128)}, u32[]{:S(2)}) copy-start(f32[512,768]{1,0:T(8,128)} %copy-done.9) | copy-start | bytes 4718596
  92.0 16.5 %collective-permute-start.6 = (bf16[192,1536]{1,0:T(8,128)(2,1)S(1)}, bf16[192,1536]{1,0:T(8,128)(2,1)S(1)}, u32[]{:S(2)}, u32[]{:S(2)}) collective-permute-start(bf16[192,1536]{1,0:T(8,128)(2,1)S(1)} %get-tuple-element.306), channel_id=1, source_target_pairs={{0,4},{4,0},{8,12},{12,8},{1,5},{5,1},{9,13},{13,9},{2,6},{6,2},{1... | collective-permute-start | bytes 1769480 | tf_op jit(solution)/shard_map/ppermute | solution.py:869
  94.9 15.0 %collective-permute-start.7 = (bf16[192,1536]{1,0:T(8,128)(2,1)S(1)}, bf16[192,1536]{1,0:T(8,128)(2,1)S(1)}, u32[]{:S(2)}, u32[]{:S(2)}) collective-permute-start(bf16[192,1536]{1,0:T(8,128)(2,1)S(1)} %get-tuple-element.307), channel_id=1, source_target_pairs={{0,8},{4,12},{8,0},{12,4},{1,9},{5,13},{9,1},{13,5},{2,10},{6,14},... | collective-permute-start | bytes 1769480 | tf_op jit(solution)/shard_map/ppermute | solution.py:869
  110.8 20.4 %collective-permute-start.10 = (bf16[288,1536]{1,0:T(8,128)(2,1)S(1)}, bf16[288,1536]{1,0:T(8,128)(2,1)S(1)}, u32[]{:S(2)}, u32[]{:S(2)}) collective-permute-start(bf16[288,1536]{1,0:T(8,128)(2,1)S(1)} %get-tuple-element.330), channel_id=1, source_target_pairs={{0,8},{4,12},{8,0},{12,4},{1,9},{5,13},{9,1},{13,5},{2,10},{6,14},... | collective-permute-start | bytes 2654216 | tf_op jit(solution)/shard_map/ppermute | solution.py:869
  112.4 20.1 %collective-permute-start.9 = (bf16[288,1536]{1,0:T(8,128)(2,1)S(1)}, bf16[288,1536]{1,0:T(8,128)(2,1)S(1)}, u32[]{:S(2)}, u32[]{:S(2)}) collective-permute-start(bf16[288,1536]{1,0:T(8,128)(2,1)S(1)} %get-tuple-element.329), channel_id=1, source_target_pairs={{0,4},{4,0},{8,12},{12,8},{1,5},{5,1},{9,13},{13,9},{2,6},{6,2},{1... | collective-permute-start | bytes 2654216 | tf_op jit(solution)/shard_map/ppermute | solution.py:869
  132.5 16.6 %collective-permute-start.14 = (bf16[4,208,1536]{2,1,0:T(8,128)(2,1)S(1)}, bf16[4,208,1536]{2,1,0:T(8,128)(2,1)S(1)}, u32[]{:S(2)}, u32[]{:S(2)}) collective-permute-start(bf16[4,208,1536]{2,1,0:T(8,128)(2,1)S(1)} %get-tuple-element.351), channel_id=1, source_target_pairs={{0,16},{16,0},{1,17},{17,1},{2,18},{18,2},{3,19},{19,3},{4,20},{20... | collective-permute-start | bytes 7667720 | tf_op jit(solution)/shard_map/ppermute | solution.py:869
  133.3 15.8 %collective-permute-start.11 = (bf16[192,1536]{1,0:T(8,128)(2,1)S(1)}, bf16[192,1536]{1,0:T(8,128)(2,1)S(1)}, u32[]{:S(2)}, u32[]{:S(2)}) collective-permute-start(bf16[192,1536]{1,0:T(8,128)(2,1)S(1)} %get-tuple-element.348), channel_id=1, source_target_pairs={{0,1},{1,0},{2,3},{3,2},{4,5},{5,4},{6,7},{7,6},{8,9},{9,8},{10,11... | collective-permute-start | bytes 1769480 | tf_op jit(solution)/shard_map/ppermute | solution.py:1085
  134.9 9.1 %collective-permute-start.12 = (bf16[96,1536]{1,0:T(8,128)(2,1)S(1)}, bf16[96,1536]{1,0:T(8,128)(2,1)S(1)}, u32[]{:S(2)}, u32[]{:S(2)}) collective-permute-start(bf16[96,1536]{1,0:T(8,128)(2,1)S(1)} %get-tuple-element.349), channel_id=1, source_target_pairs={{0,4},{4,0},{8,12},{12,8},{1,5},{5,1},{9,13},{13,9},{2,6},{6,2},{1... | collective-permute-start | bytes 884744 | tf_op jit(solution)/shard_map/ppermute | solution.py:869
  135.5 8.9 %collective-permute-start.13 = (bf16[96,1536]{1,0:T(8,128)(2,1)S(1)}, bf16[96,1536]{1,0:T(8,128)(2,1)S(1)}, u32[]{:S(2)}, u32[]{:S(2)}) collective-permute-start(bf16[96,1536]{1,0:T(8,128)(2,1)S(1)} %get-tuple-element.350), channel_id=1, source_target_pairs={{0,8},{4,12},{8,0},{12,4},{1,9},{5,13},{9,1},{13,5},{2,10},{6,14},... | collective-permute-start | bytes 884744 | tf_op jit(solution)/shard_map/ppermute | solution.py:869
  149.1 19.9 %collective-permute-start.19 = (bf16[4,192,1536]{2,1,0:T(8,128)(2,1)S(1)}, bf16[4,192,1536]{2,1,0:T(8,128)(2,1)S(1)}, u32[]{:S(2)}, u32[]{:S(2)}) collective-permute-start(bf16[4,192,1536]{2,1,0:T(8,128)(2,1)S(1)} %get-tuple-element.377), channel_id=1, source_target_pairs={{0,16},{16,0},{1,17},{17,1},{2,18},{18,2},{3,19},{19,3},{4,20},{20... | collective-permute-start | bytes 7077896 | tf_op jit(solution)/shard_map/ppermute | solution.py:869
  150.1 18.9 %collective-permute-start.17 = (bf16[224,1536]{1,0:T(8,128)(2,1)S(1)}, bf16[224,1536]{1,0:T(8,128)(2,1)S(1)}, u32[]{:S(2)}, u32[]{:S(2)}) collective-permute-start(bf16[224,1536]{1,0:T(8,128)(2,1)S(1)} %get-tuple-element.375), channel_id=1, source_target_pairs={{0,4},{4,0},{8,12},{12,8},{1,5},{5,1},{9,13},{13,9},{2,6},{6,2},{1... | collective-permute-start | bytes 2064392 | tf_op jit(solution)/shard_map/ppermute | solution.py:869
  150.8 18.2 %collective-permute-start.15 = (bf16[192,1536]{1,0:T(8,128)(2,1)S(1)}, bf16[192,1536]{1,0:T(8,128)(2,1)S(1)}, u32[]{:S(2)}, u32[]{:S(2)}) collective-permute-start(bf16[192,1536]{1,0:T(8,128)(2,1)S(1)} %get-tuple-element.373), channel_id=1, source_target_pairs={{0,1},{1,0},{2,3},{3,2},{4,5},{5,4},{6,7},{7,6},{8,9},{9,8},{10,11... | collective-permute-start | bytes 1769480 | tf_op jit(solution)/shard_map/ppermute | solution.py:1085
  152.3 16.7 %collective-permute-start.16 = (bf16[192,1536]{1,0:T(8,128)(2,1)S(1)}, bf16[192,1536]{1,0:T(8,128)(2,1)S(1)}, u32[]{:S(2)}, u32[]{:S(2)}) collective-permute-start(bf16[192,1536]{1,0:T(8,128)(2,1)S(1)} %get-tuple-element.374.refs_0_), channel_id=1, source_target_pairs={{1,2},{2,1},{5,6},{6,5},{9,10},{10,9},{13,14},{14,13},{17,18},{18,... | collective-permute-start | bytes 1769480 | tf_op jit(solution)/shard_map/ppermute | solution.py:1085
  153.2 15.8 %collective-permute-start.18 = (bf16[192,1536]{1,0:T(8,128)(2,1)S(1)}, bf16[192,1536]{1,0:T(8,128)(2,1)S(1)}, u32[]{:S(2)}, u32[]{:S(2)}) collective-permute-start(bf16[192,1536]{1,0:T(8,128)(2,1)S(1)} %get-tuple-element.376), channel_id=1, source_target_pairs={{0,8},{4,12},{8,0},{12,4},{1,9},{5,13},{9,1},{13,5},{2,10},{6,14},... | collective-permute-start | bytes 1769480 | tf_op jit(solution)/shard_map/ppermute | solution.py:869
  169.0 27.2 %collective-permute-start.24 = (bf16[4,192,1536]{2,1,0:T(8,128)(2,1)S(1)}, bf16[4,192,1536]{2,1,0:T(8,128)(2,1)S(1)}, u32[]{:S(2)}, u32[]{:S(2)}) collective-permute-start(bf16[4,192,1536]{2,1,0:T(8,128)(2,1)S(1)} %get-tuple-element.404), channel_id=1, source_target_pairs={{0,16},{16,0},{1,17},{17,1},{2,18},{18,2},{3,19},{19,3},{4,20},{20... | collective-permute-start | bytes 7077896 | tf_op jit(solution)/shard_map/ppermute | solution.py:869
  170.2 26.1 %collective-permute-start.23 = (bf16[304,1536]{1,0:T(8,128)(2,1)S(1)}, bf16[304,1536]{1,0:T(8,128)(2,1)S(1)}, u32[]{:S(2)}, u32[]{:S(2)}) collective-permute-start(bf16[304,1536]{1,0:T(8,128)(2,1)S(1)} %get-tuple-element.403), channel_id=1, source_target_pairs={{0,8},{4,12},{8,0},{12,4},{1,9},{5,13},{9,1},{13,5},{2,10},{6,14},... | collective-permute-start | bytes 2801672 | tf_op jit(solution)/shard_map/ppermute | solution.py:869
  171.7 24.5 %collective-permute-start.22 = (bf16[288,1536]{1,0:T(8,128)(2,1)S(1)}, bf16[288,1536]{1,0:T(8,128)(2,1)S(1)}, u32[]{:S(2)}, u32[]{:S(2)}) collective-permute-start(bf16[288,1536]{1,0:T(8,128)(2,1)S(1)} %get-tuple-element.402), channel_id=1, source_target_pairs={{0,4},{4,0},{8,12},{12,8},{1,5},{5,1},{9,13},{13,9},{2,6},{6,2},{1... | collective-permute-start | bytes 2654216 | tf_op jit(solution)/shard_map/ppermute | solution.py:869
  173.2 23.0 %collective-permute-start.20 = (bf16[192,1536]{1,0:T(8,128)(2,1)S(1)}, bf16[192,1536]{1,0:T(8,128)(2,1)S(1)}, u32[]{:S(2)}, u32[]{:S(2)}) collective-permute-start(bf16[192,1536]{1,0:T(8,128)(2,1)S(1)} %get-tuple-element.400), channel_id=1, source_target_pairs={{0,1},{1,0},{2,3},{3,2},{4,5},{5,4},{6,7},{7,6},{8,9},{9,8},{10,11... | collective-permute-start | bytes 1769480 | tf_op jit(solution)/shard_map/ppermute | solution.py:1085
  177.6 18.6 %collective-permute-start.21 = (bf16[192,1536]{1,0:T(8,128)(2,1)S(1)}, bf16[192,1536]{1,0:T(8,128)(2,1)S(1)}, u32[]{:S(2)}, u32[]{:S(2)}) collective-permute-start(bf16[192,1536]{1,0:T(8,128)(2,1)S(1)} %get-tuple-element.401.refs_2_), channel_id=1, source_target_pairs={{1,2},{2,1},{5,6},{6,5},{9,10},{10,9},{13,14},{14,13},{17,18},{18,... | collective-permute-start | bytes 1769480 | tf_op jit(solution)/shard_map/ppermute | solution.py:1085
  196.3 23.7 %collective-permute-start.30 = (bf16[4,208,1536]{2,1,0:T(8,128)(2,1)S(1)}, bf16[4,208,1536]{2,1,0:T(8,128)(2,1)S(1)}, u32[]{:S(2)}, u32[]{:S(2)}) collective-permute-start(bf16[4,208,1536]{2,1,0:T(8,128)(2,1)S(1)} %get-tuple-element.423), channel_id=1, source_target_pairs={{0,16},{16,0},{1,17},{17,1},{2,18},{18,2},{3,19},{19,3},{4,20},{20... | collective-permute-start | bytes 7667720 | tf_op jit(solution)/shard_map/ppermute | solution.py:869
  197.5 22.1 %collective-permute-start.28 = (bf16[288,1536]{1,0:T(8,128)(2,1)S(1)}, bf16[288,1536]{1,0:T(8,128)(2,1)S(1)}, u32[]{:S(2)}, u32[]{:S(2)}) collective-permute-start(bf16[288,1536]{1,0:T(8,128)(2,1)S(1)} %get-tuple-element.421), channel_id=1, source_target_pairs={{0,4},{4,0},{8,12},{12,8},{1,5},{5,1},{9,13},{13,9},{2,6},{6,2},{1... | collective-permute-start | bytes 2654216 | tf_op jit(solution)/shard_map/ppermute | solution.py:869
  198.2 21.8 %collective-permute-start.29 = (bf16[288,1536]{1,0:T(8,128)(2,1)S(1)}, bf16[288,1536]{1,0:T(8,128)(2,1)S(1)}, u32[]{:S(2)}, u32[]{:S(2)}) collective-permute-start(bf16[288,1536]{1,0:T(8,128)(2,1)S(1)} %get-tuple-element.422), channel_id=1, source_target_pairs={{0,8},{4,12},{8,0},{12,4},{1,9},{5,13},{9,1},{13,5},{2,10},{6,14},... | collective-permute-start | bytes 2654216 | tf_op jit(solution)/shard_map/ppermute | solution.py:869
  198.7 17.8 %collective-permute-start.27 = (bf16[208,1536]{1,0:T(8,128)(2,1)S(1)}, bf16[208,1536]{1,0:T(8,128)(2,1)S(1)}, u32[]{:S(2)}, u32[]{:S(2)}) collective-permute-start(bf16[208,1536]{1,0:T(8,128)(2,1)S(1)} %get-tuple-element.420), channel_id=1, source_target_pairs={{0,1},{1,0},{2,3},{3,2},{4,5},{5,4},{6,7},{7,6},{8,9},{9,8},{10,11... | collective-permute-start | bytes 1916936 | tf_op jit(solution)/shard_map/ppermute | solution.py:1085
  219.9 8.3 %copy-start.11 = (f32[512,768]{1,0:T(8,128)S(1)}, f32[512,768]{1,0:T(8,128)}, u32[]{:S(2)}) copy-start(f32[512,768]{1,0:T(8,128)} %get-tuple-element.405.refs_3_) | copy-start | bytes 4718596
  219.9 8.3 %copy-start.14 = (bf16[512,768]{1,0:T(8,128)(2,1)S(1)}, bf16[512,768]{1,0:T(8,128)(2,1)}, u32[]{:S(2)}) copy-start(bf16[512,768]{1,0:T(8,128)(2,1)} %get-tuple-element.331.refs_4_) | copy-start | bytes 2359300
  221.1 23.1 %collective-permute-start.33 = (bf16[320,1536]{1,0:T(8,128)(2,1)S(1)}, bf16[320,1536]{1,0:T(8,128)(2,1)S(1)}, u32[]{:S(2)}, u32[]{:S(2)}) collective-permute-start(bf16[320,1536]{1,0:T(8,128)(2,1)S(1)} %get-tuple-element.436), channel_id=1, source_target_pairs={{0,4},{4,0},{8,12},{12,8},{1,5},{5,1},{9,13},{13,9},{2,6},{6,2},{1... | collective-permute-start | bytes 2949128 | tf_op jit(solution)/shard_map/ppermute | solution.py:869
  222.6 20.7 %collective-permute-start.34 = (bf16[288,1536]{1,0:T(8,128)(2,1)S(1)}, bf16[288,1536]{1,0:T(8,128)(2,1)S(1)}, u32[]{:S(2)}, u32[]{:S(2)}) collective-permute-start(bf16[288,1536]{1,0:T(8,128)(2,1)S(1)} %get-tuple-element.437), channel_id=1, source_target_pairs={{0,8},{4,12},{8,0},{12,4},{1,9},{5,13},{9,1},{13,5},{2,10},{6,14},... | collective-permute-start | bytes 2654216 | tf_op jit(solution)/shard_map/ppermute | solution.py:869
  223.1 17.2 %collective-permute-start.32 = (bf16[208,1536]{1,0:T(8,128)(2,1)S(1)}, bf16[208,1536]{1,0:T(8,128)(2,1)S(1)}, u32[]{:S(2)}, u32[]{:S(2)}) collective-permute-start(bf16[208,1536]{1,0:T(8,128)(2,1)S(1)} %get-tuple-element.434.refs_0_), channel_id=1, source_target_pairs={{1,2},{2,1},{5,6},{6,5},{9,10},{10,9},{13,14},{14,13},{17,18},{18,... | collective-permute-start | bytes 1916936 | tf_op jit(solution)/shard_map/ppermute | solution.py:1085
  223.8 16.5 %collective-permute-start.31 = (bf16[192,1536]{1,0:T(8,128)(2,1)S(1)}, bf16[192,1536]{1,0:T(8,128)(2,1)S(1)}, u32[]{:S(2)}, u32[]{:S(2)}) collective-permute-start(bf16[192,1536]{1,0:T(8,128)(2,1)S(1)} %get-tuple-element.435), channel_id=1, source_target_pairs={{0,1},{1,0},{2,3},{3,2},{4,5},{5,4},{6,7},{7,6},{8,9},{9,8},{10,11... | collective-permute-start | bytes 1769480 | tf_op jit(solution)/shard_map/ppermute | solution.py:1085
  228.4 36.4 %collective-permute-start.25 = (f32[512,768]{1,0:T(8,128)S(1)}, f32[512,768]{1,0:T(8,128)S(1)}, u32[]{:S(2)}, u32[]{:S(2)}) collective-permute-start(f32[512,768]{1,0:T(8,128)S(1)} %convert_select_fusion), channel_id=1, source_target_pairs={{0,16},{16,0},{1,17},{17,1},{2,18},{18,2},{3,19},{19,3},{4,20},{20... | collective-permute-start | bytes 4718600 | tf_op jit(solution)/shard_map/ppermute | solution.py:869
  244.2 6.1 %copy-start.12 = (bf16[512,768]{1,0:T(8,128)(2,1)S(1)}, bf16[512,768]{1,0:T(8,128)(2,1)}, u32[]{:S(2)}) copy-start(bf16[512,768]{1,0:T(8,128)(2,1)} %get-tuple-element.313.refs_3_.refs_0_) | copy-start | bytes 2359300
  244.2 6.1 %copy-start.13 = (bf16[512,768]{1,0:T(8,128)(2,1)S(1)}, bf16[512,768]{1,0:T(8,128)(2,1)}, u32[]{:S(2)}) copy-start(bf16[512,768]{1,0:T(8,128)(2,1)} %get-tuple-element.406.refs_1_) | copy-start | bytes 2359300
  245.1 15.5 %collective-permute-start.35 = (bf16[208,1536]{1,0:T(8,128)(2,1)S(1)}, bf16[208,1536]{1,0:T(8,128)(2,1)S(1)}, u32[]{:S(2)}, u32[]{:S(2)}) collective-permute-start(bf16[208,1536]{1,0:T(8,128)(2,1)S(1)} %get-tuple-element.448), channel_id=1, source_target_pairs={{0,1},{1,0},{2,3},{3,2},{4,5},{5,4},{6,7},{7,6},{8,9},{9,8},{10,11... | collective-permute-start | bytes 1916936 | tf_op jit(solution)/shard_map/ppermute | solution.py:1085
  247.6 9.3 %collective-permute-start.36 = (bf16[192,1536]{1,0:T(8,128)(2,1)S(1)}, bf16[192,1536]{1,0:T(8,128)(2,1)S(1)}, u32[]{:S(2)}, u32[]{:S(2)}) collective-permute-start(bf16[192,1536]{1,0:T(8,128)(2,1)S(1)} %get-tuple-element.449.refs_2_), channel_id=1, source_target_pairs={{1,2},{2,1},{5,6},{6,5},{9,10},{10,9},{13,14},{14,13},{17,18},{18,... | collective-permute-start | bytes 1769480 | tf_op jit(solution)/shard_map/ppermute | solution.py:1085
  248.3 7.2 %collective-permute-start.37 = (bf16[96,1536]{1,0:T(8,128)(2,1)S(1)}, bf16[96,1536]{1,0:T(8,128)(2,1)S(1)}, u32[]{:S(2)}, u32[]{:S(2)}) collective-permute-start(bf16[96,1536]{1,0:T(8,128)(2,1)S(1)} %get-tuple-element.450), channel_id=1, source_target_pairs={{0,4},{4,0},{8,12},{12,8},{1,5},{5,1},{9,13},{13,9},{2,6},{6,2},{1... | collective-permute-start | bytes 884744 | tf_op jit(solution)/shard_map/ppermute | solution.py:869
  249.0 7.9 %collective-permute-start.38 = (bf16[112,1536]{1,0:T(8,128)(2,1)S(1)}, bf16[112,1536]{1,0:T(8,128)(2,1)S(1)}, u32[]{:S(2)}, u32[]{:S(2)}) collective-permute-start(bf16[112,1536]{1,0:T(8,128)(2,1)S(1)} %get-tuple-element.451), channel_id=1, source_target_pairs={{0,8},{4,12},{8,0},{12,4},{1,9},{5,13},{9,1},{13,5},{2,10},{6,14},... | collective-permute-start | bytes 1032200 | tf_op jit(solution)/shard_map/ppermute | solution.py:869
  255.5 9.3 %collective-permute-start.26 = (bf16[512,768]{1,0:T(8,128)(2,1)S(1)}, bf16[512,768]{1,0:T(8,128)(2,1)S(1)}, u32[]{:S(2)}, u32[]{:S(2)}) collective-permute-start(bf16[512,768]{1,0:T(8,128)(2,1)S(1)} %broadcast_select_fusion), channel_id=1, source_target_pairs={{0,16},{16,0},{1,17},{17,1},{2,18},{18,2},{3,19},{19,3},{4,20},{20... | collective-permute-start | bytes 2359304 | tf_op jit(solution)/shard_map/ppermute | solution.py:869
  261.5 14.8 %collective-permute-start.39 = (bf16[208,1536]{1,0:T(8,128)(2,1)S(1)}, bf16[208,1536]{1,0:T(8,128)(2,1)S(1)}, u32[]{:S(2)}, u32[]{:S(2)}) collective-permute-start(bf16[208,1536]{1,0:T(8,128)(2,1)S(1)} %get-tuple-element.459), channel_id=1, source_target_pairs={{0,1},{1,0},{2,3},{3,2},{4,5},{5,4},{6,7},{7,6},{8,9},{9,8},{10,11... | collective-permute-start | bytes 1916936 | tf_op jit(solution)/shard_map/ppermute | solution.py:1085
  264.1 0.7 collective-permute-start.40
  264.8 17.6 %copy-start.16 = (bf16[512,768]{1,0:T(8,128)(2,1)}, bf16[512,768]{1,0:T(8,128)(2,1)S(1)}, u32[]{:S(2)}) copy-start(bf16[512,768]{1,0:T(8,128)(2,1)S(1)} %collective-permute-done.26.refs_2_) | copy-start | bytes 2359300
  264.8 17.6 %copy-start.15 = (f32[512,768]{1,0:T(8,128)}, f32[512,768]{1,0:T(8,128)S(1)}, u32[]{:S(2)}) copy-start(f32[512,768]{1,0:T(8,128)S(1)} %collective-permute-done.25.refs_5_) | copy-start | bytes 4718596
  277.0 15.2 %collective-permute-start.42 = (bf16[208,1536]{1,0:T(8,128)(2,1)S(1)}, bf16[208,1536]{1,0:T(8,128)(2,1)S(1)}, u32[]{:S(2)}, u32[]{:S(2)}) collective-permute-start(bf16[208,1536]{1,0:T(8,128)(2,1)S(1)} %get-tuple-element.471.refs_3_), channel_id=1, source_target_pairs={{1,2},{2,1},{5,6},{6,5},{9,10},{10,9},{13,14},{14,13},{17,18},{18,... | collective-permute-start | bytes 1916936 | tf_op jit(solution)/shard_map/ppermute | solution.py:1085
  277.7 14.5 %collective-permute-start.41 = (bf16[192,1536]{1,0:T(8,128)(2,1)S(1)}, bf16[192,1536]{1,0:T(8,128)(2,1)S(1)}, u32[]{:S(2)}, u32[]{:S(2)}) collective-permute-start(bf16[192,1536]{1,0:T(8,128)(2,1)S(1)} %get-tuple-element.470), channel_id=1, source_target_pairs={{0,1},{1,0},{2,3},{3,2},{4,5},{5,4},{6,7},{7,6},{8,9},{9,8},{10,11... | collective-permute-start | bytes 1769480 | tf_op jit(solution)/shard_map/ppermute | solution.py:1085
  293.8 12.5 %collective-permute-start.44 = (bf16[208,1536]{1,0:T(8,128)(2,1)S(1)}, bf16[208,1536]{1,0:T(8,128)(2,1)S(1)}, u32[]{:S(2)}, u32[]{:S(2)}) collective-permute-start(bf16[208,1536]{1,0:T(8,128)(2,1)S(1)} %get-tuple-element.481), channel_id=1, source_target_pairs={{0,1},{1,0},{2,3},{3,2},{4,5},{5,4},{6,7},{7,6},{8,9},{9,8},{10,11... | collective-permute-start | bytes 1916936 | tf_op jit(solution)/shard_map/ppermute | solution.py:1085
  296.0 11.7 %collective-permute-start.46 = (bf16[192,1536]{1,0:T(8,128)(2,1)S(1)}, bf16[192,1536]{1,0:T(8,128)(2,1)S(1)}, u32[]{:S(2)}, u32[]{:S(2)}) collective-permute-start(bf16[192,1536]{1,0:T(8,128)(2,1)S(1)} %get-tuple-element.494), channel_id=1, source_target_pairs={{0,16},{16,0},{1,17},{17,1},{2,18},{18,2},{3,19},{19,3},{4,20},{20... | collective-permute-start | bytes 1769480 | tf_op jit(solution)/shard_map/ppermute | solution.py:869
  296.0 16.7 %collective-permute-start.43 = (bf16[192,1536]{1,0:T(8,128)(2,1)}, bf16[192,1536]{1,0:T(8,128)(2,1)}, u32[]{:S(2)}, u32[]{:S(2)}) collective-permute-start(bf16[192,1536]{1,0:T(8,128)(2,1)} %get-tuple-element.479), channel_id=1, source_target_pairs={{0,16},{16,0},{1,17},{17,1},{2,18},{18,2},{3,19},{19,3},{4,20},{20... | collective-permute-start | bytes 1769480 | tf_op jit(solution)/shard_map/ppermute | solution.py:869
  307.8 4.9 %collective-permute-start.45 = (bf16[208,1536]{1,0:T(8,128)(2,1)}, bf16[208,1536]{1,0:T(8,128)(2,1)S(1)}, u32[]{:S(2)}, u32[]{:S(2)}) collective-permute-start(bf16[208,1536]{1,0:T(8,128)(2,1)} %get-tuple-element.484), channel_id=1, source_target_pairs={{0,16},{16,0},{1,17},{17,1},{2,18},{18,2},{3,19},{19,3},{4,20},{20... | collective-permute-start | bytes 1916936 | tf_op jit(solution)/shard_map/ppermute | solution.py:869
  309.5 7.2 %copy-start.1 = (bf16[8,128,768]{2,1,0:T(8,128)(2,1)S(1)}, bf16[8,128,768]{2,1,0:T(8,128)(2,1)}, u32[]{:S(2)}) copy-start(bf16[8,128,768]{2,1,0:T(8,128)(2,1)} %param.14) | copy-start | bytes 4718596
  (3 other events, 4.0 us)

commit v6 on v5

--- a/solution.py
+++ b/solution.py
@@ -120,6 +120,14 @@
 
 
 NEAR, FAR, RAW, BOTH, FREE = "near", "far", "raw", "both", "free"
+
+
+def run(*parts):
+    for part in parts:
+        next(part)
+    for part in parts:
+        for _ in part:
+            pass
 
 
 def ready(waits):
@@ -190,8 +198,7 @@
             ctx[lanes, rows] = dot(turned, parts.astype(BF16)).astype(BF16)
 
 
-def attend_kernel(layer, sec, x, w_a, w_b, small, mask, q, k, v, probs, ctx, w, sems):
-    move = Mover(sems)
+def attend_steps(move, layer, sec, x, w_a, w_b, small, mask, q, k, v, probs, ctx, w):
     mine = sec[0] == layer
     rows, width = x.buffer.shape
     waits = x.fetch(move) + small.fetch(move) + mask.fetch(move)
@@ -199,6 +206,7 @@
         move.choose(mine, w_a.ref.at[:, pl.ds(i * width, width)], w_b.ref.at[:, pl.ds(i * width, width)], w.at[i])
         for i in (1, 0, 2)
     ]
+    yield
     ready(waits)
     x, small = x.buffer, small.buffer
     parts[0].wait()
@@ -217,6 +225,11 @@
         )
         probs.flush(move, slice(None), pl.ds(i * half, half))
     ctx.flush(move)
+
+
+def attend_kernel(layer, sec, *refs):
+    move = Mover(refs[-1])
+    run(attend_steps(move, layer, sec, *refs[:-1]))
     move.finish()
 
 
@@ -331,13 +344,55 @@
     )
 
 
-def down_grad_kernel(sec, gy, hat, scale, small, act, second, branch, sums, send, keep, turned, sems):
-    move = Mover(sems)
+def up_down_steps(
+    move, layer, sec, x, ctx, wo_a, wo_b, wu_a, wu_b, wd_a, wd_b, small,
+    hat, scale, turned, act, slope, y, two, scale_two, wo, wu, wd, low, total,
+):
+    mine = sec[0] == layer
+    blocks, _, wide = wu.shape
+    waits = ctx.fetch(move) + [move.choose(mine, wo_a.ref, wo_b.ref, wo)] + small.fetch(move) + x.fetch(move)
+    ups, downs = [], []
+    for i in range(blocks):
+        span = pl.ds(i * wide, wide)
+        ups.append(move.choose(mine, wu_a.ref.at[:, span], wu_b.ref.at[:, span], wu.at[i]))
+        downs.append(move.choose(mine, wd_a.ref.at[span], wd_b.ref.at[span], wd.at[i]))
+    yield
+    ready(waits)
+    small = small.buffer
+    summed = x.buffer[...].astype(F32) + t_dot(ctx.buffer[...], wo[...]) + small[B_OUT : B_OUT + 1]
+    unit, root = standardize(summed)
+    hat.buffer[...] = unit
+    hat.flush(move)
+    scale.buffer[...] = jnp.broadcast_to(root, scale.buffer.shape)
+    scale.flush(move)
+    normed = unit * small[GAIN_ONE : GAIN_ONE + 1] + small[OFFSET_ONE : OFFSET_ONE + 1]
+    total[...] = normed + small[B_DOWN : B_DOWN + 1]
+    low[...] = normed.astype(BF16)
+    turned.buffer[...] = low[...].T
+    turned.flush(move)
+    for i in range(blocks):
+        ups[i].wait()
+        pre = dot(low[...], wu[i]) + small[B_UP + i : B_UP + i + 1]
+        share, bell = gauss_share(pre)
+        act.buffer[i] = (pre * share).astype(BF16)
+        slope.buffer[i] = share + pre * 0.3989422804014327 * bell
+        slope.flush(move, i)
+        downs[i].wait()
+        total[...] += dot(act.buffer[i], wd[i])
+    unit, root = standardize(total[...])
+    y.buffer[...] = (unit * small[GAIN_TWO : GAIN_TWO + 1] + small[OFFSET_TWO : OFFSET_TWO + 1]).astype(BF16)
+    y.flush(move)
+    two.buffer[...] = unit
+    scale_two.buffer[...] = jnp.broadcast_to(root, scale_two.buffer.shape)
+
+
+def down_grad_steps(move, sec, gy, hat, scale, small, act, second, branch, sums, send, keep, turned):
     blocks = act.buffer.shape[0]
     low_rows, wide = send.buffer.shape[1], act.buffer.shape[2]
     tall = 2 * low_rows
     waits = gy.fetch(move) + small.fetch(move) + scale.fetch(move) + hat.fetch(move)
     parts = [act.fetch(move, i) for i in range(blocks)]
+    yield
     ready(waits)
     grad = gy.buffer[...].astype(F32)
     sums.buffer[0:1] = column_sum(grad * hat.buffer[...])
@@ -360,6 +415,12 @@
             block = dot(turned[left, :], act.buffer[i]).astype(BF16)
             out.buffer[i, :, :wide] = block[:low_rows]
             out.buffer[i, :, wide:] = block[low_rows:]
+            out.flush(move, i)
+
+
+def down_grad_kernel(sec, *refs):
+    move = Mover(refs[-1])
+    run(down_grad_steps(move, sec, *refs[:-1]))
     move.finish()
 
 
@@ -372,7 +433,7 @@
         down_grad_kernel,
         sec,
         [(gy, gy_kind), (hat, kind), (scale, kind), (small, FAR), (act, kind)],
-        [(sds(wide, F32), NEAR), (sds(wide, BF16), NEAR), (sds((8, width), F32), NEAR), (part, NEAR), (part, NEAR)],
+        [(sds(wide, F32), NEAR), (sds(wide, BF16), NEAR), (sds((8, width), F32), NEAR), (part, NEAR), (part, FAR if kind == NEAR else NEAR)],
         [((width, rows), BF16)],
         "down_grad",
         2 * rows * width * width * blocks,
@@ -601,6 +662,77 @@
     )
 
 
+def second_kernel(sec, *refs):
+    refs = list(refs)
+    take = lambda count: [refs.pop(0) for _ in range(count)]
+    inside = lambda item: Operand(None, item, False)
+    x, w_a, w_b, small, mask = take(5)
+    weights, (gy,) = take(6), take(1)
+    q, k, v, probs, ctx, hat, scale, turned, slope, y = take(10)
+    second, branch, sums, send, keep = take(5)
+    w, wo, wu, wd, low, total, act, two, scale_two, branch_turned, sems = refs
+    move = Mover(sems)
+    near = inside(small.buffer)
+    act, two, scale_two = inside(act), inside(two), inside(scale_two)
+    run(
+        attend_steps(move, 1, sec, x, w_a, w_b, small, mask, q, k, v, probs, ctx, w),
+        up_down_steps(
+            move, 1, sec, x, inside(ctx.buffer), *weights, near,
+            hat, scale, turned, act, slope, y, two, scale_two, wo, wu, wd, low, total,
+        ),
+        down_grad_steps(move, sec, gy, two, scale_two, near, act, second, branch, sums, send, keep, branch_turned),
+    )
+    move.finish()
+
+
+def second_layer(sec, x, mask, big, other, small, gy):
+    rows, width = x.shape
+    seqs = mask.shape[1]
+    pairs = width // 128
+    (w, w_other), (wo, wo_other), (wu, wu_other), (wd, wd_other) = zip(big, other)
+    blocks = wu.shape[1] // width
+    wide = (rows, width)
+    part = sds((blocks, width // 4, 2 * width), BF16)
+    square = lambda count: ((count, width, width), BF16)
+    return call(
+        second_kernel,
+        sec,
+        [(x, NEAR), (w, RAW), (w_other, RAW), (small, FAR), (mask, FAR)]
+        + [(item, RAW) for item in (wo, wo_other, wu, wu_other, wd, wd_other)]
+        + [(gy, FAR)],
+        [(sds(wide, BF16), FAR)] * 3
+        + [
+            (sds((seqs, pairs, 256, 128), F32), FAR),
+            (sds((width, rows), BF16), FAR),
+            (sds(wide, F32), FAR),
+            (sds((rows, 128), F32), FAR),
+            (sds((width, rows), BF16), FAR),
+            (sds((blocks,) + wide, F32), FAR),
+            (sds(wide, BF16), FAR),
+            (sds(wide, F32), NEAR),
+            (sds(wide, BF16), NEAR),
+            (sds((8, width), F32), NEAR),
+            (part, NEAR),
+            (part, FAR),
+        ],
+        [
+            square(3),
+            ((width, width), BF16),
+            square(blocks),
+            square(blocks),
+            (wide, BF16),
+            (wide, F32),
+            ((blocks,) + wide, BF16),
+            (wide, F32),
+            ((rows, 128), F32),
+            ((width, rows), BF16),
+        ],
+        "second_layer",
+        2 * rows * width * width * (3 * blocks + 5),
+        50 << 20,
+    )
+
+
 def up_whole_kernel(
     layer, sec, branch, second, wd_a, wd_b, slope, low, wu_a, wu_b, hat, scale, small,
     first, attend, sums, send, keep, wd, wu, pre, sems,
@@ -696,8 +828,14 @@
     near = probs.fetch(move) + v.fetch(move) + k.fetch(move) + q.fetch(move)
     later = x.fetch(move) + ctx.fetch(move) + down.fetch(move) + up.fetch(move)
     last = [
-        move.choose(mine, w_a.ref.at[:, pl.ds(i * width, width)], w_b.ref.at[:, pl.ds(i * width, width)], w.at[i])
+        move.choose(
+            mine,
+            w_a.ref.at[:, pl.ds(i * width + half * wide, wide)],
+            w_b.ref.at[:, pl.ds(i * width + half * wide, wide)],
+            w.at[:, pl.ds((3 * half + i) * wide, wide)],
+        )
         for i in range(3)
+        for half in range(2)
     ] + first.fetch(move)
     ready(waits)
     attend, q, k, v, probs = (item.buffer for item in (attend, q, k, v, probs))
@@ -706,53 +844,58 @@
     halves = lane_halves()
     lower = lax.broadcasted_iota(jnp.int32, (128, 128), 1) < 64
 
-    def attention(first_pair):
+    def attention(half):
         @pl.loop(0, pairs)
         def _(index):
-            pair = first_pair + index
-            lanes = pl.ds(pl.multiple_of(pair * 128, 128), 128)
+            lanes = pl.ds(pl.multiple_of(half * wide + index * 128, 128), 128)
+
+            def put(part, rows, value):
+                there = pl.ds(pl.multiple_of((3 * half + part) * wide + index * 128, 128), 128)
+                grads[rows, there] = value.astype(BF16)
+
             for seq in range(seqs):
                 rows = slice(seq * 128, seq * 128 + 128)
                 grad = gc[rows, lanes]
-                p = probs[seq, pair]
+                p = probs[seq, half * pairs + index]
                 full = dot(p.astype(BF16), grad)
-                grads[2, rows, lanes] = jnp.where(lower, full[:128], full[128:]).astype(BF16)
+                put(2, rows, jnp.where(lower, full[:128], full[128:]))
                 gp = dot_t(two_heads(v[rows, lanes], halves), grad)
                 parts = []
                 for side in (slice(0, 128), slice(128, 256)):
                     g, pp = gp[side], p[side]
                     parts.append(pp * (g - jnp.sum(g * pp, axis=0, keepdims=True)))
                 gs = jnp.concatenate(parts, axis=0).astype(BF16)
-                grads[0, rows, lanes] = t_dot(gs, two_heads(k[rows, lanes] * SCALE, halves)).astype(BF16)
+                put(0, rows, t_dot(gs, two_heads(k[rows, lanes] * SCALE, halves)))
                 full = dot(gs, q[rows, lanes] * SCALE)
-                grads[1, rows, lanes] = jnp.where(lower, full[:128], full[128:]).astype(BF16)
+                put(1, rows, jnp.where(lower, full[:128], full[128:]))
 
     def products(half, out):
+        three = pl.ds(pl.multiple_of(half * 3 * wide, 128), 3 * wide)
         lanes = pl.ds(pl.multiple_of(half * wide, wide), wide)
-        for part in range(4):
-            if part < 3:
-                block = dot(turned[...], grads[part, :, lanes]).astype(BF16)
-            else:
-                block = dot(ctx.buffer[...], attend[:, lanes]).astype(BF16)
-            for shard in range(shards):
-                out.buffer[shard, :tall, part * wide : part * wide + wide] = block[shard * tall : shard * tall + tall]
-
-    attention((1 - sec[0]) * pairs)
+        block = dot(turned[...], grads[:, three]).astype(BF16)
+        block_out = dot(ctx.buffer[...], attend[:, lanes]).astype(BF16)
+        for shard in range(shards):
+            out.buffer[shard, :tall, : 3 * wide] = block[shard * tall : shard * tall + tall]
+            out.buffer[shard, :tall, 3 * wide :] = block_out[shard * tall : shard * tall + tall]
+
+    attention(1 - sec[0])
     ready(later)
     turned[...] = x.buffer[...].T
     products(1 - sec[0], send)
-    attention(sec[0] * pairs)
+    attention(sec[0])
     products(sec[0], keep)
     little = jnp.concatenate([down.buffer[...], up.buffer[...]], axis=0).astype(BF16)
     for half, out in ((1 - sec[0], send), (sec[0], keep)):
-        lanes = pl.ds(pl.multiple_of(half * wide, wide), wide)
-        pad = [column_sum(grads[part, :, lanes].astype(F32)).astype(BF16) for part in (0, 2)]
+        pad = []
+        for part in (0, 2):
+            lanes = pl.ds(pl.multiple_of((3 * half + part) * wide, wide), wide)
+            pad.append(column_sum(grads[:, lanes].astype(F32)).astype(BF16))
         pad = jnp.concatenate([jnp.concatenate(pad, axis=1), jnp.zeros((15, width), BF16)], axis=0)
         for shard in range(shards):
             out.buffer[shard, tall:, 0:width] = little
             out.buffer[shard, tall:, width:] = pad
     ready(last)
-    total = first.buffer[...] + dot_t(grads[0], w[0]) + dot_t(grads[1], w[1]) + dot_t(grads[2], w[2])
+    total = first.buffer[...] + dot_t(grads[...], w[...])
     gx.buffer[...] = total
     gx.flush(move)
     gx_low.buffer[...] = total.astype(BF16)
@@ -771,7 +914,7 @@
         + [(item, FAR) for item in (x, q, k, v, probs)]
         + [(wo, RAW), (wo_other, RAW), (w, RAW), (w_other, RAW), (down, NEAR), (up, NEAR)],
         [(sds(wide, F32), FAR), (sds(wide, BF16), low_kind), (part, NEAR), (part, NEAR)],
-        [((width, rows), BF16), ((width, width), BF16), ((3, width, width), BF16), (wide, BF16), ((3,) + wide, BF16)],
+        [((width, rows), BF16), ((width, width), BF16), ((width, 3 * width), BF16), (wide, BF16), ((rows, 3 * width), BF16)],
         "attend_grad",
         2 * rows * width * width * 10,
         30 << 20,
@@ -880,7 +1023,7 @@
 class Sums:
     def __init__(self, columns):
         self.columns, self.ins, self.outs, self.code = columns, [], [], []
-        self.rows = {}
+        self.rows, self.far, self.later = {}, set(), []
 
     def use(self, array):
         for index, known in enumerate(self.ins):
@@ -903,20 +1046,39 @@
         shapes = self.outs + [sds((self.rows[way], self.columns), BF16) for way in ways]
         n_in, n_out = len(self.ins), len(self.outs)
 
+        far = sorted(self.far)
+        space = lambda index: pltpu.HBM if index in self.far else pltpu.VMEM
+
         def kernel(ids_ref, *refs):
-            sends = dict(zip(ways, refs[n_in + n_out :]))
+            first = n_in + len(shapes)
+            sends = dict(zip(ways, refs[n_in + n_out : first]))
+            ins, move = list(refs[:n_in]), Mover(refs[-1])
+            waits = []
+            for index, buffer in zip(far, refs[first:-1]):
+                move.load(ins[index], buffer)
+                waits.append(move.last)
+                ins[index] = buffer
             for code in self.code:
-                code(ids_ref, refs[:n_in], refs[n_in : n_in + n_out], sends)
+                code(ids_ref, ins, refs[n_in : n_in + n_out], sends)
+            ready(waits)
+            for code in self.later:
+                code(ids_ref, ins, refs[n_in : n_in + n_out], sends)
 
         vmem = pl.BlockSpec(memory_space=pltpu.VMEM)
         results = pl.pallas_call(
             kernel,
-            in_specs=[pl.BlockSpec(memory_space=pltpu.SMEM)] + [vmem] * n_in,
+            in_specs=[pl.BlockSpec(memory_space=pltpu.SMEM)]
+            + [pl.BlockSpec(memory_space=space(index)) for index in range(n_in)],
             out_specs=[vmem] * len(shapes),
             out_shape=shapes,
+            scratch_shapes=[pltpu.VMEM(self.ins[index].shape, BF16) for index in far]
+            + [pltpu.SemaphoreType.DMA((8,))],
             compiler_params=pltpu.CompilerParams(vmem_limit_bytes=SPARE),
             name="join_sums",
-        )(ids, *self.ins)
+        )(
+            ids,
+            *(pltpu.with_memory_space_constraint(array, space(index)) for index, array in enumerate(self.ins)),
+        )
         return results[:n_out], dict(zip(ways, results[n_out:]))
 
 
@@ -926,6 +1088,8 @@
 
 def sum_section(sums, chunk):
     kept, got = sums.use(chunk.keep), sums.use(chunk.got["section"])
+    if chunk.far:
+        sums.far |= {kept, got}
     _, rows, _ = chunk.keep.shape
     cut = chunk.cut
     rest = rows - cut
@@ -942,7 +1106,7 @@
             sends["y"][to_y + i * rest : to_y + i * rest + rest] = add(2 * (1 - high) + i, slice(cut, rows))
             outs[bottom][i] = add(2 * high + i, slice(cut, rows))
 
-    sums.code.append(code)
+    (sums.later if chunk.far else sums.code).append(code)
     return [top, bottom]
 
 
@@ -1056,7 +1220,7 @@
     def __init__(self, line, send, keep, partner):
         self.line, self.send, self.keep, self.partner = line, send, keep, partner
         self.at, self.kept, self.got, self.sent, self.done = 0, [], {}, {}, None
-        self.rows = send.shape[1]
+        self.rows, self.far = send.shape[1], len(line.chunks) == 0
         self.cut = split_at(self.rows)
 
 
@@ -1185,12 +1349,17 @@
         self.made["outs"] = assemble(self.sec, y_one, y_two, self.made["y"], one, two_low, self.made["got"])
 
 
-def last_kernel(ids, up_mine, up_got, mine, got, qkv, out, b_qv, b_out, gain, offset, b_up, b_down, w_up, sems):
+def last_kernel(ids, down_mine, down_got, up_mine, up_got, mine, got, w_down, qkv, out, b_qv, b_out, gain, offset, b_up, b_down, w_up, sems):
     move = Mover(sems)
     up_wide = w_up.buffer.shape[1] // 2
     for half, side in ((ids[0], up_mine), (1 - ids[0], up_got)):
         w_up.buffer[:, pl.ds(pl.multiple_of(half * up_wide, up_wide), up_wide)] = side.buffer[...].astype(F32)
     w_up.flush(move)
+    hidden, width = w_down.buffer.shape
+    for half, side in ((ids[0], down_mine), (1 - ids[0], down_got)):
+        rows = jnp.concatenate([side.buffer[:, :hidden], side.buffer[:, hidden:]], axis=0)
+        w_down.buffer[:, pl.ds(pl.multiple_of(half * (width // 2), width // 2), width // 2)] = rows.T.astype(F32)
+    w_down.flush(move)
     mine, got = mine.buffer, got.buffer
     tall, wide = qkv.buffer.shape[0], out.buffer.shape[1] // 2
     for half, side in ((ids[0], mine), (1 - ids[0], got)):
@@ -1227,14 +1396,14 @@
     move.finish()
 
 
-def last(ids, up, attend, width, shards):
+def last(ids, down, up, attend, width, shards):
     tall = width // shards
-    shapes = [(tall, 3 * width), (tall, width), (2, tall), (1, tall), (2, tall), (2, tall), (1, width), (1, tall)]
+    shapes = [(down[0].shape[1] // 2, width), (tall, 3 * width), (tall, width), (2, tall), (1, tall), (2, tall), (2, tall), (1, width), (1, tall)]
     shapes.append((tall, 2 * up[0].shape[1]))
     return call(
         last_kernel,
         ids,
-        [(item, NEAR) for item in (*up, *attend)],
+        [(item, NEAR) for item in (*down, *up, *attend)],
         [(sds(shape, F32), FAR) for shape in shapes],
         [],
         "last",
@@ -1278,13 +1447,15 @@
     other = (o_qkv, o_out, o_up, exchange(late_down, "section", 1))
     y_one, cache_one = layer_forward(0, sec, x, front, big, other, smalls[0])
     y_near, y_one = y_one
-    front = attend_forward(1, sec, y_near, NEAR, big[0], o_qkv, smalls[1], mask)
-    y_two, cache_two = layer_forward(1, sec, y_near, front, big, other, smalls[1], y_one)
+    made = second_layer(sec, y_near, mask, big, other, smalls[1], gy)
+    q, k, v, probs, ctx, hat_one, scale_one, low, slope, y_two = made[:10]
+    cache_two = (y_one, q, k, v, probs, ctx, hat_one, scale_one, low, None, slope, None, None)
     line = Line(sec)
     two = Backward(line, 1, sec, cache_two, big, other, smalls[1], shards)
     one = Backward(line, 0, sec, cache_one, big, other, smalls[0], shards)
+    two.made.update(second=made[10], branch=made[11], down_sums=made[12])
+    line.add(made[13], made[14])
     exchanged_y = exchange(jnp.where(section == 0, y_two, y_one), "section", 1)
-    line.advance(two, lambda: two.down(gy))
     line.advance(two, two.up_first)
     line.advance(two, two.up_last)
     line.advance(two, two.attention)
@@ -1304,14 +1475,9 @@
     activations = activations.reshape(seqs_local, length, width)
     input_grads = input_grads.reshape(seqs_local, length, width)
     down, up, attend = line.finish()
-    g_w_qkv, g_w_out, g_b_qv, g_b_out, g_gain, g_offset, g_b_up, g_b_down, g_w_up = last(
-        line.ids, up, attend, width, shards
-    )
-    mine, got = down
-    down = (jnp.where(section == 0, mine, got), jnp.where(section == 0, got, mine))
-    g_w_down = jnp.concatenate(
-        [side[:, i * width : (i + 1) * width] for side in down for i in range(2)], axis=0
-    ).T.astype(F32)
+    g_w_down, g_w_qkv, g_w_out, g_b_qv, g_b_out, g_gain, g_offset, g_b_up, g_b_down, g_w_up = last(
+        line.ids, down, up, attend, width, shards
+    )
     return (
         activations[None],
         input_grads[None],

time: 322 us -> 310 us (0.963)
  local copies, waits for them, and re-layouts: 14.5 us -> 6.54 us
  Pallas kernels: 160 us -> 153 us
  waiting for transfers between devices: 83.3 us -> 86.9 us
    pallas_call x15 -> x12, Pallas kernels: 147 us -> 139 us  [call(): pl.pallas_call(body, in_specs=[pl.BlockSpec(memory_space=pltpu.SMEM)] + [...]
    unnamed x42 -> x35, local copies, waits for them, and re-layouts: 11 us -> 3.12 us
  transfers between devices with their start and end apart: 47 -> 47, of which waited for: 20 -> 22; matrix products, arithmetic and copies ran while one was open for 4% -> 3% of each run, Pallas kernels for 34% -> 36%
where the time goes in v6:
time: 310 us; the launch traced here: 306 us
  Pallas kernels  153 us (49%)
  waiting for transfers between devices  86.9 us (28%)
  starting transfers between devices  53.1 us (17%)
  local copies, waits for them, and re-layouts  6.54 us (2%)
  other arithmetic  4.52 us (1%)
    pallas_call x12, Pallas kernels, call(): pl.pallas_call(body, in_specs=[pl.BlockSpec(memory_space=pltpu.SMEM)] + [...  139 us
    ppermute x15, waiting for transfers between devices, move(): lax.ppermute(array, 'outer', [(0, 1), (1, 0), (2, 3), (3, 2)] if way == '...  60.9 us
    ppermute x15, starting transfers between devices, move(): lax.ppermute(array, 'outer', [(0, 1), (1, 0), (2, 3), (3, 2)] if way == '...  32.9 us
    ppermute x32, waiting for transfers between devices, exchange(): return lax.ppermute(array, axis, [(i, i ^ bit) for i in range(length)])  26.1 us
    ppermute x32, starting transfers between devices, exchange(): return lax.ppermute(array, axis, [(i, i ^ bit) for i in range(length)])  20.2 us
    pallas_call x12, Pallas kernels, run(): pl.pallas_call(kernel, in_specs=[pl.BlockSpec(memory_space=pltpu.SMEM)] +...  13.9 us
  transfers between devices with their start and end apart: 47, of which 22 were waited for; matrix products, arithmetic and copies ran while one was open for 3% of the time, Pallas kernels for 36%

profile of v6, /device:TPU:0, one launch (start us, length us, event | category | flops | bytes accessed | tf_op | source)
XLA Modules:
  0.0 305.6 jit_solution(9651285950083835734)
XLA Ops:
  1.7 1.4 reduce.3
  5.5 1.0 constant_dynamic-slice_fusion
  8.5 8.5 %attend_forward.1 = (bf16[512,768]{1,0:T(8,128)(2,1)}, bf16[512,768]{1,0:T(8,128)(2,1)}, bf16[512,768]{1,0:T(8,128)(2,1)}, f32[4,6,256,128]{3,2,1,0:T(8,128)}, b...) custom-call(s32[1]{0:T(128)} %bitcast.ids_ref, bf16[512,768]{1,0:T(8,128)(2,1)} %bitcast.38, ...), custom_call_target="tpu_custom_call" | custom-call | flops 2415919104 | bytes 12582912 | tf_op jit(solution)/shard_map/attend_forward/pallas_call | solution.py:161
  17.0 0.9 collective-permute-done.2.refs_3_.refs_6_.refs_9_
  18.4 1.4 dynamic-slice_select_fusion
  19.8 12.5 %up_forward.1 = (f32[512,768]{1,0:T(8,128)S(1)}, f32[512,768]{1,0:T(8,128)}, f32[512,128]{1,0:T(8,128)}, bf16[768,512]{1,0:T(8,128)(2,1)}, bf16[4,512,768]{2,1,0...) custom-call(s32[1]{0:T(128)} %bitcast.ids_ref, bf16[512,768]{1,0:T(8,128)(2,1)} %bitcast.39, ...), custom_call_target="tpu_custom_call" | custom-call | flops 3019898880 | bytes 20971520 | tf_op jit(solution)/shard_map/up_forward/pallas_call | solution.py:161
  32.3 9.0 %down_forward.1 = (bf16[512,768]{1,0:T(8,128)(2,1)S(1)}, bf16[512,768]{1,0:T(8,128)(2,1)}, f32[512,768]{1,0:T(8,128)}, f32[512,128]{1,0:T(8,128)}) custom-call(s32[1]{0:T(128)} %bitcast.ids_ref, bf16[4,512,768]{2,1,0:T(8,128)(2,1)S(1)} %get-tuple-element.260.refs_0_, bf16[3072,768]{1,0:T(8,128)(2,1)} %bitcast.24, ...), custom_call_target="tpu_custom_call" | custom-call | flops 2415919104 | bytes 12582912 | tf_op jit(solution)/shard_map/down_forward/pallas_call | solution.py:161
  41.3 25.2 %second_layer.1 = (bf16[512,768]{1,0:T(8,128)(2,1)}, bf16[512,768]{1,0:T(8,128)(2,1)}, bf16[512,768]{1,0:T(8,128)(2,1)}, f32[4,6,256,128]{3,2,1,0:T(8,128)}, bf1...) custom-call(s32[1]{0:T(128)} %bitcast.ids_ref, ...), custom_call_target="tpu_custom_call" | custom-call | flops 10267656192 | bytes 52428800 | tf_op jit(solution)/shard_map/second_layer/pallas_call | solution.py:161
  66.6 8.7 %up_grad_first.1 = (f32[512,768]{1,0:T(8,128)S(1)}, f32[8,768]{1,0:T(8,128)S(1)}, bf16[4,192,1536]{2,1,0:T(8,128)(2,1)}) custom-call(s32[1]{0:T(128)} %bitcast.ids_ref, bf16[512,768]{1,0:T(8,128)(2,1)S(1)} %get-tuple-element.275.refs_0_, f32[512,768]{1,0:T(8,128)S(1)} %get-tuple-element.267.refs_1_, bf16[3072,768]{1,0:T(8,128)(2,1)} %bitcast.26, ...), custom_call_target="tpu_custom_call" | custom-call | flops 3623878656 | bytes 15728640 | tf_op jit(solution)/shard_map/up_grad_first/pallas_call | solution.py:161
  75.3 1.1 copy-done.4
  76.5 1.4 copy-done.11
  78.5 3.2 %join_sums.12 = (bf16[2,96,1536]{2,1,0:T(8,128)(2,1)S(1)}, bf16[2,96,1536]{2,1,0:T(8,128)(2,1)S(1)}, bf16[192,1536]{1,0:T(8,128)(2,1)S(1)}, bf16[192,1536]{1,0:T(8,128)(2,1)S(1)}) custom-call(s32[5]{0:T(128)S(1)} %stack.24.ids_ref, bf16[4,192,1536]{2,1,0:T(8,128)(2,1)} %get-tuple-element.285.refs_0_, bf16[4,192,1536]{2,1,0:T(8,128)(2,1)} %copy-done.11), custom_call_target="tpu_custom_call" | custom-call | tf_op jit(solution)/shard_map/join_sums/pallas_call | solution.py:1068
  81.7 3.0 collective-permute-start.6
  84.7 1.5 collective-permute-start.7
  86.2 8.6 %up_grad_last.1 = (f32[512,768]{1,0:T(8,128)S(1)}, bf16[512,768]{1,0:T(8,128)(2,1)S(1)}, f32[8,768]{1,0:T(8,128)S(1)}, bf16[4,192,1536]{2,1,0:T(8,128)(2,1)S(1)}) custom-call(s32[1]{0:T(128)} %bitcast.ids_ref, bf16[512,768]{1,0:T(8,128)(2,1)S(1)} %get-tuple-element.275.refs_0_, f32[512,768]{1,0:T(8,128)S(1)} %copy-done.5, bf16[3072,768]{1,0:T(8,128)(2,1)} %bitcast.27, ...), custom_call_target="tpu_custom_call" | custom-call | flops 3623878656 | bytes 15728640 | tf_op jit(solution)/shard_map/up_grad_last/pallas_call | solution.py:161
  94.8 3.4 %collective-permute-done.6.refs_2_ = bf16[192,1536]{1,0:T(8,128)(2,1)S(1)} collective-permute-done((bf16[192,1536]{1,0:T(8,128)(2,1)S(1)}, bf16[192,1536]{1,0:T(8,128)(2,1)S(1)}, u32[]{:S(2)}, u32[]{:S(2)}) %collective-permute-start.6) | collective-permute-done | bytes 589856 | tf_op jit(solution)/shard_map/ppermute | solution.py:1012
  98.2 1.5 collective-permute-done.7.refs_3_
  99.7 1.0 join_sums.13
  100.6 1.6 collective-permute-start.10
  102.8 17.4 %attend_grad.2 = (f32[512,768]{1,0:T(8,128)}, bf16[512,768]{1,0:T(8,128)(2,1)S(1)}, bf16[512,768]{1,0:T(8,128)(2,1)}, bf16[4,208,1536]{2,1,0:T(8,128)(2,1)S(1)}, bf16[4,208,1536]{2,1,0:T(8,128)(2,1)S(1)}) custom-call(s32[1]{0:T(128)} %bitcast.ids_ref, bf16[512,768]{1,0:T(8,128)(2,1)S(1)} %get-tuple-element.290.refs_0_, ...), custom_call_target="tpu_custom_call" | custom-call | flops 6039797760 | bytes 31457280 | tf_op jit(solution)/shard_map/attend_grad/pallas_call | solution.py:161
  120.2 0.9 collective-permute-done.10.refs_3_
  121.1 1.2 collective-permute-done.9.refs_2_
  123.2 1.6 collective-permute-start.11
  125.9 6.8 %down_grad.1 = (f32[512,768]{1,0:T(8,128)S(1)}, bf16[512,768]{1,0:T(8,128)(2,1)S(1)}, f32[8,768]{1,0:T(8,128)S(1)}, bf16[4,192,1536]{2,1,0:T(8,128)(2,1)S(1)}, bf16[4,192,1536]{2,1,0:T(8,128)(2,1)S(1)}) custom-call(s32[1]{0:T(128)} %bitcast.ids_ref, bf16[512,768]{1,0:T(8,128)(2,1)S(1)} %get-tuple-element.313.refs_0_, f32[512,768]{1,0:T(8,128)} %get-tuple-element.314.refs_1_, ...), custom_call_target="tpu_custom_call" | custom-call | flops 2415919104 | bytes 14680064 | tf_op jit(solution)/shard_map/down_grad/pallas_call | solution.py:161
  132.7 1.2 collective-permute-done.12.refs_4_
  134.2 4.7 %collective-permute-done.11.refs_1_ = bf16[192,1536]{1,0:T(8,128)(2,1)S(1)} collective-permute-done((bf16[192,1536]{1,0:T(8,128)(2,1)S(1)}, bf16[192,1536]{1,0:T(8,128)(2,1)S(1)}, u32[]{:S(2)}, u32[]{:S(2)}) %collective-permute-start.11) | collective-permute-done | bytes 589856 | tf_op jit(solution)/shard_map/ppermute | solution.py:1249
  139.0 1.1 join_sums.15
  140.8 1.5 collective-permute-start.15
  142.3 0.9 collective-permute-start.16
  143.8 15.2 %up_grad.1 = (f32[512,768]{1,0:T(8,128)S(1)}, bf16[512,768]{1,0:T(8,128)(2,1)S(1)}, f32[8,768]{1,0:T(8,128)S(1)}, bf16[4,192,1536]{2,1,0:T(8,128)(2,1)S(1)}, bf16[4,192,1536]{2,1,0:T(8,128)(2,1)S(1)}) custom-call(s32[1]{0:T(128)} %bitcast.ids_ref, bf16[512,768]{1,0:T(8,128)(2,1)S(1)} %get-tuple-element.333.refs_0_, ...), custom_call_target="tpu_custom_call" | custom-call | flops 7247757312 | bytes 31457280 | tf_op jit(solution)/shard_map/up_grad/pallas_call | solution.py:161
  159.1 1.1 join_sums.16
  160.2 1.6 collective-permute-start.23
  161.8 1.4 collective-permute-start.22
  163.2 4.5 %collective-permute-start.20 = (bf16[192,1536]{1,0:T(8,128)(2,1)S(1)}, bf16[192,1536]{1,0:T(8,128)(2,1)S(1)}, u32[]{:S(2)}, u32[]{:S(2)}) collective-permute-start(bf16[192,1536]{1,0:T(8,128)(2,1)S(1)} %get-tuple-element.381), channel_id=1, source_target_pairs={{0,1},{1,0},{2,3},{3,2},{4,5},{5,4},{6,7},{7,6},{8,9},{9,8},{10,11... | collective-permute-start | bytes 1769480 | tf_op jit(solution)/shard_map/ppermute | solution.py:1249
  167.7 0.9 collective-permute-start.21
  168.7 17.2 %attend_grad.3 = (f32[512,768]{1,0:T(8,128)}, bf16[512,768]{1,0:T(8,128)(2,1)}, bf16[4,208,1536]{2,1,0:T(8,128)(2,1)S(1)}, bf16[4,208,1536]{2,1,0:T(8,128)(2,1)S(1)}) custom-call(s32[1]{0:T(128)} %bitcast.ids_ref, bf16[512,768]{1,0:T(8,128)(2,1)S(1)} %get-tuple-element.359.refs_0_, bf16[768,512]{1,0:T(8,128)(2,1)} %get-tuple-element.362.refs_1_, ...), custom_call_target="tpu_custom_call" | custom-call | flops 6039797760 | bytes 31457280 | tf_op jit(solution)/shard_map/attend_grad/pallas_call | solution.py:161
  186.0 1.2 join_sums.17
  188.4 3.7 %collective-permute-start.27 = (bf16[208,1536]{1,0:T(8,128)(2,1)S(1)}, bf16[208,1536]{1,0:T(8,128)(2,1)S(1)}, u32[]{:S(2)}, u32[]{:S(2)}) collective-permute-start(bf16[208,1536]{1,0:T(8,128)(2,1)S(1)} %get-tuple-element.401), channel_id=1, source_target_pairs={{0,1},{1,0},{2,3},{3,2},{4,5},{5,4},{6,7},{7,6},{8,9},{9,8},{10,11... | collective-permute-start | bytes 1916936 | tf_op jit(solution)/shard_map/ppermute | solution.py:1249
  192.1 14.5 %collective-permute-done.27.refs_1_ = bf16[208,1536]{1,0:T(8,128)(2,1)S(1)} collective-permute-done((bf16[208,1536]{1,0:T(8,128)(2,1)S(1)}, bf16[208,1536]{1,0:T(8,128)(2,1)S(1)}, u32[]{:S(2)}, u32[]{:S(2)}) %collective-permute-start.27) | collective-permute-done | bytes 639008 | tf_op jit(solution)/shard_map/ppermute | solution.py:1249
  206.6 2.8 collective-permute-done.28.refs_5_
  209.7 1.2 join_sums.18
  210.9 1.5 collective-permute-start.33
  213.6 4.5 %collective-permute-start.31 = (bf16[192,1536]{1,0:T(8,128)(2,1)S(1)}, bf16[192,1536]{1,0:T(8,128)(2,1)S(1)}, u32[]{:S(2)}, u32[]{:S(2)}) collective-permute-start(bf16[192,1536]{1,0:T(8,128)(2,1)S(1)} %get-tuple-element.416), channel_id=1, source_target_pairs={{0,1},{1,0},{2,3},{3,2},{4,5},{5,4},{6,7},{7,6},{8,9},{9,8},{10,11... | collective-permute-start | bytes 1769480 | tf_op jit(solution)/shard_map/ppermute | solution.py:1249
  218.3 11.8 %collective-permute-done.31.refs_3_ = bf16[192,1536]{1,0:T(8,128)(2,1)S(1)} collective-permute-done((bf16[192,1536]{1,0:T(8,128)(2,1)S(1)}, bf16[192,1536]{1,0:T(8,128)(2,1)S(1)}, u32[]{:S(2)}, u32[]{:S(2)}) %collective-permute-start.31) | collective-permute-done | bytes 589856 | tf_op jit(solution)/shard_map/ppermute | solution.py:1249
  230.1 2.9 collective-permute-done.34.refs_7_
  233.1 1.0 collective-permute-done.33.refs_6_
  234.0 1.0 join_sums.19
  235.0 2.9 collective-permute-start.35
  239.3 1.3 collective-permute-start.38
  240.7 5.0 %collective-permute-done.37.refs_7_ = bf16[96,1536]{1,0:T(8,128)(2,1)S(1)} collective-permute-done((bf16[96,1536]{1,0:T(8,128)(2,1)S(1)}, bf16[96,1536]{1,0:T(8,128)(2,1)S(1)}, u32[]{:S(2)}, u32[]{:S(2)}) %collective-permute-start.37) | collective-permute-done | bytes 294944 | tf_op jit(solution)/shard_map/ppermute | solution.py:1012
  245.8 1.4 collective-permute-done.38.refs_8_
  247.2 3.7 %collective-permute-done.35.refs_1_ = bf16[208,1536]{1,0:T(8,128)(2,1)S(1)} collective-permute-done((bf16[208,1536]{1,0:T(8,128)(2,1)S(1)}, bf16[208,1536]{1,0:T(8,128)(2,1)S(1)}, u32[]{:S(2)}, u32[]{:S(2)}) %collective-permute-start.35) | collective-permute-done | bytes 639008 | tf_op jit(solution)/shard_map/ppermute | solution.py:1249
  250.9 0.9 join_sums.20
  251.8 2.7 collective-permute-start.39
  255.2 11.3 %collective-permute-done.39.refs_1_ = bf16[208,1536]{1,0:T(8,128)(2,1)S(1)} collective-permute-done((bf16[208,1536]{1,0:T(8,128)(2,1)S(1)}, bf16[208,1536]{1,0:T(8,128)(2,1)S(1)}, u32[]{:S(2)}, u32[]{:S(2)}) %collective-permute-start.39) | collective-permute-done | bytes 639008 | tf_op jit(solution)/shard_map/ppermute | solution.py:1249
  266.6 0.9 join_sums.21
  268.2 4.3 %collective-permute-start.41 = (bf16[192,1536]{1,0:T(8,128)(2,1)S(1)}, bf16[192,1536]{1,0:T(8,128)(2,1)S(1)}, u32[]{:S(2)}, u32[]{:S(2)}) collective-permute-start(bf16[192,1536]{1,0:T(8,128)(2,1)S(1)} %get-tuple-element.451), channel_id=1, source_target_pairs={{0,1},{1,0},{2,3},{3,2},{4,5},{5,4},{6,7},{7,6},{8,9},{9,8},{10,11... | collective-permute-start | bytes 1769480 | tf_op jit(solution)/shard_map/ppermute | solution.py:1249
  272.5 5.4 %assemble.1 = (bf16[2,512,768]{2,1,0:T(8,128)(2,1)}, f32[2,512,768]{2,1,0:T(8,128)}) custom-call(s32[1]{0:T(128)} %bitcast.ids_ref, bf16[512,768]{1,0:T(8,128)(2,1)} %get-tuple-element.294.refs_3_.refs_0_, bf16[512,768]{1,0:T(8,128)(2,1)} %get-tuple-element.387.refs_1_, bf16[512,768]{1,0:T(8,128)(2,1)} %copy-done.13, f32[512,768]{1,0:T(8,128)} %get-tuple-element.386.refs_3_, ...), custom_call_target="tpu_custom_call" | custom-call | flops 1000 | bytes 10485760 | tf_op jit(solution)/shard_map/assemble/pallas_call | solution.py:161
  277.9 4.5 %collective-permute-done.41.refs_1_ = bf16[192,1536]{1,0:T(8,128)(2,1)S(1)} collective-permute-done((bf16[192,1536]{1,0:T(8,128)(2,1)S(1)}, bf16[192,1536]{1,0:T(8,128)(2,1)S(1)}, u32[]{:S(2)}, u32[]{:S(2)}) %collective-permute-start.41) | collective-permute-done | bytes 589856 | tf_op jit(solution)/shard_map/ppermute | solution.py:1249
  283.1 2.7 collective-permute-start.45
  285.8 10.3 %collective-permute-done.45.refs_1_ = bf16[208,1536]{1,0:T(8,128)(2,1)S(1)} collective-permute-done((bf16[208,1536]{1,0:T(8,128)(2,1)S(1)}, bf16[208,1536]{1,0:T(8,128)(2,1)S(1)}, u32[]{:S(2)}, u32[]{:S(2)}) %collective-permute-start.45) | collective-permute-done | bytes 639008 | tf_op jit(solution)/shard_map/ppermute | solution.py:1249
  297.4 2.3 collective-permute-done.43.refs_1_
  299.8 0.8 collective-permute-done.44.refs_3_
  300.6 4.5 %last.1 = (f32[768,768]{1,0:T(8,128)}, f32[192,2304]{1,0:T(8,128)}, f32[192,768]{1,0:T(8,128)}, f32[2,192]{1,0:T(2,128)}, f32[1,192]{1,0:T(1,128)}, /*index=5*/f...) custom-call(s32[5]{0:T(128)S(1)} %stack.24.ids_ref, ...), custom_call_target="tpu_custom_call" | custom-call | flops 1000 | bytes 5242880 | tf_op jit(solution)/shard_map/last/pallas_call | solution.py:161
  (106 shorter events, 18.8 us)
Async XLA Ops:
  0.6 4.9 %copy-start = (bf16[8,128,768]{2,1,0:T(8,128)(2,1)S(1)}, bf16[8,128,768]{2,1,0:T(8,128)(2,1)}, u32[]{:S(2)}) copy-start(bf16[8,128,768]{2,1,0:T(8,128)(2,1)} %param.14) | copy-start | bytes 4718596
  0.7 7.4 %collective-permute-start = (bf16[768,2304]{1,0:T(8,128)(2,1)}, bf16[768,2304]{1,0:T(8,128)(2,1)}, u32[]{:S(2)}, u32[]{:S(2)}) collective-permute-start(bf16[768,2304]{1,0:T(8,128)(2,1)} %bitcast.52), channel_id=1, source_target_pairs={{0,16},{16,0},{1,17},{17,1},{2,18},{18,2},{3,19},{19,3},{4,20},{20... | collective-permute-start | bytes 10616840 | tf_op jit(solution)/shard_map/ppermute | solution.py:1012
  3.9 3.5 %collective-permute-start.1 = (f32[16,768]{1,0:T(8,128)S(1)}, f32[16,768]{1,0:T(8,128)S(1)}, u32[]{:S(2)}, u32[]{:S(2)}) collective-permute-start(f32[16,768]{1,0:T(8,128)S(1)} %concatenate.6), channel_id=1, source_target_pairs={{0,16},{16,0},{1,17},{17,1},{2,18},{18,2},{3,19},{19,3},{4,20},{20... | collective-permute-start | bytes 147464 | tf_op jit(solution)/shard_map/ppermute | solution.py:1012
  7.4 10.5 %slice-start = ((s8[4718592]{0:T(1024)(128)(4,1)}), s8[4194304]{0:T(1024)(128)(4,1)S(1)}, s32[]{:S(2)}) async-start(s8[4718592]{0:T(1024)(128)(4,1)} %bitcast.29), calls=%async_computation | async-start | bytes 8388608
  8.0 9.9 %collective-permute-start.3 = (bf16[768,3072]{1,0:T(8,128)(2,1)}, bf16[768,3072]{1,0:T(8,128)(2,1)S(1)}, u32[]{:S(2)}, u32[]{:S(2)}) collective-permute-start(bf16[768,3072]{1,0:T(8,128)(2,1)} %bitcast.32), channel_id=1, source_target_pairs={{0,16},{16,0},{1,17},{17,1},{2,18},{18,2},{3,19},{19,3},{4,20},{20... | collective-permute-start | bytes 14155784 | tf_op jit(solution)/shard_map/ppermute | solution.py:1012
  8.5 9.4 %collective-permute-start.2 = (bf16[768,768]{1,0:T(8,128)(2,1)}, bf16[768,768]{1,0:T(8,128)(2,1)S(1)}, u32[]{:S(2)}, u32[]{:S(2)}) collective-permute-start(bf16[768,768]{1,0:T(8,128)(2,1)} %bitcast.41), channel_id=1, source_target_pairs={{0,16},{16,0},{1,17},{17,1},{2,18},{18,2},{3,19},{19,3},{4,20},{20... | collective-permute-start | bytes 3538952 | tf_op jit(solution)/shard_map/ppermute | solution.py:1012
  8.5 9.4 %slice-start.1 = ((s8[4718592]{0:T(1024)(128)(4,1)}), s8[524288]{0:T(1024)(128)(4,1)S(1)}, s32[]{:S(2)}) async-start(s8[4718592]{0:T(1024)(128)(4,1)} %bitcast.29), calls=%async_computation.1 | async-start | bytes 1048576
  8.5 9.8 %copy-start.14 = (bf16[8,128,768]{2,1,0:T(8,128)(2,1)S(1)}, bf16[8,128,768]{2,1,0:T(8,128)(2,1)}, u32[]{:S(2)}) copy-start(bf16[8,128,768]{2,1,0:T(8,128)(2,1)} %param.17) | copy-start | bytes 4718596
  17.9 14.4 %copy-start.6 = (bf16[768,768]{1,0:T(8,128)(2,1)}, bf16[768,768]{1,0:T(8,128)(2,1)S(1)}, u32[]{:S(2)}) copy-start(bf16[768,768]{1,0:T(8,128)(2,1)S(1)} %collective-permute-done.2.refs_3_.refs_6_.refs_9_) | copy-start | bytes 3538948
  17.9 14.4 %copy-start.3 = (bf16[768,3072]{1,0:T(8,128)(2,1)}, bf16[768,3072]{1,0:T(8,128)(2,1)S(1)}, u32[]{:S(2)}) copy-start(bf16[768,3072]{1,0:T(8,128)(2,1)S(1)} %collective-permute-done.3.refs_5_.refs_8_.refs_7_) | copy-start | bytes 14155780
  17.9 14.4 %collective-permute-start.4 = (bf16[3072,768]{1,0:T(8,128)(2,1)S(1)}, bf16[3072,768]{1,0:T(8,128)(2,1)S(1)}, u32[]{:S(2)}, u32[]{:S(2)}) collective-permute-start(bf16[3072,768]{1,0:T(8,128)(2,1)S(1)} %bitcast.31), channel_id=1, source_target_pairs={{0,16},{16,0},{1,17},{17,1},{2,18},{18,2},{3,19},{19,3},{4,20},{20... | collective-permute-start | bytes 14155784 | tf_op jit(solution)/shard_map/ppermute | solution.py:1012
  32.3 9.0 %copy-start.2 = (bf16[3072,768]{1,0:T(8,128)(2,1)}, bf16[3072,768]{1,0:T(8,128)(2,1)S(1)}, u32[]{:S(2)}) copy-start(bf16[3072,768]{1,0:T(8,128)(2,1)S(1)} %collective-permute-done.4.refs_2_.refs_10_.refs_3_) | copy-start | bytes 14155780
  66.5 9.9 %collective-permute-start.5 = (bf16[4,192,1536]{2,1,0:T(8,128)(2,1)S(1)}, bf16[4,192,1536]{2,1,0:T(8,128)(2,1)S(1)}, u32[]{:S(2)}, u32[]{:S(2)}) collective-permute-start(bf16[4,192,1536]{2,1,0:T(8,128)(2,1)S(1)} %get-tuple-element.274), channel_id=1, source_target_pairs={{0,16},{16,0},{1,17},{17,1},{2,18},{18,2},{3,19},{19,3},{4,20},{20... | collective-permute-start | bytes 7077896 | tf_op jit(solution)/shard_map/ppermute | solution.py:1012
  75.3 1.2 copy-start.4
  76.5 1.4 copy-start.11
  77.9 21.8 %collective-permute-start.8 = (bf16[4,192,1536]{2,1,0:T(8,128)(2,1)}, bf16[4,192,1536]{2,1,0:T(8,128)(2,1)S(1)}, u32[]{:S(2)}, u32[]{:S(2)}) collective-permute-start(bf16[4,192,1536]{2,1,0:T(8,128)(2,1)} %get-tuple-element.289), channel_id=1, source_target_pairs={{0,16},{16,0},{1,17},{17,1},{2,18},{18,2},{3,19},{19,3},{4,20},{20... | collective-permute-start | bytes 7077896 | tf_op jit(solution)/shard_map/ppermute | solution.py:1012
  78.5 7.7 %copy-start.5 = (f32[512,768]{1,0:T(8,128)S(1)}, f32[512,768]{1,0:T(8,128)}, u32[]{:S(2)}) copy-start(f32[512,768]{1,0:T(8,128)} %copy-done.4) | copy-start | bytes 4718596
  81.7 16.5 %collective-permute-start.6 = (bf16[192,1536]{1,0:T(8,128)(2,1)S(1)}, bf16[192,1536]{1,0:T(8,128)(2,1)S(1)}, u32[]{:S(2)}, u32[]{:S(2)}) collective-permute-start(bf16[192,1536]{1,0:T(8,128)(2,1)S(1)} %get-tuple-element.287), channel_id=1, source_target_pairs={{0,4},{4,0},{8,12},{12,8},{1,5},{5,1},{9,13},{13,9},{2,6},{6,2},{1... | collective-permute-start | bytes 1769480 | tf_op jit(solution)/shard_map/ppermute | solution.py:1012
  84.7 15.0 %collective-permute-start.7 = (bf16[192,1536]{1,0:T(8,128)(2,1)S(1)}, bf16[192,1536]{1,0:T(8,128)(2,1)S(1)}, u32[]{:S(2)}, u32[]{:S(2)}) collective-permute-start(bf16[192,1536]{1,0:T(8,128)(2,1)S(1)} %get-tuple-element.288), channel_id=1, source_target_pairs={{0,8},{4,12},{8,0},{12,4},{1,9},{5,13},{9,1},{13,5},{2,10},{6,14},... | collective-permute-start | bytes 1769480 | tf_op jit(solution)/shard_map/ppermute | solution.py:1012
  100.6 20.4 %collective-permute-start.10 = (bf16[288,1536]{1,0:T(8,128)(2,1)S(1)}, bf16[288,1536]{1,0:T(8,128)(2,1)S(1)}, u32[]{:S(2)}, u32[]{:S(2)}) collective-permute-start(bf16[288,1536]{1,0:T(8,128)(2,1)S(1)} %get-tuple-element.311), channel_id=1, source_target_pairs={{0,8},{4,12},{8,0},{12,4},{1,9},{5,13},{9,1},{13,5},{2,10},{6,14},... | collective-permute-start | bytes 2654216 | tf_op jit(solution)/shard_map/ppermute | solution.py:1012
  102.2 20.1 %collective-permute-start.9 = (bf16[288,1536]{1,0:T(8,128)(2,1)S(1)}, bf16[288,1536]{1,0:T(8,128)(2,1)S(1)}, u32[]{:S(2)}, u32[]{:S(2)}) collective-permute-start(bf16[288,1536]{1,0:T(8,128)(2,1)S(1)} %get-tuple-element.310), channel_id=1, source_target_pairs={{0,4},{4,0},{8,12},{12,8},{1,5},{5,1},{9,13},{13,9},{2,6},{6,2},{1... | collective-permute-start | bytes 2654216 | tf_op jit(solution)/shard_map/ppermute | solution.py:1012
  122.3 16.7 %collective-permute-start.14 = (bf16[4,208,1536]{2,1,0:T(8,128)(2,1)S(1)}, bf16[4,208,1536]{2,1,0:T(8,128)(2,1)S(1)}, u32[]{:S(2)}, u32[]{:S(2)}) collective-permute-start(bf16[4,208,1536]{2,1,0:T(8,128)(2,1)S(1)} %get-tuple-element.332), channel_id=1, source_target_pairs={{0,16},{16,0},{1,17},{17,1},{2,18},{18,2},{3,19},{19,3},{4,20},{20... | collective-permute-start | bytes 7667720 | tf_op jit(solution)/shard_map/ppermute | solution.py:1012
  123.2 15.8 %collective-permute-start.11 = (bf16[192,1536]{1,0:T(8,128)(2,1)S(1)}, bf16[192,1536]{1,0:T(8,128)(2,1)S(1)}, u32[]{:S(2)}, u32[]{:S(2)}) collective-permute-start(bf16[192,1536]{1,0:T(8,128)(2,1)S(1)} %get-tuple-element.329), channel_id=1, source_target_pairs={{0,1},{1,0},{2,3},{3,2},{4,5},{5,4},{6,7},{7,6},{8,9},{9,8},{10,11... | collective-permute-start | bytes 1769480 | tf_op jit(solution)/shard_map/ppermute | solution.py:1249
  124.8 9.1 %collective-permute-start.12 = (bf16[96,1536]{1,0:T(8,128)(2,1)S(1)}, bf16[96,1536]{1,0:T(8,128)(2,1)S(1)}, u32[]{:S(2)}, u32[]{:S(2)}) collective-permute-start(bf16[96,1536]{1,0:T(8,128)(2,1)S(1)} %get-tuple-element.330), channel_id=1, source_target_pairs={{0,4},{4,0},{8,12},{12,8},{1,5},{5,1},{9,13},{13,9},{2,6},{6,2},{1... | collective-permute-start | bytes 884744 | tf_op jit(solution)/shard_map/ppermute | solution.py:1012
  125.4 8.9 %collective-permute-start.13 = (bf16[96,1536]{1,0:T(8,128)(2,1)S(1)}, bf16[96,1536]{1,0:T(8,128)(2,1)S(1)}, u32[]{:S(2)}, u32[]{:S(2)}) collective-permute-start(bf16[96,1536]{1,0:T(8,128)(2,1)S(1)} %get-tuple-element.331), channel_id=1, source_target_pairs={{0,8},{4,12},{8,0},{12,4},{1,9},{5,13},{9,1},{13,5},{2,10},{6,14},... | collective-permute-start | bytes 884744 | tf_op jit(solution)/shard_map/ppermute | solution.py:1012
  139.0 20.0 %collective-permute-start.19 = (bf16[4,192,1536]{2,1,0:T(8,128)(2,1)S(1)}, bf16[4,192,1536]{2,1,0:T(8,128)(2,1)S(1)}, u32[]{:S(2)}, u32[]{:S(2)}) collective-permute-start(bf16[4,192,1536]{2,1,0:T(8,128)(2,1)S(1)} %get-tuple-element.358), channel_id=1, source_target_pairs={{0,16},{16,0},{1,17},{17,1},{2,18},{18,2},{3,19},{19,3},{4,20},{20... | collective-permute-start | bytes 7077896 | tf_op jit(solution)/shard_map/ppermute | solution.py:1012
  140.1 18.9 %collective-permute-start.17 = (bf16[224,1536]{1,0:T(8,128)(2,1)S(1)}, bf16[224,1536]{1,0:T(8,128)(2,1)S(1)}, u32[]{:S(2)}, u32[]{:S(2)}) collective-permute-start(bf16[224,1536]{1,0:T(8,128)(2,1)S(1)} %get-tuple-element.356), channel_id=1, source_target_pairs={{0,4},{4,0},{8,12},{12,8},{1,5},{5,1},{9,13},{13,9},{2,6},{6,2},{1... | collective-permute-start | bytes 2064392 | tf_op jit(solution)/shard_map/ppermute | solution.py:1012
  140.8 18.2 %collective-permute-start.15 = (bf16[192,1536]{1,0:T(8,128)(2,1)S(1)}, bf16[192,1536]{1,0:T(8,128)(2,1)S(1)}, u32[]{:S(2)}, u32[]{:S(2)}) collective-permute-start(bf16[192,1536]{1,0:T(8,128)(2,1)S(1)} %get-tuple-element.354), channel_id=1, source_target_pairs={{0,1},{1,0},{2,3},{3,2},{4,5},{5,4},{6,7},{7,6},{8,9},{9,8},{10,11... | collective-permute-start | bytes 1769480 | tf_op jit(solution)/shard_map/ppermute | solution.py:1249
  142.3 16.7 %collective-permute-start.16 = (bf16[192,1536]{1,0:T(8,128)(2,1)S(1)}, bf16[192,1536]{1,0:T(8,128)(2,1)S(1)}, u32[]{:S(2)}, u32[]{:S(2)}) collective-permute-start(bf16[192,1536]{1,0:T(8,128)(2,1)S(1)} %get-tuple-element.355.refs_0_), channel_id=1, source_target_pairs={{1,2},{2,1},{5,6},{6,5},{9,10},{10,9},{13,14},{14,13},{17,18},{18,... | collective-permute-start | bytes 1769480 | tf_op jit(solution)/shard_map/ppermute | solution.py:1249
  143.2 15.8 %collective-permute-start.18 = (bf16[192,1536]{1,0:T(8,128)(2,1)S(1)}, bf16[192,1536]{1,0:T(8,128)(2,1)S(1)}, u32[]{:S(2)}, u32[]{:S(2)}) collective-permute-start(bf16[192,1536]{1,0:T(8,128)(2,1)S(1)} %get-tuple-element.357), channel_id=1, source_target_pairs={{0,8},{4,12},{8,0},{12,4},{1,9},{5,13},{9,1},{13,5},{2,10},{6,14},... | collective-permute-start | bytes 1769480 | tf_op jit(solution)/shard_map/ppermute | solution.py:1012
  159.0 26.9 %collective-permute-start.24 = (bf16[4,192,1536]{2,1,0:T(8,128)(2,1)S(1)}, bf16[4,192,1536]{2,1,0:T(8,128)(2,1)S(1)}, u32[]{:S(2)}, u32[]{:S(2)}) collective-permute-start(bf16[4,192,1536]{2,1,0:T(8,128)(2,1)S(1)} %get-tuple-element.385), channel_id=1, source_target_pairs={{0,16},{16,0},{1,17},{17,1},{2,18},{18,2},{3,19},{19,3},{4,20},{20... | collective-permute-start | bytes 7077896 | tf_op jit(solution)/shard_map/ppermute | solution.py:1012
  160.2 25.7 %collective-permute-start.23 = (bf16[304,1536]{1,0:T(8,128)(2,1)S(1)}, bf16[304,1536]{1,0:T(8,128)(2,1)S(1)}, u32[]{:S(2)}, u32[]{:S(2)}) collective-permute-start(bf16[304,1536]{1,0:T(8,128)(2,1)S(1)} %get-tuple-element.384), channel_id=1, source_target_pairs={{0,8},{4,12},{8,0},{12,4},{1,9},{5,13},{9,1},{13,5},{2,10},{6,14},... | collective-permute-start | bytes 2801672 | tf_op jit(solution)/shard_map/ppermute | solution.py:1012
  161.8 24.1 %collective-permute-start.22 = (bf16[288,1536]{1,0:T(8,128)(2,1)S(1)}, bf16[288,1536]{1,0:T(8,128)(2,1)S(1)}, u32[]{:S(2)}, u32[]{:S(2)}) collective-permute-start(bf16[288,1536]{1,0:T(8,128)(2,1)S(1)} %get-tuple-element.383), channel_id=1, source_target_pairs={{0,4},{4,0},{8,12},{12,8},{1,5},{5,1},{9,13},{13,9},{2,6},{6,2},{1... | collective-permute-start | bytes 2654216 | tf_op jit(solution)/shard_map/ppermute | solution.py:1012
  163.2 22.7 %collective-permute-start.20 = (bf16[192,1536]{1,0:T(8,128)(2,1)S(1)}, bf16[192,1536]{1,0:T(8,128)(2,1)S(1)}, u32[]{:S(2)}, u32[]{:S(2)}) collective-permute-start(bf16[192,1536]{1,0:T(8,128)(2,1)S(1)} %get-tuple-element.381), channel_id=1, source_target_pairs={{0,1},{1,0},{2,3},{3,2},{4,5},{5,4},{6,7},{7,6},{8,9},{9,8},{10,11... | collective-permute-start | bytes 1769480 | tf_op jit(solution)/shard_map/ppermute | solution.py:1249
  167.7 18.2 %collective-permute-start.21 = (bf16[192,1536]{1,0:T(8,128)(2,1)S(1)}, bf16[192,1536]{1,0:T(8,128)(2,1)S(1)}, u32[]{:S(2)}, u32[]{:S(2)}) collective-permute-start(bf16[192,1536]{1,0:T(8,128)(2,1)S(1)} %get-tuple-element.382.refs_2_), channel_id=1, source_target_pairs={{1,2},{2,1},{5,6},{6,5},{9,10},{10,9},{13,14},{14,13},{17,18},{18,... | collective-permute-start | bytes 1769480 | tf_op jit(solution)/shard_map/ppermute | solution.py:1249
  186.0 23.7 %collective-permute-start.30 = (bf16[4,208,1536]{2,1,0:T(8,128)(2,1)S(1)}, bf16[4,208,1536]{2,1,0:T(8,128)(2,1)S(1)}, u32[]{:S(2)}, u32[]{:S(2)}) collective-permute-start(bf16[4,208,1536]{2,1,0:T(8,128)(2,1)S(1)} %get-tuple-element.404), channel_id=1, source_target_pairs={{0,16},{16,0},{1,17},{17,1},{2,18},{18,2},{3,19},{19,3},{4,20},{20... | collective-permute-start | bytes 7667720 | tf_op jit(solution)/shard_map/ppermute | solution.py:1012
  187.3 22.1 %collective-permute-start.28 = (bf16[288,1536]{1,0:T(8,128)(2,1)S(1)}, bf16[288,1536]{1,0:T(8,128)(2,1)S(1)}, u32[]{:S(2)}, u32[]{:S(2)}) collective-permute-start(bf16[288,1536]{1,0:T(8,128)(2,1)S(1)} %get-tuple-element.402), channel_id=1, source_target_pairs={{0,4},{4,0},{8,12},{12,8},{1,5},{5,1},{9,13},{13,9},{2,6},{6,2},{1... | collective-permute-start | bytes 2654216 | tf_op jit(solution)/shard_map/ppermute | solution.py:1012
  187.9 21.8 %collective-permute-start.29 = (bf16[288,1536]{1,0:T(8,128)(2,1)S(1)}, bf16[288,1536]{1,0:T(8,128)(2,1)S(1)}, u32[]{:S(2)}, u32[]{:S(2)}) collective-permute-start(bf16[288,1536]{1,0:T(8,128)(2,1)S(1)} %get-tuple-element.403), channel_id=1, source_target_pairs={{0,8},{4,12},{8,0},{12,4},{1,9},{5,13},{9,1},{13,5},{2,10},{6,14},... | collective-permute-start | bytes 2654216 | tf_op jit(solution)/shard_map/ppermute | solution.py:1012
  188.4 18.1 %collective-permute-start.27 = (bf16[208,1536]{1,0:T(8,128)(2,1)S(1)}, bf16[208,1536]{1,0:T(8,128)(2,1)S(1)}, u32[]{:S(2)}, u32[]{:S(2)}) collective-permute-start(bf16[208,1536]{1,0:T(8,128)(2,1)S(1)} %get-tuple-element.401), channel_id=1, source_target_pairs={{0,1},{1,0},{2,3},{3,2},{4,5},{5,4},{6,7},{7,6},{8,9},{9,8},{10,11... | collective-permute-start | bytes 1916936 | tf_op jit(solution)/shard_map/ppermute | solution.py:1249
  209.7 8.4 %copy-start.7 = (f32[512,768]{1,0:T(8,128)S(1)}, f32[512,768]{1,0:T(8,128)}, u32[]{:S(2)}) copy-start(f32[512,768]{1,0:T(8,128)} %get-tuple-element.386.refs_3_) | copy-start | bytes 4718596
  209.7 8.4 %copy-start.10 = (bf16[512,768]{1,0:T(8,128)(2,1)S(1)}, bf16[512,768]{1,0:T(8,128)(2,1)}, u32[]{:S(2)}) copy-start(bf16[512,768]{1,0:T(8,128)(2,1)} %get-tuple-element.312.refs_4_) | copy-start | bytes 2359300
  210.9 23.1 %collective-permute-start.33 = (bf16[320,1536]{1,0:T(8,128)(2,1)S(1)}, bf16[320,1536]{1,0:T(8,128)(2,1)S(1)}, u32[]{:S(2)}, u32[]{:S(2)}) collective-permute-start(bf16[320,1536]{1,0:T(8,128)(2,1)S(1)} %get-tuple-element.417), channel_id=1, source_target_pairs={{0,4},{4,0},{8,12},{12,8},{1,5},{5,1},{9,13},{13,9},{2,6},{6,2},{1... | collective-permute-start | bytes 2949128 | tf_op jit(solution)/shard_map/ppermute | solution.py:1012
  212.4 20.7 %collective-permute-start.34 = (bf16[288,1536]{1,0:T(8,128)(2,1)S(1)}, bf16[288,1536]{1,0:T(8,128)(2,1)S(1)}, u32[]{:S(2)}, u32[]{:S(2)}) collective-permute-start(bf16[288,1536]{1,0:T(8,128)(2,1)S(1)} %get-tuple-element.418), channel_id=1, source_target_pairs={{0,8},{4,12},{8,0},{12,4},{1,9},{5,13},{9,1},{13,5},{2,10},{6,14},... | collective-permute-start | bytes 2654216 | tf_op jit(solution)/shard_map/ppermute | solution.py:1012
  212.9 17.2 %collective-permute-start.32 = (bf16[208,1536]{1,0:T(8,128)(2,1)S(1)}, bf16[208,1536]{1,0:T(8,128)(2,1)S(1)}, u32[]{:S(2)}, u32[]{:S(2)}) collective-permute-start(bf16[208,1536]{1,0:T(8,128)(2,1)S(1)} %get-tuple-element.415.refs_0_), channel_id=1, source_target_pairs={{1,2},{2,1},{5,6},{6,5},{9,10},{10,9},{13,14},{14,13},{17,18},{18,... | collective-permute-start | bytes 1916936 | tf_op jit(solution)/shard_map/ppermute | solution.py:1249
  213.6 16.5 %collective-permute-start.31 = (bf16[192,1536]{1,0:T(8,128)(2,1)S(1)}, bf16[192,1536]{1,0:T(8,128)(2,1)S(1)}, u32[]{:S(2)}, u32[]{:S(2)}) collective-permute-start(bf16[192,1536]{1,0:T(8,128)(2,1)S(1)} %get-tuple-element.416), channel_id=1, source_target_pairs={{0,1},{1,0},{2,3},{3,2},{4,5},{5,4},{6,7},{7,6},{8,9},{9,8},{10,11... | collective-permute-start | bytes 1769480 | tf_op jit(solution)/shard_map/ppermute | solution.py:1249
  218.2 37.0 %collective-permute-start.25 = (f32[512,768]{1,0:T(8,128)S(1)}, f32[512,768]{1,0:T(8,128)S(1)}, u32[]{:S(2)}, u32[]{:S(2)}) collective-permute-start(f32[512,768]{1,0:T(8,128)S(1)} %convert_select_fusion), channel_id=1, source_target_pairs={{0,16},{16,0},{1,17},{17,1},{2,18},{18,2},{3,19},{19,3},{4,20},{20... | collective-permute-start | bytes 4718600 | tf_op jit(solution)/shard_map/ppermute | solution.py:1012
  234.0 6.6 %copy-start.8 = (bf16[512,768]{1,0:T(8,128)(2,1)S(1)}, bf16[512,768]{1,0:T(8,128)(2,1)}, u32[]{:S(2)}) copy-start(bf16[512,768]{1,0:T(8,128)(2,1)} %get-tuple-element.294.refs_3_.refs_0_) | copy-start | bytes 2359300
  234.0 6.6 %copy-start.9 = (bf16[512,768]{1,0:T(8,128)(2,1)S(1)}, bf16[512,768]{1,0:T(8,128)(2,1)}, u32[]{:S(2)}) copy-start(bf16[512,768]{1,0:T(8,128)(2,1)} %get-tuple-element.387.refs_1_) | copy-start | bytes 2359300
  235.0 15.9 %collective-permute-start.35 = (bf16[208,1536]{1,0:T(8,128)(2,1)S(1)}, bf16[208,1536]{1,0:T(8,128)(2,1)S(1)}, u32[]{:S(2)}, u32[]{:S(2)}) collective-permute-start(bf16[208,1536]{1,0:T(8,128)(2,1)S(1)} %get-tuple-element.429), channel_id=1, source_target_pairs={{0,1},{1,0},{2,3},{3,2},{4,5},{5,4},{6,7},{7,6},{8,9},{9,8},{10,11... | collective-permute-start | bytes 1916936 | tf_op jit(solution)/shard_map/ppermute | solution.py:1249
  237.9 9.3 %collective-permute-start.36 = (bf16[192,1536]{1,0:T(8,128)(2,1)S(1)}, bf16[192,1536]{1,0:T(8,128)(2,1)S(1)}, u32[]{:S(2)}, u32[]{:S(2)}) collective-permute-start(bf16[192,1536]{1,0:T(8,128)(2,1)S(1)} %get-tuple-element.430.refs_2_), channel_id=1, source_target_pairs={{1,2},{2,1},{5,6},{6,5},{9,10},{10,9},{13,14},{14,13},{17,18},{18,... | collective-permute-start | bytes 1769480 | tf_op jit(solution)/shard_map/ppermute | solution.py:1249
  238.6 7.2 %collective-permute-start.37 = (bf16[96,1536]{1,0:T(8,128)(2,1)S(1)}, bf16[96,1536]{1,0:T(8,128)(2,1)S(1)}, u32[]{:S(2)}, u32[]{:S(2)}) collective-permute-start(bf16[96,1536]{1,0:T(8,128)(2,1)S(1)} %get-tuple-element.431), channel_id=1, source_target_pairs={{0,4},{4,0},{8,12},{12,8},{1,5},{5,1},{9,13},{13,9},{2,6},{6,2},{1... | collective-permute-start | bytes 884744 | tf_op jit(solution)/shard_map/ppermute | solution.py:1012
  239.3 7.9 %collective-permute-start.38 = (bf16[112,1536]{1,0:T(8,128)(2,1)S(1)}, bf16[112,1536]{1,0:T(8,128)(2,1)S(1)}, u32[]{:S(2)}, u32[]{:S(2)}) collective-permute-start(bf16[112,1536]{1,0:T(8,128)(2,1)S(1)} %get-tuple-element.432), channel_id=1, source_target_pairs={{0,8},{4,12},{8,0},{12,4},{1,9},{5,13},{9,1},{13,5},{2,10},{6,14},... | collective-permute-start | bytes 1032200 | tf_op jit(solution)/shard_map/ppermute | solution.py:1012
  245.8 9.4 %collective-permute-start.26 = (bf16[512,768]{1,0:T(8,128)(2,1)S(1)}, bf16[512,768]{1,0:T(8,128)(2,1)S(1)}, u32[]{:S(2)}, u32[]{:S(2)}) collective-permute-start(bf16[512,768]{1,0:T(8,128)(2,1)S(1)} %broadcast_select_fusion), channel_id=1, source_target_pairs={{0,16},{16,0},{1,17},{17,1},{2,18},{18,2},{3,19},{19,3},{4,20},{20... | collective-permute-start | bytes 2359304 | tf_op jit(solution)/shard_map/ppermute | solution.py:1012
  251.8 14.8 %collective-permute-start.39 = (bf16[208,1536]{1,0:T(8,128)(2,1)S(1)}, bf16[208,1536]{1,0:T(8,128)(2,1)S(1)}, u32[]{:S(2)}, u32[]{:S(2)}) collective-permute-start(bf16[208,1536]{1,0:T(8,128)(2,1)S(1)} %get-tuple-element.440), channel_id=1, source_target_pairs={{0,1},{1,0},{2,3},{3,2},{4,5},{5,4},{6,7},{7,6},{8,9},{9,8},{10,11... | collective-permute-start | bytes 1916936 | tf_op jit(solution)/shard_map/ppermute | solution.py:1249
  254.5 0.7 collective-permute-start.40
  255.2 17.3 %copy-start.13 = (bf16[512,768]{1,0:T(8,128)(2,1)}, bf16[512,768]{1,0:T(8,128)(2,1)S(1)}, u32[]{:S(2)}) copy-start(bf16[512,768]{1,0:T(8,128)(2,1)S(1)} %collective-permute-done.26.refs_2_) | copy-start | bytes 2359300
  255.2 17.3 %copy-start.12 = (f32[512,768]{1,0:T(8,128)}, f32[512,768]{1,0:T(8,128)S(1)}, u32[]{:S(2)}) copy-start(f32[512,768]{1,0:T(8,128)S(1)} %collective-permute-done.25.refs_5_) | copy-start | bytes 4718596
  267.5 14.9 %collective-permute-start.42 = (bf16[208,1536]{1,0:T(8,128)(2,1)S(1)}, bf16[208,1536]{1,0:T(8,128)(2,1)S(1)}, u32[]{:S(2)}, u32[]{:S(2)}) collective-permute-start(bf16[208,1536]{1,0:T(8,128)(2,1)S(1)} %get-tuple-element.452.refs_3_), channel_id=1, source_target_pairs={{1,2},{2,1},{5,6},{6,5},{9,10},{10,9},{13,14},{14,13},{17,18},{18,... | collective-permute-start | bytes 1916936 | tf_op jit(solution)/shard_map/ppermute | solution.py:1249
  268.2 14.2 %collective-permute-start.41 = (bf16[192,1536]{1,0:T(8,128)(2,1)S(1)}, bf16[192,1536]{1,0:T(8,128)(2,1)S(1)}, u32[]{:S(2)}, u32[]{:S(2)}) collective-permute-start(bf16[192,1536]{1,0:T(8,128)(2,1)S(1)} %get-tuple-element.451), channel_id=1, source_target_pairs={{0,1},{1,0},{2,3},{3,2},{4,5},{5,4},{6,7},{7,6},{8,9},{9,8},{10,11... | collective-permute-start | bytes 1769480 | tf_op jit(solution)/shard_map/ppermute | solution.py:1249
  283.1 12.9 %collective-permute-start.45 = (bf16[208,1536]{1,0:T(8,128)(2,1)S(1)}, bf16[208,1536]{1,0:T(8,128)(2,1)S(1)}, u32[]{:S(2)}, u32[]{:S(2)}) collective-permute-start(bf16[208,1536]{1,0:T(8,128)(2,1)S(1)} %get-tuple-element.464), channel_id=1, source_target_pairs={{0,1},{1,0},{2,3},{3,2},{4,5},{5,4},{6,7},{7,6},{8,9},{9,8},{10,11... | collective-permute-start | bytes 1916936 | tf_op jit(solution)/shard_map/ppermute | solution.py:1249
  296.0 9.1 %copy-start.1 = (bf16[8,128,768]{2,1,0:T(8,128)(2,1)S(1)}, bf16[8,128,768]{2,1,0:T(8,128)(2,1)}, u32[]{:S(2)}) copy-start(bf16[8,128,768]{2,1,0:T(8,128)(2,1)} %param.14) | copy-start | bytes 4718596
  296.8 3.8 %collective-permute-start.46 = (bf16[208,1536]{1,0:T(8,128)(2,1)S(1)}, bf16[208,1536]{1,0:T(8,128)(2,1)S(1)}, u32[]{:S(2)}, u32[]{:S(2)}) collective-permute-start(bf16[208,1536]{1,0:T(8,128)(2,1)S(1)} %get-tuple-element.467), channel_id=1, source_target_pairs={{0,16},{16,0},{1,17},{17,1},{2,18},{18,2},{3,19},{19,3},{4,20},{20... | collective-permute-start | bytes 1916936 | tf_op jit(solution)/shard_map/ppermute | solution.py:1012
  296.9 2.9 collective-permute-start.43
  297.4 3.3 %collective-permute-start.44 = (bf16[192,1536]{1,0:T(8,128)(2,1)S(1)}, bf16[192,1536]{1,0:T(8,128)(2,1)S(1)}, u32[]{:S(2)}, u32[]{:S(2)}) collective-permute-start(bf16[192,1536]{1,0:T(8,128)(2,1)S(1)} %get-tuple-element.462), channel_id=1, source_target_pairs={{0,16},{16,0},{1,17},{17,1},{2,18},{18,2},{3,19},{19,3},{4,20},{20... | collective-permute-start | bytes 1769480 | tf_op jit(solution)/shard_map/ppermute | solution.py:1012

commit v7 on v6

--- a/solution.py
+++ b/solution.py
@@ -749,27 +749,36 @@
         parts.append(
             [move.choose(mine, wd_a.ref.at[span[i]], wd_b.ref.at[span[i]], wd.at[i])]
             + slope.fetch(move, at[i])
-            + [move.choose(mine, wu_a.ref.at[:, span[i]], wu_b.ref.at[:, span[i]], wu.at[i])]
+            + [
+                move.choose(
+                    mine,
+                    wu_a.ref.at[:, span[i]],
+                    wu_b.ref.at[:, span[i]],
+                    wu.at[i // half, :, pl.ds(i % half * wide, wide)],
+                )
+            ]
         )
         if i == 0:
             early += low.fetch(move)
     late = second.fetch(move) + hat.fetch(move) + scale.fetch(move) + small.fetch(move)
     ready(early)
     branch, low, total = branch.buffer, low.buffer, first.buffer
-    for i in range(blocks):
-        ready(parts[i])
-        pre[...] = (dot_t(branch[...], wd[i]) * slope.buffer[at[i]]).astype(BF16)
-        sums.buffer[pl.ds(3 + at[i], 1)] = column_sum(pre[...].astype(F32))
-        out, place = (send, i) if i < half else (keep, i - half)
-        block = dot(low[...], pre[...]).astype(BF16)
+    for side, out in enumerate((send, keep)):
+        for i in range(half):
+            block = side * half + i
+            ready(parts[block])
+            lanes = slice(i * wide, i * wide + wide)
+            pre[:, lanes] = (dot_t(branch[...], wd[block]) * slope.buffer[at[block]]).astype(BF16)
+            sums.buffer[pl.ds(3 + at[block], 1)] = column_sum(pre[:, lanes].astype(F32))
+        product = dot(low[...], pre[...]).astype(BF16)
         shards, tall, _ = out.buffer.shape
         for shard in range(shards):
-            out.buffer[shard, :, place * wide : place * wide + wide] = block[shard * tall : shard * tall + tall]
-        if i == 0:
+            out.buffer[shard] = product[shard * tall : shard * tall + tall]
+        if side == 0:
             ready(late)
-            total[...] = second.buffer[...] + dot_t(pre[...], wu[i])
+            total[...] = second.buffer[...] + dot_t(pre[...], wu[side])
         else:
-            total[...] += dot_t(pre[...], wu[i])
+            total[...] += dot_t(pre[...], wu[side])
     grad = total[...]
     sums.buffer[0:1] = column_sum(grad * hat.buffer[...])
     sums.buffer[1:2] = column_sum(grad)
@@ -806,7 +815,7 @@
             (small, FAR),
         ],
         [(sds(wide, F32), NEAR), (sds(wide, BF16), NEAR), (sds((8, width), F32), NEAR), (part, NEAR), (part, NEAR)],
-        [square, square, (wide, BF16)],
+        [square, ((2, width, blocks // 2 * width), BF16), ((rows, blocks // 2 * width), BF16)],
         "up_grad",
         6 * rows * width * width * blocks,
         30 << 20,
@@ -845,11 +854,10 @@
     lower = lax.broadcasted_iota(jnp.int32, (128, 128), 1) < 64
 
     def attention(half):
-        @pl.loop(0, pairs)
-        def _(index):
+        for index in range(pairs):
             lanes = pl.ds(pl.multiple_of(half * wide + index * 128, 128), 128)
 
-            def put(part, rows, value):
+            def put(part, rows, value, index=index):
                 there = pl.ds(pl.multiple_of((3 * half + part) * wide + index * 128, 128), 128)
                 grads[rows, there] = value.astype(BF16)
 

time: 310 us -> 309 us (level)
  Pallas kernels: 153 us -> 149 us
    pallas_call x12, Pallas kernels: 139 us -> 135 us  [call(): pl.pallas_call(body, in_specs=[pl.BlockSpec(memory_space=pltpu.SMEM)] + [...]
  transfers between devices with their start and end apart: 47 -> 47, of which waited for: 22 -> 23; matrix products, arithmetic and copies ran while one was open for 3% -> 3% of each run, Pallas kernels for 36% -> 35%
where the time goes in v7:
time: 309 us; the launch traced here: 305 us
  Pallas kernels  149 us (48%)
  waiting for transfers between devices  87.9 us (28%)
  starting transfers between devices  55 us (18%)
  local copies, waits for them, and re-layouts  6.54 us (2%)
  other arithmetic  4.52 us (1%)
    pallas_call x12, Pallas kernels, call(): pl.pallas_call(body, in_specs=[pl.BlockSpec(memory_space=pltpu.SMEM)] + [...  135 us
    ppermute x15, waiting for transfers between devices, move(): lax.ppermute(array, 'outer', [(0, 1), (1, 0), (2, 3), (3, 2)] if way == '...  60.8 us
    ppermute x15, starting transfers between devices, move(): lax.ppermute(array, 'outer', [(0, 1), (1, 0), (2, 3), (3, 2)] if way == '...  35.3 us
    ppermute x32, waiting for transfers between devices, exchange(): return lax.ppermute(array, axis, [(i, i ^ bit) for i in range(length)])  27.1 us
    ppermute x32, starting transfers between devices, exchange(): return lax.ppermute(array, axis, [(i, i ^ bit) for i in range(length)])  19.7 us
    pallas_call x12, Pallas kernels, run(): pl.pallas_call(kernel, in_specs=[pl.BlockSpec(memory_space=pltpu.SMEM)] +...  14 us
  transfers between devices with their start and end apart: 47, of which 23 were waited for; matrix products, arithmetic and copies ran while one was open for 3% of the time, Pallas kernels for 35%

profile of v7, /device:TPU:0, one launch (start us, length us, event | category | flops | bytes accessed | tf_op | source)
XLA Modules:
  0.0 304.6 jit_solution(18185581516685838184)
XLA Ops:
  1.7 1.4 reduce.3
  5.5 1.0 constant_dynamic-slice_fusion
  8.5 8.5 %attend_forward.1 = (bf16[512,768]{1,0:T(8,128)(2,1)}, bf16[512,768]{1,0:T(8,128)(2,1)}, bf16[512,768]{1,0:T(8,128)(2,1)}, f32[4,6,256,128]{3,2,1,0:T(8,128)}, b...) custom-call(s32[1]{0:T(128)} %bitcast.ids_ref, bf16[512,768]{1,0:T(8,128)(2,1)} %bitcast.38, ...), custom_call_target="tpu_custom_call" | custom-call | flops 2415919104 | bytes 12582912 | tf_op jit(solution)/shard_map/attend_forward/pallas_call | solution.py:161
  17.0 0.9 collective-permute-done.2.refs_3_.refs_6_.refs_9_
  18.4 1.4 dynamic-slice_select_fusion
  19.8 12.5 %up_forward.1 = (f32[512,768]{1,0:T(8,128)S(1)}, f32[512,768]{1,0:T(8,128)}, f32[512,128]{1,0:T(8,128)}, bf16[768,512]{1,0:T(8,128)(2,1)}, bf16[4,512,768]{2,1,0...) custom-call(s32[1]{0:T(128)} %bitcast.ids_ref, bf16[512,768]{1,0:T(8,128)(2,1)} %bitcast.39, ...), custom_call_target="tpu_custom_call" | custom-call | flops 3019898880 | bytes 20971520 | tf_op jit(solution)/shard_map/up_forward/pallas_call | solution.py:161
  32.4 9.0 %down_forward.1 = (bf16[512,768]{1,0:T(8,128)(2,1)S(1)}, bf16[512,768]{1,0:T(8,128)(2,1)}, f32[512,768]{1,0:T(8,128)}, f32[512,128]{1,0:T(8,128)}) custom-call(s32[1]{0:T(128)} %bitcast.ids_ref, bf16[4,512,768]{2,1,0:T(8,128)(2,1)S(1)} %get-tuple-element.260.refs_0_, bf16[3072,768]{1,0:T(8,128)(2,1)} %bitcast.24, ...), custom_call_target="tpu_custom_call" | custom-call | flops 2415919104 | bytes 12582912 | tf_op jit(solution)/shard_map/down_forward/pallas_call | solution.py:161
  41.3 25.2 %second_layer.1 = (bf16[512,768]{1,0:T(8,128)(2,1)}, bf16[512,768]{1,0:T(8,128)(2,1)}, bf16[512,768]{1,0:T(8,128)(2,1)}, f32[4,6,256,128]{3,2,1,0:T(8,128)}, bf1...) custom-call(s32[1]{0:T(128)} %bitcast.ids_ref, ...), custom_call_target="tpu_custom_call" | custom-call | flops 10267656192 | bytes 52428800 | tf_op jit(solution)/shard_map/second_layer/pallas_call | solution.py:161
  66.6 8.7 %up_grad_first.1 = (f32[512,768]{1,0:T(8,128)S(1)}, f32[8,768]{1,0:T(8,128)S(1)}, bf16[4,192,1536]{2,1,0:T(8,128)(2,1)}) custom-call(s32[1]{0:T(128)} %bitcast.ids_ref, bf16[512,768]{1,0:T(8,128)(2,1)S(1)} %get-tuple-element.275.refs_0_, f32[512,768]{1,0:T(8,128)S(1)} %get-tuple-element.267.refs_1_, bf16[3072,768]{1,0:T(8,128)(2,1)} %bitcast.26, ...), custom_call_target="tpu_custom_call" | custom-call | flops 3623878656 | bytes 15728640 | tf_op jit(solution)/shard_map/up_grad_first/pallas_call | solution.py:161
  75.3 1.1 copy-done.4
  76.5 1.4 copy-done.11
  78.5 3.2 %join_sums.12 = (bf16[2,96,1536]{2,1,0:T(8,128)(2,1)S(1)}, bf16[2,96,1536]{2,1,0:T(8,128)(2,1)S(1)}, bf16[192,1536]{1,0:T(8,128)(2,1)S(1)}, bf16[192,1536]{1,0:T(8,128)(2,1)S(1)}) custom-call(s32[5]{0:T(128)S(1)} %stack.24.ids_ref, bf16[4,192,1536]{2,1,0:T(8,128)(2,1)} %get-tuple-element.285.refs_0_, bf16[4,192,1536]{2,1,0:T(8,128)(2,1)} %copy-done.11), custom_call_target="tpu_custom_call" | custom-call | tf_op jit(solution)/shard_map/join_sums/pallas_call | solution.py:1076
  81.8 3.0 collective-permute-start.6
  84.7 1.5 collective-permute-start.7
  86.2 8.6 %up_grad_last.1 = (f32[512,768]{1,0:T(8,128)S(1)}, bf16[512,768]{1,0:T(8,128)(2,1)S(1)}, f32[8,768]{1,0:T(8,128)S(1)}, bf16[4,192,1536]{2,1,0:T(8,128)(2,1)S(1)}) custom-call(s32[1]{0:T(128)} %bitcast.ids_ref, bf16[512,768]{1,0:T(8,128)(2,1)S(1)} %get-tuple-element.275.refs_0_, f32[512,768]{1,0:T(8,128)S(1)} %copy-done.5, bf16[3072,768]{1,0:T(8,128)(2,1)} %bitcast.27, ...), custom_call_target="tpu_custom_call" | custom-call | flops 3623878656 | bytes 15728640 | tf_op jit(solution)/shard_map/up_grad_last/pallas_call | solution.py:161
  94.8 3.4 %collective-permute-done.6.refs_2_ = bf16[192,1536]{1,0:T(8,128)(2,1)S(1)} collective-permute-done((bf16[192,1536]{1,0:T(8,128)(2,1)S(1)}, bf16[192,1536]{1,0:T(8,128)(2,1)S(1)}, u32[]{:S(2)}, u32[]{:S(2)}) %collective-permute-start.6) | collective-permute-done | bytes 589856 | tf_op jit(solution)/shard_map/ppermute | solution.py:1020
  98.2 1.5 collective-permute-done.7.refs_3_
  99.7 1.0 join_sums.13
  100.7 1.6 collective-permute-start.10
  102.8 16.2 %attend_grad.2 = (f32[512,768]{1,0:T(8,128)}, bf16[512,768]{1,0:T(8,128)(2,1)S(1)}, bf16[512,768]{1,0:T(8,128)(2,1)}, bf16[4,208,1536]{2,1,0:T(8,128)(2,1)S(1)}, bf16[4,208,1536]{2,1,0:T(8,128)(2,1)S(1)}) custom-call(s32[1]{0:T(128)} %bitcast.ids_ref, bf16[512,768]{1,0:T(8,128)(2,1)S(1)} %get-tuple-element.290.refs_0_, ...), custom_call_target="tpu_custom_call" | custom-call | flops 6039797760 | bytes 31457280 | tf_op jit(solution)/shard_map/attend_grad/pallas_call | solution.py:161
  119.0 2.1 collective-permute-done.10.refs_3_
  121.1 1.2 collective-permute-done.9.refs_2_
  123.2 1.6 collective-permute-start.11
  125.9 6.8 %down_grad.1 = (f32[512,768]{1,0:T(8,128)S(1)}, bf16[512,768]{1,0:T(8,128)(2,1)S(1)}, f32[8,768]{1,0:T(8,128)S(1)}, bf16[4,192,1536]{2,1,0:T(8,128)(2,1)S(1)}, bf16[4,192,1536]{2,1,0:T(8,128)(2,1)S(1)}) custom-call(s32[1]{0:T(128)} %bitcast.ids_ref, bf16[512,768]{1,0:T(8,128)(2,1)S(1)} %get-tuple-element.313.refs_0_, f32[512,768]{1,0:T(8,128)} %get-tuple-element.314.refs_1_, ...), custom_call_target="tpu_custom_call" | custom-call | flops 2415919104 | bytes 14680064 | tf_op jit(solution)/shard_map/down_grad/pallas_call | solution.py:161
  132.8 1.2 collective-permute-done.12.refs_4_
  134.3 4.7 %collective-permute-done.11.refs_1_ = bf16[192,1536]{1,0:T(8,128)(2,1)S(1)} collective-permute-done((bf16[192,1536]{1,0:T(8,128)(2,1)S(1)}, bf16[192,1536]{1,0:T(8,128)(2,1)S(1)}, u32[]{:S(2)}, u32[]{:S(2)}) %collective-permute-start.11) | collective-permute-done | bytes 589856 | tf_op jit(solution)/shard_map/ppermute | solution.py:1257
  139.0 1.1 join_sums.15
  140.8 1.5 collective-permute-start.15
  142.3 0.9 collective-permute-start.16
  143.8 13.6 %up_grad.1 = (f32[512,768]{1,0:T(8,128)S(1)}, bf16[512,768]{1,0:T(8,128)(2,1)S(1)}, f32[8,768]{1,0:T(8,128)S(1)}, bf16[4,192,1536]{2,1,0:T(8,128)(2,1)S(1)}, bf16[4,192,1536]{2,1,0:T(8,128)(2,1)S(1)}) custom-call(s32[1]{0:T(128)} %bitcast.ids_ref, bf16[512,768]{1,0:T(8,128)(2,1)S(1)} %get-tuple-element.333.refs_0_, ...), custom_call_target="tpu_custom_call" | custom-call | flops 7247757312 | bytes 31457280 | tf_op jit(solution)/shard_map/up_grad/pallas_call | solution.py:161
  157.4 1.0 collective-permute-done.18.refs_7_
  158.5 1.1 join_sums.16
  160.3 1.4 collective-permute-start.22
  161.7 4.5 %collective-permute-start.20 = (bf16[192,1536]{1,0:T(8,128)(2,1)S(1)}, bf16[192,1536]{1,0:T(8,128)(2,1)S(1)}, u32[]{:S(2)}, u32[]{:S(2)}) collective-permute-start(bf16[192,1536]{1,0:T(8,128)(2,1)S(1)} %get-tuple-element.381), channel_id=1, source_target_pairs={{0,1},{1,0},{2,3},{3,2},{4,5},{5,4},{6,7},{7,6},{8,9},{9,8},{10,11... | collective-permute-start | bytes 1769480 | tf_op jit(solution)/shard_map/ppermute | solution.py:1257
  166.1 0.9 collective-permute-start.21
  167.1 16.1 %attend_grad.3 = (f32[512,768]{1,0:T(8,128)}, bf16[512,768]{1,0:T(8,128)(2,1)}, bf16[4,208,1536]{2,1,0:T(8,128)(2,1)S(1)}, bf16[4,208,1536]{2,1,0:T(8,128)(2,1)S(1)}) custom-call(s32[1]{0:T(128)} %bitcast.ids_ref, bf16[512,768]{1,0:T(8,128)(2,1)S(1)} %get-tuple-element.359.refs_0_, bf16[768,512]{1,0:T(8,128)(2,1)} %get-tuple-element.362.refs_1_, ...), custom_call_target="tpu_custom_call" | custom-call | flops 6039797760 | bytes 31457280 | tf_op jit(solution)/shard_map/attend_grad/pallas_call | solution.py:161
  183.3 1.2 join_sums.17
  184.5 1.0 collective-permute-start.28
  186.3 4.2 %collective-permute-start.27 = (bf16[208,1536]{1,0:T(8,128)(2,1)S(1)}, bf16[208,1536]{1,0:T(8,128)(2,1)S(1)}, u32[]{:S(2)}, u32[]{:S(2)}) collective-permute-start(bf16[208,1536]{1,0:T(8,128)(2,1)S(1)} %get-tuple-element.401), channel_id=1, source_target_pairs={{0,1},{1,0},{2,3},{3,2},{4,5},{5,4},{6,7},{7,6},{8,9},{9,8},{10,11... | collective-permute-start | bytes 1916936 | tf_op jit(solution)/shard_map/ppermute | solution.py:1257
  190.5 14.5 %collective-permute-done.27.refs_1_ = bf16[208,1536]{1,0:T(8,128)(2,1)S(1)} collective-permute-done((bf16[208,1536]{1,0:T(8,128)(2,1)S(1)}, bf16[208,1536]{1,0:T(8,128)(2,1)S(1)}, u32[]{:S(2)}, u32[]{:S(2)}) %collective-permute-start.27) | collective-permute-done | bytes 639008 | tf_op jit(solution)/shard_map/ppermute | solution.py:1257
  205.0 1.6 collective-permute-done.28.refs_5_
  207.3 1.2 join_sums.18
  208.5 1.2 collective-permute-start.33
  209.7 1.1 collective-permute-start.34
  211.5 4.7 %collective-permute-start.31 = (bf16[192,1536]{1,0:T(8,128)(2,1)S(1)}, bf16[192,1536]{1,0:T(8,128)(2,1)S(1)}, u32[]{:S(2)}, u32[]{:S(2)}) collective-permute-start(bf16[192,1536]{1,0:T(8,128)(2,1)S(1)} %get-tuple-element.416), channel_id=1, source_target_pairs={{0,1},{1,0},{2,3},{3,2},{4,5},{5,4},{6,7},{7,6},{8,9},{9,8},{10,11... | collective-permute-start | bytes 1769480 | tf_op jit(solution)/shard_map/ppermute | solution.py:1257
  216.5 12.0 %collective-permute-done.31.refs_3_ = bf16[192,1536]{1,0:T(8,128)(2,1)S(1)} collective-permute-done((bf16[192,1536]{1,0:T(8,128)(2,1)S(1)}, bf16[192,1536]{1,0:T(8,128)(2,1)S(1)}, u32[]{:S(2)}, u32[]{:S(2)}) %collective-permute-start.31) | collective-permute-done | bytes 589856 | tf_op jit(solution)/shard_map/ppermute | solution.py:1257
  228.5 1.8 collective-permute-done.34.refs_7_
  230.3 1.3 collective-permute-done.33.refs_6_
  231.6 1.0 join_sums.19
  232.6 4.2 %collective-permute-start.35 = (bf16[208,1536]{1,0:T(8,128)(2,1)S(1)}, bf16[208,1536]{1,0:T(8,128)(2,1)S(1)}, u32[]{:S(2)}, u32[]{:S(2)}) collective-permute-start(bf16[208,1536]{1,0:T(8,128)(2,1)S(1)} %get-tuple-element.429), channel_id=1, source_target_pairs={{0,1},{1,0},{2,3},{3,2},{4,5},{5,4},{6,7},{7,6},{8,9},{9,8},{10,11... | collective-permute-start | bytes 1916936 | tf_op jit(solution)/shard_map/ppermute | solution.py:1257
  236.8 1.0 collective-permute-start.36
  239.5 5.5 %collective-permute-done.37.refs_7_ = bf16[96,1536]{1,0:T(8,128)(2,1)S(1)} collective-permute-done((bf16[96,1536]{1,0:T(8,128)(2,1)S(1)}, bf16[96,1536]{1,0:T(8,128)(2,1)S(1)}, u32[]{:S(2)}, u32[]{:S(2)}) %collective-permute-start.37) | collective-permute-done | bytes 294944 | tf_op jit(solution)/shard_map/ppermute | solution.py:1020
  245.0 1.4 collective-permute-done.38.refs_8_
  246.4 3.5 %collective-permute-done.35.refs_1_ = bf16[208,1536]{1,0:T(8,128)(2,1)S(1)} collective-permute-done((bf16[208,1536]{1,0:T(8,128)(2,1)S(1)}, bf16[208,1536]{1,0:T(8,128)(2,1)S(1)}, u32[]{:S(2)}, u32[]{:S(2)}) %collective-permute-start.35) | collective-permute-done | bytes 639008 | tf_op jit(solution)/shard_map/ppermute | solution.py:1257
  249.9 0.9 join_sums.20
  250.8 2.7 collective-permute-start.39
  254.2 11.4 %collective-permute-done.39.refs_1_ = bf16[208,1536]{1,0:T(8,128)(2,1)S(1)} collective-permute-done((bf16[208,1536]{1,0:T(8,128)(2,1)S(1)}, bf16[208,1536]{1,0:T(8,128)(2,1)S(1)}, u32[]{:S(2)}, u32[]{:S(2)}) %collective-permute-start.39) | collective-permute-done | bytes 639008 | tf_op jit(solution)/shard_map/ppermute | solution.py:1257
  267.1 4.2 %collective-permute-start.41 = (bf16[192,1536]{1,0:T(8,128)(2,1)S(1)}, bf16[192,1536]{1,0:T(8,128)(2,1)S(1)}, u32[]{:S(2)}, u32[]{:S(2)}) collective-permute-start(bf16[192,1536]{1,0:T(8,128)(2,1)S(1)} %get-tuple-element.451), channel_id=1, source_target_pairs={{0,1},{1,0},{2,3},{3,2},{4,5},{5,4},{6,7},{7,6},{8,9},{9,8},{10,11... | collective-permute-start | bytes 1769480 | tf_op jit(solution)/shard_map/ppermute | solution.py:1257
  271.3 5.4 %assemble.1 = (bf16[2,512,768]{2,1,0:T(8,128)(2,1)}, f32[2,512,768]{2,1,0:T(8,128)}) custom-call(s32[1]{0:T(128)} %bitcast.ids_ref, bf16[512,768]{1,0:T(8,128)(2,1)} %get-tuple-element.294.refs_3_.refs_0_, bf16[512,768]{1,0:T(8,128)(2,1)} %get-tuple-element.387.refs_1_, bf16[512,768]{1,0:T(8,128)(2,1)} %copy-done.13, f32[512,768]{1,0:T(8,128)} %get-tuple-element.386.refs_3_, ...), custom_call_target="tpu_custom_call" | custom-call | flops 1000 | bytes 10485760 | tf_op jit(solution)/shard_map/assemble/pallas_call | solution.py:161
  276.7 4.5 %collective-permute-done.41.refs_1_ = bf16[192,1536]{1,0:T(8,128)(2,1)S(1)} collective-permute-done((bf16[192,1536]{1,0:T(8,128)(2,1)S(1)}, bf16[192,1536]{1,0:T(8,128)(2,1)S(1)}, u32[]{:S(2)}, u32[]{:S(2)}) %collective-permute-start.41) | collective-permute-done | bytes 589856 | tf_op jit(solution)/shard_map/ppermute | solution.py:1257
  282.0 2.8 collective-permute-start.45
  284.8 10.3 %collective-permute-done.45.refs_1_ = bf16[208,1536]{1,0:T(8,128)(2,1)S(1)} collective-permute-done((bf16[208,1536]{1,0:T(8,128)(2,1)S(1)}, bf16[208,1536]{1,0:T(8,128)(2,1)S(1)}, u32[]{:S(2)}, u32[]{:S(2)}) %collective-permute-start.45) | collective-permute-done | bytes 639008 | tf_op jit(solution)/shard_map/ppermute | solution.py:1257
  296.4 2.3 collective-permute-done.43.refs_1_
  299.6 4.5 %last.1 = (f32[768,768]{1,0:T(8,128)}, f32[192,2304]{1,0:T(8,128)}, f32[192,768]{1,0:T(8,128)}, f32[2,192]{1,0:T(2,128)}, f32[1,192]{1,0:T(1,128)}, /*index=5*/f...) custom-call(s32[5]{0:T(128)S(1)} %stack.24.ids_ref, ...), custom_call_target="tpu_custom_call" | custom-call | flops 1000 | bytes 5242880 | tf_op jit(solution)/shard_map/last/pallas_call | solution.py:161
  (106 shorter events, 20.8 us)
Async XLA Ops:
  0.6 4.9 %copy-start = (bf16[8,128,768]{2,1,0:T(8,128)(2,1)S(1)}, bf16[8,128,768]{2,1,0:T(8,128)(2,1)}, u32[]{:S(2)}) copy-start(bf16[8,128,768]{2,1,0:T(8,128)(2,1)} %param.14) | copy-start | bytes 4718596
  0.7 7.4 %collective-permute-start = (bf16[768,2304]{1,0:T(8,128)(2,1)}, bf16[768,2304]{1,0:T(8,128)(2,1)}, u32[]{:S(2)}, u32[]{:S(2)}) collective-permute-start(bf16[768,2304]{1,0:T(8,128)(2,1)} %bitcast.52), channel_id=1, source_target_pairs={{0,16},{16,0},{1,17},{17,1},{2,18},{18,2},{3,19},{19,3},{4,20},{20... | collective-permute-start | bytes 10616840 | tf_op jit(solution)/shard_map/ppermute | solution.py:1020
  3.9 3.5 %collective-permute-start.1 = (f32[16,768]{1,0:T(8,128)S(1)}, f32[16,768]{1,0:T(8,128)S(1)}, u32[]{:S(2)}, u32[]{:S(2)}) collective-permute-start(f32[16,768]{1,0:T(8,128)S(1)} %concatenate.6), channel_id=1, source_target_pairs={{0,16},{16,0},{1,17},{17,1},{2,18},{18,2},{3,19},{19,3},{4,20},{20... | collective-permute-start | bytes 147464 | tf_op jit(solution)/shard_map/ppermute | solution.py:1020
  7.4 10.5 %slice-start = ((s8[4718592]{0:T(1024)(128)(4,1)}), s8[4194304]{0:T(1024)(128)(4,1)S(1)}, s32[]{:S(2)}) async-start(s8[4718592]{0:T(1024)(128)(4,1)} %bitcast.29), calls=%async_computation | async-start | bytes 8388608
  8.0 9.9 %collective-permute-start.3 = (bf16[768,3072]{1,0:T(8,128)(2,1)}, bf16[768,3072]{1,0:T(8,128)(2,1)S(1)}, u32[]{:S(2)}, u32[]{:S(2)}) collective-permute-start(bf16[768,3072]{1,0:T(8,128)(2,1)} %bitcast.32), channel_id=1, source_target_pairs={{0,16},{16,0},{1,17},{17,1},{2,18},{18,2},{3,19},{19,3},{4,20},{20... | collective-permute-start | bytes 14155784 | tf_op jit(solution)/shard_map/ppermute | solution.py:1020
  8.5 9.4 %collective-permute-start.2 = (bf16[768,768]{1,0:T(8,128)(2,1)}, bf16[768,768]{1,0:T(8,128)(2,1)S(1)}, u32[]{:S(2)}, u32[]{:S(2)}) collective-permute-start(bf16[768,768]{1,0:T(8,128)(2,1)} %bitcast.41), channel_id=1, source_target_pairs={{0,16},{16,0},{1,17},{17,1},{2,18},{18,2},{3,19},{19,3},{4,20},{20... | collective-permute-start | bytes 3538952 | tf_op jit(solution)/shard_map/ppermute | solution.py:1020
  8.5 9.4 %slice-start.1 = ((s8[4718592]{0:T(1024)(128)(4,1)}), s8[524288]{0:T(1024)(128)(4,1)S(1)}, s32[]{:S(2)}) async-start(s8[4718592]{0:T(1024)(128)(4,1)} %bitcast.29), calls=%async_computation.1 | async-start | bytes 1048576
  8.5 9.8 %copy-start.14 = (bf16[8,128,768]{2,1,0:T(8,128)(2,1)S(1)}, bf16[8,128,768]{2,1,0:T(8,128)(2,1)}, u32[]{:S(2)}) copy-start(bf16[8,128,768]{2,1,0:T(8,128)(2,1)} %param.17) | copy-start | bytes 4718596
  17.9 14.4 %copy-start.6 = (bf16[768,768]{1,0:T(8,128)(2,1)}, bf16[768,768]{1,0:T(8,128)(2,1)S(1)}, u32[]{:S(2)}) copy-start(bf16[768,768]{1,0:T(8,128)(2,1)S(1)} %collective-permute-done.2.refs_3_.refs_6_.refs_9_) | copy-start | bytes 3538948
  17.9 14.4 %copy-start.3 = (bf16[768,3072]{1,0:T(8,128)(2,1)}, bf16[768,3072]{1,0:T(8,128)(2,1)S(1)}, u32[]{:S(2)}) copy-start(bf16[768,3072]{1,0:T(8,128)(2,1)S(1)} %collective-permute-done.3.refs_5_.refs_8_.refs_7_) | copy-start | bytes 14155780
  17.9 14.4 %collective-permute-start.4 = (bf16[3072,768]{1,0:T(8,128)(2,1)S(1)}, bf16[3072,768]{1,0:T(8,128)(2,1)S(1)}, u32[]{:S(2)}, u32[]{:S(2)}) collective-permute-start(bf16[3072,768]{1,0:T(8,128)(2,1)S(1)} %bitcast.31), channel_id=1, source_target_pairs={{0,16},{16,0},{1,17},{17,1},{2,18},{18,2},{3,19},{19,3},{4,20},{20... | collective-permute-start | bytes 14155784 | tf_op jit(solution)/shard_map/ppermute | solution.py:1020
  32.3 9.0 %copy-start.2 = (bf16[3072,768]{1,0:T(8,128)(2,1)}, bf16[3072,768]{1,0:T(8,128)(2,1)S(1)}, u32[]{:S(2)}) copy-start(bf16[3072,768]{1,0:T(8,128)(2,1)S(1)} %collective-permute-done.4.refs_2_.refs_10_.refs_3_) | copy-start | bytes 14155780
  66.6 9.9 %collective-permute-start.5 = (bf16[4,192,1536]{2,1,0:T(8,128)(2,1)S(1)}, bf16[4,192,1536]{2,1,0:T(8,128)(2,1)S(1)}, u32[]{:S(2)}, u32[]{:S(2)}) collective-permute-start(bf16[4,192,1536]{2,1,0:T(8,128)(2,1)S(1)} %get-tuple-element.274), channel_id=1, source_target_pairs={{0,16},{16,0},{1,17},{17,1},{2,18},{18,2},{3,19},{19,3},{4,20},{20... | collective-permute-start | bytes 7077896 | tf_op jit(solution)/shard_map/ppermute | solution.py:1020
  75.3 1.2 copy-start.4
  76.5 1.4 copy-start.11
  77.9 21.8 %collective-permute-start.8 = (bf16[4,192,1536]{2,1,0:T(8,128)(2,1)}, bf16[4,192,1536]{2,1,0:T(8,128)(2,1)S(1)}, u32[]{:S(2)}, u32[]{:S(2)}) collective-permute-start(bf16[4,192,1536]{2,1,0:T(8,128)(2,1)} %get-tuple-element.289), channel_id=1, source_target_pairs={{0,16},{16,0},{1,17},{17,1},{2,18},{18,2},{3,19},{19,3},{4,20},{20... | collective-permute-start | bytes 7077896 | tf_op jit(solution)/shard_map/ppermute | solution.py:1020
  78.5 7.7 %copy-start.5 = (f32[512,768]{1,0:T(8,128)S(1)}, f32[512,768]{1,0:T(8,128)}, u32[]{:S(2)}) copy-start(f32[512,768]{1,0:T(8,128)} %copy-done.4) | copy-start | bytes 4718596
  81.8 16.5 %collective-permute-start.6 = (bf16[192,1536]{1,0:T(8,128)(2,1)S(1)}, bf16[192,1536]{1,0:T(8,128)(2,1)S(1)}, u32[]{:S(2)}, u32[]{:S(2)}) collective-permute-start(bf16[192,1536]{1,0:T(8,128)(2,1)S(1)} %get-tuple-element.287), channel_id=1, source_target_pairs={{0,4},{4,0},{8,12},{12,8},{1,5},{5,1},{9,13},{13,9},{2,6},{6,2},{1... | collective-permute-start | bytes 1769480 | tf_op jit(solution)/shard_map/ppermute | solution.py:1020
  84.7 15.0 %collective-permute-start.7 = (bf16[192,1536]{1,0:T(8,128)(2,1)S(1)}, bf16[192,1536]{1,0:T(8,128)(2,1)S(1)}, u32[]{:S(2)}, u32[]{:S(2)}) collective-permute-start(bf16[192,1536]{1,0:T(8,128)(2,1)S(1)} %get-tuple-element.288), channel_id=1, source_target_pairs={{0,8},{4,12},{8,0},{12,4},{1,9},{5,13},{9,1},{13,5},{2,10},{6,14},... | collective-permute-start | bytes 1769480 | tf_op jit(solution)/shard_map/ppermute | solution.py:1020
  100.7 20.4 %collective-permute-start.10 = (bf16[288,1536]{1,0:T(8,128)(2,1)S(1)}, bf16[288,1536]{1,0:T(8,128)(2,1)S(1)}, u32[]{:S(2)}, u32[]{:S(2)}) collective-permute-start(bf16[288,1536]{1,0:T(8,128)(2,1)S(1)} %get-tuple-element.311), channel_id=1, source_target_pairs={{0,8},{4,12},{8,0},{12,4},{1,9},{5,13},{9,1},{13,5},{2,10},{6,14},... | collective-permute-start | bytes 2654216 | tf_op jit(solution)/shard_map/ppermute | solution.py:1020
  102.2 20.1 %collective-permute-start.9 = (bf16[288,1536]{1,0:T(8,128)(2,1)S(1)}, bf16[288,1536]{1,0:T(8,128)(2,1)S(1)}, u32[]{:S(2)}, u32[]{:S(2)}) collective-permute-start(bf16[288,1536]{1,0:T(8,128)(2,1)S(1)} %get-tuple-element.310), channel_id=1, source_target_pairs={{0,4},{4,0},{8,12},{12,8},{1,5},{5,1},{9,13},{13,9},{2,6},{6,2},{1... | collective-permute-start | bytes 2654216 | tf_op jit(solution)/shard_map/ppermute | solution.py:1020
  122.3 16.7 %collective-permute-start.14 = (bf16[4,208,1536]{2,1,0:T(8,128)(2,1)S(1)}, bf16[4,208,1536]{2,1,0:T(8,128)(2,1)S(1)}, u32[]{:S(2)}, u32[]{:S(2)}) collective-permute-start(bf16[4,208,1536]{2,1,0:T(8,128)(2,1)S(1)} %get-tuple-element.332), channel_id=1, source_target_pairs={{0,16},{16,0},{1,17},{17,1},{2,18},{18,2},{3,19},{19,3},{4,20},{20... | collective-permute-start | bytes 7667720 | tf_op jit(solution)/shard_map/ppermute | solution.py:1020
  123.2 15.8 %collective-permute-start.11 = (bf16[192,1536]{1,0:T(8,128)(2,1)S(1)}, bf16[192,1536]{1,0:T(8,128)(2,1)S(1)}, u32[]{:S(2)}, u32[]{:S(2)}) collective-permute-start(bf16[192,1536]{1,0:T(8,128)(2,1)S(1)} %get-tuple-element.329), channel_id=1, source_target_pairs={{0,1},{1,0},{2,3},{3,2},{4,5},{5,4},{6,7},{7,6},{8,9},{9,8},{10,11... | collective-permute-start | bytes 1769480 | tf_op jit(solution)/shard_map/ppermute | solution.py:1257
  124.8 9.1 %collective-permute-start.12 = (bf16[96,1536]{1,0:T(8,128)(2,1)S(1)}, bf16[96,1536]{1,0:T(8,128)(2,1)S(1)}, u32[]{:S(2)}, u32[]{:S(2)}) collective-permute-start(bf16[96,1536]{1,0:T(8,128)(2,1)S(1)} %get-tuple-element.330), channel_id=1, source_target_pairs={{0,4},{4,0},{8,12},{12,8},{1,5},{5,1},{9,13},{13,9},{2,6},{6,2},{1... | collective-permute-start | bytes 884744 | tf_op jit(solution)/shard_map/ppermute | solution.py:1020
  125.4 8.9 %collective-permute-start.13 = (bf16[96,1536]{1,0:T(8,128)(2,1)S(1)}, bf16[96,1536]{1,0:T(8,128)(2,1)S(1)}, u32[]{:S(2)}, u32[]{:S(2)}) collective-permute-start(bf16[96,1536]{1,0:T(8,128)(2,1)S(1)} %get-tuple-element.331), channel_id=1, source_target_pairs={{0,8},{4,12},{8,0},{12,4},{1,9},{5,13},{9,1},{13,5},{2,10},{6,14},... | collective-permute-start | bytes 884744 | tf_op jit(solution)/shard_map/ppermute | solution.py:1020
  139.0 19.5 %collective-permute-start.19 = (bf16[4,192,1536]{2,1,0:T(8,128)(2,1)S(1)}, bf16[4,192,1536]{2,1,0:T(8,128)(2,1)S(1)}, u32[]{:S(2)}, u32[]{:S(2)}) collective-permute-start(bf16[4,192,1536]{2,1,0:T(8,128)(2,1)S(1)} %get-tuple-element.358), channel_id=1, source_target_pairs={{0,16},{16,0},{1,17},{17,1},{2,18},{18,2},{3,19},{19,3},{4,20},{20... | collective-permute-start | bytes 7077896 | tf_op jit(solution)/shard_map/ppermute | solution.py:1020
  140.1 18.3 %collective-permute-start.17 = (bf16[224,1536]{1,0:T(8,128)(2,1)S(1)}, bf16[224,1536]{1,0:T(8,128)(2,1)S(1)}, u32[]{:S(2)}, u32[]{:S(2)}) collective-permute-start(bf16[224,1536]{1,0:T(8,128)(2,1)S(1)} %get-tuple-element.356), channel_id=1, source_target_pairs={{0,4},{4,0},{8,12},{12,8},{1,5},{5,1},{9,13},{13,9},{2,6},{6,2},{1... | collective-permute-start | bytes 2064392 | tf_op jit(solution)/shard_map/ppermute | solution.py:1020
  140.8 16.6 %collective-permute-start.15 = (bf16[192,1536]{1,0:T(8,128)(2,1)S(1)}, bf16[192,1536]{1,0:T(8,128)(2,1)S(1)}, u32[]{:S(2)}, u32[]{:S(2)}) collective-permute-start(bf16[192,1536]{1,0:T(8,128)(2,1)S(1)} %get-tuple-element.354), channel_id=1, source_target_pairs={{0,1},{1,0},{2,3},{3,2},{4,5},{5,4},{6,7},{7,6},{8,9},{9,8},{10,11... | collective-permute-start | bytes 1769480 | tf_op jit(solution)/shard_map/ppermute | solution.py:1257
  142.3 15.1 %collective-permute-start.16 = (bf16[192,1536]{1,0:T(8,128)(2,1)S(1)}, bf16[192,1536]{1,0:T(8,128)(2,1)S(1)}, u32[]{:S(2)}, u32[]{:S(2)}) collective-permute-start(bf16[192,1536]{1,0:T(8,128)(2,1)S(1)} %get-tuple-element.355.refs_0_), channel_id=1, source_target_pairs={{1,2},{2,1},{5,6},{6,5},{9,10},{10,9},{13,14},{14,13},{17,18},{18,... | collective-permute-start | bytes 1769480 | tf_op jit(solution)/shard_map/ppermute | solution.py:1257
  143.2 15.2 %collective-permute-start.18 = (bf16[192,1536]{1,0:T(8,128)(2,1)S(1)}, bf16[192,1536]{1,0:T(8,128)(2,1)S(1)}, u32[]{:S(2)}, u32[]{:S(2)}) collective-permute-start(bf16[192,1536]{1,0:T(8,128)(2,1)S(1)} %get-tuple-element.357), channel_id=1, source_target_pairs={{0,8},{4,12},{8,0},{12,4},{1,9},{5,13},{9,1},{13,5},{2,10},{6,14},... | collective-permute-start | bytes 1769480 | tf_op jit(solution)/shard_map/ppermute | solution.py:1020
  158.5 24.7 %collective-permute-start.24 = (bf16[4,192,1536]{2,1,0:T(8,128)(2,1)S(1)}, bf16[4,192,1536]{2,1,0:T(8,128)(2,1)S(1)}, u32[]{:S(2)}, u32[]{:S(2)}) collective-permute-start(bf16[4,192,1536]{2,1,0:T(8,128)(2,1)S(1)} %get-tuple-element.385), channel_id=1, source_target_pairs={{0,16},{16,0},{1,17},{17,1},{2,18},{18,2},{3,19},{19,3},{4,20},{20... | collective-permute-start | bytes 7077896 | tf_op jit(solution)/shard_map/ppermute | solution.py:1020
  159.6 23.6 %collective-permute-start.23 = (bf16[304,1536]{1,0:T(8,128)(2,1)S(1)}, bf16[304,1536]{1,0:T(8,128)(2,1)S(1)}, u32[]{:S(2)}, u32[]{:S(2)}) collective-permute-start(bf16[304,1536]{1,0:T(8,128)(2,1)S(1)} %get-tuple-element.384), channel_id=1, source_target_pairs={{0,8},{4,12},{8,0},{12,4},{1,9},{5,13},{9,1},{13,5},{2,10},{6,14},... | collective-permute-start | bytes 2801672 | tf_op jit(solution)/shard_map/ppermute | solution.py:1020
  160.3 22.9 %collective-permute-start.22 = (bf16[288,1536]{1,0:T(8,128)(2,1)S(1)}, bf16[288,1536]{1,0:T(8,128)(2,1)S(1)}, u32[]{:S(2)}, u32[]{:S(2)}) collective-permute-start(bf16[288,1536]{1,0:T(8,128)(2,1)S(1)} %get-tuple-element.383), channel_id=1, source_target_pairs={{0,4},{4,0},{8,12},{12,8},{1,5},{5,1},{9,13},{13,9},{2,6},{6,2},{1... | collective-permute-start | bytes 2654216 | tf_op jit(solution)/shard_map/ppermute | solution.py:1020
  161.7 21.5 %collective-permute-start.20 = (bf16[192,1536]{1,0:T(8,128)(2,1)S(1)}, bf16[192,1536]{1,0:T(8,128)(2,1)S(1)}, u32[]{:S(2)}, u32[]{:S(2)}) collective-permute-start(bf16[192,1536]{1,0:T(8,128)(2,1)S(1)} %get-tuple-element.381), channel_id=1, source_target_pairs={{0,1},{1,0},{2,3},{3,2},{4,5},{5,4},{6,7},{7,6},{8,9},{9,8},{10,11... | collective-permute-start | bytes 1769480 | tf_op jit(solution)/shard_map/ppermute | solution.py:1257
  166.1 17.0 %collective-permute-start.21 = (bf16[192,1536]{1,0:T(8,128)(2,1)S(1)}, bf16[192,1536]{1,0:T(8,128)(2,1)S(1)}, u32[]{:S(2)}, u32[]{:S(2)}) collective-permute-start(bf16[192,1536]{1,0:T(8,128)(2,1)S(1)} %get-tuple-element.382.refs_2_), channel_id=1, source_target_pairs={{1,2},{2,1},{5,6},{6,5},{9,10},{10,9},{13,14},{14,13},{17,18},{18,... | collective-permute-start | bytes 1769480 | tf_op jit(solution)/shard_map/ppermute | solution.py:1257
  183.2 24.1 %collective-permute-start.30 = (bf16[4,208,1536]{2,1,0:T(8,128)(2,1)S(1)}, bf16[4,208,1536]{2,1,0:T(8,128)(2,1)S(1)}, u32[]{:S(2)}, u32[]{:S(2)}) collective-permute-start(bf16[4,208,1536]{2,1,0:T(8,128)(2,1)S(1)} %get-tuple-element.404), channel_id=1, source_target_pairs={{0,16},{16,0},{1,17},{17,1},{2,18},{18,2},{3,19},{19,3},{4,20},{20... | collective-permute-start | bytes 7667720 | tf_op jit(solution)/shard_map/ppermute | solution.py:1020
  184.5 22.1 %collective-permute-start.28 = (bf16[288,1536]{1,0:T(8,128)(2,1)S(1)}, bf16[288,1536]{1,0:T(8,128)(2,1)S(1)}, u32[]{:S(2)}, u32[]{:S(2)}) collective-permute-start(bf16[288,1536]{1,0:T(8,128)(2,1)S(1)} %get-tuple-element.402), channel_id=1, source_target_pairs={{0,4},{4,0},{8,12},{12,8},{1,5},{5,1},{9,13},{13,9},{2,6},{6,2},{1... | collective-permute-start | bytes 2654216 | tf_op jit(solution)/shard_map/ppermute | solution.py:1020
  185.5 21.8 %collective-permute-start.29 = (bf16[288,1536]{1,0:T(8,128)(2,1)S(1)}, bf16[288,1536]{1,0:T(8,128)(2,1)S(1)}, u32[]{:S(2)}, u32[]{:S(2)}) collective-permute-start(bf16[288,1536]{1,0:T(8,128)(2,1)S(1)} %get-tuple-element.403), channel_id=1, source_target_pairs={{0,8},{4,12},{8,0},{12,4},{1,9},{5,13},{9,1},{13,5},{2,10},{6,14},... | collective-permute-start | bytes 2654216 | tf_op jit(solution)/shard_map/ppermute | solution.py:1020
  186.3 18.7 %collective-permute-start.27 = (bf16[208,1536]{1,0:T(8,128)(2,1)S(1)}, bf16[208,1536]{1,0:T(8,128)(2,1)S(1)}, u32[]{:S(2)}, u32[]{:S(2)}) collective-permute-start(bf16[208,1536]{1,0:T(8,128)(2,1)S(1)} %get-tuple-element.401), channel_id=1, source_target_pairs={{0,1},{1,0},{2,3},{3,2},{4,5},{5,4},{6,7},{7,6},{8,9},{9,8},{10,11... | collective-permute-start | bytes 1916936 | tf_op jit(solution)/shard_map/ppermute | solution.py:1257
  207.3 9.0 %copy-start.7 = (f32[512,768]{1,0:T(8,128)S(1)}, f32[512,768]{1,0:T(8,128)}, u32[]{:S(2)}) copy-start(f32[512,768]{1,0:T(8,128)} %get-tuple-element.386.refs_3_) | copy-start | bytes 4718596
  207.3 9.0 %copy-start.10 = (bf16[512,768]{1,0:T(8,128)(2,1)S(1)}, bf16[512,768]{1,0:T(8,128)(2,1)}, u32[]{:S(2)}) copy-start(bf16[512,768]{1,0:T(8,128)(2,1)} %get-tuple-element.312.refs_4_) | copy-start | bytes 2359300
  208.5 23.1 %collective-permute-start.33 = (bf16[320,1536]{1,0:T(8,128)(2,1)S(1)}, bf16[320,1536]{1,0:T(8,128)(2,1)S(1)}, u32[]{:S(2)}, u32[]{:S(2)}) collective-permute-start(bf16[320,1536]{1,0:T(8,128)(2,1)S(1)} %get-tuple-element.417), channel_id=1, source_target_pairs={{0,4},{4,0},{8,12},{12,8},{1,5},{5,1},{9,13},{13,9},{2,6},{6,2},{1... | collective-permute-start | bytes 2949128 | tf_op jit(solution)/shard_map/ppermute | solution.py:1020
  209.7 20.7 %collective-permute-start.34 = (bf16[288,1536]{1,0:T(8,128)(2,1)S(1)}, bf16[288,1536]{1,0:T(8,128)(2,1)S(1)}, u32[]{:S(2)}, u32[]{:S(2)}) collective-permute-start(bf16[288,1536]{1,0:T(8,128)(2,1)S(1)} %get-tuple-element.418), channel_id=1, source_target_pairs={{0,8},{4,12},{8,0},{12,4},{1,9},{5,13},{9,1},{13,5},{2,10},{6,14},... | collective-permute-start | bytes 2654216 | tf_op jit(solution)/shard_map/ppermute | solution.py:1020
  210.8 17.7 %collective-permute-start.32 = (bf16[208,1536]{1,0:T(8,128)(2,1)S(1)}, bf16[208,1536]{1,0:T(8,128)(2,1)S(1)}, u32[]{:S(2)}, u32[]{:S(2)}) collective-permute-start(bf16[208,1536]{1,0:T(8,128)(2,1)S(1)} %get-tuple-element.415.refs_0_), channel_id=1, source_target_pairs={{1,2},{2,1},{5,6},{6,5},{9,10},{10,9},{13,14},{14,13},{17,18},{18,... | collective-permute-start | bytes 1916936 | tf_op jit(solution)/shard_map/ppermute | solution.py:1257
  211.5 17.0 %collective-permute-start.31 = (bf16[192,1536]{1,0:T(8,128)(2,1)S(1)}, bf16[192,1536]{1,0:T(8,128)(2,1)S(1)}, u32[]{:S(2)}, u32[]{:S(2)}) collective-permute-start(bf16[192,1536]{1,0:T(8,128)(2,1)S(1)} %get-tuple-element.416), channel_id=1, source_target_pairs={{0,1},{1,0},{2,3},{3,2},{4,5},{5,4},{6,7},{7,6},{8,9},{9,8},{10,11... | collective-permute-start | bytes 1769480 | tf_op jit(solution)/shard_map/ppermute | solution.py:1257
  216.4 37.7 %collective-permute-start.25 = (f32[512,768]{1,0:T(8,128)S(1)}, f32[512,768]{1,0:T(8,128)S(1)}, u32[]{:S(2)}, u32[]{:S(2)}) collective-permute-start(f32[512,768]{1,0:T(8,128)S(1)} %convert_select_fusion), channel_id=1, source_target_pairs={{0,16},{16,0},{1,17},{17,1},{2,18},{18,2},{3,19},{19,3},{4,20},{20... | collective-permute-start | bytes 4718600 | tf_op jit(solution)/shard_map/ppermute | solution.py:1020
  231.6 7.7 %copy-start.8 = (bf16[512,768]{1,0:T(8,128)(2,1)S(1)}, bf16[512,768]{1,0:T(8,128)(2,1)}, u32[]{:S(2)}) copy-start(bf16[512,768]{1,0:T(8,128)(2,1)} %get-tuple-element.294.refs_3_.refs_0_) | copy-start | bytes 2359300
  231.6 7.7 %copy-start.9 = (bf16[512,768]{1,0:T(8,128)(2,1)S(1)}, bf16[512,768]{1,0:T(8,128)(2,1)}, u32[]{:S(2)}) copy-start(bf16[512,768]{1,0:T(8,128)(2,1)} %get-tuple-element.387.refs_1_) | copy-start | bytes 2359300
  232.6 17.2 %collective-permute-start.35 = (bf16[208,1536]{1,0:T(8,128)(2,1)S(1)}, bf16[208,1536]{1,0:T(8,128)(2,1)S(1)}, u32[]{:S(2)}, u32[]{:S(2)}) collective-permute-start(bf16[208,1536]{1,0:T(8,128)(2,1)S(1)} %get-tuple-element.429), channel_id=1, source_target_pairs={{0,1},{1,0},{2,3},{3,2},{4,5},{5,4},{6,7},{7,6},{8,9},{9,8},{10,11... | collective-permute-start | bytes 1916936 | tf_op jit(solution)/shard_map/ppermute | solution.py:1257
  236.8 9.6 %collective-permute-start.36 = (bf16[192,1536]{1,0:T(8,128)(2,1)S(1)}, bf16[192,1536]{1,0:T(8,128)(2,1)S(1)}, u32[]{:S(2)}, u32[]{:S(2)}) collective-permute-start(bf16[192,1536]{1,0:T(8,128)(2,1)S(1)} %get-tuple-element.430.refs_2_), channel_id=1, source_target_pairs={{1,2},{2,1},{5,6},{6,5},{9,10},{10,9},{13,14},{14,13},{17,18},{18,... | collective-permute-start | bytes 1769480 | tf_op jit(solution)/shard_map/ppermute | solution.py:1257
  237.8 7.2 %collective-permute-start.37 = (bf16[96,1536]{1,0:T(8,128)(2,1)S(1)}, bf16[96,1536]{1,0:T(8,128)(2,1)S(1)}, u32[]{:S(2)}, u32[]{:S(2)}) collective-permute-start(bf16[96,1536]{1,0:T(8,128)(2,1)S(1)} %get-tuple-element.431), channel_id=1, source_target_pairs={{0,4},{4,0},{8,12},{12,8},{1,5},{5,1},{9,13},{13,9},{2,6},{6,2},{1... | collective-permute-start | bytes 884744 | tf_op jit(solution)/shard_map/ppermute | solution.py:1020
  238.5 7.9 %collective-permute-start.38 = (bf16[112,1536]{1,0:T(8,128)(2,1)S(1)}, bf16[112,1536]{1,0:T(8,128)(2,1)S(1)}, u32[]{:S(2)}, u32[]{:S(2)}) collective-permute-start(bf16[112,1536]{1,0:T(8,128)(2,1)S(1)} %get-tuple-element.432), channel_id=1, source_target_pairs={{0,8},{4,12},{8,0},{12,4},{1,9},{5,13},{9,1},{13,5},{2,10},{6,14},... | collective-permute-start | bytes 1032200 | tf_op jit(solution)/shard_map/ppermute | solution.py:1020
  245.0 9.1 %collective-permute-start.26 = (bf16[512,768]{1,0:T(8,128)(2,1)S(1)}, bf16[512,768]{1,0:T(8,128)(2,1)S(1)}, u32[]{:S(2)}, u32[]{:S(2)}) collective-permute-start(bf16[512,768]{1,0:T(8,128)(2,1)S(1)} %broadcast_select_fusion), channel_id=1, source_target_pairs={{0,16},{16,0},{1,17},{17,1},{2,18},{18,2},{3,19},{19,3},{4,20},{20... | collective-permute-start | bytes 2359304 | tf_op jit(solution)/shard_map/ppermute | solution.py:1020
  250.8 14.8 %collective-permute-start.39 = (bf16[208,1536]{1,0:T(8,128)(2,1)S(1)}, bf16[208,1536]{1,0:T(8,128)(2,1)S(1)}, u32[]{:S(2)}, u32[]{:S(2)}) collective-permute-start(bf16[208,1536]{1,0:T(8,128)(2,1)S(1)} %get-tuple-element.440), channel_id=1, source_target_pairs={{0,1},{1,0},{2,3},{3,2},{4,5},{5,4},{6,7},{7,6},{8,9},{9,8},{10,11... | collective-permute-start | bytes 1916936 | tf_op jit(solution)/shard_map/ppermute | solution.py:1257
  253.4 0.7 collective-permute-start.40
  254.1 17.2 %copy-start.13 = (bf16[512,768]{1,0:T(8,128)(2,1)}, bf16[512,768]{1,0:T(8,128)(2,1)S(1)}, u32[]{:S(2)}) copy-start(bf16[512,768]{1,0:T(8,128)(2,1)S(1)} %collective-permute-done.26.refs_2_) | copy-start | bytes 2359300
  254.1 17.2 %copy-start.12 = (f32[512,768]{1,0:T(8,128)}, f32[512,768]{1,0:T(8,128)S(1)}, u32[]{:S(2)}) copy-start(f32[512,768]{1,0:T(8,128)S(1)} %collective-permute-done.25.refs_5_) | copy-start | bytes 4718596
  266.4 14.8 %collective-permute-start.42 = (bf16[208,1536]{1,0:T(8,128)(2,1)S(1)}, bf16[208,1536]{1,0:T(8,128)(2,1)S(1)}, u32[]{:S(2)}, u32[]{:S(2)}) collective-permute-start(bf16[208,1536]{1,0:T(8,128)(2,1)S(1)} %get-tuple-element.452.refs_3_), channel_id=1, source_target_pairs={{1,2},{2,1},{5,6},{6,5},{9,10},{10,9},{13,14},{14,13},{17,18},{18,... | collective-permute-start | bytes 1916936 | tf_op jit(solution)/shard_map/ppermute | solution.py:1257
  267.1 14.1 %collective-permute-start.41 = (bf16[192,1536]{1,0:T(8,128)(2,1)S(1)}, bf16[192,1536]{1,0:T(8,128)(2,1)S(1)}, u32[]{:S(2)}, u32[]{:S(2)}) collective-permute-start(bf16[192,1536]{1,0:T(8,128)(2,1)S(1)} %get-tuple-element.451), channel_id=1, source_target_pairs={{0,1},{1,0},{2,3},{3,2},{4,5},{5,4},{6,7},{7,6},{8,9},{9,8},{10,11... | collective-permute-start | bytes 1769480 | tf_op jit(solution)/shard_map/ppermute | solution.py:1257
  282.0 13.1 %collective-permute-start.45 = (bf16[208,1536]{1,0:T(8,128)(2,1)S(1)}, bf16[208,1536]{1,0:T(8,128)(2,1)S(1)}, u32[]{:S(2)}, u32[]{:S(2)}) collective-permute-start(bf16[208,1536]{1,0:T(8,128)(2,1)S(1)} %get-tuple-element.464), channel_id=1, source_target_pairs={{0,1},{1,0},{2,3},{3,2},{4,5},{5,4},{6,7},{7,6},{8,9},{9,8},{10,11... | collective-permute-start | bytes 1916936 | tf_op jit(solution)/shard_map/ppermute | solution.py:1257
  295.0 9.1 %copy-start.1 = (bf16[8,128,768]{2,1,0:T(8,128)(2,1)S(1)}, bf16[8,128,768]{2,1,0:T(8,128)(2,1)}, u32[]{:S(2)}) copy-start(bf16[8,128,768]{2,1,0:T(8,128)(2,1)} %param.14) | copy-start | bytes 4718596
  295.8 3.8 %collective-permute-start.46 = (bf16[208,1536]{1,0:T(8,128)(2,1)S(1)}, bf16[208,1536]{1,0:T(8,128)(2,1)S(1)}, u32[]{:S(2)}, u32[]{:S(2)}) collective-permute-start(bf16[208,1536]{1,0:T(8,128)(2,1)S(1)} %get-tuple-element.467), channel_id=1, source_target_pairs={{0,16},{16,0},{1,17},{17,1},{2,18},{18,2},{3,19},{19,3},{4,20},{20... | collective-permute-start | bytes 1916936 | tf_op jit(solution)/shard_map/ppermute | solution.py:1020
  295.8 2.9 collective-permute-start.43
  296.3 3.3 %collective-permute-start.44 = (bf16[192,1536]{1,0:T(8,128)(2,1)S(1)}, bf16[192,1536]{1,0:T(8,128)(2,1)S(1)}, u32[]{:S(2)}, u32[]{:S(2)}) collective-permute-start(bf16[192,1536]{1,0:T(8,128)(2,1)S(1)} %get-tuple-element.462), channel_id=1, source_target_pairs={{0,16},{16,0},{1,17},{17,1},{2,18},{18,2},{3,19},{19,3},{4,20},{20... | collective-permute-start | bytes 1769480 | tf_op jit(solution)/shard_map/ppermute | solution.py:1020

commit v8 on v7

--- a/solution.py
+++ b/solution.py
@@ -1464,8 +1464,7 @@
     two.made.update(second=made[10], branch=made[11], down_sums=made[12])
     line.add(made[13], made[14])
     exchanged_y = exchange(jnp.where(section == 0, y_two, y_one), "section", 1)
-    line.advance(two, two.up_first)
-    line.advance(two, two.up_last)
+    line.advance(two, two.up)
     line.advance(two, two.attention)
     gx_two_near, gx_two_low = two.made["gx_low"]
     line.advance(one, lambda: one.down(gx_two_near))

time: 309 us -> 308 us (level)
  waiting for transfers between devices: 87.9 us -> 99.9 us
  starting transfers between devices: 55 us -> 44.6 us
    ppermute x32 -> x30, waiting for transfers between devices: 27.1 us -> 44.2 us  [exchange(): return lax.ppermute(array, axis, [(i, i ^ bit) for i in range(length)])]
    ppermute x15 -> x14, starting transfers between devices: 35.3 us -> 26.3 us  [move(): lax.ppermute(array, 'outer', [(0, 1), (1, 0), (2, 3), (3, 2)] if way == '...]
    ppermute x15 -> x14, waiting for transfers between devices: 60.8 us -> 55.6 us  [move(): lax.ppermute(array, 'outer', [(0, 1), (1, 0), (2, 3), (3, 2)] if way == '...]
    pallas_call x12 -> x11, Pallas kernels: 135 us -> 132 us  [call(): pl.pallas_call(body, in_specs=[pl.BlockSpec(memory_space=pltpu.SMEM)] + [...]
    ppermute x32 -> x30, starting transfers between devices: 19.7 us -> 18.3 us  [exchange(): return lax.ppermute(array, axis, [(i, i ^ bit) for i in range(length)])]
    pallas_call x12 -> x11, Pallas kernels: 14 us -> 14.7 us  [run(): pl.pallas_call(kernel, in_specs=[pl.BlockSpec(memory_space=pltpu.SMEM)] +...]
  transfers between devices with their start and end apart: 47 -> 44, of which waited for: 23 -> 21; matrix products, arithmetic and copies ran while one was open for 3% -> 3% of each run, Pallas kernels for 35% -> 34%
where the time goes in v8:
time: 308 us; the launch traced here: 304 us
  Pallas kernels  147 us (48%)
  waiting for transfers between devices  99.9 us (32%)
  starting transfers between devices  44.6 us (14%)
  local copies, waits for them, and re-layouts  6.54 us (2%)
  other arithmetic  4.57 us (1%)
    pallas_call x11, Pallas kernels, call(): pl.pallas_call(body, in_specs=[pl.BlockSpec(memory_space=pltpu.SMEM)] + [...  132 us
    ppermute x14, waiting for transfers between devices, move(): lax.ppermute(array, 'outer', [(0, 1), (1, 0), (2, 3), (3, 2)] if way == '...  55.6 us
    ppermute x30, waiting for transfers between devices, exchange(): return lax.ppermute(array, axis, [(i, i ^ bit) for i in range(length)])  44.2 us
    ppermute x14, starting transfers between devices, move(): lax.ppermute(array, 'outer', [(0, 1), (1, 0), (2, 3), (3, 2)] if way == '...  26.3 us
    ppermute x30, starting transfers between devices, exchange(): return lax.ppermute(array, axis, [(i, i ^ bit) for i in range(length)])  18.3 us
    pallas_call x11, Pallas kernels, run(): pl.pallas_call(kernel, in_specs=[pl.BlockSpec(memory_space=pltpu.SMEM)] +...  14.7 us
  transfers between devices with their start and end apart: 44, of which 21 were waited for; matrix products, arithmetic and copies ran while one was open for 3% of the time, Pallas kernels for 34%

profile of v8, /device:TPU:0, one launch (start us, length us, event | category | flops | bytes accessed | tf_op | source)
XLA Modules:
  0.0 303.7 jit_solution(2115438794390508467)
XLA Ops:
  1.7 1.4 reduce.3
  3.1 0.8 concatenate.6
  5.5 0.9 constant_dynamic-slice_fusion
  6.5 0.8 copy.27
  8.5 8.4 %attend_forward.1 = (bf16[512,768]{1,0:T(8,128)(2,1)}, bf16[512,768]{1,0:T(8,128)(2,1)}, bf16[512,768]{1,0:T(8,128)(2,1)}, f32[4,6,256,128]{3,2,1,0:T(8,128)}, b...) custom-call(s32[1]{0:T(128)} %bitcast.ids_ref, bf16[512,768]{1,0:T(8,128)(2,1)} %bitcast.36, ...), custom_call_target="tpu_custom_call" | custom-call | flops 2415919104 | bytes 12582912 | tf_op jit(solution)/shard_map/attend_forward/pallas_call | solution.py:161
  16.9 0.9 collective-permute-done.2.refs_3_.refs_6_.refs_9_
  18.3 1.4 dynamic-slice_select_fusion
  19.7 12.5 %up_forward.1 = (f32[512,768]{1,0:T(8,128)S(1)}, f32[512,768]{1,0:T(8,128)}, f32[512,128]{1,0:T(8,128)}, bf16[768,512]{1,0:T(8,128)(2,1)}, bf16[4,512,768]{2,1,0...) custom-call(s32[1]{0:T(128)} %bitcast.ids_ref, bf16[512,768]{1,0:T(8,128)(2,1)} %bitcast.37, ...), custom_call_target="tpu_custom_call" | custom-call | flops 3019898880 | bytes 20971520 | tf_op jit(solution)/shard_map/up_forward/pallas_call | solution.py:161
  32.3 9.0 %down_forward.1 = (bf16[512,768]{1,0:T(8,128)(2,1)S(1)}, bf16[512,768]{1,0:T(8,128)(2,1)}, f32[512,768]{1,0:T(8,128)}, f32[512,128]{1,0:T(8,128)}) custom-call(s32[1]{0:T(128)} %bitcast.ids_ref, bf16[4,512,768]{2,1,0:T(8,128)(2,1)S(1)} %get-tuple-element.249.refs_0_, bf16[3072,768]{1,0:T(8,128)(2,1)} %bitcast.24, ...), custom_call_target="tpu_custom_call" | custom-call | flops 2415919104 | bytes 12582912 | tf_op jit(solution)/shard_map/down_forward/pallas_call | solution.py:161
  41.3 25.2 %second_layer.1 = (bf16[512,768]{1,0:T(8,128)(2,1)}, bf16[512,768]{1,0:T(8,128)(2,1)}, bf16[512,768]{1,0:T(8,128)(2,1)}, f32[4,6,256,128]{3,2,1,0:T(8,128)}, bf1...) custom-call(s32[1]{0:T(128)} %bitcast.ids_ref, ...), custom_call_target="tpu_custom_call" | custom-call | flops 10267656192 | bytes 52428800 | tf_op jit(solution)/shard_map/second_layer/pallas_call | solution.py:161
  66.6 14.0 %up_grad.2 = (f32[512,768]{1,0:T(8,128)S(1)}, bf16[512,768]{1,0:T(8,128)(2,1)S(1)}, f32[8,768]{1,0:T(8,128)S(1)}, bf16[4,192,1536]{2,1,0:T(8,128)(2,1)}, bf16[4,192,1536]{2,1,0:T(8,128)(2,1)S(1)}) custom-call(s32[1]{0:T(128)} %bitcast.ids_ref, bf16[512,768]{1,0:T(8,128)(2,1)S(1)} %get-tuple-element.254.refs_0_, f32[512,768]{1,0:T(8,128)S(1)} %get-tuple-element.255.refs_1_, ...), custom_call_target="tpu_custom_call" | custom-call | flops 7247757312 | bytes 31457280 | tf_op jit(solution)/shard_map/up_grad/pallas_call | solution.py:161
  80.6 1.2 copy-done.5
  81.9 1.4 copy-done.11
  83.8 3.2 %join_sums.11 = (bf16[2,96,1536]{2,1,0:T(8,128)(2,1)S(1)}, bf16[2,96,1536]{2,1,0:T(8,128)(2,1)S(1)}, bf16[192,1536]{1,0:T(8,128)(2,1)S(1)}, bf16[192,1536]{1,0:T(8,128)(2,1)S(1)}) custom-call(s32[5]{0:T(128)S(1)} %stack.24.ids_ref, bf16[4,192,1536]{2,1,0:T(8,128)(2,1)} %get-tuple-element.283.refs_0_, bf16[4,192,1536]{2,1,0:T(8,128)(2,1)} %copy-done.11), custom_call_target="tpu_custom_call" | custom-call | tf_op jit(solution)/shard_map/join_sums/pallas_call | solution.py:1076
  87.0 3.0 collective-permute-start.6
  90.0 1.5 collective-permute-start.7
  91.5 16.3 %attend_grad.2 = (f32[512,768]{1,0:T(8,128)}, bf16[512,768]{1,0:T(8,128)(2,1)S(1)}, bf16[512,768]{1,0:T(8,128)(2,1)}, bf16[4,208,1536]{2,1,0:T(8,128)(2,1)S(1)}, bf16[4,208,1536]{2,1,0:T(8,128)(2,1)S(1)}) custom-call(s32[1]{0:T(128)} %bitcast.ids_ref, bf16[512,768]{1,0:T(8,128)(2,1)S(1)} %get-tuple-element.268.refs_0_, ...), custom_call_target="tpu_custom_call" | custom-call | flops 6039797760 | bytes 31457280 | tf_op jit(solution)/shard_map/attend_grad/pallas_call | solution.py:161
  107.9 2.1 join_sums.12
  110.7 6.8 %down_grad.1 = (f32[512,768]{1,0:T(8,128)S(1)}, bf16[512,768]{1,0:T(8,128)(2,1)S(1)}, f32[8,768]{1,0:T(8,128)S(1)}, bf16[4,192,1536]{2,1,0:T(8,128)(2,1)S(1)}, bf16[4,192,1536]{2,1,0:T(8,128)(2,1)S(1)}) custom-call(s32[1]{0:T(128)} %bitcast.ids_ref, bf16[512,768]{1,0:T(8,128)(2,1)S(1)} %get-tuple-element.289.refs_0_, f32[512,768]{1,0:T(8,128)} %get-tuple-element.290.refs_1_, ...), custom_call_target="tpu_custom_call" | custom-call | flops 2415919104 | bytes 14680064 | tf_op jit(solution)/shard_map/down_grad/pallas_call | solution.py:161
  117.5 14.6 %collective-permute-done.9.refs_2_ = bf16[288,1536]{1,0:T(8,128)(2,1)S(1)} collective-permute-done((bf16[288,1536]{1,0:T(8,128)(2,1)S(1)}, bf16[288,1536]{1,0:T(8,128)(2,1)S(1)}, u32[]{:S(2)}, u32[]{:S(2)}) %collective-permute-start.9) | collective-permute-done | bytes 884768 | tf_op jit(solution)/shard_map/ppermute | solution.py:1020
  132.4 1.4 join_sums.13
  133.8 1.6 collective-permute-start.13
  135.8 1.5 collective-permute-start.12
  137.4 13.6 %up_grad.3 = (f32[512,768]{1,0:T(8,128)S(1)}, bf16[512,768]{1,0:T(8,128)(2,1)S(1)}, f32[8,768]{1,0:T(8,128)S(1)}, bf16[4,192,1536]{2,1,0:T(8,128)(2,1)S(1)}, bf16[4,192,1536]{2,1,0:T(8,128)(2,1)S(1)}) custom-call(s32[1]{0:T(128)} %bitcast.ids_ref, bf16[512,768]{1,0:T(8,128)(2,1)S(1)} %get-tuple-element.308.refs_0_, ...), custom_call_target="tpu_custom_call" | custom-call | flops 7247757312 | bytes 31457280 | tf_op jit(solution)/shard_map/up_grad/pallas_call | solution.py:161
  151.0 6.1 %collective-permute-done.14.refs_5_ = bf16[288,1536]{1,0:T(8,128)(2,1)S(1)} collective-permute-done((bf16[288,1536]{1,0:T(8,128)(2,1)S(1)}, bf16[288,1536]{1,0:T(8,128)(2,1)S(1)}, u32[]{:S(2)}, u32[]{:S(2)}) %collective-permute-start.14) | collective-permute-done | bytes 884768 | tf_op jit(solution)/shard_map/ppermute | solution.py:1020
  157.1 0.9 collective-permute-done.13.refs_4_
  158.0 1.2 join_sums.14
  159.6 1.7 collective-permute-start.18
  161.2 1.5 collective-permute-start.16
  162.7 0.9 collective-permute-start.17
  163.7 16.1 %attend_grad.3 = (f32[512,768]{1,0:T(8,128)}, bf16[512,768]{1,0:T(8,128)(2,1)}, bf16[4,208,1536]{2,1,0:T(8,128)(2,1)S(1)}, bf16[4,208,1536]{2,1,0:T(8,128)(2,1)S(1)}) custom-call(s32[1]{0:T(128)} %bitcast.ids_ref, bf16[512,768]{1,0:T(8,128)(2,1)S(1)} %get-tuple-element.333.refs_0_, bf16[768,512]{1,0:T(8,128)(2,1)} %get-tuple-element.336.refs_1_, ...), custom_call_target="tpu_custom_call" | custom-call | flops 6039797760 | bytes 31457280 | tf_op jit(solution)/shard_map/attend_grad/pallas_call | solution.py:161
  179.8 1.6 collective-permute-done.18.refs_6_
  181.4 1.0 collective-permute-done.19.refs_7_
  182.3 1.2 join_sums.15
  183.6 1.6 collective-permute-start.25
  185.9 1.8 collective-permute-start.23
  188.4 13.8 %collective-permute-done.23.refs_1_ = bf16[208,1536]{1,0:T(8,128)(2,1)S(1)} collective-permute-done((bf16[208,1536]{1,0:T(8,128)(2,1)S(1)}, bf16[208,1536]{1,0:T(8,128)(2,1)S(1)}, u32[]{:S(2)}, u32[]{:S(2)}) %collective-permute-start.23) | collective-permute-done | bytes 639008 | tf_op jit(solution)/shard_map/ppermute | solution.py:1257
  202.1 3.6 %collective-permute-done.25.refs_7_ = bf16[288,1536]{1,0:T(8,128)(2,1)S(1)} collective-permute-done((bf16[288,1536]{1,0:T(8,128)(2,1)S(1)}, bf16[288,1536]{1,0:T(8,128)(2,1)S(1)}, u32[]{:S(2)}, u32[]{:S(2)}) %collective-permute-start.25) | collective-permute-done | bytes 884768 | tf_op jit(solution)/shard_map/ppermute | solution.py:1020
  205.7 1.2 collective-permute-done.26.refs_8_
  206.9 1.4 join_sums.16
  210.3 4.3 %collective-permute-start.28 = (bf16[192,1536]{1,0:T(8,128)(2,1)S(1)}, bf16[192,1536]{1,0:T(8,128)(2,1)S(1)}, u32[]{:S(2)}, u32[]{:S(2)}) collective-permute-start(bf16[192,1536]{1,0:T(8,128)(2,1)S(1)} %get-tuple-element.393), channel_id=1, source_target_pairs={{0,1},{1,0},{2,3},{3,2},{4,5},{5,4},{6,7},{7,6},{8,9},{9,8},{10,11... | collective-permute-start | bytes 1769480 | tf_op jit(solution)/shard_map/ppermute | solution.py:1257
  214.9 11.8 %collective-permute-done.28.refs_1_ = bf16[192,1536]{1,0:T(8,128)(2,1)S(1)} collective-permute-done((bf16[192,1536]{1,0:T(8,128)(2,1)S(1)}, bf16[192,1536]{1,0:T(8,128)(2,1)S(1)}, u32[]{:S(2)}, u32[]{:S(2)}) %collective-permute-start.28) | collective-permute-done | bytes 589856 | tf_op jit(solution)/shard_map/ppermute | solution.py:1257
  226.8 2.9 collective-permute-done.31.refs_8_
  229.6 1.8 collective-permute-done.30.refs_7_
  231.4 1.0 join_sums.17
  232.5 1.6 collective-permute-start.32
  234.0 1.0 collective-permute-start.33
  235.0 1.0 collective-permute-start.34
  236.0 1.5 collective-permute-start.35
  237.7 4.5 %collective-permute-done.34.refs_7_ = bf16[96,1536]{1,0:T(8,128)(2,1)S(1)} collective-permute-done((bf16[96,1536]{1,0:T(8,128)(2,1)S(1)}, bf16[96,1536]{1,0:T(8,128)(2,1)S(1)}, u32[]{:S(2)}, u32[]{:S(2)}) %collective-permute-start.34) | collective-permute-done | bytes 294944 | tf_op jit(solution)/shard_map/ppermute | solution.py:1020
  242.2 1.7 collective-permute-done.35.refs_8_
  243.9 3.4 %collective-permute-done.32.refs_1_ = bf16[208,1536]{1,0:T(8,128)(2,1)S(1)} collective-permute-done((bf16[208,1536]{1,0:T(8,128)(2,1)S(1)}, bf16[208,1536]{1,0:T(8,128)(2,1)S(1)}, u32[]{:S(2)}, u32[]{:S(2)}) %collective-permute-start.32) | collective-permute-done | bytes 639008 | tf_op jit(solution)/shard_map/ppermute | solution.py:1257
  247.3 0.9 join_sums.18
  248.2 3.6 %collective-permute-start.36 = (bf16[208,1536]{1,0:T(8,128)(2,1)S(1)}, bf16[208,1536]{1,0:T(8,128)(2,1)S(1)}, u32[]{:S(2)}, u32[]{:S(2)}) collective-permute-start(bf16[208,1536]{1,0:T(8,128)(2,1)S(1)} %get-tuple-element.418), channel_id=1, source_target_pairs={{0,1},{1,0},{2,3},{3,2},{4,5},{5,4},{6,7},{7,6},{8,9},{9,8},{10,11... | collective-permute-start | bytes 1916936 | tf_op jit(solution)/shard_map/ppermute | solution.py:1257
  252.6 11.4 %collective-permute-done.36.refs_1_ = bf16[208,1536]{1,0:T(8,128)(2,1)S(1)} collective-permute-done((bf16[208,1536]{1,0:T(8,128)(2,1)S(1)}, bf16[208,1536]{1,0:T(8,128)(2,1)S(1)}, u32[]{:S(2)}, u32[]{:S(2)}) %collective-permute-start.36) | collective-permute-done | bytes 639008 | tf_op jit(solution)/shard_map/ppermute | solution.py:1257
  263.9 0.9 join_sums.19
  265.5 5.4 %collective-permute-start.38 = (bf16[192,1536]{1,0:T(8,128)(2,1)S(1)}, bf16[192,1536]{1,0:T(8,128)(2,1)S(1)}, u32[]{:S(2)}, u32[]{:S(2)}) collective-permute-start(bf16[192,1536]{1,0:T(8,128)(2,1)S(1)} %get-tuple-element.429), channel_id=1, source_target_pairs={{0,1},{1,0},{2,3},{3,2},{4,5},{5,4},{6,7},{7,6},{8,9},{9,8},{10,11... | collective-permute-start | bytes 1769480 | tf_op jit(solution)/shard_map/ppermute | solution.py:1257
  270.9 5.4 %assemble.1 = (bf16[2,512,768]{2,1,0:T(8,128)(2,1)}, f32[2,512,768]{2,1,0:T(8,128)}) custom-call(s32[1]{0:T(128)} %bitcast.ids_ref, bf16[512,768]{1,0:T(8,128)(2,1)} %get-tuple-element.272.refs_3_.refs_0_, bf16[512,768]{1,0:T(8,128)(2,1)} %get-tuple-element.362.refs_1_, bf16[512,768]{1,0:T(8,128)(2,1)} %copy-done.13, f32[512,768]{1,0:T(8,128)} %get-tuple-element.361.refs_3_, ...), custom_call_target="tpu_custom_call" | custom-call | flops 1000 | bytes 10485760 | tf_op jit(solution)/shard_map/assemble/pallas_call | solution.py:161
  276.3 4.8 %collective-permute-done.38.refs_1_ = bf16[192,1536]{1,0:T(8,128)(2,1)S(1)} collective-permute-done((bf16[192,1536]{1,0:T(8,128)(2,1)S(1)}, bf16[192,1536]{1,0:T(8,128)(2,1)S(1)}, u32[]{:S(2)}, u32[]{:S(2)}) %collective-permute-start.38) | collective-permute-done | bytes 589856 | tf_op jit(solution)/shard_map/ppermute | solution.py:1257
  281.9 1.8 collective-permute-start.42
  283.7 10.4 %collective-permute-done.42.refs_1_ = bf16[208,1536]{1,0:T(8,128)(2,1)S(1)} collective-permute-done((bf16[208,1536]{1,0:T(8,128)(2,1)S(1)}, bf16[208,1536]{1,0:T(8,128)(2,1)S(1)}, u32[]{:S(2)}, u32[]{:S(2)}) %collective-permute-start.42) | collective-permute-done | bytes 639008 | tf_op jit(solution)/shard_map/ppermute | solution.py:1257
  295.5 2.3 collective-permute-done.40.refs_1_
  297.9 0.8 collective-permute-done.41.refs_3_
  298.7 4.5 %last.1 = (f32[768,768]{1,0:T(8,128)}, f32[192,2304]{1,0:T(8,128)}, f32[192,768]{1,0:T(8,128)}, f32[2,192]{1,0:T(2,128)}, f32[1,192]{1,0:T(1,128)}, /*index=5*/f...) custom-call(s32[5]{0:T(128)S(1)} %stack.24.ids_ref, ...), custom_call_target="tpu_custom_call" | custom-call | flops 1000 | bytes 5242880 | tf_op jit(solution)/shard_map/last/pallas_call | solution.py:161
  (98 shorter events, 14.2 us)
Async XLA Ops:
  0.6 4.9 %copy-start = (bf16[8,128,768]{2,1,0:T(8,128)(2,1)S(1)}, bf16[8,128,768]{2,1,0:T(8,128)(2,1)}, u32[]{:S(2)}) copy-start(bf16[8,128,768]{2,1,0:T(8,128)(2,1)} %param.14) | copy-start | bytes 4718596
  0.7 7.3 %collective-permute-start = (bf16[768,2304]{1,0:T(8,128)(2,1)}, bf16[768,2304]{1,0:T(8,128)(2,1)}, u32[]{:S(2)}, u32[]{:S(2)}) collective-permute-start(bf16[768,2304]{1,0:T(8,128)(2,1)} %bitcast.50), channel_id=1, source_target_pairs={{0,16},{16,0},{1,17},{17,1},{2,18},{18,2},{3,19},{19,3},{4,20},{20... | collective-permute-start | bytes 10616840 | tf_op jit(solution)/shard_map/ppermute | solution.py:1020
  3.9 3.4 %collective-permute-start.1 = (f32[16,768]{1,0:T(8,128)S(1)}, f32[16,768]{1,0:T(8,128)S(1)}, u32[]{:S(2)}, u32[]{:S(2)}) collective-permute-start(f32[16,768]{1,0:T(8,128)S(1)} %concatenate.6), channel_id=1, source_target_pairs={{0,16},{16,0},{1,17},{17,1},{2,18},{18,2},{3,19},{19,3},{4,20},{20... | collective-permute-start | bytes 147464 | tf_op jit(solution)/shard_map/ppermute | solution.py:1020
  7.3 10.5 %slice-start = ((s8[4718592]{0:T(1024)(128)(4,1)}), s8[4194304]{0:T(1024)(128)(4,1)S(1)}, s32[]{:S(2)}) async-start(s8[4718592]{0:T(1024)(128)(4,1)} %bitcast.28), calls=%async_computation | async-start | bytes 8388608
  7.9 9.9 %collective-permute-start.3 = (bf16[768,3072]{1,0:T(8,128)(2,1)}, bf16[768,3072]{1,0:T(8,128)(2,1)S(1)}, u32[]{:S(2)}, u32[]{:S(2)}) collective-permute-start(bf16[768,3072]{1,0:T(8,128)(2,1)} %bitcast.31), channel_id=1, source_target_pairs={{0,16},{16,0},{1,17},{17,1},{2,18},{18,2},{3,19},{19,3},{4,20},{20... | collective-permute-start | bytes 14155784 | tf_op jit(solution)/shard_map/ppermute | solution.py:1020
  8.4 9.4 %collective-permute-start.2 = (bf16[768,768]{1,0:T(8,128)(2,1)}, bf16[768,768]{1,0:T(8,128)(2,1)S(1)}, u32[]{:S(2)}, u32[]{:S(2)}) collective-permute-start(bf16[768,768]{1,0:T(8,128)(2,1)} %bitcast.39), channel_id=1, source_target_pairs={{0,16},{16,0},{1,17},{17,1},{2,18},{18,2},{3,19},{19,3},{4,20},{20... | collective-permute-start | bytes 3538952 | tf_op jit(solution)/shard_map/ppermute | solution.py:1020
  8.5 9.4 %slice-start.1 = ((s8[4718592]{0:T(1024)(128)(4,1)}), s8[524288]{0:T(1024)(128)(4,1)S(1)}, s32[]{:S(2)}) async-start(s8[4718592]{0:T(1024)(128)(4,1)} %bitcast.28), calls=%async_computation.1 | async-start | bytes 1048576
  8.5 9.8 %copy-start.14 = (bf16[8,128,768]{2,1,0:T(8,128)(2,1)S(1)}, bf16[8,128,768]{2,1,0:T(8,128)(2,1)}, u32[]{:S(2)}) copy-start(bf16[8,128,768]{2,1,0:T(8,128)(2,1)} %param.17) | copy-start | bytes 4718596
  17.8 14.4 %copy-start.4 = (bf16[768,768]{1,0:T(8,128)(2,1)}, bf16[768,768]{1,0:T(8,128)(2,1)S(1)}, u32[]{:S(2)}) copy-start(bf16[768,768]{1,0:T(8,128)(2,1)S(1)} %collective-permute-done.2.refs_3_.refs_6_.refs_9_) | copy-start | bytes 3538948
  17.8 14.4 %copy-start.3 = (bf16[768,3072]{1,0:T(8,128)(2,1)}, bf16[768,3072]{1,0:T(8,128)(2,1)S(1)}, u32[]{:S(2)}) copy-start(bf16[768,3072]{1,0:T(8,128)(2,1)S(1)} %collective-permute-done.3.refs_5_.refs_8_.refs_7_) | copy-start | bytes 14155780
  17.9 14.4 %collective-permute-start.4 = (bf16[3072,768]{1,0:T(8,128)(2,1)S(1)}, bf16[3072,768]{1,0:T(8,128)(2,1)S(1)}, u32[]{:S(2)}, u32[]{:S(2)}) collective-permute-start(bf16[3072,768]{1,0:T(8,128)(2,1)S(1)} %bitcast.30), channel_id=1, source_target_pairs={{0,16},{16,0},{1,17},{17,1},{2,18},{18,2},{3,19},{19,3},{4,20},{20... | collective-permute-start | bytes 14155784 | tf_op jit(solution)/shard_map/ppermute | solution.py:1020
  32.3 9.0 %copy-start.2 = (bf16[3072,768]{1,0:T(8,128)(2,1)}, bf16[3072,768]{1,0:T(8,128)(2,1)S(1)}, u32[]{:S(2)}) copy-start(bf16[3072,768]{1,0:T(8,128)(2,1)S(1)} %collective-permute-done.4.refs_2_.refs_10_.refs_3_) | copy-start | bytes 14155780
  66.5 15.3 %collective-permute-start.5 = (bf16[4,192,1536]{2,1,0:T(8,128)(2,1)S(1)}, bf16[4,192,1536]{2,1,0:T(8,128)(2,1)S(1)}, u32[]{:S(2)}, u32[]{:S(2)}) collective-permute-start(bf16[4,192,1536]{2,1,0:T(8,128)(2,1)S(1)} %get-tuple-element.267), channel_id=1, source_target_pairs={{0,16},{16,0},{1,17},{17,1},{2,18},{18,2},{3,19},{19,3},{4,20},{20... | collective-permute-start | bytes 7077896 | tf_op jit(solution)/shard_map/ppermute | solution.py:1020
  80.6 1.2 copy-start.5
  81.9 1.4 copy-start.11
  83.2 24.5 %collective-permute-start.8 = (bf16[4,192,1536]{2,1,0:T(8,128)(2,1)}, bf16[4,192,1536]{2,1,0:T(8,128)(2,1)}, u32[]{:S(2)}, u32[]{:S(2)}) collective-permute-start(bf16[4,192,1536]{2,1,0:T(8,128)(2,1)} %get-tuple-element.287), channel_id=1, source_target_pairs={{0,16},{16,0},{1,17},{17,1},{2,18},{18,2},{3,19},{19,3},{4,20},{20... | collective-permute-start | bytes 7077896 | tf_op jit(solution)/shard_map/ppermute | solution.py:1020
  83.8 7.7 %copy-start.6 = (f32[512,768]{1,0:T(8,128)S(1)}, f32[512,768]{1,0:T(8,128)}, u32[]{:S(2)}) copy-start(f32[512,768]{1,0:T(8,128)} %copy-done.5) | copy-start | bytes 4718596
  87.0 20.7 %collective-permute-start.6 = (bf16[192,1536]{1,0:T(8,128)(2,1)S(1)}, bf16[192,1536]{1,0:T(8,128)(2,1)S(1)}, u32[]{:S(2)}, u32[]{:S(2)}) collective-permute-start(bf16[192,1536]{1,0:T(8,128)(2,1)S(1)} %get-tuple-element.285), channel_id=1, source_target_pairs={{0,4},{4,0},{8,12},{12,8},{1,5},{5,1},{9,13},{13,9},{2,6},{6,2},{1... | collective-permute-start | bytes 1769480 | tf_op jit(solution)/shard_map/ppermute | solution.py:1020
  90.0 17.8 %collective-permute-start.7 = (bf16[192,1536]{1,0:T(8,128)(2,1)S(1)}, bf16[192,1536]{1,0:T(8,128)(2,1)S(1)}, u32[]{:S(2)}, u32[]{:S(2)}) collective-permute-start(bf16[192,1536]{1,0:T(8,128)(2,1)S(1)} %get-tuple-element.286), channel_id=1, source_target_pairs={{0,8},{4,12},{8,0},{12,4},{1,9},{5,13},{9,1},{13,5},{2,10},{6,14},... | collective-permute-start | bytes 1769480 | tf_op jit(solution)/shard_map/ppermute | solution.py:1020
  107.8 24.6 %collective-permute-start.11 = (bf16[4,208,1536]{2,1,0:T(8,128)(2,1)S(1)}, bf16[4,208,1536]{2,1,0:T(8,128)(2,1)S(1)}, u32[]{:S(2)}, u32[]{:S(2)}) collective-permute-start(bf16[4,208,1536]{2,1,0:T(8,128)(2,1)S(1)} %get-tuple-element.307), channel_id=1, source_target_pairs={{0,16},{16,0},{1,17},{17,1},{2,18},{18,2},{3,19},{19,3},{4,20},{20... | collective-permute-start | bytes 7667720 | tf_op jit(solution)/shard_map/ppermute | solution.py:1020
  110.0 22.1 %collective-permute-start.9 = (bf16[288,1536]{1,0:T(8,128)(2,1)S(1)}, bf16[288,1536]{1,0:T(8,128)(2,1)S(1)}, u32[]{:S(2)}, u32[]{:S(2)}) collective-permute-start(bf16[288,1536]{1,0:T(8,128)(2,1)S(1)} %get-tuple-element.305), channel_id=1, source_target_pairs={{0,4},{4,0},{8,12},{12,8},{1,5},{5,1},{9,13},{13,9},{2,6},{6,2},{1... | collective-permute-start | bytes 2654216 | tf_op jit(solution)/shard_map/ppermute | solution.py:1020
  110.6 21.8 %collective-permute-start.10 = (bf16[288,1536]{1,0:T(8,128)(2,1)S(1)}, bf16[288,1536]{1,0:T(8,128)(2,1)S(1)}, u32[]{:S(2)}, u32[]{:S(2)}) collective-permute-start(bf16[288,1536]{1,0:T(8,128)(2,1)S(1)} %get-tuple-element.306), channel_id=1, source_target_pairs={{0,8},{4,12},{8,0},{12,4},{1,9},{5,13},{9,1},{13,5},{2,10},{6,14},... | collective-permute-start | bytes 2654216 | tf_op jit(solution)/shard_map/ppermute | solution.py:1020
  132.4 25.6 %collective-permute-start.15 = (bf16[4,192,1536]{2,1,0:T(8,128)(2,1)S(1)}, bf16[4,192,1536]{2,1,0:T(8,128)(2,1)S(1)}, u32[]{:S(2)}, u32[]{:S(2)}) collective-permute-start(bf16[4,192,1536]{2,1,0:T(8,128)(2,1)S(1)} %get-tuple-element.332), channel_id=1, source_target_pairs={{0,16},{16,0},{1,17},{17,1},{2,18},{18,2},{3,19},{19,3},{4,20},{20... | collective-permute-start | bytes 7077896 | tf_op jit(solution)/shard_map/ppermute | solution.py:1020
  133.8 24.2 %collective-permute-start.13 = (bf16[320,1536]{1,0:T(8,128)(2,1)S(1)}, bf16[320,1536]{1,0:T(8,128)(2,1)S(1)}, u32[]{:S(2)}, u32[]{:S(2)}) collective-permute-start(bf16[320,1536]{1,0:T(8,128)(2,1)S(1)} %get-tuple-element.330), channel_id=1, source_target_pairs={{0,4},{4,0},{8,12},{12,8},{1,5},{5,1},{9,13},{13,9},{2,6},{6,2},{1... | collective-permute-start | bytes 2949128 | tf_op jit(solution)/shard_map/ppermute | solution.py:1020
  135.3 21.8 %collective-permute-start.14 = (bf16[288,1536]{1,0:T(8,128)(2,1)S(1)}, bf16[288,1536]{1,0:T(8,128)(2,1)S(1)}, u32[]{:S(2)}, u32[]{:S(2)}) collective-permute-start(bf16[288,1536]{1,0:T(8,128)(2,1)S(1)} %get-tuple-element.331), channel_id=1, source_target_pairs={{0,8},{4,12},{8,0},{12,4},{1,9},{5,13},{9,1},{13,5},{2,10},{6,14},... | collective-permute-start | bytes 2654216 | tf_op jit(solution)/shard_map/ppermute | solution.py:1020
  135.8 15.2 %collective-permute-start.12 = (bf16[192,1536]{1,0:T(8,128)(2,1)S(1)}, bf16[192,1536]{1,0:T(8,128)(2,1)S(1)}, u32[]{:S(2)}, u32[]{:S(2)}) collective-permute-start(bf16[192,1536]{1,0:T(8,128)(2,1)S(1)} %get-tuple-element.329), channel_id=1, source_target_pairs={{0,1},{1,0},{2,3},{3,2},{4,5},{5,4},{6,7},{7,6},{8,9},{9,8},{10,11... | collective-permute-start | bytes 1769480 | tf_op jit(solution)/shard_map/ppermute | solution.py:1257
  158.0 24.3 %collective-permute-start.20 = (bf16[4,192,1536]{2,1,0:T(8,128)(2,1)S(1)}, bf16[4,192,1536]{2,1,0:T(8,128)(2,1)S(1)}, u32[]{:S(2)}, u32[]{:S(2)}) collective-permute-start(bf16[4,192,1536]{2,1,0:T(8,128)(2,1)S(1)} %get-tuple-element.360), channel_id=1, source_target_pairs={{0,16},{16,0},{1,17},{17,1},{2,18},{18,2},{3,19},{19,3},{4,20},{20... | collective-permute-start | bytes 7077896 | tf_op jit(solution)/shard_map/ppermute | solution.py:1020
  159.2 23.2 %collective-permute-start.19 = (bf16[304,1536]{1,0:T(8,128)(2,1)S(1)}, bf16[304,1536]{1,0:T(8,128)(2,1)S(1)}, u32[]{:S(2)}, u32[]{:S(2)}) collective-permute-start(bf16[304,1536]{1,0:T(8,128)(2,1)S(1)} %get-tuple-element.359), channel_id=1, source_target_pairs={{0,8},{4,12},{8,0},{12,4},{1,9},{5,13},{9,1},{13,5},{2,10},{6,14},... | collective-permute-start | bytes 2801672 | tf_op jit(solution)/shard_map/ppermute | solution.py:1020
  159.6 21.8 %collective-permute-start.18 = (bf16[288,1536]{1,0:T(8,128)(2,1)S(1)}, bf16[288,1536]{1,0:T(8,128)(2,1)S(1)}, u32[]{:S(2)}, u32[]{:S(2)}) collective-permute-start(bf16[288,1536]{1,0:T(8,128)(2,1)S(1)} %get-tuple-element.358), channel_id=1, source_target_pairs={{0,4},{4,0},{8,12},{12,8},{1,5},{5,1},{9,13},{13,9},{2,6},{6,2},{1... | collective-permute-start | bytes 2654216 | tf_op jit(solution)/shard_map/ppermute | solution.py:1020
  161.2 18.5 %collective-permute-start.16 = (bf16[192,1536]{1,0:T(8,128)(2,1)S(1)}, bf16[192,1536]{1,0:T(8,128)(2,1)S(1)}, u32[]{:S(2)}, u32[]{:S(2)}) collective-permute-start(bf16[192,1536]{1,0:T(8,128)(2,1)S(1)} %get-tuple-element.356), channel_id=1, source_target_pairs={{0,1},{1,0},{2,3},{3,2},{4,5},{5,4},{6,7},{7,6},{8,9},{9,8},{10,11... | collective-permute-start | bytes 1769480 | tf_op jit(solution)/shard_map/ppermute | solution.py:1257
  162.7 17.0 %collective-permute-start.17 = (bf16[192,1536]{1,0:T(8,128)(2,1)S(1)}, bf16[192,1536]{1,0:T(8,128)(2,1)S(1)}, u32[]{:S(2)}, u32[]{:S(2)}) collective-permute-start(bf16[192,1536]{1,0:T(8,128)(2,1)S(1)} %get-tuple-element.357.refs_0_), channel_id=1, source_target_pairs={{1,2},{2,1},{5,6},{6,5},{9,10},{10,9},{13,14},{14,13},{17,18},{18,... | collective-permute-start | bytes 1769480 | tf_op jit(solution)/shard_map/ppermute | solution.py:1257
  182.3 24.6 %collective-permute-start.27 = (bf16[4,208,1536]{2,1,0:T(8,128)(2,1)S(1)}, bf16[4,208,1536]{2,1,0:T(8,128)(2,1)S(1)}, u32[]{:S(2)}, u32[]{:S(2)}) collective-permute-start(bf16[4,208,1536]{2,1,0:T(8,128)(2,1)S(1)} %get-tuple-element.380), channel_id=1, source_target_pairs={{0,16},{16,0},{1,17},{17,1},{2,18},{18,2},{3,19},{19,3},{4,20},{20... | collective-permute-start | bytes 7667720 | tf_op jit(solution)/shard_map/ppermute | solution.py:1020
  183.6 22.1 %collective-permute-start.25 = (bf16[288,1536]{1,0:T(8,128)(2,1)S(1)}, bf16[288,1536]{1,0:T(8,128)(2,1)S(1)}, u32[]{:S(2)}, u32[]{:S(2)}) collective-permute-start(bf16[288,1536]{1,0:T(8,128)(2,1)S(1)} %get-tuple-element.378), channel_id=1, source_target_pairs={{0,4},{4,0},{8,12},{12,8},{1,5},{5,1},{9,13},{13,9},{2,6},{6,2},{1... | collective-permute-start | bytes 2654216 | tf_op jit(solution)/shard_map/ppermute | solution.py:1020
  185.1 21.8 %collective-permute-start.26 = (bf16[288,1536]{1,0:T(8,128)(2,1)S(1)}, bf16[288,1536]{1,0:T(8,128)(2,1)S(1)}, u32[]{:S(2)}, u32[]{:S(2)}) collective-permute-start(bf16[288,1536]{1,0:T(8,128)(2,1)S(1)} %get-tuple-element.379), channel_id=1, source_target_pairs={{0,8},{4,12},{8,0},{12,4},{1,9},{5,13},{9,1},{13,5},{2,10},{6,14},... | collective-permute-start | bytes 2654216 | tf_op jit(solution)/shard_map/ppermute | solution.py:1020
  185.9 16.3 %collective-permute-start.23 = (bf16[208,1536]{1,0:T(8,128)(2,1)S(1)}, bf16[208,1536]{1,0:T(8,128)(2,1)S(1)}, u32[]{:S(2)}, u32[]{:S(2)}) collective-permute-start(bf16[208,1536]{1,0:T(8,128)(2,1)S(1)} %get-tuple-element.376), channel_id=1, source_target_pairs={{0,1},{1,0},{2,3},{3,2},{4,5},{5,4},{6,7},{7,6},{8,9},{9,8},{10,11... | collective-permute-start | bytes 1916936 | tf_op jit(solution)/shard_map/ppermute | solution.py:1257
  187.7 0.7 collective-permute-start.24
  206.9 7.7 %copy-start.7 = (f32[512,768]{1,0:T(8,128)S(1)}, f32[512,768]{1,0:T(8,128)}, u32[]{:S(2)}) copy-start(f32[512,768]{1,0:T(8,128)} %get-tuple-element.361.refs_3_) | copy-start | bytes 4718596
  206.9 7.7 %copy-start.10 = (bf16[512,768]{1,0:T(8,128)(2,1)S(1)}, bf16[512,768]{1,0:T(8,128)(2,1)}, u32[]{:S(2)}) copy-start(bf16[512,768]{1,0:T(8,128)(2,1)} %get-tuple-element.288.refs_4_) | copy-start | bytes 2359300
  208.3 23.1 %collective-permute-start.30 = (bf16[320,1536]{1,0:T(8,128)(2,1)S(1)}, bf16[320,1536]{1,0:T(8,128)(2,1)S(1)}, u32[]{:S(2)}, u32[]{:S(2)}) collective-permute-start(bf16[320,1536]{1,0:T(8,128)(2,1)S(1)} %get-tuple-element.395), channel_id=1, source_target_pairs={{0,4},{4,0},{8,12},{12,8},{1,5},{5,1},{9,13},{13,9},{2,6},{6,2},{1... | collective-permute-start | bytes 2949128 | tf_op jit(solution)/shard_map/ppermute | solution.py:1020
  208.9 20.8 %collective-permute-start.31 = (bf16[288,1536]{1,0:T(8,128)(2,1)S(1)}, bf16[288,1536]{1,0:T(8,128)(2,1)S(1)}, u32[]{:S(2)}, u32[]{:S(2)}) collective-permute-start(bf16[288,1536]{1,0:T(8,128)(2,1)S(1)} %get-tuple-element.396), channel_id=1, source_target_pairs={{0,8},{4,12},{8,0},{12,4},{1,9},{5,13},{9,1},{13,5},{2,10},{6,14},... | collective-permute-start | bytes 2654216 | tf_op jit(solution)/shard_map/ppermute | solution.py:1020
  209.6 17.2 %collective-permute-start.29 = (bf16[208,1536]{1,0:T(8,128)(2,1)S(1)}, bf16[208,1536]{1,0:T(8,128)(2,1)S(1)}, u32[]{:S(2)}, u32[]{:S(2)}) collective-permute-start(bf16[208,1536]{1,0:T(8,128)(2,1)S(1)} %get-tuple-element.394.refs_2_), channel_id=1, source_target_pairs={{1,2},{2,1},{5,6},{6,5},{9,10},{10,9},{13,14},{14,13},{17,18},{18,... | collective-permute-start | bytes 1916936 | tf_op jit(solution)/shard_map/ppermute | solution.py:1257
  210.3 16.5 %collective-permute-start.28 = (bf16[192,1536]{1,0:T(8,128)(2,1)S(1)}, bf16[192,1536]{1,0:T(8,128)(2,1)S(1)}, u32[]{:S(2)}, u32[]{:S(2)}) collective-permute-start(bf16[192,1536]{1,0:T(8,128)(2,1)S(1)} %get-tuple-element.393), channel_id=1, source_target_pairs={{0,1},{1,0},{2,3},{3,2},{4,5},{5,4},{6,7},{7,6},{8,9},{9,8},{10,11... | collective-permute-start | bytes 1769480 | tf_op jit(solution)/shard_map/ppermute | solution.py:1257
  214.8 37.7 %collective-permute-start.21 = (f32[512,768]{1,0:T(8,128)S(1)}, f32[512,768]{1,0:T(8,128)S(1)}, u32[]{:S(2)}, u32[]{:S(2)}) collective-permute-start(f32[512,768]{1,0:T(8,128)S(1)} %convert_select_fusion), channel_id=1, source_target_pairs={{0,16},{16,0},{1,17},{17,1},{2,18},{18,2},{3,19},{19,3},{4,20},{20... | collective-permute-start | bytes 4718600 | tf_op jit(solution)/shard_map/ppermute | solution.py:1020
  231.4 6.2 %copy-start.8 = (bf16[512,768]{1,0:T(8,128)(2,1)S(1)}, bf16[512,768]{1,0:T(8,128)(2,1)}, u32[]{:S(2)}) copy-start(bf16[512,768]{1,0:T(8,128)(2,1)} %get-tuple-element.272.refs_3_.refs_0_) | copy-start | bytes 2359300
  231.4 6.2 %copy-start.9 = (bf16[512,768]{1,0:T(8,128)(2,1)S(1)}, bf16[512,768]{1,0:T(8,128)(2,1)}, u32[]{:S(2)}) copy-start(bf16[512,768]{1,0:T(8,128)(2,1)} %get-tuple-element.362.refs_1_) | copy-start | bytes 2359300
  232.5 14.8 %collective-permute-start.32 = (bf16[208,1536]{1,0:T(8,128)(2,1)S(1)}, bf16[208,1536]{1,0:T(8,128)(2,1)S(1)}, u32[]{:S(2)}, u32[]{:S(2)}) collective-permute-start(bf16[208,1536]{1,0:T(8,128)(2,1)S(1)} %get-tuple-element.407), channel_id=1, source_target_pairs={{0,1},{1,0},{2,3},{3,2},{4,5},{5,4},{6,7},{7,6},{8,9},{9,8},{10,11... | collective-permute-start | bytes 1916936 | tf_op jit(solution)/shard_map/ppermute | solution.py:1257
  234.0 9.9 %collective-permute-start.33 = (bf16[192,1536]{1,0:T(8,128)(2,1)S(1)}, bf16[192,1536]{1,0:T(8,128)(2,1)S(1)}, u32[]{:S(2)}, u32[]{:S(2)}) collective-permute-start(bf16[192,1536]{1,0:T(8,128)(2,1)S(1)} %get-tuple-element.408.refs_2_), channel_id=1, source_target_pairs={{1,2},{2,1},{5,6},{6,5},{9,10},{10,9},{13,14},{14,13},{17,18},{18,... | collective-permute-start | bytes 1769480 | tf_op jit(solution)/shard_map/ppermute | solution.py:1257
  235.0 7.2 %collective-permute-start.34 = (bf16[96,1536]{1,0:T(8,128)(2,1)S(1)}, bf16[96,1536]{1,0:T(8,128)(2,1)S(1)}, u32[]{:S(2)}, u32[]{:S(2)}) collective-permute-start(bf16[96,1536]{1,0:T(8,128)(2,1)S(1)} %get-tuple-element.409), channel_id=1, source_target_pairs={{0,4},{4,0},{8,12},{12,8},{1,5},{5,1},{9,13},{13,9},{2,6},{6,2},{1... | collective-permute-start | bytes 884744 | tf_op jit(solution)/shard_map/ppermute | solution.py:1020
  236.0 7.9 %collective-permute-start.35 = (bf16[112,1536]{1,0:T(8,128)(2,1)S(1)}, bf16[112,1536]{1,0:T(8,128)(2,1)S(1)}, u32[]{:S(2)}, u32[]{:S(2)}) collective-permute-start(bf16[112,1536]{1,0:T(8,128)(2,1)S(1)} %get-tuple-element.410), channel_id=1, source_target_pairs={{0,8},{4,12},{8,0},{12,4},{1,9},{5,13},{9,1},{13,5},{2,10},{6,14},... | collective-permute-start | bytes 1032200 | tf_op jit(solution)/shard_map/ppermute | solution.py:1020
  242.2 10.3 %collective-permute-start.22 = (bf16[512,768]{1,0:T(8,128)(2,1)S(1)}, bf16[512,768]{1,0:T(8,128)(2,1)S(1)}, u32[]{:S(2)}, u32[]{:S(2)}) collective-permute-start(bf16[512,768]{1,0:T(8,128)(2,1)S(1)} %broadcast_select_fusion), channel_id=1, source_target_pairs={{0,16},{16,0},{1,17},{17,1},{2,18},{18,2},{3,19},{19,3},{4,20},{20... | collective-permute-start | bytes 2359304 | tf_op jit(solution)/shard_map/ppermute | solution.py:1020
  248.2 15.7 %collective-permute-start.36 = (bf16[208,1536]{1,0:T(8,128)(2,1)S(1)}, bf16[208,1536]{1,0:T(8,128)(2,1)S(1)}, u32[]{:S(2)}, u32[]{:S(2)}) collective-permute-start(bf16[208,1536]{1,0:T(8,128)(2,1)S(1)} %get-tuple-element.418), channel_id=1, source_target_pairs={{0,1},{1,0},{2,3},{3,2},{4,5},{5,4},{6,7},{7,6},{8,9},{9,8},{10,11... | collective-permute-start | bytes 1916936 | tf_op jit(solution)/shard_map/ppermute | solution.py:1257
  251.8 0.7 collective-permute-start.37
  252.5 18.4 %copy-start.13 = (bf16[512,768]{1,0:T(8,128)(2,1)}, bf16[512,768]{1,0:T(8,128)(2,1)S(1)}, u32[]{:S(2)}) copy-start(bf16[512,768]{1,0:T(8,128)(2,1)S(1)} %collective-permute-done.22.refs_2_) | copy-start | bytes 2359300
  252.5 18.3 %copy-start.12 = (f32[512,768]{1,0:T(8,128)}, f32[512,768]{1,0:T(8,128)S(1)}, u32[]{:S(2)}) copy-start(f32[512,768]{1,0:T(8,128)S(1)} %collective-permute-done.21.refs_5_) | copy-start | bytes 4718596
  264.8 16.3 %collective-permute-start.39 = (bf16[208,1536]{1,0:T(8,128)(2,1)S(1)}, bf16[208,1536]{1,0:T(8,128)(2,1)S(1)}, u32[]{:S(2)}, u32[]{:S(2)}) collective-permute-start(bf16[208,1536]{1,0:T(8,128)(2,1)S(1)} %get-tuple-element.430.refs_3_), channel_id=1, source_target_pairs={{1,2},{2,1},{5,6},{6,5},{9,10},{10,9},{13,14},{14,13},{17,18},{18,... | collective-permute-start | bytes 1916936 | tf_op jit(solution)/shard_map/ppermute | solution.py:1257
  265.5 15.6 %collective-permute-start.38 = (bf16[192,1536]{1,0:T(8,128)(2,1)S(1)}, bf16[192,1536]{1,0:T(8,128)(2,1)S(1)}, u32[]{:S(2)}, u32[]{:S(2)}) collective-permute-start(bf16[192,1536]{1,0:T(8,128)(2,1)S(1)} %get-tuple-element.429), channel_id=1, source_target_pairs={{0,1},{1,0},{2,3},{3,2},{4,5},{5,4},{6,7},{7,6},{8,9},{9,8},{10,11... | collective-permute-start | bytes 1769480 | tf_op jit(solution)/shard_map/ppermute | solution.py:1257
  281.9 12.3 %collective-permute-start.42 = (bf16[208,1536]{1,0:T(8,128)(2,1)S(1)}, bf16[208,1536]{1,0:T(8,128)(2,1)S(1)}, u32[]{:S(2)}, u32[]{:S(2)}) collective-permute-start(bf16[208,1536]{1,0:T(8,128)(2,1)S(1)} %get-tuple-element.442), channel_id=1, source_target_pairs={{0,1},{1,0},{2,3},{3,2},{4,5},{5,4},{6,7},{7,6},{8,9},{9,8},{10,11... | collective-permute-start | bytes 1916936 | tf_op jit(solution)/shard_map/ppermute | solution.py:1257
  294.2 9.1 %copy-start.1 = (bf16[8,128,768]{2,1,0:T(8,128)(2,1)S(1)}, bf16[8,128,768]{2,1,0:T(8,128)(2,1)}, u32[]{:S(2)}) copy-start(bf16[8,128,768]{2,1,0:T(8,128)(2,1)} %param.14) | copy-start | bytes 4718596
  294.9 3.8 %collective-permute-start.43 = (bf16[208,1536]{1,0:T(8,128)(2,1)S(1)}, bf16[208,1536]{1,0:T(8,128)(2,1)S(1)}, u32[]{:S(2)}, u32[]{:S(2)}) collective-permute-start(bf16[208,1536]{1,0:T(8,128)(2,1)S(1)} %get-tuple-element.445), channel_id=1, source_target_pairs={{0,16},{16,0},{1,17},{17,1},{2,18},{18,2},{3,19},{19,3},{4,20},{20... | collective-permute-start | bytes 1916936 | tf_op jit(solution)/shard_map/ppermute | solution.py:1020
  295.0 2.9 collective-permute-start.40
  295.5 3.3 %collective-permute-start.41 = (bf16[192,1536]{1,0:T(8,128)(2,1)S(1)}, bf16[192,1536]{1,0:T(8,128)(2,1)S(1)}, u32[]{:S(2)}, u32[]{:S(2)}) collective-permute-start(bf16[192,1536]{1,0:T(8,128)(2,1)S(1)} %get-tuple-element.440), channel_id=1, source_target_pairs={{0,16},{16,0},{1,17},{17,1},{2,18},{18,2},{3,19},{19,3},{4,20},{20... | collective-permute-start | bytes 1769480 | tf_op jit(solution)/shard_map/ppermute | solution.py:1020

commit v9 on v8

--- a/solution.py
+++ b/solution.py
@@ -1061,16 +1061,18 @@
             first = n_in + len(shapes)
             sends = dict(zip(ways, refs[n_in + n_out : first]))
             ins, move = list(refs[:n_in]), Mover(refs[-1])
-            waits = []
-            for index, buffer in zip(far, refs[first:-1]):
-                move.load(ins[index], buffer)
-                waits.append(move.last)
-                ins[index] = buffer
+            waits = {}
+            for shard in range(self.ins[far[0]].shape[0] if far else 0):
+                for index, buffer in zip(far, refs[first:-1]):
+                    move.load(refs[index].at[shard], buffer.at[shard])
+                    waits.setdefault(shard, []).append(move.last)
+                    ins[index] = buffer
             for code in self.code:
                 code(ids_ref, ins, refs[n_in : n_in + n_out], sends)
-            ready(waits)
-            for code in self.later:
-                code(ids_ref, ins, refs[n_in : n_in + n_out], sends)
+            for shard, items in waits.items():
+                ready(items)
+                for code in self.later:
+                    code(ids_ref, ins, refs[n_in : n_in + n_out], sends, shard)
 
         vmem = pl.BlockSpec(memory_space=pltpu.VMEM)
         results = pl.pallas_call(
@@ -1105,6 +1107,27 @@
     chunk.first = {"x": sums.region("x", 2 * cut), "y": sums.region("y", 2 * rest)}
     to_x, to_y = chunk.first["x"], chunk.first["y"]
 
+    def code_shard(ids, ins, outs, sends, shard):
+        upper = ins[kept][shard, :cut] + ins[got][shard, :cut]
+        lower = ins[kept][shard, cut:] + ins[got][shard, cut:]
+        row, column = shard // 2, shard % 2
+
+        @pl.when(ids[1] == column)
+        def _():
+            outs[top][row] = upper
+
+        @pl.when(ids[1] != column)
+        def _():
+            sends["x"][to_x + row * cut : to_x + row * cut + cut] = upper
+
+        @pl.when(ids[2] == row)
+        def _():
+            outs[bottom][column] = lower
+
+        @pl.when(ids[2] != row)
+        def _():
+            sends["y"][to_y + column * rest : to_y + column * rest + rest] = lower
+
     def code(ids, ins, outs, sends):
         low, high = ids[1], ids[2]
         for i in range(2):
@@ -1114,7 +1137,10 @@
             sends["y"][to_y + i * rest : to_y + i * rest + rest] = add(2 * (1 - high) + i, slice(cut, rows))
             outs[bottom][i] = add(2 * high + i, slice(cut, rows))
 
-    (sums.later if chunk.far else sums.code).append(code)
+    if chunk.far:
+        sums.later.append(code_shard)
+    else:
+        sums.code.append(code)
     return [top, bottom]
 
 

time: 308 us -> 308 us (level)
  no operation moved by 1% of the time
where the time goes in v9:
time: 308 us; the launch traced here: 303 us
  Pallas kernels  146 us (47%)
  waiting for transfers between devices  99.8 us (32%)
  starting transfers between devices  44.2 us (14%)
  local copies, waits for them, and re-layouts  6.54 us (2%)
  other arithmetic  4.57 us (1%)
    pallas_call x11, Pallas kernels, call(): pl.pallas_call(body, in_specs=[pl.BlockSpec(memory_space=pltpu.SMEM)] + [...  132 us
    ppermute x14, waiting for transfers between devices, move(): lax.ppermute(array, 'outer', [(0, 1), (1, 0), (2, 3), (3, 2)] if way == '...  55.8 us
    ppermute x30, waiting for transfers between devices, exchange(): return lax.ppermute(array, axis, [(i, i ^ bit) for i in range(length)])  44 us
    ppermute x14, starting transfers between devices, move(): lax.ppermute(array, 'outer', [(0, 1), (1, 0), (2, 3), (3, 2)] if way == '...  26 us
    ppermute x30, starting transfers between devices, exchange(): return lax.ppermute(array, axis, [(i, i ^ bit) for i in range(length)])  18.2 us
    pallas_call x11, Pallas kernels, run(): pl.pallas_call(kernel, in_specs=[pl.BlockSpec(memory_space=pltpu.SMEM)] +...  14.3 us
  transfers between devices with their start and end apart: 44, of which 21 were waited for; matrix products, arithmetic and copies ran while one was open for 3% of the time, Pallas kernels for 34%

profile of v9, /device:TPU:0, one launch (start us, length us, event | category | flops | bytes accessed | tf_op | source)
XLA Modules:
  0.0 302.8 jit_solution(15081437168885322628)
XLA Ops:
  1.7 1.4 reduce.3
  3.1 0.8 concatenate.6
  5.5 0.9 constant_dynamic-slice_fusion
  6.5 0.8 copy.27
  8.5 8.4 %attend_forward.1 = (bf16[512,768]{1,0:T(8,128)(2,1)}, bf16[512,768]{1,0:T(8,128)(2,1)}, bf16[512,768]{1,0:T(8,128)(2,1)}, f32[4,6,256,128]{3,2,1,0:T(8,128)}, b...) custom-call(s32[1]{0:T(128)} %bitcast.ids_ref, bf16[512,768]{1,0:T(8,128)(2,1)} %bitcast.36, ...), custom_call_target="tpu_custom_call" | custom-call | flops 2415919104 | bytes 12582912 | tf_op jit(solution)/shard_map/attend_forward/pallas_call | solution.py:161
  16.9 0.9 collective-permute-done.2.refs_3_.refs_6_.refs_9_
  18.3 1.4 dynamic-slice_select_fusion
  19.7 12.5 %up_forward.1 = (f32[512,768]{1,0:T(8,128)S(1)}, f32[512,768]{1,0:T(8,128)}, f32[512,128]{1,0:T(8,128)}, bf16[768,512]{1,0:T(8,128)(2,1)}, bf16[4,512,768]{2,1,0...) custom-call(s32[1]{0:T(128)} %bitcast.ids_ref, bf16[512,768]{1,0:T(8,128)(2,1)} %bitcast.37, ...), custom_call_target="tpu_custom_call" | custom-call | flops 3019898880 | bytes 20971520 | tf_op jit(solution)/shard_map/up_forward/pallas_call | solution.py:161
  32.3 9.0 %down_forward.1 = (bf16[512,768]{1,0:T(8,128)(2,1)S(1)}, bf16[512,768]{1,0:T(8,128)(2,1)}, f32[512,768]{1,0:T(8,128)}, f32[512,128]{1,0:T(8,128)}) custom-call(s32[1]{0:T(128)} %bitcast.ids_ref, bf16[4,512,768]{2,1,0:T(8,128)(2,1)S(1)} %get-tuple-element.249.refs_0_, bf16[3072,768]{1,0:T(8,128)(2,1)} %bitcast.24, ...), custom_call_target="tpu_custom_call" | custom-call | flops 2415919104 | bytes 12582912 | tf_op jit(solution)/shard_map/down_forward/pallas_call | solution.py:161
  41.3 25.4 %second_layer.1 = (bf16[512,768]{1,0:T(8,128)(2,1)}, bf16[512,768]{1,0:T(8,128)(2,1)}, bf16[512,768]{1,0:T(8,128)(2,1)}, f32[4,6,256,128]{3,2,1,0:T(8,128)}, bf1...) custom-call(s32[1]{0:T(128)} %bitcast.ids_ref, ...), custom_call_target="tpu_custom_call" | custom-call | flops 10267656192 | bytes 52428800 | tf_op jit(solution)/shard_map/second_layer/pallas_call | solution.py:161
  66.8 13.8 %up_grad.2 = (f32[512,768]{1,0:T(8,128)S(1)}, bf16[512,768]{1,0:T(8,128)(2,1)S(1)}, f32[8,768]{1,0:T(8,128)S(1)}, bf16[4,192,1536]{2,1,0:T(8,128)(2,1)}, bf16[4,192,1536]{2,1,0:T(8,128)(2,1)S(1)}) custom-call(s32[1]{0:T(128)} %bitcast.ids_ref, bf16[512,768]{1,0:T(8,128)(2,1)S(1)} %get-tuple-element.254.refs_0_, f32[512,768]{1,0:T(8,128)S(1)} %get-tuple-element.255.refs_1_, ...), custom_call_target="tpu_custom_call" | custom-call | flops 7247757312 | bytes 31457280 | tf_op jit(solution)/shard_map/up_grad/pallas_call | solution.py:161
  80.6 1.2 copy-done.5
  81.8 1.4 copy-done.11
  83.8 3.0 join_sums.11
  86.8 3.0 collective-permute-start.6
  89.8 1.5 collective-permute-start.7
  91.3 16.1 %attend_grad.2 = (f32[512,768]{1,0:T(8,128)}, bf16[512,768]{1,0:T(8,128)(2,1)S(1)}, bf16[512,768]{1,0:T(8,128)(2,1)}, bf16[4,208,1536]{2,1,0:T(8,128)(2,1)S(1)}, bf16[4,208,1536]{2,1,0:T(8,128)(2,1)S(1)}) custom-call(s32[1]{0:T(128)} %bitcast.ids_ref, bf16[512,768]{1,0:T(8,128)(2,1)S(1)} %get-tuple-element.268.refs_0_, ...), custom_call_target="tpu_custom_call" | custom-call | flops 6039797760 | bytes 31457280 | tf_op jit(solution)/shard_map/attend_grad/pallas_call | solution.py:161
  107.5 2.1 join_sums.12
  110.3 7.2 %down_grad.1 = (f32[512,768]{1,0:T(8,128)S(1)}, bf16[512,768]{1,0:T(8,128)(2,1)S(1)}, f32[8,768]{1,0:T(8,128)S(1)}, bf16[4,192,1536]{2,1,0:T(8,128)(2,1)S(1)}, bf16[4,192,1536]{2,1,0:T(8,128)(2,1)S(1)}) custom-call(s32[1]{0:T(128)} %bitcast.ids_ref, bf16[512,768]{1,0:T(8,128)(2,1)S(1)} %get-tuple-element.289.refs_0_, f32[512,768]{1,0:T(8,128)} %get-tuple-element.290.refs_1_, ...), custom_call_target="tpu_custom_call" | custom-call | flops 2415919104 | bytes 14680064 | tf_op jit(solution)/shard_map/down_grad/pallas_call | solution.py:161
  117.5 14.2 %collective-permute-done.9.refs_2_ = bf16[288,1536]{1,0:T(8,128)(2,1)S(1)} collective-permute-done((bf16[288,1536]{1,0:T(8,128)(2,1)S(1)}, bf16[288,1536]{1,0:T(8,128)(2,1)S(1)}, u32[]{:S(2)}, u32[]{:S(2)}) %collective-permute-start.9) | collective-permute-done | bytes 884768 | tf_op jit(solution)/shard_map/ppermute | solution.py:1020
  132.0 1.2 join_sums.13
  133.2 1.5 collective-permute-start.13
  135.2 1.5 collective-permute-start.12
  136.8 13.6 %up_grad.3 = (f32[512,768]{1,0:T(8,128)S(1)}, bf16[512,768]{1,0:T(8,128)(2,1)S(1)}, f32[8,768]{1,0:T(8,128)S(1)}, bf16[4,192,1536]{2,1,0:T(8,128)(2,1)S(1)}, bf16[4,192,1536]{2,1,0:T(8,128)(2,1)S(1)}) custom-call(s32[1]{0:T(128)} %bitcast.ids_ref, bf16[512,768]{1,0:T(8,128)(2,1)S(1)} %get-tuple-element.308.refs_0_, ...), custom_call_target="tpu_custom_call" | custom-call | flops 7247757312 | bytes 31457280 | tf_op jit(solution)/shard_map/up_grad/pallas_call | solution.py:161
  150.4 6.1 %collective-permute-done.14.refs_5_ = bf16[288,1536]{1,0:T(8,128)(2,1)S(1)} collective-permute-done((bf16[288,1536]{1,0:T(8,128)(2,1)S(1)}, bf16[288,1536]{1,0:T(8,128)(2,1)S(1)}, u32[]{:S(2)}, u32[]{:S(2)}) %collective-permute-start.14) | collective-permute-done | bytes 884768 | tf_op jit(solution)/shard_map/ppermute | solution.py:1020
  156.5 0.9 collective-permute-done.13.refs_4_
  157.4 1.2 join_sums.14
  158.9 1.7 collective-permute-start.18
  160.6 1.5 collective-permute-start.16
  162.1 0.9 collective-permute-start.17
  163.0 16.1 %attend_grad.3 = (f32[512,768]{1,0:T(8,128)}, bf16[512,768]{1,0:T(8,128)(2,1)}, bf16[4,208,1536]{2,1,0:T(8,128)(2,1)S(1)}, bf16[4,208,1536]{2,1,0:T(8,128)(2,1)S(1)}) custom-call(s32[1]{0:T(128)} %bitcast.ids_ref, bf16[512,768]{1,0:T(8,128)(2,1)S(1)} %get-tuple-element.333.refs_0_, bf16[768,512]{1,0:T(8,128)(2,1)} %get-tuple-element.336.refs_1_, ...), custom_call_target="tpu_custom_call" | custom-call | flops 6039797760 | bytes 31457280 | tf_op jit(solution)/shard_map/attend_grad/pallas_call | solution.py:161
  179.1 1.7 collective-permute-done.18.refs_6_
  180.8 1.0 collective-permute-done.19.refs_7_
  181.7 1.2 join_sums.15
  183.0 1.5 collective-permute-start.25
  185.2 1.7 collective-permute-start.23
  187.7 13.8 %collective-permute-done.23.refs_1_ = bf16[208,1536]{1,0:T(8,128)(2,1)S(1)} collective-permute-done((bf16[208,1536]{1,0:T(8,128)(2,1)S(1)}, bf16[208,1536]{1,0:T(8,128)(2,1)S(1)}, u32[]{:S(2)}, u32[]{:S(2)}) %collective-permute-start.23) | collective-permute-done | bytes 639008 | tf_op jit(solution)/shard_map/ppermute | solution.py:1283
  201.5 3.6 %collective-permute-done.25.refs_7_ = bf16[288,1536]{1,0:T(8,128)(2,1)S(1)} collective-permute-done((bf16[288,1536]{1,0:T(8,128)(2,1)S(1)}, bf16[288,1536]{1,0:T(8,128)(2,1)S(1)}, u32[]{:S(2)}, u32[]{:S(2)}) %collective-permute-start.25) | collective-permute-done | bytes 884768 | tf_op jit(solution)/shard_map/ppermute | solution.py:1020
  205.1 1.2 collective-permute-done.26.refs_8_
  206.3 1.4 join_sums.16
  209.7 4.3 %collective-permute-start.28 = (bf16[192,1536]{1,0:T(8,128)(2,1)S(1)}, bf16[192,1536]{1,0:T(8,128)(2,1)S(1)}, u32[]{:S(2)}, u32[]{:S(2)}) collective-permute-start(bf16[192,1536]{1,0:T(8,128)(2,1)S(1)} %get-tuple-element.393), channel_id=1, source_target_pairs={{0,1},{1,0},{2,3},{3,2},{4,5},{5,4},{6,7},{7,6},{8,9},{9,8},{10,11... | collective-permute-start | bytes 1769480 | tf_op jit(solution)/shard_map/ppermute | solution.py:1283
  214.3 11.8 %collective-permute-done.28.refs_1_ = bf16[192,1536]{1,0:T(8,128)(2,1)S(1)} collective-permute-done((bf16[192,1536]{1,0:T(8,128)(2,1)S(1)}, bf16[192,1536]{1,0:T(8,128)(2,1)S(1)}, u32[]{:S(2)}, u32[]{:S(2)}) %collective-permute-start.28) | collective-permute-done | bytes 589856 | tf_op jit(solution)/shard_map/ppermute | solution.py:1283
  226.1 2.9 collective-permute-done.31.refs_8_
  229.0 1.8 collective-permute-done.30.refs_7_
  230.8 1.0 join_sums.17
  231.8 1.6 collective-permute-start.32
  233.4 0.9 collective-permute-start.33
  234.3 0.9 collective-permute-start.34
  235.2 1.5 collective-permute-start.35
  236.9 4.6 %collective-permute-done.34.refs_7_ = bf16[96,1536]{1,0:T(8,128)(2,1)S(1)} collective-permute-done((bf16[96,1536]{1,0:T(8,128)(2,1)S(1)}, bf16[96,1536]{1,0:T(8,128)(2,1)S(1)}, u32[]{:S(2)}, u32[]{:S(2)}) %collective-permute-start.34) | collective-permute-done | bytes 294944 | tf_op jit(solution)/shard_map/ppermute | solution.py:1020
  241.5 1.6 collective-permute-done.35.refs_8_
  243.1 3.6 %collective-permute-done.32.refs_1_ = bf16[208,1536]{1,0:T(8,128)(2,1)S(1)} collective-permute-done((bf16[208,1536]{1,0:T(8,128)(2,1)S(1)}, bf16[208,1536]{1,0:T(8,128)(2,1)S(1)}, u32[]{:S(2)}, u32[]{:S(2)}) %collective-permute-start.32) | collective-permute-done | bytes 639008 | tf_op jit(solution)/shard_map/ppermute | solution.py:1283
  246.7 0.9 join_sums.18
  247.6 3.6 %collective-permute-start.36 = (bf16[208,1536]{1,0:T(8,128)(2,1)S(1)}, bf16[208,1536]{1,0:T(8,128)(2,1)S(1)}, u32[]{:S(2)}, u32[]{:S(2)}) collective-permute-start(bf16[208,1536]{1,0:T(8,128)(2,1)S(1)} %get-tuple-element.418), channel_id=1, source_target_pairs={{0,1},{1,0},{2,3},{3,2},{4,5},{5,4},{6,7},{7,6},{8,9},{9,8},{10,11... | collective-permute-start | bytes 1916936 | tf_op jit(solution)/shard_map/ppermute | solution.py:1283
  252.0 11.4 %collective-permute-done.36.refs_1_ = bf16[208,1536]{1,0:T(8,128)(2,1)S(1)} collective-permute-done((bf16[208,1536]{1,0:T(8,128)(2,1)S(1)}, bf16[208,1536]{1,0:T(8,128)(2,1)S(1)}, u32[]{:S(2)}, u32[]{:S(2)}) %collective-permute-start.36) | collective-permute-done | bytes 639008 | tf_op jit(solution)/shard_map/ppermute | solution.py:1283
  263.3 0.9 join_sums.19
  264.9 5.4 %collective-permute-start.38 = (bf16[192,1536]{1,0:T(8,128)(2,1)S(1)}, bf16[192,1536]{1,0:T(8,128)(2,1)S(1)}, u32[]{:S(2)}, u32[]{:S(2)}) collective-permute-start(bf16[192,1536]{1,0:T(8,128)(2,1)S(1)} %get-tuple-element.429), channel_id=1, source_target_pairs={{0,1},{1,0},{2,3},{3,2},{4,5},{5,4},{6,7},{7,6},{8,9},{9,8},{10,11... | collective-permute-start | bytes 1769480 | tf_op jit(solution)/shard_map/ppermute | solution.py:1283
  270.3 5.4 %assemble.1 = (bf16[2,512,768]{2,1,0:T(8,128)(2,1)}, f32[2,512,768]{2,1,0:T(8,128)}) custom-call(s32[1]{0:T(128)} %bitcast.ids_ref, bf16[512,768]{1,0:T(8,128)(2,1)} %get-tuple-element.272.refs_3_.refs_0_, bf16[512,768]{1,0:T(8,128)(2,1)} %get-tuple-element.362.refs_1_, bf16[512,768]{1,0:T(8,128)(2,1)} %copy-done.13, f32[512,768]{1,0:T(8,128)} %get-tuple-element.361.refs_3_, ...), custom_call_target="tpu_custom_call" | custom-call | flops 1000 | bytes 10485760 | tf_op jit(solution)/shard_map/assemble/pallas_call | solution.py:161
  275.6 4.8 %collective-permute-done.38.refs_1_ = bf16[192,1536]{1,0:T(8,128)(2,1)S(1)} collective-permute-done((bf16[192,1536]{1,0:T(8,128)(2,1)S(1)}, bf16[192,1536]{1,0:T(8,128)(2,1)S(1)}, u32[]{:S(2)}, u32[]{:S(2)}) %collective-permute-start.38) | collective-permute-done | bytes 589856 | tf_op jit(solution)/shard_map/ppermute | solution.py:1283
  281.3 1.8 collective-permute-start.42
  283.1 10.4 %collective-permute-done.42.refs_1_ = bf16[208,1536]{1,0:T(8,128)(2,1)S(1)} collective-permute-done((bf16[208,1536]{1,0:T(8,128)(2,1)S(1)}, bf16[208,1536]{1,0:T(8,128)(2,1)S(1)}, u32[]{:S(2)}, u32[]{:S(2)}) %collective-permute-start.42) | collective-permute-done | bytes 639008 | tf_op jit(solution)/shard_map/ppermute | solution.py:1283
  294.9 2.3 collective-permute-done.40.refs_1_
  297.2 0.8 collective-permute-done.41.refs_3_
  298.1 4.5 %last.1 = (f32[768,768]{1,0:T(8,128)}, f32[192,2304]{1,0:T(8,128)}, f32[192,768]{1,0:T(8,128)}, f32[2,192]{1,0:T(2,128)}, f32[1,192]{1,0:T(1,128)}, /*index=5*/f...) custom-call(s32[5]{0:T(128)S(1)} %stack.24.ids_ref, ...), custom_call_target="tpu_custom_call" | custom-call | flops 1000 | bytes 5242880 | tf_op jit(solution)/shard_map/last/pallas_call | solution.py:161
  (98 shorter events, 14.2 us)
Async XLA Ops:
  0.6 4.9 %copy-start = (bf16[8,128,768]{2,1,0:T(8,128)(2,1)S(1)}, bf16[8,128,768]{2,1,0:T(8,128)(2,1)}, u32[]{:S(2)}) copy-start(bf16[8,128,768]{2,1,0:T(8,128)(2,1)} %param.14) | copy-start | bytes 4718596
  0.7 7.3 %collective-permute-start = (bf16[768,2304]{1,0:T(8,128)(2,1)}, bf16[768,2304]{1,0:T(8,128)(2,1)}, u32[]{:S(2)}, u32[]{:S(2)}) collective-permute-start(bf16[768,2304]{1,0:T(8,128)(2,1)} %bitcast.50), channel_id=1, source_target_pairs={{0,16},{16,0},{1,17},{17,1},{2,18},{18,2},{3,19},{19,3},{4,20},{20... | collective-permute-start | bytes 10616840 | tf_op jit(solution)/shard_map/ppermute | solution.py:1020
  3.9 3.4 %collective-permute-start.1 = (f32[16,768]{1,0:T(8,128)S(1)}, f32[16,768]{1,0:T(8,128)S(1)}, u32[]{:S(2)}, u32[]{:S(2)}) collective-permute-start(f32[16,768]{1,0:T(8,128)S(1)} %concatenate.6), channel_id=1, source_target_pairs={{0,16},{16,0},{1,17},{17,1},{2,18},{18,2},{3,19},{19,3},{4,20},{20... | collective-permute-start | bytes 147464 | tf_op jit(solution)/shard_map/ppermute | solution.py:1020
  7.3 10.5 %slice-start = ((s8[4718592]{0:T(1024)(128)(4,1)}), s8[4194304]{0:T(1024)(128)(4,1)S(1)}, s32[]{:S(2)}) async-start(s8[4718592]{0:T(1024)(128)(4,1)} %bitcast.28), calls=%async_computation | async-start | bytes 8388608
  7.9 9.9 %collective-permute-start.3 = (bf16[768,3072]{1,0:T(8,128)(2,1)}, bf16[768,3072]{1,0:T(8,128)(2,1)S(1)}, u32[]{:S(2)}, u32[]{:S(2)}) collective-permute-start(bf16[768,3072]{1,0:T(8,128)(2,1)} %bitcast.31), channel_id=1, source_target_pairs={{0,16},{16,0},{1,17},{17,1},{2,18},{18,2},{3,19},{19,3},{4,20},{20... | collective-permute-start | bytes 14155784 | tf_op jit(solution)/shard_map/ppermute | solution.py:1020
  8.4 9.4 %collective-permute-start.2 = (bf16[768,768]{1,0:T(8,128)(2,1)}, bf16[768,768]{1,0:T(8,128)(2,1)S(1)}, u32[]{:S(2)}, u32[]{:S(2)}) collective-permute-start(bf16[768,768]{1,0:T(8,128)(2,1)} %bitcast.39), channel_id=1, source_target_pairs={{0,16},{16,0},{1,17},{17,1},{2,18},{18,2},{3,19},{19,3},{4,20},{20... | collective-permute-start | bytes 3538952 | tf_op jit(solution)/shard_map/ppermute | solution.py:1020
  8.5 9.4 %slice-start.1 = ((s8[4718592]{0:T(1024)(128)(4,1)}), s8[524288]{0:T(1024)(128)(4,1)S(1)}, s32[]{:S(2)}) async-start(s8[4718592]{0:T(1024)(128)(4,1)} %bitcast.28), calls=%async_computation.1 | async-start | bytes 1048576
  8.5 9.8 %copy-start.14 = (bf16[8,128,768]{2,1,0:T(8,128)(2,1)S(1)}, bf16[8,128,768]{2,1,0:T(8,128)(2,1)}, u32[]{:S(2)}) copy-start(bf16[8,128,768]{2,1,0:T(8,128)(2,1)} %param.17) | copy-start | bytes 4718596
  17.8 14.4 %copy-start.4 = (bf16[768,768]{1,0:T(8,128)(2,1)}, bf16[768,768]{1,0:T(8,128)(2,1)S(1)}, u32[]{:S(2)}) copy-start(bf16[768,768]{1,0:T(8,128)(2,1)S(1)} %collective-permute-done.2.refs_3_.refs_6_.refs_9_) | copy-start | bytes 3538948
  17.8 14.4 %copy-start.3 = (bf16[768,3072]{1,0:T(8,128)(2,1)}, bf16[768,3072]{1,0:T(8,128)(2,1)S(1)}, u32[]{:S(2)}) copy-start(bf16[768,3072]{1,0:T(8,128)(2,1)S(1)} %collective-permute-done.3.refs_5_.refs_8_.refs_7_) | copy-start | bytes 14155780
  17.9 14.4 %collective-permute-start.4 = (bf16[3072,768]{1,0:T(8,128)(2,1)S(1)}, bf16[3072,768]{1,0:T(8,128)(2,1)S(1)}, u32[]{:S(2)}, u32[]{:S(2)}) collective-permute-start(bf16[3072,768]{1,0:T(8,128)(2,1)S(1)} %bitcast.30), channel_id=1, source_target_pairs={{0,16},{16,0},{1,17},{17,1},{2,18},{18,2},{3,19},{19,3},{4,20},{20... | collective-permute-start | bytes 14155784 | tf_op jit(solution)/shard_map/ppermute | solution.py:1020
  32.3 9.0 %copy-start.2 = (bf16[3072,768]{1,0:T(8,128)(2,1)}, bf16[3072,768]{1,0:T(8,128)(2,1)S(1)}, u32[]{:S(2)}) copy-start(bf16[3072,768]{1,0:T(8,128)(2,1)S(1)} %collective-permute-done.4.refs_2_.refs_10_.refs_3_) | copy-start | bytes 14155780
  66.7 15.1 %collective-permute-start.5 = (bf16[4,192,1536]{2,1,0:T(8,128)(2,1)S(1)}, bf16[4,192,1536]{2,1,0:T(8,128)(2,1)S(1)}, u32[]{:S(2)}, u32[]{:S(2)}) collective-permute-start(bf16[4,192,1536]{2,1,0:T(8,128)(2,1)S(1)} %get-tuple-element.267), channel_id=1, source_target_pairs={{0,16},{16,0},{1,17},{17,1},{2,18},{18,2},{3,19},{19,3},{4,20},{20... | collective-permute-start | bytes 7077896 | tf_op jit(solution)/shard_map/ppermute | solution.py:1020
  80.6 1.2 copy-start.5
  81.8 1.4 copy-start.11
  83.2 24.2 %collective-permute-start.8 = (bf16[4,192,1536]{2,1,0:T(8,128)(2,1)}, bf16[4,192,1536]{2,1,0:T(8,128)(2,1)}, u32[]{:S(2)}, u32[]{:S(2)}) collective-permute-start(bf16[4,192,1536]{2,1,0:T(8,128)(2,1)} %get-tuple-element.287), channel_id=1, source_target_pairs={{0,16},{16,0},{1,17},{17,1},{2,18},{18,2},{3,19},{19,3},{4,20},{20... | collective-permute-start | bytes 7077896 | tf_op jit(solution)/shard_map/ppermute | solution.py:1020
  83.8 7.5 %copy-start.6 = (f32[512,768]{1,0:T(8,128)S(1)}, f32[512,768]{1,0:T(8,128)}, u32[]{:S(2)}) copy-start(f32[512,768]{1,0:T(8,128)} %copy-done.5) | copy-start | bytes 4718596
  86.8 20.6 %collective-permute-start.6 = (bf16[192,1536]{1,0:T(8,128)(2,1)S(1)}, bf16[192,1536]{1,0:T(8,128)(2,1)S(1)}, u32[]{:S(2)}, u32[]{:S(2)}) collective-permute-start(bf16[192,1536]{1,0:T(8,128)(2,1)S(1)} %get-tuple-element.285), channel_id=1, source_target_pairs={{0,4},{4,0},{8,12},{12,8},{1,5},{5,1},{9,13},{13,9},{2,6},{6,2},{1... | collective-permute-start | bytes 1769480 | tf_op jit(solution)/shard_map/ppermute | solution.py:1020
  89.8 17.6 %collective-permute-start.7 = (bf16[192,1536]{1,0:T(8,128)(2,1)S(1)}, bf16[192,1536]{1,0:T(8,128)(2,1)S(1)}, u32[]{:S(2)}, u32[]{:S(2)}) collective-permute-start(bf16[192,1536]{1,0:T(8,128)(2,1)S(1)} %get-tuple-element.286), channel_id=1, source_target_pairs={{0,8},{4,12},{8,0},{12,4},{1,9},{5,13},{9,1},{13,5},{2,10},{6,14},... | collective-permute-start | bytes 1769480 | tf_op jit(solution)/shard_map/ppermute | solution.py:1020
  107.4 24.6 %collective-permute-start.11 = (bf16[4,208,1536]{2,1,0:T(8,128)(2,1)S(1)}, bf16[4,208,1536]{2,1,0:T(8,128)(2,1)S(1)}, u32[]{:S(2)}, u32[]{:S(2)}) collective-permute-start(bf16[4,208,1536]{2,1,0:T(8,128)(2,1)S(1)} %get-tuple-element.307), channel_id=1, source_target_pairs={{0,16},{16,0},{1,17},{17,1},{2,18},{18,2},{3,19},{19,3},{4,20},{20... | collective-permute-start | bytes 7667720 | tf_op jit(solution)/shard_map/ppermute | solution.py:1020
  109.6 22.1 %collective-permute-start.9 = (bf16[288,1536]{1,0:T(8,128)(2,1)S(1)}, bf16[288,1536]{1,0:T(8,128)(2,1)S(1)}, u32[]{:S(2)}, u32[]{:S(2)}) collective-permute-start(bf16[288,1536]{1,0:T(8,128)(2,1)S(1)} %get-tuple-element.305), channel_id=1, source_target_pairs={{0,4},{4,0},{8,12},{12,8},{1,5},{5,1},{9,13},{13,9},{2,6},{6,2},{1... | collective-permute-start | bytes 2654216 | tf_op jit(solution)/shard_map/ppermute | solution.py:1020
  110.2 21.8 %collective-permute-start.10 = (bf16[288,1536]{1,0:T(8,128)(2,1)S(1)}, bf16[288,1536]{1,0:T(8,128)(2,1)S(1)}, u32[]{:S(2)}, u32[]{:S(2)}) collective-permute-start(bf16[288,1536]{1,0:T(8,128)(2,1)S(1)} %get-tuple-element.306), channel_id=1, source_target_pairs={{0,8},{4,12},{8,0},{12,4},{1,9},{5,13},{9,1},{13,5},{2,10},{6,14},... | collective-permute-start | bytes 2654216 | tf_op jit(solution)/shard_map/ppermute | solution.py:1020
  132.0 25.4 %collective-permute-start.15 = (bf16[4,192,1536]{2,1,0:T(8,128)(2,1)S(1)}, bf16[4,192,1536]{2,1,0:T(8,128)(2,1)S(1)}, u32[]{:S(2)}, u32[]{:S(2)}) collective-permute-start(bf16[4,192,1536]{2,1,0:T(8,128)(2,1)S(1)} %get-tuple-element.332), channel_id=1, source_target_pairs={{0,16},{16,0},{1,17},{17,1},{2,18},{18,2},{3,19},{19,3},{4,20},{20... | collective-permute-start | bytes 7077896 | tf_op jit(solution)/shard_map/ppermute | solution.py:1020
  133.2 24.2 %collective-permute-start.13 = (bf16[320,1536]{1,0:T(8,128)(2,1)S(1)}, bf16[320,1536]{1,0:T(8,128)(2,1)S(1)}, u32[]{:S(2)}, u32[]{:S(2)}) collective-permute-start(bf16[320,1536]{1,0:T(8,128)(2,1)S(1)} %get-tuple-element.330), channel_id=1, source_target_pairs={{0,4},{4,0},{8,12},{12,8},{1,5},{5,1},{9,13},{13,9},{2,6},{6,2},{1... | collective-permute-start | bytes 2949128 | tf_op jit(solution)/shard_map/ppermute | solution.py:1020
  134.7 21.8 %collective-permute-start.14 = (bf16[288,1536]{1,0:T(8,128)(2,1)S(1)}, bf16[288,1536]{1,0:T(8,128)(2,1)S(1)}, u32[]{:S(2)}, u32[]{:S(2)}) collective-permute-start(bf16[288,1536]{1,0:T(8,128)(2,1)S(1)} %get-tuple-element.331), channel_id=1, source_target_pairs={{0,8},{4,12},{8,0},{12,4},{1,9},{5,13},{9,1},{13,5},{2,10},{6,14},... | collective-permute-start | bytes 2654216 | tf_op jit(solution)/shard_map/ppermute | solution.py:1020
  135.2 15.2 %collective-permute-start.12 = (bf16[192,1536]{1,0:T(8,128)(2,1)S(1)}, bf16[192,1536]{1,0:T(8,128)(2,1)S(1)}, u32[]{:S(2)}, u32[]{:S(2)}) collective-permute-start(bf16[192,1536]{1,0:T(8,128)(2,1)S(1)} %get-tuple-element.329), channel_id=1, source_target_pairs={{0,1},{1,0},{2,3},{3,2},{4,5},{5,4},{6,7},{7,6},{8,9},{9,8},{10,11... | collective-permute-start | bytes 1769480 | tf_op jit(solution)/shard_map/ppermute | solution.py:1283
  157.4 24.3 %collective-permute-start.20 = (bf16[4,192,1536]{2,1,0:T(8,128)(2,1)S(1)}, bf16[4,192,1536]{2,1,0:T(8,128)(2,1)S(1)}, u32[]{:S(2)}, u32[]{:S(2)}) collective-permute-start(bf16[4,192,1536]{2,1,0:T(8,128)(2,1)S(1)} %get-tuple-element.360), channel_id=1, source_target_pairs={{0,16},{16,0},{1,17},{17,1},{2,18},{18,2},{3,19},{19,3},{4,20},{20... | collective-permute-start | bytes 7077896 | tf_op jit(solution)/shard_map/ppermute | solution.py:1020
  158.6 23.2 %collective-permute-start.19 = (bf16[304,1536]{1,0:T(8,128)(2,1)S(1)}, bf16[304,1536]{1,0:T(8,128)(2,1)S(1)}, u32[]{:S(2)}, u32[]{:S(2)}) collective-permute-start(bf16[304,1536]{1,0:T(8,128)(2,1)S(1)} %get-tuple-element.359), channel_id=1, source_target_pairs={{0,8},{4,12},{8,0},{12,4},{1,9},{5,13},{9,1},{13,5},{2,10},{6,14},... | collective-permute-start | bytes 2801672 | tf_op jit(solution)/shard_map/ppermute | solution.py:1020
  158.9 21.8 %collective-permute-start.18 = (bf16[288,1536]{1,0:T(8,128)(2,1)S(1)}, bf16[288,1536]{1,0:T(8,128)(2,1)S(1)}, u32[]{:S(2)}, u32[]{:S(2)}) collective-permute-start(bf16[288,1536]{1,0:T(8,128)(2,1)S(1)} %get-tuple-element.358), channel_id=1, source_target_pairs={{0,4},{4,0},{8,12},{12,8},{1,5},{5,1},{9,13},{13,9},{2,6},{6,2},{1... | collective-permute-start | bytes 2654216 | tf_op jit(solution)/shard_map/ppermute | solution.py:1020
  160.6 18.4 %collective-permute-start.16 = (bf16[192,1536]{1,0:T(8,128)(2,1)S(1)}, bf16[192,1536]{1,0:T(8,128)(2,1)S(1)}, u32[]{:S(2)}, u32[]{:S(2)}) collective-permute-start(bf16[192,1536]{1,0:T(8,128)(2,1)S(1)} %get-tuple-element.356), channel_id=1, source_target_pairs={{0,1},{1,0},{2,3},{3,2},{4,5},{5,4},{6,7},{7,6},{8,9},{9,8},{10,11... | collective-permute-start | bytes 1769480 | tf_op jit(solution)/shard_map/ppermute | solution.py:1283
  162.1 16.9 %collective-permute-start.17 = (bf16[192,1536]{1,0:T(8,128)(2,1)S(1)}, bf16[192,1536]{1,0:T(8,128)(2,1)S(1)}, u32[]{:S(2)}, u32[]{:S(2)}) collective-permute-start(bf16[192,1536]{1,0:T(8,128)(2,1)S(1)} %get-tuple-element.357.refs_0_), channel_id=1, source_target_pairs={{1,2},{2,1},{5,6},{6,5},{9,10},{10,9},{13,14},{14,13},{17,18},{18,... | collective-permute-start | bytes 1769480 | tf_op jit(solution)/shard_map/ppermute | solution.py:1283
  181.7 24.6 %collective-permute-start.27 = (bf16[4,208,1536]{2,1,0:T(8,128)(2,1)S(1)}, bf16[4,208,1536]{2,1,0:T(8,128)(2,1)S(1)}, u32[]{:S(2)}, u32[]{:S(2)}) collective-permute-start(bf16[4,208,1536]{2,1,0:T(8,128)(2,1)S(1)} %get-tuple-element.380), channel_id=1, source_target_pairs={{0,16},{16,0},{1,17},{17,1},{2,18},{18,2},{3,19},{19,3},{4,20},{20... | collective-permute-start | bytes 7667720 | tf_op jit(solution)/shard_map/ppermute | solution.py:1020
  183.0 22.1 %collective-permute-start.25 = (bf16[288,1536]{1,0:T(8,128)(2,1)S(1)}, bf16[288,1536]{1,0:T(8,128)(2,1)S(1)}, u32[]{:S(2)}, u32[]{:S(2)}) collective-permute-start(bf16[288,1536]{1,0:T(8,128)(2,1)S(1)} %get-tuple-element.378), channel_id=1, source_target_pairs={{0,4},{4,0},{8,12},{12,8},{1,5},{5,1},{9,13},{13,9},{2,6},{6,2},{1... | collective-permute-start | bytes 2654216 | tf_op jit(solution)/shard_map/ppermute | solution.py:1020
  184.5 21.8 %collective-permute-start.26 = (bf16[288,1536]{1,0:T(8,128)(2,1)S(1)}, bf16[288,1536]{1,0:T(8,128)(2,1)S(1)}, u32[]{:S(2)}, u32[]{:S(2)}) collective-permute-start(bf16[288,1536]{1,0:T(8,128)(2,1)S(1)} %get-tuple-element.379), channel_id=1, source_target_pairs={{0,8},{4,12},{8,0},{12,4},{1,9},{5,13},{9,1},{13,5},{2,10},{6,14},... | collective-permute-start | bytes 2654216 | tf_op jit(solution)/shard_map/ppermute | solution.py:1020
  185.2 16.2 %collective-permute-start.23 = (bf16[208,1536]{1,0:T(8,128)(2,1)S(1)}, bf16[208,1536]{1,0:T(8,128)(2,1)S(1)}, u32[]{:S(2)}, u32[]{:S(2)}) collective-permute-start(bf16[208,1536]{1,0:T(8,128)(2,1)S(1)} %get-tuple-element.376), channel_id=1, source_target_pairs={{0,1},{1,0},{2,3},{3,2},{4,5},{5,4},{6,7},{7,6},{8,9},{9,8},{10,11... | collective-permute-start | bytes 1916936 | tf_op jit(solution)/shard_map/ppermute | solution.py:1283
  187.0 0.7 collective-permute-start.24
  206.3 7.7 %copy-start.7 = (f32[512,768]{1,0:T(8,128)S(1)}, f32[512,768]{1,0:T(8,128)}, u32[]{:S(2)}) copy-start(f32[512,768]{1,0:T(8,128)} %get-tuple-element.361.refs_3_) | copy-start | bytes 4718596
  206.3 7.7 %copy-start.10 = (bf16[512,768]{1,0:T(8,128)(2,1)S(1)}, bf16[512,768]{1,0:T(8,128)(2,1)}, u32[]{:S(2)}) copy-start(bf16[512,768]{1,0:T(8,128)(2,1)} %get-tuple-element.288.refs_4_) | copy-start | bytes 2359300
  207.7 23.1 %collective-permute-start.30 = (bf16[320,1536]{1,0:T(8,128)(2,1)S(1)}, bf16[320,1536]{1,0:T(8,128)(2,1)S(1)}, u32[]{:S(2)}, u32[]{:S(2)}) collective-permute-start(bf16[320,1536]{1,0:T(8,128)(2,1)S(1)} %get-tuple-element.395), channel_id=1, source_target_pairs={{0,4},{4,0},{8,12},{12,8},{1,5},{5,1},{9,13},{13,9},{2,6},{6,2},{1... | collective-permute-start | bytes 2949128 | tf_op jit(solution)/shard_map/ppermute | solution.py:1020
  208.3 20.8 %collective-permute-start.31 = (bf16[288,1536]{1,0:T(8,128)(2,1)S(1)}, bf16[288,1536]{1,0:T(8,128)(2,1)S(1)}, u32[]{:S(2)}, u32[]{:S(2)}) collective-permute-start(bf16[288,1536]{1,0:T(8,128)(2,1)S(1)} %get-tuple-element.396), channel_id=1, source_target_pairs={{0,8},{4,12},{8,0},{12,4},{1,9},{5,13},{9,1},{13,5},{2,10},{6,14},... | collective-permute-start | bytes 2654216 | tf_op jit(solution)/shard_map/ppermute | solution.py:1020
  209.0 17.2 %collective-permute-start.29 = (bf16[208,1536]{1,0:T(8,128)(2,1)S(1)}, bf16[208,1536]{1,0:T(8,128)(2,1)S(1)}, u32[]{:S(2)}, u32[]{:S(2)}) collective-permute-start(bf16[208,1536]{1,0:T(8,128)(2,1)S(1)} %get-tuple-element.394.refs_2_), channel_id=1, source_target_pairs={{1,2},{2,1},{5,6},{6,5},{9,10},{10,9},{13,14},{14,13},{17,18},{18,... | collective-permute-start | bytes 1916936 | tf_op jit(solution)/shard_map/ppermute | solution.py:1283
  209.7 16.5 %collective-permute-start.28 = (bf16[192,1536]{1,0:T(8,128)(2,1)S(1)}, bf16[192,1536]{1,0:T(8,128)(2,1)S(1)}, u32[]{:S(2)}, u32[]{:S(2)}) collective-permute-start(bf16[192,1536]{1,0:T(8,128)(2,1)S(1)} %get-tuple-element.393), channel_id=1, source_target_pairs={{0,1},{1,0},{2,3},{3,2},{4,5},{5,4},{6,7},{7,6},{8,9},{9,8},{10,11... | collective-permute-start | bytes 1769480 | tf_op jit(solution)/shard_map/ppermute | solution.py:1283
  214.2 37.7 %collective-permute-start.21 = (f32[512,768]{1,0:T(8,128)S(1)}, f32[512,768]{1,0:T(8,128)S(1)}, u32[]{:S(2)}, u32[]{:S(2)}) collective-permute-start(f32[512,768]{1,0:T(8,128)S(1)} %convert_select_fusion), channel_id=1, source_target_pairs={{0,16},{16,0},{1,17},{17,1},{2,18},{18,2},{3,19},{19,3},{4,20},{20... | collective-permute-start | bytes 4718600 | tf_op jit(solution)/shard_map/ppermute | solution.py:1020
  230.8 6.0 %copy-start.8 = (bf16[512,768]{1,0:T(8,128)(2,1)S(1)}, bf16[512,768]{1,0:T(8,128)(2,1)}, u32[]{:S(2)}) copy-start(bf16[512,768]{1,0:T(8,128)(2,1)} %get-tuple-element.272.refs_3_.refs_0_) | copy-start | bytes 2359300
  230.8 6.0 %copy-start.9 = (bf16[512,768]{1,0:T(8,128)(2,1)S(1)}, bf16[512,768]{1,0:T(8,128)(2,1)}, u32[]{:S(2)}) copy-start(bf16[512,768]{1,0:T(8,128)(2,1)} %get-tuple-element.362.refs_1_) | copy-start | bytes 2359300
  231.8 14.8 %collective-permute-start.32 = (bf16[208,1536]{1,0:T(8,128)(2,1)S(1)}, bf16[208,1536]{1,0:T(8,128)(2,1)S(1)}, u32[]{:S(2)}, u32[]{:S(2)}) collective-permute-start(bf16[208,1536]{1,0:T(8,128)(2,1)S(1)} %get-tuple-element.407), channel_id=1, source_target_pairs={{0,1},{1,0},{2,3},{3,2},{4,5},{5,4},{6,7},{7,6},{8,9},{9,8},{10,11... | collective-permute-start | bytes 1916936 | tf_op jit(solution)/shard_map/ppermute | solution.py:1283
  233.4 9.7 %collective-permute-start.33 = (bf16[192,1536]{1,0:T(8,128)(2,1)S(1)}, bf16[192,1536]{1,0:T(8,128)(2,1)S(1)}, u32[]{:S(2)}, u32[]{:S(2)}) collective-permute-start(bf16[192,1536]{1,0:T(8,128)(2,1)S(1)} %get-tuple-element.408.refs_2_), channel_id=1, source_target_pairs={{1,2},{2,1},{5,6},{6,5},{9,10},{10,9},{13,14},{14,13},{17,18},{18,... | collective-permute-start | bytes 1769480 | tf_op jit(solution)/shard_map/ppermute | solution.py:1283
  234.3 7.2 %collective-permute-start.34 = (bf16[96,1536]{1,0:T(8,128)(2,1)S(1)}, bf16[96,1536]{1,0:T(8,128)(2,1)S(1)}, u32[]{:S(2)}, u32[]{:S(2)}) collective-permute-start(bf16[96,1536]{1,0:T(8,128)(2,1)S(1)} %get-tuple-element.409), channel_id=1, source_target_pairs={{0,4},{4,0},{8,12},{12,8},{1,5},{5,1},{9,13},{13,9},{2,6},{6,2},{1... | collective-permute-start | bytes 884744 | tf_op jit(solution)/shard_map/ppermute | solution.py:1020
  235.2 7.9 %collective-permute-start.35 = (bf16[112,1536]{1,0:T(8,128)(2,1)S(1)}, bf16[112,1536]{1,0:T(8,128)(2,1)S(1)}, u32[]{:S(2)}, u32[]{:S(2)}) collective-permute-start(bf16[112,1536]{1,0:T(8,128)(2,1)S(1)} %get-tuple-element.410), channel_id=1, source_target_pairs={{0,8},{4,12},{8,0},{12,4},{1,9},{5,13},{9,1},{13,5},{2,10},{6,14},... | collective-permute-start | bytes 1032200 | tf_op jit(solution)/shard_map/ppermute | solution.py:1020
  241.5 10.4 %collective-permute-start.22 = (bf16[512,768]{1,0:T(8,128)(2,1)S(1)}, bf16[512,768]{1,0:T(8,128)(2,1)S(1)}, u32[]{:S(2)}, u32[]{:S(2)}) collective-permute-start(bf16[512,768]{1,0:T(8,128)(2,1)S(1)} %broadcast_select_fusion), channel_id=1, source_target_pairs={{0,16},{16,0},{1,17},{17,1},{2,18},{18,2},{3,19},{19,3},{4,20},{20... | collective-permute-start | bytes 2359304 | tf_op jit(solution)/shard_map/ppermute | solution.py:1020
  247.6 15.7 %collective-permute-start.36 = (bf16[208,1536]{1,0:T(8,128)(2,1)S(1)}, bf16[208,1536]{1,0:T(8,128)(2,1)S(1)}, u32[]{:S(2)}, u32[]{:S(2)}) collective-permute-start(bf16[208,1536]{1,0:T(8,128)(2,1)S(1)} %get-tuple-element.418), channel_id=1, source_target_pairs={{0,1},{1,0},{2,3},{3,2},{4,5},{5,4},{6,7},{7,6},{8,9},{9,8},{10,11... | collective-permute-start | bytes 1916936 | tf_op jit(solution)/shard_map/ppermute | solution.py:1283
  251.2 0.7 collective-permute-start.37
  251.9 18.4 %copy-start.13 = (bf16[512,768]{1,0:T(8,128)(2,1)}, bf16[512,768]{1,0:T(8,128)(2,1)S(1)}, u32[]{:S(2)}) copy-start(bf16[512,768]{1,0:T(8,128)(2,1)S(1)} %collective-permute-done.22.refs_2_) | copy-start | bytes 2359300
  251.9 18.3 %copy-start.12 = (f32[512,768]{1,0:T(8,128)}, f32[512,768]{1,0:T(8,128)S(1)}, u32[]{:S(2)}) copy-start(f32[512,768]{1,0:T(8,128)S(1)} %collective-permute-done.21.refs_5_) | copy-start | bytes 4718596
  264.2 16.3 %collective-permute-start.39 = (bf16[208,1536]{1,0:T(8,128)(2,1)S(1)}, bf16[208,1536]{1,0:T(8,128)(2,1)S(1)}, u32[]{:S(2)}, u32[]{:S(2)}) collective-permute-start(bf16[208,1536]{1,0:T(8,128)(2,1)S(1)} %get-tuple-element.430.refs_3_), channel_id=1, source_target_pairs={{1,2},{2,1},{5,6},{6,5},{9,10},{10,9},{13,14},{14,13},{17,18},{18,... | collective-permute-start | bytes 1916936 | tf_op jit(solution)/shard_map/ppermute | solution.py:1283
  264.9 15.6 %collective-permute-start.38 = (bf16[192,1536]{1,0:T(8,128)(2,1)S(1)}, bf16[192,1536]{1,0:T(8,128)(2,1)S(1)}, u32[]{:S(2)}, u32[]{:S(2)}) collective-permute-start(bf16[192,1536]{1,0:T(8,128)(2,1)S(1)} %get-tuple-element.429), channel_id=1, source_target_pairs={{0,1},{1,0},{2,3},{3,2},{4,5},{5,4},{6,7},{7,6},{8,9},{9,8},{10,11... | collective-permute-start | bytes 1769480 | tf_op jit(solution)/shard_map/ppermute | solution.py:1283
  281.3 12.3 %collective-permute-start.42 = (bf16[208,1536]{1,0:T(8,128)(2,1)S(1)}, bf16[208,1536]{1,0:T(8,128)(2,1)S(1)}, u32[]{:S(2)}, u32[]{:S(2)}) collective-permute-start(bf16[208,1536]{1,0:T(8,128)(2,1)S(1)} %get-tuple-element.442), channel_id=1, source_target_pairs={{0,1},{1,0},{2,3},{3,2},{4,5},{5,4},{6,7},{7,6},{8,9},{9,8},{10,11... | collective-permute-start | bytes 1916936 | tf_op jit(solution)/shard_map/ppermute | solution.py:1283
  293.5 9.1 %copy-start.1 = (bf16[8,128,768]{2,1,0:T(8,128)(2,1)S(1)}, bf16[8,128,768]{2,1,0:T(8,128)(2,1)}, u32[]{:S(2)}) copy-start(bf16[8,128,768]{2,1,0:T(8,128)(2,1)} %param.14) | copy-start | bytes 4718596
  294.3 3.8 %collective-permute-start.43 = (bf16[208,1536]{1,0:T(8,128)(2,1)S(1)}, bf16[208,1536]{1,0:T(8,128)(2,1)S(1)}, u32[]{:S(2)}, u32[]{:S(2)}) collective-permute-start(bf16[208,1536]{1,0:T(8,128)(2,1)S(1)} %get-tuple-element.445), channel_id=1, source_target_pairs={{0,16},{16,0},{1,17},{17,1},{2,18},{18,2},{3,19},{19,3},{4,20},{20... | collective-permute-start | bytes 1916936 | tf_op jit(solution)/shard_map/ppermute | solution.py:1020
  294.3 2.9 collective-permute-start.40
  294.8 3.3 %collective-permute-start.41 = (bf16[192,1536]{1,0:T(8,128)(2,1)S(1)}, bf16[192,1536]{1,0:T(8,128)(2,1)S(1)}, u32[]{:S(2)}, u32[]{:S(2)}) collective-permute-start(bf16[192,1536]{1,0:T(8,128)(2,1)S(1)} %get-tuple-element.440), channel_id=1, source_target_pairs={{0,16},{16,0},{1,17},{17,1},{2,18},{18,2},{3,19},{19,3},{4,20},{20... | collective-permute-start | bytes 1769480 | tf_op jit(solution)/shard_map/ppermute | solution.py:1020
